TPU v7x, 32 devices: a whole 2x2x4 slice. The times are simulated.
32 devices in a mesh: ctx: 8 (over y, x, core), sp: 4 (over z).
Axes of the slice: x: 2, y: 2, z: 4, core: 2. Of those that a mesh axis runs over, the one named last changes fastest.
Arguments:
- hidden_in: bfloat16 [2, 6144, 1024], P(None, ('ctx', 'sp')), may hold values from -6 to 6
- out_grad: bfloat16 [2, 6144, 1024], P(None, ('ctx', 'sp')), may hold values from -6 to 6
- lengths: int32 [2], replicated, may hold values from 1536 to 6144, as said below
- input_gain: bfloat16 [1024], P(('ctx', 'sp')), may hold values from 0.5 to 1.5
- attn_in_weight: bfloat16 [1024, 768], P(('ctx', 'sp')), may hold values from -0.1875 to 0.1875
- attn_out_weight: bfloat16 [512, 1024], P(('ctx', 'sp')), may hold values from -1 to 1
- zgate_weight: bfloat16 [1024, 1536], P(('ctx', 'sp')), may hold values from -0.1875 to 0.1875
- mixer_in_weight: bfloat16 [1024, 1792], P(('ctx', 'sp')), may hold values from -0.1875 to 0.1875
- step_weight: bfloat16 [1024, 24], P(('ctx', 'sp')), may hold values from -0.75 to 0.75
- conv_weight: bfloat16 [4, 1792], P(None, ('ctx', 'sp')), may hold values from -2.5 to 2.5
- conv_bias: bfloat16 [1792], P(('ctx', 'sp')), may hold values from -2.5 to 2.5
- step_bias: float32 [24], P('sp'), may hold values from -4 to -2
- decay_log: float32 [24], P('sp'), may hold values from -10 to -1
- skip_scale: float32 [24], P('sp'), may hold values from 0.5 to 1.5
- mixer_gain: bfloat16 [1536], P(('ctx', 'sp')), may hold values from 0.5 to 1.5
- mixer_out_weight: bfloat16 [1536, 1024], P(('ctx', 'sp')), may hold values from -0.15625 to 0.15625
- post_gain: bfloat16 [1024], P(('ctx', 'sp')), may hold values from 0.5 to 1.5
- gate_weight: bfloat16 [1024, 2048], P(('ctx', 'sp')), may hold values from -0.1875 to 0.1875
- up_weight: bfloat16 [1024, 2048], P(('ctx', 'sp')), may hold values from -0.1875 to 0.1875
- down_weight: bfloat16 [2048, 1024], P(('ctx', 'sp')), may hold values from -0.125 to 0.125
Outputs:
- layer_out: bfloat16 [2, 6144, 1024], P(None, ('ctx', 'sp'))
- input_grad: float32 [2, 6144, 1024], P(None, ('ctx', 'sp'))
- grad_input_gain: float32 [1024], P(('ctx', 'sp'))
- grad_attn_in: float32 [1024, 768], P(('ctx', 'sp'))
- grad_attn_out: float32 [512, 1024], P(('ctx', 'sp'))
- grad_zgate: float32 [1024, 1536], P(('ctx', 'sp'))
- grad_mixer_in: float32 [1024, 1792], P(('ctx', 'sp'))
- grad_step_weight: float32 [1024, 24], P(('ctx', 'sp'))
- grad_conv_weight: float32 [4, 1792], P(None, ('ctx', 'sp'))
- grad_conv_bias: float32 [1792], P(('ctx', 'sp'))
- grad_step_bias: float32 [24], P('sp')
- grad_decay_log: float32 [24], P('sp')
- grad_skip_scale: float32 [24], P('sp')
- grad_mixer_gain: float32 [1536], P(('ctx', 'sp'))
- grad_mixer_out: float32 [1536, 1024], P(('ctx', 'sp'))
- grad_post_gain: float32 [1024], P(('ctx', 'sp'))
- grad_gate: float32 [1024, 2048], P(('ctx', 'sp'))
- grad_up: float32 [1024, 2048], P(('ctx', 'sp'))
- grad_down: float32 [2048, 1024], P(('ctx', 'sp'))
Inputs may be any that keep to these rules, and one draw needn't show every extreme that they name: Slot b's valid positions are its first lengths[b]; in every draw some slot is full, with 6144.
All inputs are finite; a program needn't handle non-finite values.
Results may differ from a plain program's by a relative error of at most 0.025.
Values may be sent and summed in bfloat16 or wider, within the bound.
No kernel may reach another device: no remote copies, remote signals or barrier semaphores. Data moves between devices by JAX's collectives and lax.ppermute only.
A program may use at most 256 MiB of HBM per device.

v0:
```python
import math

import jax
import jax.numpy as jnp
from jax import lax
from jax.sharding import PartitionSpec as P

QH = 8
KVH = 2
HD = 64
SH = 24
SHD = 64
NS = 128
KC = 4


MASKED = -1e30


def passed_along(x, axis, by):
    length = lax.axis_size(axis)
    pairs = [(i, i + by) for i in range(length) if 0 <= i + by < length]
    return lax.ppermute(x, axis, pairs)


def entering(x, axis, combine, identity, reverse):
    length, place = (lax.axis_size(axis), lax.axis_index(axis))
    everything = jax.tree.map(
        lambda part, kind: lax.all_gather(part.astype(kind), axis), x, (jnp.bfloat16, jnp.bfloat16)
    )
    start = jax.tree.map(
        lambda part, zero: jnp.broadcast_to(jnp.asarray(zero, part.dtype), part.shape), x, identity
    )

    def hop(k, before):
        at = length - 1 - k if reverse else k
        reached = at > place if reverse else at < place
        new = combine(
            before, jax.tree.map(lambda part, own: part[at].astype(own.dtype), everything, x)
        )
        return jax.tree.map(lambda a, b: jnp.where(reached, a, b), new, before)

    return lax.fori_loop(0, length, hop, start)


def product(form, left, right):
    return jnp.einsum(
        form, left, right, precision=lax.Precision.HIGHEST, preferred_element_type=jnp.float32
    )


def forward_product(left, right):
    return jnp.dot(left, right, preferred_element_type=jnp.float32)


def weight_product(left, right):
    return lax.dot_general(
        left, right, (((0,), (0,)), ((), ())), preferred_element_type=jnp.float32
    )


def back_product(left, right):
    return lax.dot_general(
        left, right, (((1,), (1,)), ((), ())), preferred_element_type=jnp.float32
    )


def rms_scale(value, gain):
    return value * lax.rsqrt(jnp.mean(value * value, axis=-1, keepdims=True) + 1e-05) * gain


def gate_norm(ssd_values, gate_values, gain):
    return rms_scale(ssd_values * jax.nn.silu(gate_values), gain)


def rotary_tables(positions, width):
    half_width = width // 2
    inverse = 100000000000.0 ** (-jnp.arange(half_width, dtype=jnp.float32) * 2.0 / width)
    angles = positions.astype(jnp.float32)[:, None] * inverse[None, :]
    return (jnp.cos(angles), jnp.sin(angles))


def rotate(value, cos_table, sin_table):
    half_width = value.shape[-1] // 2
    first_half = value[..., :half_width]
    second_half = value[..., half_width:]
    cos_part = cos_table[:, None, :]
    sin_part = sin_table[:, None, :]
    return jnp.concatenate(
        [
            first_half * cos_part - second_half * sin_part,
            second_half * cos_part + first_half * sin_part,
        ],
        axis=-1,
    )


def conv_apply(padded, weight, bias):
    tap_count = weight.shape[0]
    out_rows = padded.shape[-2] - tap_count + 1
    running = bias
    for tap_index in range(tap_count):
        running = running + weight[tap_index] * lax.slice_in_dim(
            padded, tap_index, tap_index + out_rows, axis=padded.ndim - 2
        )
    return jax.nn.silu(running)


def block_local(features, inject, readout, step_sizes, decay_rates):
    log_decay = jnp.cumsum(step_sizes * decay_rates[None, :], axis=0)
    length = features.shape[0]
    causal = jnp.arange(length)[:, None] >= jnp.arange(length)[None, :]
    gap_logs = jnp.where(causal[:, :, None], log_decay[:, None, :] - log_decay[None, :, :], MASKED)
    kernel = (
        product("tn,jn->tj", readout, inject)[:, :, None]
        * jnp.exp(gap_logs)
        * step_sizes[None, :, :]
    )
    within = product("tjh,jhp->thp", kernel, features)
    tail_decay = jnp.exp(log_decay[-1][None, :] - log_decay) * step_sizes
    local_state = product("jhp,jn->hpn", features * tail_decay[:, :, None], inject)
    return (within, jnp.exp(log_decay[-1]), local_state, log_decay)


def block_carry(readout, log_decay, state):
    return jnp.exp(log_decay)[:, :, None] * product("tn,hpn->thp", readout, state)


def mixer_heads(features, inject, readout, step_raw, bias, log_rates, skip_terms, state):
    step_sizes = jax.nn.softplus(step_raw + bias[None, :])
    decay_rates = -jnp.exp(log_rates)
    within, decay, local_state, log_decay = block_local(
        features, inject, readout, step_sizes, decay_rates
    )
    output = within + block_carry(readout, log_decay, state) + skip_terms[None, :, None] * features
    return (output, decay, local_state)


def combine(earlier, later):
    return (earlier[0] * later[0], later[0][..., None, None] * earlier[1] + later[1])


def shards(
    hidden_in,
    out_grad,
    lengths,
    input_gain,
    attn_in_weight,
    attn_out_weight,
    zgate_weight,
    mixer_in_weight,
    step_weight,
    conv_weight,
    conv_bias,
    step_bias,
    decay_log,
    skip_scale,
    mixer_gain,
    mixer_out_weight,
    post_gain,
    gate_weight,
    up_weight,
    down_weight,
):
    groups = lax.axis_size("sp")
    span_count = lax.axis_size("ctx")
    span_index = lax.axis_index("ctx")
    piece_index = lax.axis_index("sp")
    slots, piece, width = hidden_in.shape
    span = piece * groups
    seq_rows = span * span_count
    head_share = QH // groups
    head_group = QH // KVH
    mixer_share = SH // groups
    query_width = head_share * HD
    mixer_width = mixer_share * SHD
    ssd_width = SH * SHD
    conv_width = ssd_width + 2 * NS
    kv_owner = [dest * head_share // head_group for dest in range(groups)]
    scale = HD ** (-0.5)
    (
        full_gain_in,
        full_attn_in,
        full_attn_out,
        full_zgate,
        full_mixer_in,
        full_step,
        full_conv_weight,
        full_conv_bias,
        full_mixer_gain,
        full_mixer_out,
        full_post_gain,
        full_gate,
        full_up,
        full_down,
    ) = (
        lax.all_gather(input_gain, ("ctx", "sp"), axis=0, tiled=True),
        lax.all_gather(attn_in_weight, ("ctx", "sp"), axis=0, tiled=True),
        lax.all_gather(attn_out_weight, ("ctx", "sp"), axis=0, tiled=True),
        lax.all_gather(zgate_weight, ("ctx", "sp"), axis=0, tiled=True),
        lax.all_gather(mixer_in_weight, ("ctx", "sp"), axis=0, tiled=True),
        lax.all_gather(step_weight, ("ctx", "sp"), axis=0, tiled=True),
        lax.all_gather(conv_weight, ("ctx", "sp"), axis=1, tiled=True),
        lax.all_gather(conv_bias, ("ctx", "sp"), axis=0, tiled=True),
        lax.all_gather(mixer_gain, ("ctx", "sp"), axis=0, tiled=True),
        lax.all_gather(mixer_out_weight, ("ctx", "sp"), axis=0, tiled=True),
        lax.all_gather(post_gain, ("ctx", "sp"), axis=0, tiled=True),
        lax.all_gather(gate_weight, ("ctx", "sp"), axis=0, tiled=True),
        lax.all_gather(up_weight, ("ctx", "sp"), axis=0, tiled=True),
        lax.all_gather(down_weight, ("ctx", "sp"), axis=0, tiled=True),
    )
    positions = span_index * span + piece_index * piece + jnp.arange(piece, dtype=jnp.int32)
    valid_rows = (positions[None, :] < lengths[:, None]).astype(jnp.float32)
    tokens = hidden_in.astype(jnp.float32)
    gain_in = full_gain_in.astype(jnp.float32)
    normed = rms_scale(tokens, gain_in).astype(jnp.bfloat16)
    rows = normed.reshape(slots * piece, width)
    linear = forward_product(rows, full_attn_in).reshape(slots, piece, -1)
    query_lin = linear[..., : QH * HD].reshape(slots, piece, QH, HD)
    key_lin = linear[..., QH * HD : (QH + KVH) * HD].reshape(slots, piece, KVH, HD)
    value_heads = linear[..., (QH + KVH) * HD :].reshape(slots, piece, KVH, HD).astype(jnp.bfloat16)
    cos_table, sin_table = rotary_tables(positions, HD)
    queries = rotate(query_lin, cos_table, sin_table).astype(jnp.bfloat16)
    key_heads = rotate(key_lin, cos_table, sin_table).astype(jnp.bfloat16)
    mixer_gate = (
        forward_product(rows, full_zgate).astype(jnp.bfloat16).reshape(slots, piece, ssd_width)
    )
    mixed_raw = (
        forward_product(rows, full_mixer_in).astype(jnp.bfloat16).reshape(slots, piece, conv_width)
    )
    step_raw = forward_product(rows, full_step).astype(jnp.bfloat16).reshape(slots, piece, SH)
    rim_rows = passed_along(mixed_raw[:, piece - KC + 1 :], ("ctx", "sp"), 1)
    padded = jnp.concatenate([rim_rows, mixed_raw], axis=1).astype(jnp.float32)
    conv_taps = full_conv_weight.astype(jnp.float32)
    conv_shift = full_conv_bias.astype(jnp.float32)
    conv_out = conv_apply(padded, conv_taps, conv_shift).astype(jnp.bfloat16)
    outgoing = []
    for dest in range(groups):
        outgoing.append(
            jnp.concatenate(
                [
                    queries[:, :, dest * head_share : (dest + 1) * head_share].reshape(
                        slots, piece, query_width
                    ),
                    key_heads[:, :, kv_owner[dest]],
                    value_heads[:, :, kv_owner[dest]],
                    conv_out[..., dest * mixer_width : (dest + 1) * mixer_width],
                    conv_out[..., ssd_width:],
                ],
                axis=-1,
            )
        )
    outgoing = jnp.stack(outgoing, axis=2)
    step_parts = step_raw.reshape(slots, piece, groups, mixer_share)
    incoming, step_in = (
        lax.all_to_all(outgoing, "sp", split_axis=2, concat_axis=1, tiled=True),
        lax.all_to_all(step_parts, "sp", split_axis=2, concat_axis=1, tiled=True),
    )
    incoming = incoming[:, :, 0]
    step_in = step_in[:, :, 0].astype(jnp.float32)
    head_queries = incoming[..., :query_width].reshape(slots, span, head_share, HD)
    head_kv = incoming[..., query_width : query_width + 2 * HD]
    offset = query_width + 2 * HD
    features = (
        incoming[..., offset : offset + mixer_width]
        .reshape(slots, span, mixer_share, SHD)
        .astype(jnp.float32)
    )
    inject = incoming[..., offset + mixer_width : offset + mixer_width + NS].astype(jnp.float32)
    readout = incoming[..., offset + mixer_width + NS :].astype(jnp.float32)
    query_pos = span_index * span + jnp.arange(span, dtype=jnp.int32)
    last_query = span_index * span + span - 1

    def key_blocks(piece_kv, carry, compute):
        rows_here = piece_kv.shape[1]
        size = math.gcd(rows_here, span)

        def visit(index, state):
            first_key = index * size
            block = lax.dynamic_slice_in_dim(piece_kv, index * size, size, 1)
            key_pos = first_key + jnp.arange(size, dtype=jnp.int32)
            causal_keep = key_pos[None, :] <= query_pos[:, None]
            return lax.cond(
                first_key > last_query,
                lambda current: current,
                lambda current: compute(current, block, causal_keep, first_key),
                state,
            )

        return lax.fori_loop(0, rows_here // size, visit, carry)

    def forward_block(state, block, causal_keep, first_key):
        row_max, row_sum, accum = state
        scores = (
            jnp.einsum(
                "sqhd,skd->shqk", head_queries, block[..., :HD], preferred_element_type=jnp.float32
            )
            * scale
        )
        masked = jnp.where(causal_keep, scores, MASKED)
        new_max = jnp.maximum(row_max, jnp.max(masked, axis=-1))
        weights_now = jnp.where(causal_keep, jnp.exp(scores - new_max[..., None]), 0.0)
        ratio = jnp.exp(row_max - new_max)
        row_sum = row_sum * ratio + jnp.sum(weights_now, axis=-1)
        accum = accum * ratio[..., None] + jnp.einsum(
            "shqk,skd->shqd",
            weights_now.astype(jnp.bfloat16),
            block[..., HD:],
            preferred_element_type=jnp.float32,
        )
        return (new_max, row_sum, accum)

    initial = (
        jnp.full((slots, head_share, span), MASKED, jnp.float32),
        jnp.zeros((slots, head_share, span), jnp.float32),
        jnp.zeros((slots, head_share, span, HD), jnp.float32),
    )
    row_max, row_sum, accum = key_blocks(
        lax.all_gather(head_kv, "ctx", axis=1, tiled=True), initial, forward_block
    )
    attended = jnp.transpose(accum / row_sum[..., None], (0, 2, 1, 3)).astype(jnp.bfloat16)
    log_total = row_max + jnp.log(row_sum)
    step_sizes = jax.nn.softplus(step_in + step_bias)
    decay_rates = -jnp.exp(decay_log)
    within, decay, local_state, log_decay = lax.map(
        lambda items: block_local(items[0], items[1], items[2], items[3], decay_rates),
        (features, inject, readout, step_sizes),
    )
    identity = (jnp.ones_like(decay), jnp.zeros_like(local_state))
    _, state_in = entering((decay, local_state), "ctx", combine, identity, False)
    mixer_value = (
        within
        + jnp.exp(log_decay)[..., None] * product("stn,shpn->sthp", readout, state_in)
        + skip_scale[None, None, :, None] * features
    )
    mixer_low = mixer_value.astype(jnp.bfloat16)
    head_rows = jnp.concatenate(
        [attended.reshape(slots, span, query_width), mixer_low.reshape(slots, span, mixer_width)],
        axis=-1,
    )[:, :, None]
    returned = lax.all_to_all(head_rows, "sp", split_axis=1, concat_axis=2, tiled=True)
    attn_rows = returned[..., :query_width].reshape(slots * piece, QH * HD)
    ssd_rows = returned[..., query_width:].reshape(slots, piece, ssd_width)
    attn_part = forward_product(attn_rows, full_attn_out)
    gain_mixer = full_mixer_gain.astype(jnp.float32)
    gated = gate_norm(
        ssd_rows.astype(jnp.float32), mixer_gate.astype(jnp.float32), gain_mixer
    ).astype(jnp.bfloat16)
    gated_rows = gated.reshape(slots * piece, ssd_width)
    mixer_part = forward_product(gated_rows, full_mixer_out)
    residual = tokens + (attn_part + mixer_part).reshape(slots, piece, width)
    gain_post = full_post_gain.astype(jnp.float32)
    post_norm = rms_scale(residual, gain_post).astype(jnp.bfloat16).reshape(slots * piece, width)
    gate_lin = forward_product(post_norm, full_gate)
    up_lin = forward_product(post_norm, full_up)
    hidden = (jax.nn.silu(gate_lin) * up_lin).astype(jnp.bfloat16)
    layer_out = (
        valid_rows[..., None]
        * (residual + forward_product(hidden, full_down).reshape(slots, piece, width))
    ).astype(jnp.bfloat16)
    (
        full_gain_in,
        full_attn_in,
        full_attn_out,
        full_zgate,
        full_mixer_in,
        full_step,
        full_conv_weight,
        full_conv_bias,
        full_mixer_gain,
        full_mixer_out,
        full_post_gain,
        full_gate,
        full_up,
        full_down,
    ) = (
        lax.all_gather(input_gain, ("ctx", "sp"), axis=0, tiled=True),
        lax.all_gather(attn_in_weight, ("ctx", "sp"), axis=0, tiled=True),
        lax.all_gather(attn_out_weight, ("ctx", "sp"), axis=0, tiled=True),
        lax.all_gather(zgate_weight, ("ctx", "sp"), axis=0, tiled=True),
        lax.all_gather(mixer_in_weight, ("ctx", "sp"), axis=0, tiled=True),
        lax.all_gather(step_weight, ("ctx", "sp"), axis=0, tiled=True),
        lax.all_gather(conv_weight, ("ctx", "sp"), axis=1, tiled=True),
        lax.all_gather(conv_bias, ("ctx", "sp"), axis=0, tiled=True),
        lax.all_gather(mixer_gain, ("ctx", "sp"), axis=0, tiled=True),
        lax.all_gather(mixer_out_weight, ("ctx", "sp"), axis=0, tiled=True),
        lax.all_gather(post_gain, ("ctx", "sp"), axis=0, tiled=True),
        lax.all_gather(gate_weight, ("ctx", "sp"), axis=0, tiled=True),
        lax.all_gather(up_weight, ("ctx", "sp"), axis=0, tiled=True),
        lax.all_gather(down_weight, ("ctx", "sp"), axis=0, tiled=True),
    )
    grad_rows = out_grad.astype(jnp.float32) * valid_rows[..., None]
    grad_low = grad_rows.astype(jnp.bfloat16).reshape(slots * piece, width)
    grad_down = weight_product(hidden, grad_low)
    grad_hidden = back_product(grad_low, full_down)
    _, swiglu_back = jax.vjp(lambda gate_in, up_in: jax.nn.silu(gate_in) * up_in, gate_lin, up_lin)
    grad_gate_lin, grad_up_lin = swiglu_back(grad_hidden)
    grad_gate_lin = grad_gate_lin.astype(jnp.bfloat16)
    grad_up_lin = grad_up_lin.astype(jnp.bfloat16)
    grad_gate = weight_product(post_norm, grad_gate_lin)
    grad_up = weight_product(post_norm, grad_up_lin)
    grad_post = back_product(grad_gate_lin, full_gate) + back_product(grad_up_lin, full_up)
    _, post_back = jax.vjp(rms_scale, residual, gain_post)
    grad_resid_norm, grad_post_gain = post_back(grad_post.reshape(slots, piece, width))
    grad_residual = grad_rows + grad_resid_norm
    grad_mixed = grad_residual.astype(jnp.bfloat16).reshape(slots * piece, width)
    grad_attn_out = weight_product(attn_rows, grad_mixed)
    grad_mixer_out = weight_product(gated_rows, grad_mixed)
    grad_attended = (
        back_product(grad_mixed, full_attn_out).astype(jnp.bfloat16).reshape(slots, piece, QH * HD)
    )
    grad_gated = back_product(grad_mixed, full_mixer_out).reshape(slots, piece, ssd_width)
    _, norm_back = jax.vjp(
        gate_norm, ssd_rows.astype(jnp.float32), mixer_gate.astype(jnp.float32), gain_mixer
    )
    grad_ssd, grad_gate_z, grad_mixer_gain = norm_back(grad_gated)
    grad_ssd = grad_ssd.astype(jnp.bfloat16)
    outgoing = []
    for dest in range(groups):
        outgoing.append(
            jnp.concatenate(
                [
                    grad_attended[..., dest * query_width : (dest + 1) * query_width],
                    grad_ssd[..., dest * mixer_width : (dest + 1) * mixer_width],
                ],
                axis=-1,
            )
        )
    outgoing = jnp.stack(outgoing, axis=2)
    head_grads = lax.all_to_all(outgoing, "sp", split_axis=2, concat_axis=1, tiled=True)[:, :, 0]
    head_dout = head_grads[..., :query_width].reshape(slots, span, head_share, HD)
    head_dssd = (
        head_grads[..., query_width:].reshape(slots, span, mixer_share, SHD).astype(jnp.float32)
    )
    weighted = jnp.exp(log_decay)[..., None] * head_dssd
    direct = product("sthp,stn->shpn", weighted, readout)
    _, later_grad = entering((decay, direct), "ctx", combine, identity, True)
    grad_decay = jnp.sum(later_grad * state_in, axis=(-2, -1))

    def slot_back(items):
        (
            feat_slot,
            inject_slot,
            readout_slot,
            raw_slot,
            state_slot,
            dssd_slot,
            ddecay_slot,
            dlocal_slot,
        ) = items

        def heads_value(
            feat_value, inject_value, readout_value, raw_value, bias_value, log_value, skip_value
        ):
            return mixer_heads(
                feat_value,
                inject_value,
                readout_value,
                raw_value,
                bias_value,
                log_value,
                skip_value,
                state_slot,
            )

        _, pullback = jax.vjp(
            heads_value,
            feat_slot,
            inject_slot,
            readout_slot,
            raw_slot,
            step_bias,
            decay_log,
            skip_scale,
        )
        return pullback((dssd_slot, ddecay_slot, dlocal_slot))

    (
        grad_feat,
        grad_inject,
        grad_readout,
        grad_raw,
        grad_bias_slots,
        grad_log_slots,
        grad_skip_slots,
    ) = lax.map(
        slot_back, (features, inject, readout, step_in, state_in, head_dssd, grad_decay, later_grad)
    )
    head_terms = jnp.concatenate(
        [
            jnp.sum(grad_bias_slots, axis=0),
            jnp.sum(grad_log_slots, axis=0),
            jnp.sum(grad_skip_slots, axis=0),
        ]
    )
    delta = jnp.transpose(
        jnp.sum(head_dout.astype(jnp.float32) * attended.astype(jnp.float32), axis=-1), (0, 2, 1)
    )

    def backward_block(state, block, causal_keep, first_key):
        grad_query, grad_kv = state
        scores = (
            jnp.einsum(
                "sqhd,skd->shqk", head_queries, block[..., :HD], preferred_element_type=jnp.float32
            )
            * scale
        )
        attn_probs = jnp.where(causal_keep, jnp.exp(scores - log_total[..., None]), 0.0)
        grad_probs = jnp.einsum(
            "sqhd,skd->shqk", head_dout, block[..., HD:], preferred_element_type=jnp.float32
        )
        grad_scores = (attn_probs * (grad_probs - delta[..., None])).astype(jnp.bfloat16)
        grad_query = (
            grad_query
            + jnp.einsum(
                "shqk,skd->shqd", grad_scores, block[..., :HD], preferred_element_type=jnp.float32
            )
            * scale
        )
        grad_keys = (
            jnp.einsum(
                "shqk,sqhd->skd", grad_scores, head_queries, preferred_element_type=jnp.float32
            )
            * scale
        )
        grad_values = jnp.einsum(
            "shqk,sqhd->skd",
            attn_probs.astype(jnp.bfloat16),
            head_dout,
            preferred_element_type=jnp.float32,
        )
        grad_kv = lax.dynamic_update_slice_in_dim(
            grad_kv, jnp.concatenate([grad_keys, grad_values], axis=-1), first_key, 1
        )
        return (grad_query, grad_kv)

    initial = (
        jnp.zeros((slots, head_share, span, HD), jnp.float32),
        jnp.zeros((slots, seq_rows, 2 * HD), jnp.float32),
    )
    grad_query, grad_kv = key_blocks(
        lax.all_gather(head_kv, "ctx", axis=1, tiled=True), initial, backward_block
    )
    head_member = jnp.broadcast_to(head_terms[None, None, :], (1, span_count, 3 * mixer_share))
    kv_mine, head_sums = (
        lax.psum_scatter(
            grad_kv.astype(jnp.bfloat16), "ctx", scatter_dimension=1, tiled=True
        ).astype(jnp.float32),
        lax.psum_scatter(
            head_member.astype(jnp.bfloat16), "ctx", scatter_dimension=1, tiled=True
        ).astype(jnp.float32),
    )
    head_flat = head_sums[0, 0]
    back_rows = jnp.concatenate(
        [
            jnp.transpose(grad_query, (0, 2, 1, 3)).reshape(slots, span, query_width),
            kv_mine,
            grad_feat.reshape(slots, span, mixer_width),
            grad_inject,
            grad_readout,
        ],
        axis=-1,
    )[:, :, None]
    back_steps = grad_raw[:, :, None]
    seq_back, seq_steps = (
        lax.all_to_all(
            back_rows.astype(jnp.bfloat16), "sp", split_axis=1, concat_axis=2, tiled=True
        ).astype(back_rows.dtype),
        lax.all_to_all(
            back_steps.astype(jnp.bfloat16), "sp", split_axis=1, concat_axis=2, tiled=True
        ).astype(back_steps.dtype),
    )
    grad_query_lin = seq_back[..., :query_width].reshape(slots, piece, QH, HD)
    key_grads = []
    value_grads = []
    for owner in range(KVH):
        members = [dest for dest in range(groups) if kv_owner[dest] == owner]
        key_grads.append(
            sum((seq_back[:, :, dest, query_width : query_width + HD] for dest in members))
        )
        value_grads.append(
            sum((seq_back[:, :, dest, query_width + HD : query_width + 2 * HD] for dest in members))
        )
    grad_key_lin = jnp.stack(key_grads, axis=2)
    grad_value_lin = jnp.stack(value_grads, axis=2)
    grad_features = seq_back[..., offset : offset + mixer_width].reshape(slots, piece, ssd_width)
    grad_inject_all = jnp.sum(
        seq_back[..., offset + mixer_width : offset + mixer_width + NS], axis=2
    )
    grad_readout_all = jnp.sum(seq_back[..., offset + mixer_width + NS :], axis=2)
    grad_step_raw = seq_steps.reshape(slots, piece, SH).astype(jnp.bfloat16)
    _, query_rotate_back = jax.vjp(lambda value: rotate(value, cos_table, sin_table), query_lin)
    _, key_rotate_back = jax.vjp(lambda value: rotate(value, cos_table, sin_table), key_lin)
    (grad_query_pre,) = query_rotate_back(grad_query_lin)
    (grad_key_pre,) = key_rotate_back(grad_key_lin)
    grad_linear = (
        jnp.concatenate(
            [
                grad_query_pre.reshape(slots, piece, QH * HD),
                grad_key_pre.reshape(slots, piece, KVH * HD),
                grad_value_lin.reshape(slots, piece, KVH * HD),
            ],
            axis=-1,
        )
        .astype(jnp.bfloat16)
        .reshape(slots * piece, -1)
    )
    grad_conv_out = jnp.concatenate([grad_features, grad_inject_all, grad_readout_all], axis=-1)
    _, conv_back = jax.vjp(conv_apply, padded, conv_taps, conv_shift)
    grad_padded, grad_conv_weight, grad_conv_bias = conv_back(grad_conv_out)
    rim_back = passed_along(
        grad_padded[:, : KC - 1].astype(jnp.bfloat16), ("ctx", "sp"), -1
    ).astype(jnp.float32)
    grad_core = grad_padded[:, KC - 1 :]
    grad_mixed_raw = jnp.concatenate(
        [grad_core[:, : piece - KC + 1], grad_core[:, piece - KC + 1 :] + rim_back], axis=1
    ).astype(jnp.bfloat16)
    zgate_rows = grad_gate_z.astype(jnp.bfloat16).reshape(slots * piece, ssd_width)
    mixed_rows = grad_mixed_raw.reshape(slots * piece, conv_width)
    step_rows = grad_step_raw.reshape(slots * piece, SH)
    grad_attn_in = weight_product(rows, grad_linear)
    grad_zgate = weight_product(rows, zgate_rows)
    grad_mixer_in = weight_product(rows, mixed_rows)
    grad_step_weight = weight_product(rows, step_rows)
    grad_normed = (
        back_product(grad_linear, full_attn_in)
        + back_product(zgate_rows, full_zgate)
        + back_product(mixed_rows, full_mixer_in)
        + back_product(step_rows, full_step)
    )
    _, input_back = jax.vjp(rms_scale, tokens, gain_in)
    grad_tokens, grad_input_gain = input_back(grad_normed.reshape(slots, piece, width))
    input_grad = grad_residual + grad_tokens
    summed = (
        lax.psum_scatter(grad_input_gain, ("ctx", "sp"), scatter_dimension=0, tiled=True),
        lax.psum_scatter(grad_attn_in, ("ctx", "sp"), scatter_dimension=0, tiled=True),
        lax.psum_scatter(grad_attn_out, ("ctx", "sp"), scatter_dimension=0, tiled=True),
        lax.psum_scatter(grad_zgate, ("ctx", "sp"), scatter_dimension=0, tiled=True),
        lax.psum_scatter(grad_mixer_in, ("ctx", "sp"), scatter_dimension=0, tiled=True),
        lax.psum_scatter(grad_step_weight, ("ctx", "sp"), scatter_dimension=0, tiled=True),
        lax.psum_scatter(grad_conv_weight, ("ctx", "sp"), scatter_dimension=1, tiled=True),
        lax.psum_scatter(grad_conv_bias, ("ctx", "sp"), scatter_dimension=0, tiled=True),
        lax.psum_scatter(grad_mixer_gain, ("ctx", "sp"), scatter_dimension=0, tiled=True),
        lax.psum_scatter(grad_mixer_out, ("ctx", "sp"), scatter_dimension=0, tiled=True),
        lax.psum_scatter(grad_post_gain, ("ctx", "sp"), scatter_dimension=0, tiled=True),
        lax.psum_scatter(grad_gate, ("ctx", "sp"), scatter_dimension=0, tiled=True),
        lax.psum_scatter(grad_up, ("ctx", "sp"), scatter_dimension=0, tiled=True),
        lax.psum_scatter(grad_down, ("ctx", "sp"), scatter_dimension=0, tiled=True),
    )
    return (
        layer_out,
        input_grad,
        summed[0],
        summed[1],
        summed[2],
        summed[3],
        summed[4],
        summed[5],
        summed[6],
        summed[7],
        head_flat[:mixer_share],
        head_flat[mixer_share : 2 * mixer_share],
        head_flat[2 * mixer_share :],
        summed[8],
        summed[9],
        summed[10],
        summed[11],
        summed[12],
        summed[13],
    )


def solution(mesh):
    in_specs = (
        P(None, ("ctx", "sp"), None),
        P(None, ("ctx", "sp"), None),
        P(),
        P(("ctx", "sp")),
        P(("ctx", "sp"), None),
        P(("ctx", "sp"), None),
        P(("ctx", "sp"), None),
        P(("ctx", "sp"), None),
        P(("ctx", "sp"), None),
        P(None, ("ctx", "sp")),
        P(("ctx", "sp")),
        P("sp"),
        P("sp"),
        P("sp"),
        P(("ctx", "sp")),
        P(("ctx", "sp"), None),
        P(("ctx", "sp")),
        P(("ctx", "sp"), None),
        P(("ctx", "sp"), None),
        P(("ctx", "sp"), None),
    )
    out_specs = (
        P(None, ("ctx", "sp"), None),
        P(None, ("ctx", "sp"), None),
        P(("ctx", "sp")),
        P(("ctx", "sp"), None),
        P(("ctx", "sp"), None),
        P(("ctx", "sp"), None),
        P(("ctx", "sp"), None),
        P(("ctx", "sp"), None),
        P(None, ("ctx", "sp")),
        P(("ctx", "sp")),
        P("sp"),
        P("sp"),
        P("sp"),
        P(("ctx", "sp")),
        P(("ctx", "sp"), None),
        P(("ctx", "sp")),
        P(("ctx", "sp"), None),
        P(("ctx", "sp"), None),
        P(("ctx", "sp"), None),
    )
    return jax.shard_map(shards, mesh=mesh, in_specs=in_specs, out_specs=out_specs, check_vma=False)
```

profile of v0, /device:TPU:0, one launch (start us, length us, event | category | flops | bytes accessed | tf_op | source)
XLA Modules:
  0.0 2616.3 jit_solution(12613880140182868840)
XLA Ops:
  12.1 42.3 %all-reduce.25 = (bf16[1024]{0:T(1024)(128)(2,1)S(1)}, bf16[1792]{0:T(1024)(128)(2,1)S(1)}, bf16[1536]{0:T(1024)(128)(2,1)}, bf16[1024]{0:T(1024)(128)(2,1)}) all-reduce(bf16[1024]{0:T(1024)(128)(2,1)S(1)} %dynamic-update-slice, bf16[1792]{0:T(1024)(128)(2,1)S(1)} %dynamic-update-slice.1, ...), channel_id=1, replica_groups=mesh['ctx'=8,'sp'=4] {'ctx','sp'}, use_global_device_ids=true, to_apply=%add.14 | all-reduce | flops 5376 | bytes 21504
  54.4 68.8 %all-gather.4 = bf16[32,32,24]{1,2,0:T(8,128)(2,1)S(1)} all-gather(bf16[1,32,24]{1,2,0:T(8,128)(2,1)} %bitcast.904), channel_id=1, replica_groups=mesh['ctx'=8,'sp'=4] {'ctx','sp'}, dimensions={0}, use_global_device_ids=true | all-gather | bytes 50688 | tf_op jit(solution)/shard_map/all_gather | solution.py:202
  131.6 65.4 %all-gather.3 = bf16[32,56,4]{1,2,0:T(4,128)(2,1)S(1)} all-gather(bf16[1,56,4]{1,2,0:T(4,128)(2,1)S(1)} %bitcast.906), channel_id=1, replica_groups=mesh['ctx'=8,'sp'=4] {'ctx','sp'}, dimensions={0}, use_global_device_ids=true | all-gather | bytes 14784 | tf_op jit(solution)/shard_map/all_gather | solution.py:203
  223.6 58.4 %all-to-all-done = bf16[2,192,4,896]{3,1,0,2:T(8,128)(2,1)S(1)} async-done(((bf16[2,192,4,896]{3,1,0,2:T(8,128)(2,1)}), bf16[2,192,4,896]{3,1,0,2:T(8,128)(2,1)S(1)}, u32[]{:S(2)}, u32[]{:S(2)}) %all-to-all-start) | async-done | bytes 2752544 | tf_op jit(solution)/shard_map/all_to_all | solution.py:256
  288.0 47.6 %while.111 = (s32[]{:T(128)}, f32[2,768,6,64]{1,3,2,0:T(8,128)}, bf16[2,6]{0,1:T(8,128)(2,1)S(1)}, bf16[2,6,64,128]{3,2,1,0:T(8,128)(2,1)S(1)}, f32[2,768,6]{1,2...) while((s32[]{:T(128)}, f32[2,768,6,64]{1,3,2,0:T(8,128)}, ...), condition=%wide.region_10.11_spmd.clone, body=%wide.region_7.10_spmd.sunk.clone | while | flops 4092507904 | bytes 30153268 | solution.py:325
  293.7 16.6 fusion.411
  317.5 16.6 fusion.411
  343.0 9.1 all-gather.5
  353.5 6.8 all-gather.36.cloned.1.call-done
  360.4 8.7 while.115
  377.1 17.4 all-gather.22.cloned.1.call-done
  399.3 12.5 while.113
  399.3 11.8 conditional.8
  422.0 43.3 %all-gather.26.cloned.1.call-done = bf16[1024,1536]{1,0:T(8,128)(2,1)} async-done(((bf16[32,1536]{1,0:T(8,128)(2,1)}), bf16[1024,1536]{1,0:T(8,128)(2,1)}) %all-gather.26.cloned.1.call-update) | async-done | bytes 3145744 | tf_op jit(solution)/shard_map/all_gather | solution.py:200
  484.9 53.9 %all-gather.28.cloned.1.call-done = bf16[1536,1024]{1,0:T(8,128)(2,1)} async-done(((bf16[48,1024]{1,0:T(8,128)(2,1)}), bf16[1536,1024]{1,0:T(8,128)(2,1)}) %all-gather.28.cloned.1.call-update) | async-done | bytes 3145744 | tf_op jit(solution)/shard_map/all_gather | solution.py:206
  544.2 51.7 %all-gather.24.cloned.1.call-done = bf16[512,1024]{1,0:T(8,128)(2,1)} async-done(((bf16[16,1024]{1,0:T(8,128)(2,1)}), bf16[512,1024]{1,0:T(8,128)(2,1)}) %all-gather.24.cloned.1.call-update) | async-done | bytes 1048592 | tf_op jit(solution)/shard_map/all_gather | solution.py:199
  600.0 60.0 %all-gather.30.cloned.1.call-done = bf16[1024,2048]{1,0:T(8,128)(2,1)} async-done(((bf16[32,2048]{1,0:T(8,128)(2,1)}), bf16[1024,2048]{1,0:T(8,128)(2,1)}) %all-gather.30.cloned.1.call-update) | async-done | bytes 4194320 | tf_op jit(solution)/shard_map/all_gather | solution.py:208
  665.6 58.0 %all-gather.32.cloned.1.call-done = bf16[1024,2048]{1,0:T(8,128)(2,1)} async-done(((bf16[32,2048]{1,0:T(8,128)(2,1)}), bf16[1024,2048]{1,0:T(8,128)(2,1)}) %all-gather.32.cloned.1.call-update) | async-done | bytes 4194320 | tf_op jit(solution)/shard_map/all_gather | solution.py:209
  729.3 57.9 %all-gather.34.cloned.1.call-done = bf16[2048,1024]{1,0:T(8,128)(2,1)} async-done(((bf16[64,1024]{1,0:T(8,128)(2,1)}), bf16[2048,1024]{1,0:T(8,128)(2,1)}) %all-gather.34.cloned.1.call-update) | async-done | bytes 4194320 | tf_op jit(solution)/shard_map/all_gather | solution.py:210
  787.2 8.4 multiply_convert_fusion
  814.6 40.3 %all_to_all.87 = bf16[2,192,4,512]{3,1,0,2:T(8,128)(2,1)S(1)} all-to-all(bf16[2,192,4,512]{3,1,0,2:T(8,128)(2,1)S(1)} %pad_maximum_fusion.2), channel_id=1, replica_groups=mesh['ctx'=8,'sp'=4] {'sp'}, dimensions={2} | all-to-all | bytes 3145728 | tf_op jit(solution)/shard_map/all_to_all | solution.py:430
  873.4 20.5 while.114
  873.8 19.6 conditional.9
  873.9 5.9 fusion.78
  881.1 6.0 fusion.66
  895.2 13.9 while.116
  909.8 209.6 %while.112 = (s32[]{:T(128)}, bf16[2,768,6,64]{1,3,2,0:T(8,128)(2,1)}, bf16[2,768,128]{1,2,0:T(8,128)(2,1)}, bf16[2,768,128]{1,2,0:T(8,128)(2,1)}, bf16[2,768,6]...) while((s32[]{:T(128)}, ...), condition=%wide.region_41.42_spmd.clone, body=%wide.region_26.41_spmd.sunk.clone | while | flops 10031226880 | bytes 62920272 | solution.py:486
  936.7 21.8 fusion.431
  971.4 8.7 reduce-window.58
  1004.3 15.5 fusion.435
  1027.9 21.8 fusion.431
  1062.6 8.7 reduce-window.58
  1095.5 15.6 fusion.435
  1121.5 8.6 all_to_all.88
  1136.1 6.6 convolution_bitcast_fusion.3
  1154.9 7.6 copy.589
  1162.5 59.9 %all_to_all.89 = bf16[2,768,1,896]{3,0,2,1:T(2,128)(2,1)S(1)} all-to-all(bf16[2,768,1,896]{3,0,2,1:T(2,128)(2,1)S(1)} %copy.589), channel_id=1, replica_groups=mesh['ctx'=8,'sp'=4] {'sp'}, dimensions={1} | all-to-all | bytes 5505024 | tf_op jit(solution)/shard_map/all_to_all | solution.py:566
  1252.7 5.7 fusion.276
  1293.2 141.7 %all-reduce.21 = bf16[1,8,18]{2,1,0:T(8,128)(2,1)S(1)} all-reduce(bf16[1,8,18]{2,1,0:T(8,128)(2,1)S(1)} %broadcast_in_dim.251), channel_id=14, replica_groups=mesh['ctx'=8,'sp'=4] {'ctx'}, use_global_device_ids=true, to_apply=%region_62.63.clone | all-reduce | flops 144 | bytes 576
  1448.9 38.4 %all-reduce.24 = (f32[1024]{0:T(1024)S(1)}, f32[4,1792]{1,0:T(4,128)S(1)}, f32[1792]{0:T(1024)S(1)}, f32[1536]{0:T(1024)S(1)}, f32[1024]{0:T(1024)S(1)}) all-reduce(f32[1024]{0:T(1024)S(1)} %get-tuple-element.1654, f32[4,1792]{1,0:T(4,128)S(1)} %pad_add_fusion.1, ...), channel_id=6, replica_groups=mesh['ctx'=8,'sp'=4] {'ctx','sp'}, use_global_device_ids=true, to_apply=%region_46.47.clone | all-reduce | flops 12544 | bytes 100352
  1495.2 41.9 %reduce-scatter.19.cloned.1.call-done = f32[16,1024]{1,0:T(8,128)} async-done(((f32[512,1024]{1,0:T(8,128)}), f32[16,1024]{1,0:T(8,128)}) %reduce-scatter.19.cloned.1.call-update) | async-done | bytes 65552 | tf_op jit(solution)/shard_map/reduce_scatter | solution.py:637
  1537.1 119.4 %reduce-scatter.25.cloned.1.call-done = f32[48,1024]{1,0:T(8,128)} async-done(((f32[1536,1024]{1,0:T(8,128)}), f32[48,1024]{1,0:T(8,128)}) %reduce-scatter.25.cloned.1.call-update) | async-done | bytes 196624 | tf_op jit(solution)/shard_map/reduce_scatter | solution.py:644
  1656.5 119.7 %reduce-scatter.21.cloned.1.call-done = f32[32,1536]{1,0:T(8,128)} async-done(((f32[1024,1536]{1,0:T(8,128)}), f32[32,1536]{1,0:T(8,128)}) %reduce-scatter.21.cloned.1.call-update) | async-done | bytes 196624 | tf_op jit(solution)/shard_map/reduce_scatter | solution.py:638
  1776.2 107.5 %reduce-scatter.17.cloned.1.call-done = f32[32,768]{1,0:T(8,128)} async-done(((f32[1024,768]{1,0:T(8,128)}), f32[32,768]{1,0:T(8,128)}) %reduce-scatter.17.cloned.1.call-update) | async-done | bytes 98320 | tf_op jit(solution)/shard_map/reduce_scatter | solution.py:636
  1883.7 187.7 %reduce-scatter.27.cloned.1.call-done = f32[32,2048]{1,0:T(8,128)} async-done(((f32[1024,2048]{1,0:T(8,128)}), f32[32,2048]{1,0:T(8,128)}) %reduce-scatter.27.cloned.1.call-update) | async-done | bytes 262160 | tf_op jit(solution)/shard_map/reduce_scatter | solution.py:646
  2071.3 186.5 %reduce-scatter.29.cloned.1.call-done = f32[32,2048]{1,0:T(8,128)} async-done(((f32[1024,2048]{1,0:T(8,128)}), f32[32,2048]{1,0:T(8,128)}) %reduce-scatter.29.cloned.1.call-update) | async-done | bytes 262160 | tf_op jit(solution)/shard_map/reduce_scatter | solution.py:647
  2257.8 186.3 %reduce-scatter.31.cloned.1.call-done = f32[64,1024]{1,0:T(8,128)} async-done(((f32[2048,1024]{1,0:T(8,128)}), f32[64,1024]{1,0:T(8,128)}) %reduce-scatter.31.cloned.1.call-update) | async-done | bytes 262160 | tf_op jit(solution)/shard_map/reduce_scatter | solution.py:648
  2444.1 164.8 %reduce-scatter.23.cloned.1.call-done = f32[32,1792]{1,0:T(8,128)} async-done(((f32[1024,1792]{1,0:T(8,128)}), f32[32,1792]{1,0:T(8,128)}) %reduce-scatter.23.cloned.1.call-update) | async-done | bytes 229392 | tf_op jit(solution)/shard_map/reduce_scatter | solution.py:639
  (867 shorter events, 408.6 us)
Async XLA Ops:
  7.2 118.3 %copy-start.19 = (bf16[2,192,1024]{2,1,0:T(8,128)(2,1)S(1)}, bf16[2,192,1024]{2,1,0:T(8,128)(2,1)}, u32[]{:S(2)}) copy-start(bf16[2,192,1024]{2,1,0:T(8,128)(2,1)} %param.36) | copy-start | bytes 2359300
  7.2 124.4 %copy-start.139 = (bf16[4,56]{1,0:T(4,128)(2,1)S(1)}, bf16[4,56]{1,0:T(4,128)(2,1)}, u32[]{:S(2)}) copy-start(bf16[4,56]{1,0:T(4,128)(2,1)} %param.45) | copy-start | bytes 1348
  7.2 190.9 %all-gather.18.cloned.1.call-start = ((), (), s32[]{:S(2)}) async-start(), calls=%async_computation.16 | async-start | bytes 1622016 | tf_op jit(solution)/shard_map/all_gather | solution.py:198
  7.9 194.1 %all-gather.20.cloned.1.call-start = ((), (), s32[]{:S(2)}) async-start(), calls=%async_computation.17 | async-start | bytes 3784704 | tf_op jit(solution)/shard_map/all_gather | solution.py:201
  54.4 145.9 %copy-start.106 = (f32[1024]{0:T(1024)}, f32[1024]{0:T(1024)S(1)}, u32[]{:S(2)}) copy-start(f32[1024]{0:T(1024)S(1)} %convert_element_type.326) | copy-start | bytes 12292
  123.5 76.8 %copy-start.83 = (bf16[1024,24]{0,1:T(8,128)(2,1)}, bf16[1024,24]{0,1:T(8,128)(2,1)S(1)}, u32[]{:S(2)}) copy-start(bf16[1024,24]{0,1:T(8,128)(2,1)S(1)} %reshape.717) | copy-start | bytes 147460
  126.1 76.0 %copy-start.37 = (bf16[2,192,1024]{2,1,0:T(8,128)(2,1)}, bf16[2,192,1024]{2,1,0:T(8,128)(2,1)S(1)}, u32[]{:S(2)}) copy-start(bf16[2,192,1024]{2,1,0:T(8,128)(2,1)S(1)} %fusion.203) | copy-start | bytes 2359300
  127.1 90.8 %all-to-all-start.1 = ((bf16[2,192,4,6]{1,0,3,2:T(2,128)(2,1)}), bf16[2,192,4,6]{1,0,3,2:T(2,128)(2,1)}, u32[]{:S(2)}, u32[]{:S(2)}) async-start(bf16[2,192,4,6]{1,0,3,2:T(2,128)(2,1)} %reshape_reshape.3), calls=%async_computation.1 | async-start | bytes 49152 | tf_op jit(solution)/shard_map/all_to_all | solution.py:257
  205.8 4.5 collective-permute-start
  217.9 64.1 %all-to-all-start = ((bf16[2,192,4,896]{3,1,0,2:T(8,128)(2,1)}), bf16[2,192,4,896]{3,1,0,2:T(8,128)(2,1)S(1)}, u32[]{:S(2)}, u32[]{:S(2)}) async-start(bf16[2,192,4,896]{3,1,0,2:T(8,128)(2,1)} %pad_maximum_fusion), calls=%async_computation | async-start | bytes 5505024 | tf_op jit(solution)/shard_map/all_to_all | solution.py:256
  221.7 138.7 %all-gather.36.cloned.1.call-start = ((), (), s32[]{:S(2)}) async-start(), calls=%async_computation.34 | async-start | bytes 1769472 | tf_op jit(solution)/shard_map/all_gather | solution.py:29
  223.5 58.9 %copy-start.80 = (f32[2,768,6]{1,0,2:T(2,128)}, f32[2,768,6]{1,0,2:T(2,128)S(1)}, u32[]{:S(2)}) copy-start(f32[2,768,6]{1,0,2:T(2,128)S(1)} %reshape.694) | copy-start | bytes 110596
  336.4 58.1 %all-gather.22.cloned.1.call-start = ((), (), s32[]{:S(2)}) async-start(), calls=%async_computation.18 | async-start | bytes 3538944 | tf_op jit(solution)/shard_map/all_gather | solution.py:319
  336.9 128.3 %all-gather.26.cloned.1.call-start = ((), (), s32[]{:S(2)}) async-start(), calls=%async_computation.20 | async-start | bytes 3244032 | tf_op jit(solution)/shard_map/all_gather | solution.py:200
  337.5 201.2 %all-gather.28.cloned.1.call-start = ((), (), s32[]{:S(2)}) async-start(), calls=%async_computation.21 | async-start | bytes 3244032 | tf_op jit(solution)/shard_map/all_gather | solution.py:206
  338.1 257.8 %all-gather.24.cloned.1.call-start = ((), (), s32[]{:S(2)}) async-start(), calls=%async_computation.19 | async-start | bytes 1081344 | tf_op jit(solution)/shard_map/all_gather | solution.py:199
  338.9 321.1 %all-gather.30.cloned.1.call-start = ((), (), s32[]{:S(2)}) async-start(), calls=%async_computation.22 | async-start | bytes 4325376 | tf_op jit(solution)/shard_map/all_gather | solution.py:208
  339.6 384.1 %all-gather.32.cloned.1.call-start = ((), (), s32[]{:S(2)}) async-start(), calls=%async_computation.23 | async-start | bytes 4325376 | tf_op jit(solution)/shard_map/all_gather | solution.py:209
  340.3 446.8 %all-gather.34.cloned.1.call-start = ((), (), s32[]{:S(2)}) async-start(), calls=%async_computation.24 | async-start | bytes 4325376 | tf_op jit(solution)/shard_map/all_gather | solution.py:210
  415.4 55.7 %all-to-all-start.2 = ((bf16[2,768,1,512]{3,0,2,1:T(2,128)(2,1)}), bf16[2,768,1,512]{3,0,2,1:T(2,128)(2,1)}, u32[]{:S(2)}, u32[]{:S(2)}) async-start(bf16[2,768,1,512]{3,0,2,1:T(2,128)(2,1)} %maximum_bitcast_fusion), calls=%async_computation.2 | async-start | bytes 3145728 | tf_op jit(solution)/shard_map/all_to_all | solution.py:341
  420.2 473.8 %all-gather.38.cloned.1.call-start = ((), (), s32[]{:S(2)}) async-start(), calls=%async_computation.35 | async-start | bytes 1769472 | tf_op jit(solution)/shard_map/all_gather | solution.py:29
  420.8 381.0 %copy-start.94 = (f32[1024]{0:T(1024)}, f32[1024]{0:T(1024)S(1)}, u32[]{:S(2)}) copy-start(f32[1024]{0:T(1024)S(1)} %convert_element_type.358) | copy-start | bytes 12292
  468.8 70.0 %copy-start.31 = (f32[384,1536]{1,0:T(8,128)}, f32[384,1536]{1,0:T(8,128)S(1)}, u32[]{:S(2)}) copy-start(f32[384,1536]{1,0:T(8,128)S(1)} %fusion.192) | copy-start | bytes 7077892
  544.2 54.1 %copy-start.20 = (bf16[2,192,1024]{2,1,0:T(8,128)(2,1)S(1)}, bf16[2,192,1024]{2,1,0:T(8,128)(2,1)}, u32[]{:S(2)}) copy-start(bf16[2,192,1024]{2,1,0:T(8,128)(2,1)} %param.36) | copy-start | bytes 2359300
  598.6 203.2 %copy-start.15 = (f32[2,192,1024]{2,1,0:T(8,128)}, f32[2,192,1024]{2,1,0:T(8,128)S(1)}, u32[]{:S(2)}) copy-start(f32[2,192,1024]{2,1,0:T(8,128)S(1)} %get-tuple-element.1791) | copy-start | bytes 4718596
  600.0 123.7 %copy-start.43 = (bf16[2,192,1024]{2,1,0:T(8,128)(2,1)}, bf16[2,192,1024]{2,1,0:T(8,128)(2,1)S(1)}, u32[]{:S(2)}) copy-start(bf16[2,192,1024]{2,1,0:T(8,128)(2,1)S(1)} %multiply_convert_fusion.7) | copy-start | bytes 2359300
  863.2 287.2 %reduce-scatter.15.cloned.1.call-start = ((), (), s32[]{:S(2)}) async-start(), calls=%async_computation.25 | async-start | bytes 3538944 | tf_op jit(solution)/shard_map/reduce_scatter | solution.py:546
  893.9 543.8 %reduce-scatter.33.cloned.1.call-start = ((), (), s32[]{:S(2)}) async-start(), calls=%async_computation.36 | async-start | bytes 540672
  1132.6 404.4 %reduce-scatter.19.cloned.1.call-start = ((), (), s32[]{:S(2)}) async-start(), calls=%async_computation.27 | async-start | bytes 2162688 | tf_op jit(solution)/shard_map/reduce_scatter | solution.py:637
  1136.0 520.4 %reduce-scatter.25.cloned.1.call-start = ((), (), s32[]{:S(2)}) async-start(), calls=%async_computation.30 | async-start | bytes 6488064 | tf_op jit(solution)/shard_map/reduce_scatter | solution.py:644
  1142.8 633.4 %reduce-scatter.21.cloned.1.call-start = ((), (), s32[]{:S(2)}) async-start(), calls=%async_computation.28 | async-start | bytes 6488064 | tf_op jit(solution)/shard_map/reduce_scatter | solution.py:638
  1148.5 735.1 %reduce-scatter.17.cloned.1.call-start = ((), (), s32[]{:S(2)}) async-start(), calls=%async_computation.26 | async-start | bytes 3244032 | tf_op jit(solution)/shard_map/reduce_scatter | solution.py:636
  1236.7 834.6 %reduce-scatter.27.cloned.1.call-start = ((), (), s32[]{:S(2)}) async-start(), calls=%async_computation.31 | async-start | bytes 8650752 | tf_op jit(solution)/shard_map/reduce_scatter | solution.py:646
  1244.1 1013.8 %reduce-scatter.29.cloned.1.call-start = ((), (), s32[]{:S(2)}) async-start(), calls=%async_computation.32 | async-start | bytes 8650752 | tf_op jit(solution)/shard_map/reduce_scatter | solution.py:647
  1251.1 1193.0 %reduce-scatter.31.cloned.1.call-start = ((), (), s32[]{:S(2)}) async-start(), calls=%async_computation.33 | async-start | bytes 8650752 | tf_op jit(solution)/shard_map/reduce_scatter | solution.py:648
  1258.5 1350.5 %reduce-scatter.23.cloned.1.call-start = ((), (), s32[]{:S(2)}) async-start(), calls=%async_computation.29 | async-start | bytes 7569408 | tf_op jit(solution)/shard_map/reduce_scatter | solution.py:639
  1272.8 5.9 collective-permute-start.1
  1290.0 146.1 %copy-start.91 = (bf16[2,4,192,1,6]{2,0,4,1,3:T(2,128)(2,1)S(1)}, bf16[2,4,192,1,6]{2,0,4,1,3:T(2,128)(2,1)}, u32[]{:S(2)}) copy-start(bf16[2,4,192,1,6]{2,0,4,1,3:T(2,128)(2,1)} %copy-done.90) | copy-start | bytes 55300
  1290.0 146.2 %copy-start.84 = (bf16[1024,24]{0,1:T(8,128)(2,1)S(1)}, bf16[1024,24]{0,1:T(8,128)(2,1)}, u32[]{:S(2)}) copy-start(bf16[1024,24]{0,1:T(8,128)(2,1)} %copy-done.83) | copy-start | bytes 147460
  1290.0 149.1 %copy-start.48 = (bf16[2,192,8,64]{1,3,2,0:T(8,128)(2,1)S(1)}, bf16[2,192,8,64]{1,3,2,0:T(8,128)(2,1)}, u32[]{:S(2)}) copy-start(bf16[2,192,8,64]{1,3,2,0:T(8,128)(2,1)} %copy-done.47) | copy-start | bytes 1179652
  1293.0 146.6 %copy-start.68 = (bf16[2,192,2,64]{1,3,2,0:T(8,128)(2,1)S(1)}, bf16[2,192,2,64]{1,3,2,0:T(8,128)(2,1)}, u32[]{:S(2)}) copy-start(bf16[2,192,2,64]{1,3,2,0:T(8,128)(2,1)} %copy-done.67) | copy-start | bytes 294916
  1293.0 146.8 %copy-start.70 = (bf16[2,192,2,64]{1,3,2,0:T(8,128)(2,1)S(1)}, bf16[2,192,2,64]{1,3,2,0:T(8,128)(2,1)}, u32[]{:S(2)}) copy-start(bf16[2,192,2,64]{1,3,2,0:T(8,128)(2,1)} %copy-done.69) | copy-start | bytes 294916
  1447.3 43.1 %copy-start.16 = (f32[2,192,1024]{2,1,0:T(8,128)S(1)}, f32[2,192,1024]{2,1,0:T(8,128)}, u32[]{:S(2)}) copy-start(f32[2,192,1024]{2,1,0:T(8,128)} %copy-done.15) | copy-start | bytes 4718596
  1447.3 43.1 %copy-start.42 = (bf16[2,192,1024]{2,1,0:T(8,128)(2,1)S(1)}, bf16[2,192,1024]{2,1,0:T(8,128)(2,1)}, u32[]{:S(2)}) copy-start(bf16[2,192,1024]{2,1,0:T(8,128)(2,1)} %param.37) | copy-start | bytes 2359300
  1447.3 43.1 %copy-start.95 = (f32[1024]{0:T(1024)S(1)}, f32[1024]{0:T(1024)}, u32[]{:S(2)}) copy-start(f32[1024]{0:T(1024)} %copy-done.94) | copy-start | bytes 12292
  1447.3 43.1 %copy-start.112 = (f32[2,192]{1,0:T(2,128)S(1)}, f32[2,192]{1,0:T(2,128)}, u32[]{:S(2)}) copy-start(f32[2,192]{1,0:T(2,128)} %copy-done.110) | copy-start | bytes 4612
  1447.3 43.1 %copy-start.119 = (f32[2,192]{1,0:T(2,128)S(1)}, f32[2,192]{1,0:T(2,128)}, u32[]{:S(2)}) copy-start(f32[2,192]{1,0:T(2,128)} %copy-done.117) | copy-start | bytes 4612
  1447.3 43.1 %copy-start.132 = (f32[2,192]{1,0:T(2,128)S(1)}, f32[2,192]{1,0:T(2,128)}, u32[]{:S(2)}) copy-start(f32[2,192]{1,0:T(2,128)} %copy-done.131) | copy-start | bytes 4612
  (168 other events, 1132.3 us)
Sparse Core Ops, SparseCore 0:
  10.9 57.8 all-gather.17
  71.7 59.4 all-gather.19
  336.5 23.8 all-gather.35
  362.1 32.3 all-gather.21
  397.2 68.0 all-gather.25
  468.0 70.7 all-gather.27
  541.8 54.0 all-gather.23
  598.9 61.0 all-gather.29
  663.0 60.6 all-gather.31
  726.5 60.6 all-gather.33
  863.4 23.8 all-gather.37
  894.0 180.3 reduce-scatter.14
  1132.7 266.8 reduce-scatter.32
  1402.3 134.7 reduce-scatter.18
  1544.1 112.3 reduce-scatter.24
  1662.5 113.5 reduce-scatter.20
  1782.9 100.7 reduce-scatter.16
  1886.5 184.7 reduce-scatter.26
  2074.3 183.4 reduce-scatter.28
  2260.6 183.4 reduce-scatter.30
  2447.2 161.7 reduce-scatter.22
where the time goes:
time: 2630 us; the launch traced here: 2620 us
  waiting for transfers between devices  1530 us (58%)
  blocking collectives  475 us (18%)
  matrix products  300 us (11%)
  local copies, waits for them, and re-layouts  129 us (5%)
  other arithmetic  118 us (4%)
  loops' own time  30 us (1%)
    unnamed x3, blocking collectives  222 us
    reduce_scatter x1, waiting for transfers between devices, shards(): lax.psum_scatter(grad_gate, ('ctx', 'sp'), scatter_dimension=0, tiled=True)  188 us
    reduce_scatter x1, waiting for transfers between devices, shards(): lax.psum_scatter(grad_up, ('ctx', 'sp'), scatter_dimension=0, tiled=True)  186 us
    reduce_scatter x1, waiting for transfers between devices, shards(): lax.psum_scatter(grad_down, ('ctx', 'sp'), scatter_dimension=0, tiled=True)  186 us
    dot_general x26, matrix products, product(): jnp.einsum(form, left, right, precision=lax.Precision.HIGHEST, preferred_...  174 us
    reduce_scatter x1, waiting for transfers between devices, shards(): lax.psum_scatter(grad_mixer_in, ('ctx', 'sp'), scatter_dimension=0, tiled...  165 us
    reduce_scatter x1, waiting for transfers between devices, shards(): lax.psum_scatter(grad_zgate, ('ctx', 'sp'), scatter_dimension=0, tiled=True)  120 us
    reduce_scatter x1, waiting for transfers between devices, shards(): lax.psum_scatter(grad_mixer_out, ('ctx', 'sp'), scatter_dimension=0, tile...  119 us
  transfers between devices with their start and end apart: 26, of which 18 were waited for; matrix products, arithmetic and copies ran while one was open for 17% of the time, Pallas kernels for 0%

commit v1 on v0

v1 whole, which is shorter than its diff:
```python
import functools
import math

import jax
import jax.numpy as jnp
from jax import lax
from jax.experimental import pallas as pl
from jax.experimental.pallas import tpu as pltpu
from jax.sharding import PartitionSpec as P

QH = 8
KVH = 2
HD = 64
SH = 24
SHD = 64
NS = 128
KC = 4
CORES = 2
MASKED = -1e30
AXES = ("ctx", "sp")
F32 = jnp.float32
BF16 = jnp.bfloat16
LANES = 128
HALO = 8
Q_SHARE = QH // CORES
M_SHARE = SH // CORES
VMEM = 56 * 2**20

NT = (((1,), (1,)), ((), ()))
TN = (((0,), (0,)), ((), ()))
NN = (((1,), (0,)), ((), ()))


def mm(left, right, dims=NN, precision=None):
    return lax.dot_general(
        left, right, dims, precision=precision, preferred_element_type=F32
    )


class Place:
    def __init__(self):
        ctx = lax.axis_size("ctx")
        groups = lax.axis_size("sp")
        chips = ctx // CORES
        nb = math.isqrt(chips)
        self.size = {"a": chips // nb, "b": nb, "z": groups, "c": CORES}
        self.devices = ctx * groups
        index = lax.axis_index("ctx")
        self.at = {
            "a": index // CORES // nb,
            "b": (index // CORES) % nb,
            "z": lax.axis_index("sp"),
            "c": index % CORES,
        }
        self.chip = index // CORES
        self.chips = chips
        self.flat = index * groups + self.at["z"]

    def flat_of(self, a, b, z, c):
        return ((a * self.size["b"] + b) * CORES + c) * self.size["z"] + z

    def pairs(self, dim, by):
        found = []
        for a in range(self.size["a"]):
            for b in range(self.size["b"]):
                for z in range(self.size["z"]):
                    for c in range(CORES):
                        spot = {"a": a, "b": b, "z": z, "c": c}
                        goal = dict(spot)
                        goal[dim] = (spot[dim] + by) % self.size[dim]
                        found.append((self.flat_of(**spot), self.flat_of(**goal)))
        return found

    def shift(self, x, dim, by):
        return lax.ppermute(x, AXES, self.pairs(dim, by))

    def swap(self, x):
        return self.shift(x, "c", 1)

    def by_core(self, zero, one):
        return jnp.where(self.at["c"] == 0, zero, one)

    def place(self, parts, dim, axis):
        n, v = self.size[dim], self.at[dim]
        if n == 2:
            return jnp.stack(
                [jnp.where(v == 0, parts[0], parts[1]), jnp.where(v == 0, parts[1], parts[0])],
                axis,
            )
        shape = parts[0].shape
        out = jnp.zeros(shape[:axis] + (n,) + shape[axis:], parts[0].dtype)
        for k, part in enumerate(parts):
            out = lax.dynamic_update_index_in_dim(out, part, (v - k) % n, axis)
        return out

    def gather(self, x, dim, axis):
        n = self.size[dim]
        return self.place([x] + [self.shift(x, dim, k) for k in range(1, n)], dim, axis)

    def exchange(self, x, dim, axis):
        n, v = self.size[dim], self.at[dim]
        parts = [lax.dynamic_index_in_dim(x, v, axis, False)]
        for k in range(1, n):
            parts.append(
                self.shift(lax.dynamic_index_in_dim(x, (v + k) % n, axis, False), dim, k)
            )
        return self.place(parts, dim, axis)

    def reduce(self, x, dim, axis):
        n, v = self.size[dim], self.at[dim]
        total = lax.dynamic_index_in_dim(x, v, axis, False).astype(F32)
        for k in range(1, n):
            piece = lax.dynamic_index_in_dim(x, (v + k) % n, axis, False).astype(BF16)
            total = total + self.shift(piece, dim, k).astype(F32)
        return total

    def gather_chips(self, x, z_axis, b_first):
        x = self.gather(x, "z", z_axis)
        if b_first:
            return self.gather(self.gather(x, "b", 0), "a", 0)
        return self.gather(self.gather(x, "a", 0), "b", 1)

    def reduce_chips(self, x, z_axis, b_first):
        if b_first:
            x = self.reduce(self.reduce(x, "a", 0), "b", 0)
        else:
            x = self.reduce(self.reduce(x, "b", 1), "a", 0)
        return self.reduce(x, "z", z_axis)


def rotary_tables(positions, width):
    half_width = width // 2
    inverse = 100000000000.0 ** (-jnp.arange(half_width, dtype=F32) * 2.0 / width)
    angles = positions.astype(F32)[..., None] * inverse
    return (jnp.cos(angles), jnp.sin(angles))


def rotate(value, cos_part, sin_part):
    half_width = value.shape[-1] // 2
    first = value[..., :half_width]
    second = value[..., half_width:]
    return jnp.concatenate(
        [first * cos_part - second * sin_part, second * cos_part + first * sin_part], axis=-1
    )


def inverse_rms(value):
    return lax.rsqrt(jnp.mean(value * value, axis=-1, keepdims=True) + 1e-05)


def rms_back(value, scale, gain, grad):
    scaled = grad * gain
    inner = jnp.mean(scaled * value, axis=-1, keepdims=True)
    return scale * scaled - value * (scale * scale * scale * inner)


def silu_and_slope(value):
    gate = jax.nn.sigmoid(value)
    out = value * gate
    return out, gate + out * (1.0 - gate)


def causal_keep(first_key, first_query, keys, piece, columns):
    key = first_key + lax.broadcasted_iota(jnp.int32, (keys, columns), 0)
    column = lax.broadcasted_iota(jnp.int32, (keys, columns), 1)
    head = sum((column >= piece * k).astype(jnp.int32) for k in range(1, columns // piece))
    return key <= first_query + column - head * piece


def attend_kernel(places, lengths, q_ref, kv_ref, out_ref, lse_ref, acc, top, total, *, piece):
    slot, which = pl.program_id(0), pl.program_id(1)
    first_query = places[which]
    columns = q_ref.shape[2]
    block = columns
    out_ref[...] = jnp.zeros_like(out_ref)
    lse_ref[...] = jnp.zeros_like(lse_ref)

    @pl.when(first_query < lengths[slot])
    def _():
        acc[...] = jnp.zeros_like(acc)
        top[...] = jnp.full_like(top, MASKED)
        total[...] = jnp.zeros_like(total)
        whole = first_query // block

        def visit(index, masked):
            start = pl.multiple_of(index * block, block)
            kv = kv_ref[0, pl.ds(start, block), :]
            scores = mm(kv, q_ref[0, 0], NT)
            if masked:
                keep = causal_keep(start, first_query, block, piece, columns)
                scores = jnp.where(keep, scores, MASKED)
            before = top[...]
            now = jnp.maximum(before, jnp.max(scores, axis=0, keepdims=True))
            weights = jnp.exp(scores - now)
            ratio = jnp.exp(before - now)
            total[...] = total[...] * ratio + jnp.sum(weights, axis=0, keepdims=True)
            acc[...] = acc[...] * ratio + mm(kv, weights.astype(BF16), TN)
            top[...] = now

        @pl.loop(0, whole)
        def _(index):
            visit(index, False)

        visit(whole, True)
        out_ref[0, 0] = (acc[...] / total[...]).T.astype(BF16)
        lse_ref[0, 0] = top[...] + jnp.log(total[...])


def attend(places, lengths, queries, kv, piece):
    slots, _, columns, width = queries.shape
    length = kv.shape[1]
    return pl.pallas_call(
        functools.partial(attend_kernel, piece=piece),
        grid_spec=pltpu.PrefetchScalarGridSpec(
            num_scalar_prefetch=2,
            grid=(slots, CORES),
            in_specs=[
                pl.BlockSpec((1, 1, columns, width), lambda s, e, *_: (s, e, 0, 0)),
                pl.BlockSpec((1, length, width), lambda s, e, *_: (s, 0, 0)),
            ],
            out_specs=[
                pl.BlockSpec((1, 1, columns, width), lambda s, e, *_: (s, e, 0, 0)),
                pl.BlockSpec((1, 1, 1, columns), lambda s, e, *_: (s, e, 0, 0)),
            ],
            scratch_shapes=[
                pltpu.VMEM((width, columns), F32),
                pltpu.VMEM((1, columns), F32),
                pltpu.VMEM((1, columns), F32),
            ],
        ),
        out_shape=[
            jax.ShapeDtypeStruct(queries.shape, BF16),
            jax.ShapeDtypeStruct((slots, CORES, 1, columns), F32),
        ],
        compiler_params=pltpu.CompilerParams(vmem_limit_bytes=VMEM),
        cost_estimate=pl.CostEstimate(
            flops=2 * 2 * slots * CORES * columns * length * width // 2,
            bytes_accessed=slots * length * width * 4,
            transcendentals=slots * CORES * columns * length // 2,
        ),
        name="attend",
    )(places, lengths, queries, kv)


def attend_back_kernel(
    places, lengths, q_ref, kv_ref, out_ref, dout_ref, lse_ref, dq_ref, dkv_ref, dkv, dq, *, piece
):
    slot, which = pl.program_id(0), pl.program_id(1)
    first_query = places[which]
    columns = q_ref.shape[2]
    block = columns
    dq_ref[...] = jnp.zeros_like(dq_ref)

    @pl.when(which == 0)
    def _():
        dkv[...] = jnp.zeros_like(dkv)

    @pl.when(first_query < lengths[slot])
    def _():
        dq[...] = jnp.zeros_like(dq)
        queries = q_ref[0, 0]
        dout = dout_ref[0, 0]
        both = dout.astype(F32) * out_ref[0, 0].astype(F32)
        delta = mm(jnp.ones((8, both.shape[1]), F32), both, NT, lax.Precision.HIGHEST)[:1]
        lse = lse_ref[0, 0]
        whole = first_query // block

        def visit(index, masked):
            start = pl.multiple_of(index * block, block)
            kv = kv_ref[0, pl.ds(start, block), :]
            scores = mm(kv, queries, NT)
            if masked:
                keep = causal_keep(start, first_query, block, piece, columns)
                scores = jnp.where(keep, scores, MASKED)
            probs = jnp.exp(scores - lse)
            dprobs = mm(kv, dout, NT)
            dscores = (probs * (dprobs - delta)).astype(BF16)
            probs = probs.astype(BF16)
            dkv[pl.ds(start, block), :] += mm(dscores, queries) + mm(probs, dout)
            dq[...] += mm(kv, dscores, TN)

        @pl.loop(0, whole)
        def _(index):
            visit(index, False)

        visit(whole, True)
        dq_ref[0, 0] = dq[...].T.astype(dq_ref.dtype)

    @pl.when(which == CORES - 1)
    def _():
        dkv_ref[0] = dkv[...].astype(dkv_ref.dtype)


def attend_back(places, lengths, queries, kv, out, dout, lse, piece):
    slots, _, columns, width = queries.shape
    length = kv.shape[1]
    rows = pl.BlockSpec((1, 1, columns, width), lambda s, e, *_: (s, e, 0, 0))
    keys = pl.BlockSpec((1, length, width), lambda s, e, *_: (s, 0, 0))
    return pl.pallas_call(
        functools.partial(attend_back_kernel, piece=piece),
        grid_spec=pltpu.PrefetchScalarGridSpec(
            num_scalar_prefetch=2,
            grid=(slots, CORES),
            in_specs=[
                rows,
                keys,
                rows,
                rows,
                pl.BlockSpec((1, 1, 1, columns), lambda s, e, *_: (s, e, 0, 0)),
            ],
            out_specs=[rows, keys],
            scratch_shapes=[pltpu.VMEM((length, width), F32), pltpu.VMEM((width, columns), F32)],
        ),
        out_shape=[
            jax.ShapeDtypeStruct(queries.shape, F32),
            jax.ShapeDtypeStruct(kv.shape, BF16),
        ],
        compiler_params=pltpu.CompilerParams(vmem_limit_bytes=VMEM),
        cost_estimate=pl.CostEstimate(
            flops=5 * 2 * slots * CORES * columns * length * width // 2,
            bytes_accessed=slots * length * width * 6,
            transcendentals=slots * CORES * columns * length // 2,
        ),
        name="attend_back",
    )(places, lengths, queries, kv, out, dout, lse)


def lower(rows, transposed=False):
    row = lax.broadcasted_iota(jnp.int32, (rows, rows), 0)
    column = lax.broadcasted_iota(jnp.int32, (rows, rows), 1)
    return row <= column if transposed else row >= column


def paired(first, second, shape):
    lane = lax.broadcasted_iota(jnp.int32, shape, 1)
    return jnp.where(lane < SHD, first, second)


def chunk_terms(raw_ref, raw_t_ref, bias_ref, bias_t_ref, rate_ref, rate_t_ref):
    rows = raw_ref.shape[1]
    steps = jax.nn.softplus(raw_ref[0] + bias_ref[...])
    steps_t = jax.nn.softplus(raw_t_ref[0] + bias_t_ref[...])
    high = lax.Precision.HIGHEST
    logs = mm(lower(rows).astype(F32), steps * rate_ref[...], NN, high)
    logs_t = mm(steps_t * rate_t_ref[...], lower(rows, True).astype(F32), NN, high)
    return steps, steps_t, logs, logs_t


def chunk_kernel(
    f_ref, b_ref, c_ref, raw_ref, raw_t_ref, bias_ref, bias_t_ref, rate_ref, rate_t_ref, skip_ref,
    out_ref, state_ref, logs_ref,
):
    steps, steps_t, logs, logs_t = chunk_terms(
        raw_ref, raw_t_ref, bias_ref, bias_t_ref, rate_ref, rate_t_ref
    )
    logs_ref[0] = logs
    rows = logs.shape[0]
    inject = b_ref[0]
    mix = jnp.where(lower(rows), mm(c_ref[0], inject, NT), 0.0)
    tail = jnp.exp(logs[rows - 1 :] - logs) * steps
    for pair in range(M_SHARE // 2):
        lanes = slice(pair * LANES, (pair + 1) * LANES)
        feats = f_ref[0, :, lanes]
        outs = []
        for head in (2 * pair, 2 * pair + 1):
            gap = jnp.minimum(logs[:, head : head + 1] - logs_t[head : head + 1, :], 0.0)
            kernel = mix * jnp.exp(gap) * steps_t[head : head + 1, :]
            outs.append(mm(kernel.astype(BF16), feats))
        wide = feats.astype(F32)
        out_ref[0, :, lanes] = paired(outs[0], outs[1], wide.shape) + skip_ref[:, lanes] * wide
        weight = paired(
            tail[:, 2 * pair : 2 * pair + 1], tail[:, 2 * pair + 1 : 2 * pair + 2], wide.shape
        )
        state_ref[0, lanes, :] = mm((wide * weight).astype(BF16), inject, TN).astype(BF16)


def carry_kernel(out_ref, c_ref, state_ref, logs_ref, ssd_ref):
    decay = jnp.exp(logs_ref[0])
    for pair in range(M_SHARE // 2):
        lanes = slice(pair * LANES, (pair + 1) * LANES)
        read = mm(c_ref[0], state_ref[0, lanes, :], NT)
        weight = paired(
            decay[:, 2 * pair : 2 * pair + 1], decay[:, 2 * pair + 1 : 2 * pair + 2], read.shape
        )
        ssd_ref[0, :, lanes] = (out_ref[0, :, lanes] + read * weight).astype(BF16)


def direct_kernel(d_ref, c_ref, logs_ref, direct_ref):
    decay = jnp.exp(logs_ref[0])
    for pair in range(M_SHARE // 2):
        lanes = slice(pair * LANES, (pair + 1) * LANES)
        grad = d_ref[0, :, lanes].astype(F32)
        weight = paired(
            decay[:, 2 * pair : 2 * pair + 1], decay[:, 2 * pair + 1 : 2 * pair + 2], grad.shape
        )
        direct_ref[0, lanes, :] = mm((grad * weight).astype(BF16), c_ref[0], TN).astype(BF16)


def chunk_back_kernel(
    f_ref, b_ref, c_ref, raw_ref, raw_t_ref, bias_ref, bias_t_ref, rate_ref, rate_t_ref, skip_ref,
    d_ref, state_ref, later_ref, agree_ref, df_ref, db_ref, dc_ref, draw_ref, sums_ref,
    columns, row_sums,
):
    steps, steps_t, logs, logs_t = chunk_terms(
        raw_ref, raw_t_ref, bias_ref, bias_t_ref, rate_ref, rate_t_ref
    )
    rows = logs.shape[0]
    inject, readout = b_ref[0], c_ref[0]
    keep = lower(rows)
    mix = jnp.where(keep, mm(readout, inject, NT), 0.0)
    columns[...] = jnp.zeros_like(columns)
    row_sums[...] = jnp.zeros_like(row_sums)
    decay = jnp.exp(logs)
    end_decay = jnp.exp(logs[rows - 1 :] - logs)
    tail = end_decay * steps
    dmix = jnp.zeros((rows, rows), F32)
    db = jnp.zeros((rows, NS), F32)
    dc = jnp.zeros((rows, NS), F32)
    to_state = jnp.zeros((rows, LANES), F32)
    from_state = jnp.zeros((rows, LANES), F32)
    skips = jnp.zeros((1, LANES), F32)
    head_lane = lax.broadcasted_iota(jnp.int32, (rows, LANES), 1)
    for pair in range(M_SHARE // 2):
        lanes = slice(pair * LANES, (pair + 1) * LANES)
        feats, grad = f_ref[0, :, lanes], d_ref[0, :, lanes]
        wide, wide_grad = feats.astype(F32), grad.astype(F32)
        later = later_ref[0, lanes, :]
        state = state_ref[0, lanes, :]
        pushed = mm(inject, later, NT)
        read = mm(readout, state, NT)
        push_part = wide * pushed
        read_part = wide_grad * read
        skip_part = wide * wide_grad
        grads = []
        for half, head in enumerate((2 * pair, 2 * pair + 1)):
            column = slice(head, head + 1)
            lane = lax.broadcasted_iota(jnp.int32, wide.shape, 1)
            mine = (lane < SHD) if half == 0 else (lane >= SHD)
            step_row = steps_t[column, :]
            gap = jnp.minimum(logs[:, column] - logs_t[column, :], 0.0)
            fade = jnp.exp(gap)
            dkernel = mm(jnp.where(mine, wide_grad, 0.0).astype(BF16), feats, NT)
            faded = dkernel * fade
            stepped = faded * step_row
            dmix = dmix + stepped
            kernel = mix * fade * step_row
            columns[column, 0:rows] = jnp.sum(faded * mix, axis=0, keepdims=True)
            here = head_lane == head
            row_sums[...] += jnp.where(here, jnp.sum(stepped * mix, axis=1, keepdims=True), 0.0)
            grads.append(mm(kernel.astype(BF16), grad, TN))
            to_state = to_state + jnp.where(
                here, jnp.sum(jnp.where(mine, push_part, 0.0), axis=1, keepdims=True), 0.0
            )
            from_state = from_state + jnp.where(
                here, jnp.sum(jnp.where(mine, read_part, 0.0), axis=1, keepdims=True), 0.0
            )
            skips = skips + jnp.where(
                here[:1],
                jnp.sum(
                    jnp.sum(jnp.where(mine, skip_part, 0.0), axis=1, keepdims=True),
                    axis=0,
                    keepdims=True,
                ),
                0.0,
            )
        first, second = slice(2 * pair, 2 * pair + 1), slice(2 * pair + 1, 2 * pair + 2)
        weight = paired(tail[:, first], tail[:, second], wide.shape)
        df_ref[0, :, lanes] = (
            paired(grads[0], grads[1], wide.shape) + skip_ref[:, lanes] * wide_grad + weight * pushed
        )
        db = db + mm((wide * weight).astype(BF16), later)
        seen = paired(decay[:, first], decay[:, second], wide.shape)
        dc = dc + mm((wide_grad * seen).astype(BF16), state)
    low = dmix * jnp.where(keep, 1.0, 0.0)
    low = low.astype(BF16)
    db_ref[0] = db + mm(low, readout, TN)
    dc_ref[0] = dc + mm(low, inject)
    direct = columns[...].T[:rows]
    push = end_decay * to_state
    dlogs = row_sums[...] - steps * direct + decay * from_state - steps * push
    end = jnp.sum(steps * push, axis=0, keepdims=True) + decay[rows - 1 :] * agree_ref[0]
    last = lax.broadcasted_iota(jnp.int32, (rows, LANES), 0) == rows - 1
    dlogs = dlogs + jnp.where(last, end, 0.0)
    summed = mm(lower(rows, True).astype(F32), dlogs, NN, lax.Precision.HIGHEST)
    dsteps = direct + push + summed * rate_ref[...]
    draw = dsteps * jax.nn.sigmoid(raw_ref[0] + bias_ref[...])
    draw_ref[0] = draw
    line = lax.broadcasted_iota(jnp.int32, (8, LANES), 0)
    dbias = jnp.sum(draw, axis=0, keepdims=True)
    dlog = jnp.sum(summed * steps, axis=0, keepdims=True) * rate_ref[...]
    sums_ref[0] = jnp.where(
        line == 0, dbias, jnp.where(line == 1, dlog, jnp.where(line == 2, skips, 0.0))
    )


def over_pieces(kernel, name, args, whole, outs, flops, scratch=()):
    pieces = args[0].shape[0]

    def spec(shape, split):
        if split:
            return pl.BlockSpec((1,) + shape[1:], lambda i: (i,) + (0,) * (len(shape) - 1))
        return pl.BlockSpec(shape, lambda i: (0,) * len(shape))

    shapes = [(arg.shape, index not in whole) for index, arg in enumerate(args)]
    nbytes = sum(arg.size * arg.dtype.itemsize for arg in args)
    nbytes += sum(math.prod(shape) * dtype.dtype.itemsize for shape, dtype in outs)
    return pl.pallas_call(
        kernel,
        grid=(pieces,),
        in_specs=[spec(shape, split) for shape, split in shapes],
        out_specs=[spec(shape, True) for shape, _ in outs],
        out_shape=[jax.ShapeDtypeStruct(shape, dtype) for shape, dtype in outs],
        scratch_shapes=list(scratch),
        compiler_params=pltpu.CompilerParams(vmem_limit_bytes=VMEM),
        cost_estimate=pl.CostEstimate(flops=flops, bytes_accessed=nbytes, transcendentals=0),
        name=name,
    )(*args)


def carried(place, states, decays, reverse):
    groups = place.size["z"]
    z, chips = place.at["z"], place.chips
    e, slots = states.shape[:2]
    share = M_SHARE // groups
    parts = states.reshape(e, slots, groups, share * SHD, NS)
    parts = place.exchange(parts, "z", 2)
    by_h = place.by_core(parts, parts[::-1]).astype(F32).reshape(e, slots, groups, share, SHD, NS)
    mine = lax.dynamic_slice_in_dim(decays, z * share, share, 4)
    here = lax.dynamic_index_in_dim(mine, place.chip, 0, False)
    order = [(h, k) for h in range(CORES) for k in range(groups)]
    if reverse:
        order = order[::-1]
    run = jnp.zeros((slots, share, SHD, NS), F32)
    fade = jnp.ones((slots, share), F32)
    entered, faded = {}, {}
    for h, k in order:
        entered[h, k], faded[h, k] = run, fade
        factor = here[k, h]
        run = factor[..., None, None] * run + by_h[h, :, k]
        fade = factor * fade
    totals = place.gather(place.gather(run.astype(BF16), "b", 0), "a", 0)
    totals = totals.reshape(chips, slots, share, SHD, NS)
    fades = jnp.prod(mine, axis=(1, 2))
    carry = jnp.zeros_like(run)
    for chip in range(chips)[::-1] if reverse else range(chips):
        reached = chip > place.chip if reverse else chip < place.chip
        new = fades[chip][..., None, None] * carry + totals[chip].astype(F32)
        carry = jnp.where(reached, new, carry)
    whole = [
        jnp.stack(
            [entered[h, k] + faded[h, k][..., None, None] * carry for k in range(groups)], 1
        ).astype(BF16)
        for h in range(CORES)
    ]
    back = jnp.stack([place.by_core(whole[0], whole[1]), place.by_core(whole[1], whole[0])])
    back = place.exchange(back.reshape(e, slots, groups, share * SHD, NS), "z", 2)
    return back.reshape(e, slots, M_SHARE * SHD, NS)


def shards(
    hidden_in,
    out_grad,
    lengths,
    input_gain,
    attn_in_weight,
    attn_out_weight,
    zgate_weight,
    mixer_in_weight,
    step_weight,
    conv_weight,
    conv_bias,
    step_bias,
    decay_log,
    skip_scale,
    mixer_gain,
    mixer_out_weight,
    post_gain,
    gate_weight,
    up_weight,
    down_weight,
):
    place = Place()
    core = place.at["c"]
    groups, chips, devices = place.size["z"], place.chips, place.devices
    na, nb = place.size["a"], place.size["b"]
    slots, piece, width = hidden_in.shape
    span = piece * groups
    rows_all = CORES * slots * piece
    rows_halo = CORES * slots * (piece + HALO)
    q_cols, m_cols = Q_SHARE * HD, M_SHARE * SHD
    az_cols = q_cols + 2 * HD + m_cols
    c_cols = m_cols + NS
    shard_rows = attn_in_weight.shape[0]
    out_rows, mix_rows, ff_rows = (
        attn_out_weight.shape[0],
        mixer_out_weight.shape[0],
        down_weight.shape[0],
    )
    ff_half = ff_rows * groups * chips

    rim = lax.ppermute(
        hidden_in[:, piece - KC + 1 :], AXES, [(i, i + 1) for i in range(devices - 1)]
    )
    block = jnp.concatenate(
        [jnp.zeros((slots, HALO - KC + 1, width), BF16), rim, hidden_in], axis=1
    )
    other_index = place.flat + jnp.where(core == 0, groups, -groups)
    pieces_at = jnp.stack([place.flat, other_index]) * piece
    positions = pieces_at[:, None] + jnp.arange(piece, dtype=jnp.int32)
    valid = (positions[:, None, :] < lengths[None, :, None]).astype(F32)
    tokens = jnp.stack([block, place.swap(block)]).astype(F32)
    dy_own = out_grad.astype(F32) * valid[0][..., None]
    dy_low = dy_own.astype(BF16)
    dy = jnp.stack([dy_low, place.swap(dy_low)]).reshape(rows_all, width)

    small = jnp.concatenate([input_gain, mixer_gain, post_gain, conv_bias, conv_weight.reshape(-1)])
    small_cols = -(-small.shape[0] // shard_rows)
    small = jnp.pad(small, (0, small_cols * shard_rows - small.shape[0]))
    small = small.reshape(shard_rows, small_cols)
    step_at = c_cols
    small_at = step_at + M_SHARE
    ms_cols = -(-(small_at + small_cols) // LANES) * LANES

    def ff_columns(weight, half):
        return weight.reshape(shard_rows, chips, CORES, -1)[:, :, half].reshape(shard_rows, -1)

    def half_columns(half):
        return jnp.concatenate(
            [
                attn_in_weight[:, half * q_cols : (half + 1) * q_cols],
                attn_in_weight[:, QH * HD + half * HD : QH * HD + (half + 1) * HD],
                attn_in_weight[:, (QH + KVH + half) * HD : (QH + KVH + half + 1) * HD],
                zgate_weight[:, half * m_cols : (half + 1) * m_cols],
                mixer_in_weight[:, half * m_cols : (half + 1) * m_cols],
                mixer_in_weight[:, SH * SHD + half * NS : SH * SHD + (half + 1) * NS],
                step_weight[:, half * M_SHARE : (half + 1) * M_SHARE],
                small,
                jnp.zeros((shard_rows, ms_cols - small_at - small_cols), BF16),
                ff_columns(gate_weight, half),
                ff_columns(up_weight, half),
            ],
            axis=1,
        )

    halves = (half_columns(0), half_columns(1))
    kept = place.by_core(*halves)
    got = place.swap(place.by_core(halves[1], halves[0]))
    both = jnp.stack([place.by_core(kept, got), place.by_core(got, kept)])
    cut = (0, az_cols, az_cols + ms_cols, az_cols + ms_cols + ff_half, both.shape[2])
    w_az, w_ms, w_gate, w_up = (
        place.gather_chips(both[:, :, cut[i] : cut[i + 1]], 1, i % 2 == 0).reshape(width, -1)
        for i in range(4)
    )
    w_out = place.gather_chips(
        jnp.concatenate([attn_out_weight, mixer_out_weight], axis=0), 0, True
    )
    w_out = w_out.reshape(2, chips // 2, groups, out_rows + mix_rows, width)
    kept = lax.dynamic_index_in_dim(w_out, core, 0, False)
    got = place.swap(lax.dynamic_index_in_dim(w_out, 1 - core, 0, False))
    w_out = jnp.stack([place.by_core(kept, got), place.by_core(got, kept)], 1)
    w_attn_out = w_out[..., :out_rows, :].reshape(q_cols, width)
    w_mixer_out = w_out[..., out_rows:, :].reshape(m_cols, width)
    w_down = place.gather_chips(down_weight, 0, False).reshape(ff_half, width)

    vectors = w_ms[:, small_at : small_at + small_cols].reshape(devices, -1).astype(F32)
    sizes = [input_gain.shape[0], mixer_gain.shape[0], post_gain.shape[0], conv_bias.shape[0]]
    ends = [sum(sizes[: k + 1]) for k in range(4)]
    gain_in = vectors[:, : ends[0]].reshape(-1)
    gain_mixer = vectors[:, ends[0] : ends[1]].reshape(-1)
    gain_mixer = place.by_core(gain_mixer[:m_cols], gain_mixer[m_cols:])
    gain_post = vectors[:, ends[1] : ends[2]].reshape(-1)
    shift_all = vectors[:, ends[2] : ends[3]].reshape(-1)
    taps_all = vectors[:, ends[3] : ends[3] + KC * sizes[3]].reshape(devices, KC, sizes[3])
    taps_all = jnp.transpose(taps_all, (1, 0, 2)).reshape(KC, -1)

    def conv_half(value):
        first = jnp.concatenate(
            [value[..., :m_cols], value[..., 2 * m_cols : 2 * m_cols + NS]], axis=-1
        )
        second = jnp.concatenate(
            [value[..., m_cols : 2 * m_cols], value[..., 2 * m_cols + NS :]], axis=-1
        )
        return place.by_core(first, second)

    taps, shift = conv_half(taps_all), conv_half(shift_all)
    head_terms = lax.all_gather(jnp.stack([step_bias, decay_log, skip_scale]), "sp", axis=1, tiled=True)
    head_terms = lax.dynamic_slice_in_dim(head_terms, core * M_SHARE, M_SHARE, 1)
    bias, log_rates, skip = head_terms[0], head_terms[1], head_terms[2]
    rates = -jnp.exp(log_rates)

    scale_in = inverse_rms(tokens)
    normed = (tokens * scale_in * gain_in).astype(BF16).reshape(rows_halo, width)

    def body_rows(value):
        return value.reshape(CORES, slots, piece + HALO, -1)[:, :, HALO:]

    linear = body_rows(mm(normed, w_az[:, : q_cols + 2 * HD]))
    zgate = body_rows(mm(normed, w_az[:, q_cols + 2 * HD :]).astype(BF16))
    mixed_step = mm(normed, w_ms).astype(BF16).reshape(CORES, slots, piece + HALO, ms_cols)
    mixed = mixed_step[..., :c_cols]
    step_raw = mixed_step[:, :, HALO:, step_at:small_at].astype(F32)

    cos_part, sin_part = rotary_tables(positions, HD)
    cos_part, sin_part = cos_part[:, None, :, None], sin_part[:, None, :, None]
    queries = rotate(
        linear[..., :q_cols].reshape(CORES, slots, piece, Q_SHARE, HD), cos_part, sin_part
    ).astype(BF16)
    keys = rotate(
        linear[..., q_cols : q_cols + HD][..., None, :], cos_part, sin_part
    ).astype(BF16)[..., 0, :]
    kv_own = jnp.concatenate([keys, linear[..., q_cols + HD :].astype(BF16)], axis=-1)
    kv_own = place.by_core(kv_own, kv_own[::-1])
    kv = jnp.stack(
        [
            place.gather_chips(kv_own[:, s], 1, s % 2 == 0).reshape(-1, 2 * HD)
            for s in range(slots)
        ]
    )

    def by_heads(value, before, after):
        value = jnp.transpose(value, (1, 0, 3, 2, 4)).reshape(slots, CORES, Q_SHARE * piece, HD)
        return jnp.pad(value, ((0, 0), (0, 0), (0, 0), (before, after)))

    def from_heads(value):
        value = value.reshape(slots, CORES, Q_SHARE, piece, HD)
        return jnp.transpose(value, (1, 0, 3, 2, 4))

    scale = HD ** (-0.5)
    queries = by_heads(queries * jnp.asarray(scale, BF16), 0, HD)
    heads_out, lse = attend(pieces_at, lengths, queries, kv, piece)
    attended = from_heads(heads_out[..., HD:]).reshape(rows_all, q_cols)

    pre = shift
    for tap in range(KC):
        first = HALO - KC + 1 + tap
        pre = pre + taps[tap] * mixed[:, :, first : first + piece].astype(F32)
    conv_out, conv_slope = silu_and_slope(pre)
    conv_out = conv_out.astype(BF16)
    features = conv_out[..., :m_cols].reshape(CORES * slots, piece, m_cols)
    shared = conv_out[..., m_cols:]
    shared_other = place.swap(shared)[::-1]
    inject = place.by_core(shared, shared_other).reshape(CORES * slots, piece, NS)
    readout = place.by_core(shared_other, shared).reshape(CORES * slots, piece, NS)
    raw = jnp.pad(step_raw.reshape(CORES * slots, piece, M_SHARE), ((0, 0), (0, 0), (0, LANES - M_SHARE)))
    raw_t = jnp.transpose(raw[..., :16], (0, 2, 1))
    bias_row = jnp.pad(bias, (0, LANES - M_SHARE))[None]
    rate_row = jnp.pad(rates, (0, LANES - M_SHARE))[None]
    bias_col, rate_col = bias_row[0, :16, None], rate_row[0, :16, None]
    skip_row = jnp.repeat(skip, SHD)[None]
    pieces = CORES * slots
    state_flops = 2 * pieces * piece * m_cols * (piece + 2 * NS)
    chunk_args = [
        features, inject, readout, raw, raw_t, bias_row, bias_col, rate_row, rate_col, skip_row,
    ]
    within, local_state, logs = over_pieces(
        chunk_kernel,
        "chunk",
        chunk_args,
        range(5, 10),
        [
            ((pieces, piece, m_cols), F32),
            ((pieces, m_cols, NS), BF16),
            ((pieces, piece, LANES), F32),
        ],
        state_flops,
    )
    decays = jnp.exp(logs[:, piece - 1, :M_SHARE]).reshape(CORES, slots, M_SHARE)
    decays_h = place.by_core(decays, decays[::-1])
    all_decays = lax.all_gather(decays_h, AXES, axis=0, tiled=False)
    all_decays = all_decays.reshape(chips, CORES, groups, CORES, slots, M_SHARE)
    all_decays = lax.dynamic_index_in_dim(all_decays, core, 1, False)
    state_in = carried(
        place, local_state.reshape(CORES, slots, m_cols, NS), all_decays, False
    ).reshape(pieces, m_cols, NS)
    (ssd,) = over_pieces(
        carry_kernel,
        "carry",
        [within, readout, state_in, logs],
        (),
        [((pieces, piece, m_cols), BF16)],
        2 * pieces * piece * m_cols * NS,
    )
    ssd = ssd.reshape(CORES, slots, piece, m_cols).astype(F32)
    gate_value, gate_slope = silu_and_slope(zgate.astype(F32))
    gated_raw = ssd * gate_value
    squares = jnp.sum(gated_raw * gated_raw, axis=-1)
    squares = squares + place.swap(squares)[::-1]
    scale_mixer = lax.rsqrt(squares / (SH * SHD) + 1e-05)[..., None]
    gated = (gated_raw * scale_mixer * gain_mixer).astype(BF16).reshape(rows_all, m_cols)

    def own_sum(partial):
        partial = partial.reshape(CORES, -1, partial.shape[-1])
        return partial[0] + place.swap(partial[1].astype(BF16)).astype(F32)

    def with_other(value):
        return jnp.stack([value, place.swap(value)]).reshape(-1, value.shape[-1])

    mixers = own_sum(mm(attended, w_attn_out) + mm(gated, w_mixer_out))
    residual = tokens[0][:, HALO:].reshape(-1, width) + mixers
    scale_post = inverse_rms(residual)
    post = with_other((residual * scale_post * gain_post).astype(BF16))
    gate_lin = mm(post, w_gate)
    up_lin = mm(post, w_up)
    gate_act, gate_act_slope = silu_and_slope(gate_lin)
    hidden = (gate_act * up_lin).astype(BF16)
    valid_own = valid[0].reshape(-1, 1)
    layer_out = (valid_own * (residual + own_sum(mm(hidden, w_down)))).astype(BF16)

    dhidden = mm(dy, w_down, NT)
    dgate = (dhidden * up_lin * gate_act_slope).astype(BF16)
    dup = (dhidden * gate_act).astype(BF16)

    def scatter_parity(grad, rows, b_first):
        return place.reduce_chips(grad.reshape(na, nb, groups, rows, width), 0, b_first)

    def scatter_columns(grad, b_first):
        return place.reduce_chips(
            grad.reshape(na, nb, CORES, groups, shard_rows, -1), 1, b_first
        )

    grad_down = scatter_parity(mm(hidden, dy, TN), ff_rows, True)
    grad_gate = scatter_columns(mm(post, dgate, TN), False)
    grad_up = scatter_columns(mm(post, dup, TN), True)
    dpost = own_sum(mm(dgate, w_gate, NT) + mm(dup, w_up, NT))
    dresidual = dy_own.reshape(-1, width) + rms_back(residual, scale_post, gain_post, dpost)
    grad_post_gain = jnp.sum(dpost * residual * scale_post, axis=0)
    dmix = with_other(dresidual.astype(BF16))

    dattended = mm(dmix, w_attn_out, NT).astype(BF16)
    dgated = mm(dmix, w_mixer_out, NT).reshape(CORES, slots, piece, m_cols)
    grad_outs = jnp.concatenate(
        [
            mm(attended, dmix, TN).reshape(chips // 2, CORES, groups, out_rows, width),
            mm(gated, dmix, TN).reshape(chips // 2, CORES, groups, mix_rows, width),
        ],
        axis=3,
    )
    kept = lax.dynamic_index_in_dim(grad_outs, core, 1, False)
    got = place.swap(lax.dynamic_index_in_dim(grad_outs, 1 - core, 1, False).astype(BF16))
    got = got.astype(F32)
    grad_outs = jnp.concatenate([place.by_core(kept, got), place.by_core(got, kept)], axis=0)
    grad_outs = scatter_parity(grad_outs, out_rows + mix_rows, False)
    scaled = dgated * gain_mixer
    inner = jnp.sum(scaled * gated_raw, axis=-1)
    inner = (inner + place.swap(inner)[::-1])[..., None] / (SH * SHD)
    dgated_raw = scale_mixer * scaled - gated_raw * (scale_mixer**3 * inner)
    grad_mixer_gain = jnp.sum(dgated * gated_raw * scale_mixer, axis=(0, 1, 2))
    dssd = (dgated_raw * gate_value).astype(BF16).reshape(pieces, piece, m_cols)
    dzgate = (dgated_raw * ssd * gate_slope).astype(BF16)

    (direct,) = over_pieces(
        direct_kernel,
        "direct",
        [dssd, readout, logs],
        (),
        [((pieces, m_cols, NS), BF16)],
        2 * pieces * piece * m_cols * NS,
    )
    later = carried(
        place, direct.reshape(CORES, slots, m_cols, NS), all_decays, True
    ).reshape(pieces, m_cols, NS)

    dout = by_heads(
        dattended.reshape(CORES, slots, piece, Q_SHARE, HD), HD, 0
    )
    dqueries, dkv = attend_back(pieces_at, lengths, queries, kv, heads_out, dout, lse, piece)
    dkv_own = jnp.stack(
        [
            place.reduce_chips(
                dkv[s].reshape(na, nb, CORES, groups, piece, 2 * HD), 1, s % 2 == 0
            )
            for s in range(slots)
        ],
        axis=1,
    )
    dkv_own = place.by_core(dkv_own, dkv_own[::-1])

    agree = jnp.sum(
        later.astype(F32) * state_in.astype(F32), axis=-1
    ).reshape(pieces, M_SHARE, SHD)
    agree = jnp.pad(jnp.sum(agree, axis=-1), ((0, 0), (0, LANES - M_SHARE)))[:, None]
    dfeatures, dinject, dreadout, draw, sums = over_pieces(
        chunk_back_kernel,
        "chunk_back",
        chunk_args + [dssd, state_in, later, agree],
        range(5, 10),
        [
            ((pieces, piece, m_cols), F32),
            ((pieces, piece, NS), F32),
            ((pieces, piece, NS), F32),
            ((pieces, piece, LANES), F32),
            ((pieces, 8, LANES), F32),
        ],
        4 * state_flops,
        [pltpu.VMEM((LANES, 2 * LANES), F32), pltpu.VMEM((piece, LANES), F32)],
    )
    head_sums = jnp.sum(sums, axis=0)[:3, :M_SHARE]
    nothing = jnp.zeros_like(head_sums)
    head_sums = jnp.concatenate(
        [place.by_core(head_sums, nothing), place.by_core(nothing, head_sums)], axis=1
    )
    head_sums = lax.psum(head_sums, AXES)
    head_sums = lax.dynamic_slice_in_dim(head_sums, place.at["z"] * (SH // groups), SH // groups, 1)

    dinject = dinject.reshape(CORES, slots, piece, NS)
    dreadout = dreadout.reshape(CORES, slots, piece, NS)
    dshared = place.by_core(dinject, dreadout) + place.swap(
        place.by_core(dreadout, dinject).astype(BF16)
    )[::-1].astype(F32)
    dconv = jnp.concatenate([dfeatures.reshape(CORES, slots, piece, m_cols), dshared], axis=-1)
    dpre = dconv * conv_slope
    grad_taps = []
    dmixed = jnp.zeros((CORES, slots, piece + HALO, c_cols), F32)
    for tap in range(KC):
        first = HALO - KC + 1 + tap
        seen = mixed[:, :, first : first + piece].astype(F32)
        grad_taps.append(jnp.sum(dpre * seen, axis=(0, 1, 2)))
        dmixed = dmixed + jnp.pad(
            dpre * taps[tap], ((0, 0), (0, 0), (first, KC - 1 - tap), (0, 0))
        )
    grad_shift = jnp.sum(dpre, axis=(0, 1, 2))
    dmixed = dmixed.astype(BF16)

    def halo_rows(value):
        value = value.reshape(CORES, slots, piece, -1)
        return jnp.pad(value, ((0, 0), (0, 0), (HALO, 0), (0, 0)))

    dstep = draw[..., :M_SHARE].astype(BF16)
    dms = jnp.concatenate(
        [
            dmixed,
            halo_rows(dstep),
            jnp.zeros((CORES, slots, piece + HALO, ms_cols - small_at), BF16),
        ],
        axis=-1,
    ).reshape(rows_halo, ms_cols)
    dq_rows = from_heads(dqueries[..., :HD] * scale)
    dq_rows = rotate(dq_rows, cos_part, -sin_part).reshape(CORES, slots, piece, q_cols)
    dk_rows = rotate(dkv_own[..., None, :HD], cos_part, -sin_part)[..., 0, :]
    dlin = jnp.concatenate([dq_rows, dk_rows, dkv_own[..., HD:]], axis=-1).astype(BF16)
    daz = halo_rows(jnp.concatenate([dlin, dzgate], axis=-1)).reshape(rows_halo, az_cols)
    dnormed = mm(daz, w_az, NT) + mm(dms, w_ms, NT)
    dnormed = own_sum(dnormed).reshape(slots, piece + HALO, width)
    rim_back = lax.ppermute(
        dnormed[:, HALO - KC + 1 : HALO].astype(BF16),
        AXES,
        [(i + 1, i) for i in range(devices - 1)],
    ).astype(F32)
    dnormed = dnormed[:, HALO:] + jnp.pad(rim_back, ((0, 0), (piece - KC + 1, 0), (0, 0)))
    own, own_scale = tokens[0][:, HALO:], scale_in[0][:, HALO:]
    input_grad = dresidual.reshape(slots, piece, width) + rms_back(
        own, own_scale, gain_in, dnormed
    )
    grad_input_gain = jnp.sum(dnormed * own * own_scale, axis=(0, 1))

    zero_half = jnp.zeros((m_cols,), F32)

    def conv_whole(value):
        none = jnp.zeros_like(value)
        first, second = place.by_core(value, none), place.by_core(none, value)
        return jnp.concatenate(
            [first[..., :m_cols], second[..., :m_cols], first[..., m_cols:], second[..., m_cols:]],
            axis=-1,
        )

    grad_mixer_gain = jnp.concatenate(
        [place.by_core(grad_mixer_gain, zero_half), place.by_core(zero_half, grad_mixer_gain)]
    )
    grad_taps = conv_whole(jnp.stack(grad_taps)).reshape(KC, devices, -1)
    vector_grads = jnp.concatenate(
        [
            grad_input_gain.reshape(devices, -1),
            grad_mixer_gain.reshape(devices, -1),
            grad_post_gain.reshape(devices, -1),
            conv_whole(grad_shift).reshape(devices, -1),
            jnp.transpose(grad_taps, (1, 0, 2)).reshape(devices, -1),
        ],
        axis=1,
    )
    vector_size = vector_grads.shape[1]
    vector_grads = jnp.pad(
        vector_grads, ((0, 0), (0, small_cols * shard_rows - vector_size))
    ).reshape(width, small_cols)
    grad_az = scatter_columns(mm(normed, daz, TN), False)
    grad_ms = mm(normed, dms, TN)
    grad_ms = lax.dynamic_update_slice(grad_ms, vector_grads, (0, small_at))
    grad_ms = scatter_columns(grad_ms, True)

    columns = jnp.concatenate([grad_az, grad_ms, grad_gate, grad_up], axis=-1)
    kept = lax.dynamic_index_in_dim(columns, core, 0, False)
    got = place.swap(lax.dynamic_index_in_dim(columns, 1 - core, 0, False))
    first, second = place.by_core(kept, got), place.by_core(got, kept)

    def both_halves(start, size):
        return jnp.concatenate([first[:, start : start + size], second[:, start : start + size]], 1)

    def ff_whole(start):
        parts = [
            half[:, start : start + ff_half].reshape(shard_rows, chips, 1, -1)
            for half in (first, second)
        ]
        return jnp.concatenate(parts, axis=2).reshape(shard_rows, -1)

    grad_attn_in = jnp.concatenate(
        [both_halves(0, q_cols), both_halves(q_cols, HD), both_halves(q_cols + HD, HD)], axis=1
    )
    grad_zgate = both_halves(q_cols + 2 * HD, m_cols)
    grad_mixer_in = jnp.concatenate(
        [both_halves(az_cols, m_cols), both_halves(az_cols + m_cols, NS)], axis=1
    )
    grad_step = both_halves(az_cols + step_at, M_SHARE)
    small_sum = first + second
    small_sum = small_sum[:, az_cols + small_at : az_cols + small_at + small_cols].reshape(-1)

    return (
        layer_out.reshape(slots, piece, width),
        input_grad,
        small_sum[: ends[0]],
        grad_attn_in,
        grad_outs[:out_rows],
        grad_zgate,
        grad_mixer_in,
        grad_step,
        small_sum[ends[3] : vector_size].reshape(KC, -1),
        small_sum[ends[2] : ends[3]],
        head_sums[0],
        head_sums[1],
        head_sums[2],
        small_sum[ends[0] : ends[1]],
        grad_outs[out_rows:],
        small_sum[ends[1] : ends[2]],
        ff_whole(az_cols + ms_cols),
        ff_whole(az_cols + ms_cols + ff_half),
        grad_down,
    )


def solution(mesh):
    rows, columns, vector = P(AXES, None), P(None, AXES), P(AXES)
    tokens, heads = P(None, AXES, None), P("sp")
    in_specs = (
        tokens,
        tokens,
        P(),
        vector,
        rows,
        rows,
        rows,
        rows,
        rows,
        columns,
        vector,
        heads,
        heads,
        heads,
        vector,
        rows,
        vector,
        rows,
        rows,
        rows,
    )
    out_specs = (
        tokens,
        tokens,
        vector,
        rows,
        rows,
        rows,
        rows,
        rows,
        columns,
        vector,
        heads,
        heads,
        heads,
        vector,
        rows,
        vector,
        rows,
        rows,
        rows,
    )
    return jax.shard_map(shards, mesh=mesh, in_specs=in_specs, out_specs=out_specs, check_vma=False)
```

time: 2630 us -> 1020 us (0.39); the launches traced: 2620 us -> 1040 us
  waiting for transfers between devices: 1530 us -> 281 us
  blocking collectives: 475 us -> 119 us
  matrix products: 300 us -> 57.9 us
  starting transfers between devices: 17.6 us -> 199 us
  Pallas kernels: 0 us -> 74.2 us
  local copies, waits for them, and re-layouts: 129 us -> 170 us
  loops' own time: 30 us -> 0 us
    reduce_scatter x9 -> x0, waiting for transfers between devices: 1110 us -> none  [the longest x1 188 us: shards(): lax.psum_scatter(grad_gate, ('ctx', 'sp'), scatter_dimension=0, tiled=True)]
    all_gather x11 -> x0, waiting for transfers between devices: 349 us -> none  [the longest x1 60 us: shards(): lax.all_gather(gate_weight, ('ctx', 'sp'), axis=0, tiled=True)]
    ppermute x2 -> x114, waiting for transfers between devices: 4 us -> 281 us  [the longest x112 281 us: shift(): return lax.ppermute(x, AXES, self.pairs(dim, by))]
    dot_general x60 -> x22, matrix products: 300 us -> 57.9 us  [mm(): lax.dot_general(left, right, dims, precision=precision, preferred_element...]
    unnamed x3 -> x0, blocking collectives: 222 us -> none
    ppermute x2 -> x114, starting transfers between devices: 3.92 us -> 199 us  [the longest x112 195 us: shift(): return lax.ppermute(x, AXES, self.pairs(dim, by))]
    all_to_all x3 -> x0, blocking collectives: 109 us -> none  [the longest x1 59.9 us: shards(): lax.all_to_all(back_rows.astype(jnp.bfloat16), 'sp', split_axis=1, concat...]
    pallas_call x0 -> x6, Pallas kernels: none -> 74.2 us  [the longest x4 45.9 us: over_pieces(): pl.pallas_call(kernel, grid=(pieces,), in_specs=[spec(shape, split) for s...]
  transfers between devices with their start and end apart: 26 -> 114, of which waited for: 18 -> 50; matrix products, arithmetic and copies ran while one was open for 17% -> 29% of each run, Pallas kernels for 0% -> 7%
where the time goes in v1:
time: 1020 us; the launch traced here: 1040 us
  waiting for transfers between devices  281 us (28%)
  starting transfers between devices  199 us (20%)
  local copies, waits for them, and re-layouts  170 us (17%)
  other arithmetic  128 us (13%)
  blocking collectives  119 us (12%)
  Pallas kernels  74.2 us (7%)
  matrix products  57.9 us (6%)
    ppermute x112, waiting for transfers between devices, shift(): return lax.ppermute(x, AXES, self.pairs(dim, by))  281 us
    ppermute x112, starting transfers between devices, shift(): return lax.ppermute(x, AXES, self.pairs(dim, by))  195 us
    all_gather x1, blocking collectives, shards(): all_decays = lax.all_gather(decays_h, AXES, axis=0, tiled=False)  66.4 us
    dot_general x22, matrix products, mm(): lax.dot_general(left, right, dims, precision=precision, preferred_element...  57.9 us
    pallas_call x4, Pallas kernels, over_pieces(): pl.pallas_call(kernel, grid=(pieces,), in_specs=[spec(shape, split) for s...  45.9 us
    psum x1, blocking collectives, shards(): head_sums = lax.psum(head_sums, AXES)  40.9 us
    another operation x39, other arithmetic, place(): jnp.stack([jnp.where(v == 0, parts[0], parts[1]), jnp.where(v == 0, parts...  31.2 us
    unnamed x485, local copies, waits for them, and re-layouts  28.3 us
  transfers between devices with their start and end apart: 114, of which 50 were waited for; matrix products, arithmetic and copies ran while one was open for 29% of the time, Pallas kernels for 7%

profile of v1, /device:TPU:0, one launch (start us, length us, event | category | flops | bytes accessed | tf_op | source)
XLA Modules:
  0.0 1035.1 jit_solution(12741390505519335035)
XLA Ops:
  22.4 11.9 %all-gather.1 = f32[4,6,3]{1,2,0:T(4,128)S(1)} all-gather(f32[1,6,3]{1,2,0:T(4,128)S(1)} %maximum_bitcast_fusion.1), channel_id=1, replica_groups=mesh['ctx'=8,'sp'=4] {'sp'}, dimensions={0}, use_global_device_ids=true | all-gather | bytes 360 | tf_op jit(solution)/shard_map/all_gather | solution.py:686
  68.4 6.7 collective-permute-done.47
  81.2 6.1 collective-permute-done.41
  88.0 6.9 collective-permute-done.42
  100.5 7.5 collective-permute-done.3
  108.6 5.6 collective-permute-done.4
  120.3 6.7 collective-permute-done.8
  129.2 4.9 collective-permute-done.9
  158.4 8.2 collective-permute-done.6
  175.7 13.4 %collective-permute-done.27 = bf16[2,4,64,1024]{3,2,1,0:T(8,128)(2,1)} collective-permute-done((bf16[2,4,64,1024]{3,2,1,0:T(8,128)(2,1)}, bf16[2,4,64,1024]{3,2,1,0:T(8,128)(2,1)}, u32[]{:S(2)}, u32[]{:S(2)}) %collective-permute-start.27) | collective-permute-done | bytes 1048608 | tf_op jit(solution)/shard_map/ppermute | solution.py:75
  192.2 35.6 %collective-permute-done.7 = bf16[2,2,4,32,1024]{4,3,2,1,0:T(8,128)(2,1)S(1)} collective-permute-done((bf16[2,2,4,32,1024]{4,3,2,1,0:T(8,128)(2,1)S(1)}, bf16[2,2,4,32,1024]{4,3,2,1,0:T(8,128)(2,1)S(1)}, u32[]{:S(2)}, u32[]{:S(2)}) %collective-permute-start.7) | collective-permute-done | bytes 1048608 | tf_op jit(solution)/shard_map/ppermute | solution.py:75
  249.1 8.7 chunk.1
  258.5 66.4 %all-gather = f32[64,2,12]{2,1,0:T(2,128)S(1)} all-gather(f32[2,2,12]{2,1,0:T(2,128)S(1)} %reverse_select_fusion.4), channel_id=2, replica_groups=mesh['ctx'=8,'sp'=4] {'ctx','sp'}, dimensions={0}, use_global_device_ids=true | all-gather | bytes 6336 | tf_op jit(solution)/shard_map/all_gather | solution.py:769
  373.8 7.2 collective-permute-done.18
  381.0 6.6 collective-permute-done.19
  394.4 4.8 collective-permute-start.20
  411.2 6.1 collective-permute-done.34
  435.8 5.1 carry.1
  453.4 11.6 %attend.1 = (bf16[2,2,768,128]{3,2,1,0:T(8,128)(2,1)}, f32[2,2,1,768]{3,2,1,0:T(1,128)}) custom-call(s32[2]{0:T(128)} %copy-done.227, s32[2]{0:T(128)} %lengths.3, bf16[2,2,768,128]{3,2,1,0:T(8,128)(2,1)} %pad.65.q_ref, bf16[2,6144,128]{2,1,0:T(8,128)(2,1)} %pad_maximum_fusion.1.kv_ref), custom_call_target="tpu_custom_call" | custom-call | flops 4831838208 | bytes 6291456 | tf_op jit(solution)/shard_map/attend/pallas_call | solution.py:212
  476.4 22.5 %collective-permute-start.45 = (bf16[2,2,4,32,1024]{4,3,2,1,0:T(8,128)(2,1)}, bf16[2,2,4,32,1024]{4,3,2,1,0:T(8,128)(2,1)}, u32[]{:S(2)}, u32[]{:S(2)}) collective-permute-start(bf16[2,2,4,32,1024]{4,3,2,1,0:T(8,128)(2,1)} %pad_maximum_fusion.17), channel_id=1, source_target_pairs={{0,16},{4,20},{1,17},{5,21},{2,18},{6,22},{3,19},{7,23},{8,24},{12... | collective-permute-start | bytes 3145736 | tf_op jit(solution)/shard_map/ppermute | solution.py:75
  513.4 9.2 collective-permute-done.45
  571.0 10.7 %collective-permute-start.92 = (bf16[2,2,4,32,1024]{4,3,1,2,0:T(8,128)(2,1)}, bf16[2,2,4,32,1024]{4,3,1,2,0:T(8,128)(2,1)}, u32[]{:S(2)}, u32[]{:S(2)}) collective-permute-start(bf16[2,2,4,32,1024]{4,3,1,2,0:T(8,128)(2,1)} %fusion.51), channel_id=1, source_target_pairs={{0,8},{4,12},{1,9},{5,13},{2,10},{6,14},{3,11},{7,15},{8,0},{12,4}... | collective-permute-start | bytes 3145736 | tf_op jit(solution)/shard_map/ppermute | solution.py:75
  594.1 12.0 %collective-permute-done.92 = bf16[2,2,4,32,1024]{4,3,1,2,0:T(8,128)(2,1)} collective-permute-done((bf16[2,2,4,32,1024]{4,3,1,2,0:T(8,128)(2,1)}, bf16[2,2,4,32,1024]{4,3,1,2,0:T(8,128)(2,1)}, u32[]{:S(2)}, u32[]{:S(2)}) %collective-permute-start.92) | collective-permute-done | bytes 1048608 | tf_op jit(solution)/shard_map/ppermute | solution.py:75
  626.9 16.7 %attend_back.1 = (f32[2,2,768,128]{3,2,1,0:T(8,128)}, bf16[2,6144,128]{2,1,0:T(8,128)(2,1)}) custom-call(s32[2]{0:T(128)} %copy-done.227, s32[2]{0:T(128)} %lengths.3, bf16[2,2,768,128]{3,2,1,0:T(8,128)(2,1)} %pad.65.q_ref, bf16[2,6144,128]{2,1,0:T(8,128)(2,1)} %pad_maximum_fusion.1.kv_ref, bf16[2,2,768,128]{3,2,1,0:T(8,128)(2,1)} %get-tuple-element.31.out_ref, ...), custom_call_target="tpu_custom_call" | custom-call | flops 12079595520 | bytes 9437184 | tf_op jit(solution)/shard_map/attend_back/pallas_call | solution.py:299
  656.6 26.0 %collective-permute-start.60 = (bf16[2,2,4,192,128]{4,3,1,2,0:T(8,128)(2,1)}, bf16[2,2,4,192,128]{4,3,1,2,0:T(8,128)(2,1)}, u32[]{:S(2)}, u32[]{:S(2)}) collective-permute-start(bf16[2,2,4,192,128]{4,3,1,2,0:T(8,128)(2,1)} %bitcast.1189), channel_id=1, source_target_pairs={{0,16},{4,20},{1,17},{5,21},{2,18},{6,22},{3,19},{7,23},{8,24},{12... | collective-permute-start | bytes 2359304 | tf_op jit(solution)/shard_map/ppermute | solution.py:75
  697.2 14.5 %collective-permute-start.65 = (bf16[2,2,4,192,128]{4,3,1,2,0:T(8,128)(2,1)}, bf16[2,2,4,192,128]{4,3,1,2,0:T(8,128)(2,1)}, u32[]{:S(2)}, u32[]{:S(2)}) collective-permute-start(bf16[2,2,4,192,128]{4,3,1,2,0:T(8,128)(2,1)} %bitcast.1190), channel_id=1, source_target_pairs={{0,8},{4,12},{1,9},{5,13},{2,10},{6,14},{3,11},{7,15},{8,0},{12,4}... | collective-permute-start | bytes 2359304 | tf_op jit(solution)/shard_map/ppermute | solution.py:75
  715.6 5.3 direct.1
  728.8 7.7 collective-permute-done.71
  738.1 8.6 collective-permute-done.72
  747.1 6.4 collective-permute-done.73
  765.1 5.4 collective-permute-done.75
  773.3 4.4 collective-permute-done.99
  784.5 6.4 collective-permute-done.77
  790.9 4.9 collective-permute-done.78
  797.3 26.8 %chunk_back.1 = (f32[4,192,768]{2,1,0:T(8,128)}, f32[4,192,128]{2,1,0:T(8,128)}, f32[4,192,128]{2,1,0:T(8,128)}, f32[4,192,128]{2,1,0:T(8,128)}, f32[4,8,128]{2,1,0:T(8,128)}) custom-call(bf16[4,192,768]{2,1,0:T(8,128)(2,1)} %bitcast.1132, bf16[4,192,128]{2,1,0:T(8,128)(2,1)} %bitcast.1197, bf16[4,192,128]{2,1,0:T(8,128)(2,1)} %bitcast.1142, ...), custom_call_target="tpu_custom_call" | custom-call | flops 2113929216 | bytes 8329344 | tf_op jit(solution)/shard_map/chunk_back/pallas_call | solution.py:507
  826.1 40.9 %psum.7 = f32[3,24]{1,0:T(4,128)S(1)} all-reduce(f32[3,24]{1,0:T(4,128)S(1)} %pad_maximum_fusion.48), channel_id=1, replica_groups=mesh['ctx'=8,'sp'=4] {'ctx','sp'}, use_global_device_ids=true, to_apply=%region_18.19 | all-reduce | flops 72 | bytes 576 | tf_op jit(solution)/shard_map/psum | solution.py:902
  886.6 5.8 fusion.217
  892.4 4.5 convolution_bitcast_fusion
  912.4 4.7 collective-permute-done.63
  927.2 4.4 convolution_add_fusion.1
  942.0 7.1 collective-permute-start.105
  957.0 7.7 collective-permute-done.82
  970.1 4.7 collective-permute-start.107
  974.8 9.7 collective-permute-done.87
  986.1 9.9 collective-permute-done.83
  1000.4 4.5 collective-permute-done.84
  1004.9 8.6 collective-permute-done.85
  1014.3 4.7 collective-permute-start.108
  (1175 shorter events, 494.8 us)
Async XLA Ops:
  3.8 44.1 %collective-permute-start.23 = (bf16[64,1024]{1,0:T(8,128)(2,1)}, bf16[64,1024]{1,0:T(8,128)(2,1)}, u32[]{:S(2)}, u32[]{:S(2)}) collective-permute-start(bf16[64,1024]{1,0:T(8,128)(2,1)} %constant_dynamic-update-slice_fusion), channel_id=1, source_target_pairs={{0,1},{4,5},{1,2},{5,6},{2,3},{6,7},{3,0},{7,4},{8,9},{12,13},{9,1... | collective-permute-start | bytes 393224 | tf_op jit(solution)/shard_map/ppermute | solution.py:75
  6.8 46.5 %collective-permute-start.24 = (bf16[64,1024]{1,0:T(8,128)(2,1)}, bf16[64,1024]{1,0:T(8,128)(2,1)}, u32[]{:S(2)}, u32[]{:S(2)}) collective-permute-start(bf16[64,1024]{1,0:T(8,128)(2,1)} %constant_dynamic-update-slice_fusion), channel_id=1, source_target_pairs={{0,2},{4,6},{1,3},{5,7},{2,0},{6,4},{3,1},{7,5},{8,10},{12,14},{9,... | collective-permute-start | bytes 393224 | tf_op jit(solution)/shard_map/ppermute | solution.py:75
  9.4 45.4 %collective-permute-start.25 = (bf16[64,1024]{1,0:T(8,128)(2,1)}, bf16[64,1024]{1,0:T(8,128)(2,1)}, u32[]{:S(2)}, u32[]{:S(2)}) collective-permute-start(bf16[64,1024]{1,0:T(8,128)(2,1)} %constant_dynamic-update-slice_fusion), channel_id=1, source_target_pairs={{0,3},{4,7},{1,0},{5,4},{2,1},{6,5},{3,2},{7,6},{8,11},{12,15},{9,... | collective-permute-start | bytes 393224 | tf_op jit(solution)/shard_map/ppermute | solution.py:75
  12.1 33.5 %collective-permute-start = (bf16[2,3,1024]{2,1,0:T(4,128)(2,1)}, bf16[2,3,1024]{2,1,0:T(4,128)(2,1)S(1)}, u32[]{:S(2)}, u32[]{:S(2)}) collective-permute-start(bf16[2,3,1024]{2,1,0:T(4,128)(2,1)} %slice.569), channel_id=1, source_target_pairs={{0,1},{1,2},{2,3},{3,4},{4,5},{5,6},{6,7},{7,8},{8,9},{9,10},{10,1... | collective-permute-start | bytes 36872 | tf_op jit(solution)/shard_map/ppermute | solution.py:601
  14.7 37.6 %collective-permute-start.51 = (bf16[64,1024]{1,0:T(8,128)(2,1)}, bf16[64,1024]{1,0:T(8,128)(2,1)}, u32[]{:S(2)}, u32[]{:S(2)}) collective-permute-start(bf16[64,1024]{1,0:T(8,128)(2,1)} %param.39), channel_id=1, source_target_pairs={{0,1},{4,5},{1,2},{5,6},{2,3},{6,7},{3,0},{7,4},{8,9},{12,13},{9,1... | collective-permute-start | bytes 393224 | tf_op jit(solution)/shard_map/ppermute | solution.py:75
  53.3 93.6 %collective-permute-start.57 = (bf16[2,192,1024]{2,1,0:T(8,128)(2,1)S(1)}, bf16[2,192,1024]{2,1,0:T(8,128)(2,1)S(1)}, u32[]{:S(2)}, u32[]{:S(2)}) collective-permute-start(bf16[2,192,1024]{2,1,0:T(8,128)(2,1)S(1)} %get-tuple-element.273), channel_id=1, source_target_pairs={{0,4},{4,0},{1,5},{5,1},{2,6},{6,2},{3,7},{7,3},{8,12},{12,8},{9,1... | collective-permute-start | bytes 2359304 | tf_op jit(solution)/shard_map/ppermute | solution.py:75
  54.8 94.9 %collective-permute-start.1 = (bf16[2,200,1024]{2,1,0:T(8,128)(2,1)S(1)}, bf16[2,200,1024]{2,1,0:T(8,128)(2,1)S(1)}, u32[]{:S(2)}, u32[]{:S(2)}) collective-permute-start(bf16[2,200,1024]{2,1,0:T(8,128)(2,1)S(1)} %get-tuple-element.271), channel_id=1, source_target_pairs={{0,4},{4,0},{1,5},{5,1},{2,6},{6,2},{3,7},{7,3},{8,12},{12,8},{9,1... | collective-permute-start | bytes 2457608 | tf_op jit(solution)/shard_map/ppermute | solution.py:75
  55.8 85.6 %collective-permute-start.26 = (bf16[4,64,1024]{2,1,0:T(8,128)(2,1)S(1)}, bf16[4,64,1024]{2,1,0:T(8,128)(2,1)S(1)}, u32[]{:S(2)}, u32[]{:S(2)}) collective-permute-start(bf16[4,64,1024]{2,1,0:T(8,128)(2,1)S(1)} %bitcast_dynamic-update-slice_fusion.31), channel_id=1, source_target_pairs={{0,8},{4,12},{1,9},{5,13},{2,10},{6,14},{3,11},{7,15},{8,0},{12,4}... | collective-permute-start | bytes 1572872 | tf_op jit(solution)/shard_map/ppermute | solution.py:75
  57.4 85.8 %collective-permute-start.54 = (bf16[4,64,1024]{2,1,0:T(8,128)(2,1)S(1)}, bf16[4,64,1024]{2,1,0:T(8,128)(2,1)S(1)}, u32[]{:S(2)}, u32[]{:S(2)}) collective-permute-start(bf16[4,64,1024]{2,1,0:T(8,128)(2,1)S(1)} %bitcast_dynamic-update-slice_fusion.27), channel_id=1, source_target_pairs={{0,16},{4,20},{1,17},{5,21},{2,18},{6,22},{3,19},{7,23},{8,24},{12... | collective-permute-start | bytes 1572872 | tf_op jit(solution)/shard_map/ppermute | solution.py:75
  141.4 27.2 %collective-permute-start.44 = (bf16[2,4,32,1024]{3,2,1,0:T(8,128)(2,1)}, bf16[2,4,32,1024]{3,2,1,0:T(8,128)(2,1)}, u32[]{:S(2)}, u32[]{:S(2)}) collective-permute-start(bf16[2,4,32,1024]{3,2,1,0:T(8,128)(2,1)} %bitcast_dynamic-update-slice_fusion.20), channel_id=1, source_target_pairs={{0,8},{4,12},{1,9},{5,13},{2,10},{6,14},{3,11},{7,15},{8,0},{12,4}... | collective-permute-start | bytes 1572872 | tf_op jit(solution)/shard_map/ppermute | solution.py:75
  143.4 23.3 %collective-permute-start.6 = (bf16[2,4,32,1024]{3,2,1,0:T(8,128)(2,1)}, bf16[2,4,32,1024]{3,2,1,0:T(8,128)(2,1)}, u32[]{:S(2)}, u32[]{:S(2)}) collective-permute-start(bf16[2,4,32,1024]{3,2,1,0:T(8,128)(2,1)} %bitcast_dynamic-update-slice_fusion.35), channel_id=1, source_target_pairs={{0,16},{4,20},{1,17},{5,21},{2,18},{6,22},{3,19},{7,23},{8,24},{12... | collective-permute-start | bytes 1572872 | tf_op jit(solution)/shard_map/ppermute | solution.py:75
  146.9 25.5 %collective-permute-start.11 = (bf16[2,4,32,1152]{3,2,1,0:T(8,128)(2,1)}, bf16[2,4,32,1152]{3,2,1,0:T(8,128)(2,1)}, u32[]{:S(2)}, u32[]{:S(2)}) collective-permute-start(bf16[2,4,32,1152]{3,2,1,0:T(8,128)(2,1)} %bitcast_dynamic-update-slice_fusion.12), channel_id=1, source_target_pairs={{0,8},{4,12},{1,9},{5,13},{2,10},{6,14},{3,11},{7,15},{8,0},{12,4}... | collective-permute-start | bytes 1769480 | tf_op jit(solution)/shard_map/ppermute | solution.py:75
  149.7 39.4 %collective-permute-start.27 = (bf16[2,4,64,1024]{3,2,1,0:T(8,128)(2,1)}, bf16[2,4,64,1024]{3,2,1,0:T(8,128)(2,1)}, u32[]{:S(2)}, u32[]{:S(2)}) collective-permute-start(bf16[2,4,64,1024]{3,2,1,0:T(8,128)(2,1)} %pad_maximum_fusion.16), channel_id=1, source_target_pairs={{0,16},{4,20},{1,17},{5,21},{2,18},{6,22},{3,19},{7,23},{8,24},{12... | collective-permute-start | bytes 3145736 | tf_op jit(solution)/shard_map/ppermute | solution.py:75
  155.4 343.5 %collective-permute-start.55 = (bf16[2,4,64,1024]{3,2,1,0:T(8,128)(2,1)}, bf16[2,4,64,1024]{3,2,1,0:T(8,128)(2,1)}, u32[]{:S(2)}, u32[]{:S(2)}) collective-permute-start(bf16[2,4,64,1024]{3,2,1,0:T(8,128)(2,1)} %pad_maximum_fusion.19), channel_id=1, source_target_pairs={{0,8},{4,12},{1,9},{5,13},{2,10},{6,14},{3,11},{7,15},{8,0},{12,4}... | collective-permute-start | bytes 3145736 | tf_op jit(solution)/shard_map/ppermute | solution.py:75
  166.6 335.2 %collective-permute-start.50 = (bf16[2,2,4,32,1024]{4,3,2,1,0:T(8,128)(2,1)}, bf16[2,2,4,32,1024]{4,3,2,1,0:T(8,128)(2,1)}, u32[]{:S(2)}, u32[]{:S(2)}) collective-permute-start(bf16[2,2,4,32,1024]{4,3,2,1,0:T(8,128)(2,1)} %pad_maximum_fusion.18), channel_id=1, source_target_pairs={{0,8},{4,12},{1,9},{5,13},{2,10},{6,14},{3,11},{7,15},{8,0},{12,4}... | collective-permute-start | bytes 3145736 | tf_op jit(solution)/shard_map/ppermute | solution.py:75
  168.6 59.2 %collective-permute-start.7 = (bf16[2,2,4,32,1024]{4,3,2,1,0:T(8,128)(2,1)S(1)}, bf16[2,2,4,32,1024]{4,3,2,1,0:T(8,128)(2,1)S(1)}, u32[]{:S(2)}, u32[]{:S(2)}) collective-permute-start(bf16[2,2,4,32,1024]{4,3,2,1,0:T(8,128)(2,1)S(1)} %pad_maximum_fusion.15), channel_id=1, source_target_pairs={{0,8},{4,12},{1,9},{5,13},{2,10},{6,14},{3,11},{7,15},{8,0},{12,4}... | collective-permute-start | bytes 3145736 | tf_op jit(solution)/shard_map/ppermute | solution.py:75
  175.2 169.4 %collective-permute-start.12 = (bf16[2,2,4,32,1152]{4,3,2,1,0:T(8,128)(2,1)}, bf16[2,2,4,32,1152]{4,3,2,1,0:T(8,128)(2,1)}, u32[]{:S(2)}, u32[]{:S(2)}) collective-permute-start(bf16[2,2,4,32,1152]{4,3,2,1,0:T(8,128)(2,1)} %pad_maximum_fusion.13), channel_id=1, source_target_pairs={{0,16},{4,20},{1,17},{5,21},{2,18},{6,22},{3,19},{7,23},{8,24},{12... | collective-permute-start | bytes 3538952 | tf_op jit(solution)/shard_map/ppermute | solution.py:75
  192.2 233.9 %collective-permute-start.28 = (bf16[2,4,64,1024]{3,2,1,0:T(8,128)(2,1)}, bf16[2,4,64,1024]{3,2,1,0:T(8,128)(2,1)}, u32[]{:S(2)}, u32[]{:S(2)}) collective-permute-start(bf16[2,4,64,1024]{3,2,1,0:T(8,128)(2,1)} %fusion.56), channel_id=1, source_target_pairs={{0,4},{4,0},{1,5},{5,1},{2,6},{6,2},{3,7},{7,3},{8,12},{12,8},{9,1... | collective-permute-start | bytes 3145736 | tf_op jit(solution)/shard_map/ppermute | solution.py:75
  329.3 58.4 %collective-permute-start.30 = (bf16[2,2,192,128]{3,2,1,0:T(8,128)(2,1)}, bf16[2,2,192,128]{3,2,1,0:T(8,128)(2,1)}, u32[]{:S(2)}, u32[]{:S(2)}) collective-permute-start(bf16[2,2,192,128]{3,2,1,0:T(8,128)(2,1)} %get-tuple-element.319), channel_id=1, source_target_pairs={{0,1},{4,5},{1,2},{5,6},{2,3},{6,7},{3,0},{7,4},{8,9},{12,13},{9,1... | collective-permute-start | bytes 589832 | tf_op jit(solution)/shard_map/ppermute | solution.py:75
  474.7 30.1 %collective-permute-start.39 = (bf16[384,1024]{1,0:T(8,128)(2,1)S(1)}, bf16[384,1024]{1,0:T(8,128)(2,1)}, u32[]{:S(2)}, u32[]{:S(2)}) collective-permute-start(bf16[384,1024]{1,0:T(8,128)(2,1)S(1)} %slice.1044), channel_id=1, source_target_pairs={{0,4},{4,0},{1,5},{5,1},{2,6},{6,2},{3,7},{7,3},{8,12},{12,8},{9,1... | collective-permute-start | bytes 2359304 | tf_op jit(solution)/shard_map/ppermute | solution.py:75
  476.4 46.2 %collective-permute-start.45 = (bf16[2,2,4,32,1024]{4,3,2,1,0:T(8,128)(2,1)}, bf16[2,2,4,32,1024]{4,3,2,1,0:T(8,128)(2,1)}, u32[]{:S(2)}, u32[]{:S(2)}) collective-permute-start(bf16[2,2,4,32,1024]{4,3,2,1,0:T(8,128)(2,1)} %pad_maximum_fusion.17), channel_id=1, source_target_pairs={{0,16},{4,20},{1,17},{5,21},{2,18},{6,22},{3,19},{7,23},{8,24},{12... | collective-permute-start | bytes 3145736 | tf_op jit(solution)/shard_map/ppermute | solution.py:75
  546.7 42.9 %collective-permute-start.109 = (bf16[2,4,64,1024]{3,2,1,0:T(8,128)(2,1)}, bf16[2,4,64,1024]{3,2,1,0:T(8,128)(2,1)}, u32[]{:S(2)}, u32[]{:S(2)}) collective-permute-start(bf16[2,4,64,1024]{3,2,1,0:T(8,128)(2,1)} %fusion.49), channel_id=1, source_target_pairs={{0,16},{4,20},{1,17},{5,21},{2,18},{6,22},{3,19},{7,23},{8,24},{12... | collective-permute-start | bytes 3145736 | tf_op jit(solution)/shard_map/ppermute | solution.py:75
  551.4 33.9 %collective-permute-start.56 = (bf16[384,1024]{1,0:T(8,128)(2,1)}, bf16[384,1024]{1,0:T(8,128)(2,1)}, u32[]{:S(2)}, u32[]{:S(2)}) collective-permute-start(bf16[384,1024]{1,0:T(8,128)(2,1)} %slice.1043), channel_id=1, source_target_pairs={{0,4},{4,0},{1,5},{5,1},{2,6},{6,2},{3,7},{7,3},{8,12},{12,8},{9,1... | collective-permute-start | bytes 2359304 | tf_op jit(solution)/shard_map/ppermute | solution.py:75
  562.3 21.4 %collective-permute-start.58 = (bf16[384,1024]{1,0:T(8,128)(2,1)}, bf16[384,1024]{1,0:T(8,128)(2,1)}, u32[]{:S(2)}, u32[]{:S(2)}) collective-permute-start(bf16[384,1024]{1,0:T(8,128)(2,1)} %slice.1042), channel_id=1, source_target_pairs={{0,4},{4,0},{1,5},{5,1},{2,6},{6,2},{3,7},{7,3},{8,12},{12,8},{9,1... | collective-permute-start | bytes 2359304 | tf_op jit(solution)/shard_map/ppermute | solution.py:75
  571.0 35.0 %collective-permute-start.92 = (bf16[2,2,4,32,1024]{4,3,1,2,0:T(8,128)(2,1)}, bf16[2,2,4,32,1024]{4,3,1,2,0:T(8,128)(2,1)}, u32[]{:S(2)}, u32[]{:S(2)}) collective-permute-start(bf16[2,2,4,32,1024]{4,3,1,2,0:T(8,128)(2,1)} %fusion.51), channel_id=1, source_target_pairs={{0,8},{4,12},{1,9},{5,13},{2,10},{6,14},{3,11},{7,15},{8,0},{12,4}... | collective-permute-start | bytes 3145736 | tf_op jit(solution)/shard_map/ppermute | solution.py:75
  582.8 26.7 %collective-permute-start.97 = (bf16[2,2,4,32,1024]{4,3,1,2,0:T(8,128)(2,1)}, bf16[2,2,4,32,1024]{4,3,1,2,0:T(8,128)(2,1)}, u32[]{:S(2)}, u32[]{:S(2)}) collective-permute-start(bf16[2,2,4,32,1024]{4,3,1,2,0:T(8,128)(2,1)} %fusion.52), channel_id=1, source_target_pairs={{0,16},{4,20},{1,17},{5,21},{2,18},{6,22},{3,19},{7,23},{8,24},{12... | collective-permute-start | bytes 3145736 | tf_op jit(solution)/shard_map/ppermute | solution.py:75
  588.9 29.2 %collective-permute-start.59 = (bf16[384,1024]{1,0:T(8,128)(2,1)S(1)}, bf16[384,1024]{1,0:T(8,128)(2,1)S(1)}, u32[]{:S(2)}, u32[]{:S(2)}) collective-permute-start(bf16[384,1024]{1,0:T(8,128)(2,1)S(1)} %get-tuple-element.169), channel_id=1, source_target_pairs={{0,4},{4,0},{1,5},{5,1},{2,6},{6,2},{3,7},{7,3},{8,12},{12,8},{9,1... | collective-permute-start | bytes 2359304 | tf_op jit(solution)/shard_map/ppermute | solution.py:75
  592.1 25.0 %collective-permute-start.110 = (bf16[4,64,1024]{2,1,0:T(8,128)(2,1)S(1)}, bf16[4,64,1024]{2,1,0:T(8,128)(2,1)S(1)}, u32[]{:S(2)}, u32[]{:S(2)}) collective-permute-start(bf16[4,64,1024]{2,1,0:T(8,128)(2,1)S(1)} %fusion.65), channel_id=1, source_target_pairs={{0,8},{4,12},{1,9},{5,13},{2,10},{6,14},{3,11},{7,15},{8,0},{12,4}... | collective-permute-start | bytes 1572872 | tf_op jit(solution)/shard_map/ppermute | solution.py:75
  608.7 47.9 %collective-permute-start.93 = (bf16[2,4,32,1024]{3,2,0,1:T(8,128)(2,1)}, bf16[2,4,32,1024]{3,2,0,1:T(8,128)(2,1)}, u32[]{:S(2)}, u32[]{:S(2)}) collective-permute-start(bf16[2,4,32,1024]{3,2,0,1:T(8,128)(2,1)} %fusion.62), channel_id=1, source_target_pairs={{0,16},{4,20},{1,17},{5,21},{2,18},{6,22},{3,19},{7,23},{8,24},{12... | collective-permute-start | bytes 1572872 | tf_op jit(solution)/shard_map/ppermute | solution.py:75
  612.2 74.2 %collective-permute-start.98 = (bf16[2,4,32,1024]{3,2,0,1:T(8,128)(2,1)}, bf16[2,4,32,1024]{3,2,0,1:T(8,128)(2,1)}, u32[]{:S(2)}, u32[]{:S(2)}) collective-permute-start(bf16[2,4,32,1024]{3,2,0,1:T(8,128)(2,1)} %fusion.63), channel_id=1, source_target_pairs={{0,8},{4,12},{1,9},{5,13},{2,10},{6,14},{3,11},{7,15},{8,0},{12,4}... | collective-permute-start | bytes 1572872 | tf_op jit(solution)/shard_map/ppermute | solution.py:75
  618.1 104.3 %collective-permute-start.111 = (bf16[64,1024]{1,0:T(8,128)(2,1)}, bf16[64,1024]{1,0:T(8,128)(2,1)}, u32[]{:S(2)}, u32[]{:S(2)}) collective-permute-start(bf16[64,1024]{1,0:T(8,128)(2,1)} %get-tuple-element.243), channel_id=1, source_target_pairs={{0,1},{4,5},{1,2},{5,6},{2,3},{6,7},{3,0},{7,4},{8,9},{12,13},{9,1... | collective-permute-start | bytes 393224 | tf_op jit(solution)/shard_map/ppermute | solution.py:75
  618.1 104.4 %collective-permute-start.112 = (bf16[64,1024]{1,0:T(8,128)(2,1)}, bf16[64,1024]{1,0:T(8,128)(2,1)}, u32[]{:S(2)}, u32[]{:S(2)}) collective-permute-start(bf16[64,1024]{1,0:T(8,128)(2,1)} %get-tuple-element.245), channel_id=1, source_target_pairs={{0,2},{4,6},{1,3},{5,7},{2,0},{6,4},{3,1},{7,5},{8,10},{12,14},{9,... | collective-permute-start | bytes 393224 | tf_op jit(solution)/shard_map/ppermute | solution.py:75
  618.1 104.4 %collective-permute-start.113 = (bf16[64,1024]{1,0:T(8,128)(2,1)}, bf16[64,1024]{1,0:T(8,128)(2,1)}, u32[]{:S(2)}, u32[]{:S(2)}) collective-permute-start(bf16[64,1024]{1,0:T(8,128)(2,1)} %get-tuple-element.244), channel_id=1, source_target_pairs={{0,3},{4,7},{1,0},{5,4},{2,1},{6,5},{3,2},{7,6},{8,11},{12,15},{9,... | collective-permute-start | bytes 393224 | tf_op jit(solution)/shard_map/ppermute | solution.py:75
  656.6 213.1 %collective-permute-start.60 = (bf16[2,2,4,192,128]{4,3,1,2,0:T(8,128)(2,1)}, bf16[2,2,4,192,128]{4,3,1,2,0:T(8,128)(2,1)}, u32[]{:S(2)}, u32[]{:S(2)}) collective-permute-start(bf16[2,2,4,192,128]{4,3,1,2,0:T(8,128)(2,1)} %bitcast.1189), channel_id=1, source_target_pairs={{0,16},{4,20},{1,17},{5,21},{2,18},{6,22},{3,19},{7,23},{8,24},{12... | collective-permute-start | bytes 2359304 | tf_op jit(solution)/shard_map/ppermute | solution.py:75
  697.2 177.1 %collective-permute-start.65 = (bf16[2,2,4,192,128]{4,3,1,2,0:T(8,128)(2,1)}, bf16[2,2,4,192,128]{4,3,1,2,0:T(8,128)(2,1)}, u32[]{:S(2)}, u32[]{:S(2)}) collective-permute-start(bf16[2,2,4,192,128]{4,3,1,2,0:T(8,128)(2,1)} %bitcast.1190), channel_id=1, source_target_pairs={{0,8},{4,12},{1,9},{5,13},{2,10},{6,14},{3,11},{7,15},{8,0},{12,4}... | collective-permute-start | bytes 2359304 | tf_op jit(solution)/shard_map/ppermute | solution.py:75
  722.4 34.1 %collective-permute-start.94 = (bf16[2,32,1024]{2,1,0:T(8,128)(2,1)S(1)}, bf16[2,32,1024]{2,1,0:T(8,128)(2,1)S(1)}, u32[]{:S(2)}, u32[]{:S(2)}) collective-permute-start(bf16[2,32,1024]{2,1,0:T(8,128)(2,1)S(1)} %copy-done.129), channel_id=1, source_target_pairs={{0,1},{4,5},{1,2},{5,6},{2,3},{6,7},{3,0},{7,4},{8,9},{12,13},{9,1... | collective-permute-start | bytes 393224 | tf_op jit(solution)/shard_map/ppermute | solution.py:75
  722.5 34.5 %collective-permute-start.95 = (bf16[2,32,1024]{2,1,0:T(8,128)(2,1)S(1)}, bf16[2,32,1024]{2,1,0:T(8,128)(2,1)S(1)}, u32[]{:S(2)}, u32[]{:S(2)}) collective-permute-start(bf16[2,32,1024]{2,1,0:T(8,128)(2,1)S(1)} %copy-done.128), channel_id=1, source_target_pairs={{0,2},{4,6},{1,3},{5,7},{2,0},{6,4},{3,1},{7,5},{8,10},{12,14},{9,... | collective-permute-start | bytes 393224 | tf_op jit(solution)/shard_map/ppermute | solution.py:75
  772.4 124.4 %collective-permute-start.103 = (bf16[2,4,64,1024]{3,2,1,0:T(8,128)(2,1)}, bf16[2,4,64,1024]{3,2,1,0:T(8,128)(2,1)}, u32[]{:S(2)}, u32[]{:S(2)}) collective-permute-start(bf16[2,4,64,1024]{3,2,1,0:T(8,128)(2,1)} %fusion.54), channel_id=1, source_target_pairs={{0,4},{4,0},{1,5},{5,1},{2,6},{6,2},{3,7},{7,3},{8,12},{12,8},{9,1... | collective-permute-start | bytes 3145736 | tf_op jit(solution)/shard_map/ppermute | solution.py:75
  825.2 52.1 %collective-permute-start.79 = (bf16[2,2,192,128]{3,2,1,0:T(8,128)(2,1)S(1)}, bf16[2,2,192,128]{3,2,1,0:T(8,128)(2,1)}, u32[]{:S(2)}, u32[]{:S(2)}) collective-permute-start(bf16[2,2,192,128]{3,2,1,0:T(8,128)(2,1)S(1)} %bitcast.1215), channel_id=1, source_target_pairs={{0,4},{4,0},{1,5},{5,1},{2,6},{6,2},{3,7},{7,3},{8,12},{12,8},{9,1... | collective-permute-start | bytes 589832 | tf_op jit(solution)/shard_map/ppermute | solution.py:75
  872.0 30.1 %collective-permute-start.61 = (bf16[2,4,192,128]{3,2,0,1:T(8,128)(2,1)}, bf16[2,4,192,128]{3,2,0,1:T(8,128)(2,1)}, u32[]{:S(2)}, u32[]{:S(2)}) collective-permute-start(bf16[2,4,192,128]{3,2,0,1:T(8,128)(2,1)} %fusion.67), channel_id=1, source_target_pairs={{0,8},{4,12},{1,9},{5,13},{2,10},{6,14},{3,11},{7,15},{8,0},{12,4}... | collective-permute-start | bytes 1179656 | tf_op jit(solution)/shard_map/ppermute | solution.py:75
  876.8 30.5 %collective-permute-start.66 = (bf16[2,4,192,128]{3,2,0,1:T(8,128)(2,1)}, bf16[2,4,192,128]{3,2,0,1:T(8,128)(2,1)}, u32[]{:S(2)}, u32[]{:S(2)}) collective-permute-start(bf16[2,4,192,128]{3,2,0,1:T(8,128)(2,1)} %fusion.68), channel_id=1, source_target_pairs={{0,16},{4,20},{1,17},{5,21},{2,18},{6,22},{3,19},{7,23},{8,24},{12... | collective-permute-start | bytes 1179656 | tf_op jit(solution)/shard_map/ppermute | solution.py:75
  900.6 36.9 %collective-permute-start.104 = (bf16[2,4,64,1024]{3,2,1,0:T(8,128)(2,1)}, bf16[2,4,64,1024]{3,2,1,0:T(8,128)(2,1)}, u32[]{:S(2)}, u32[]{:S(2)}) collective-permute-start(bf16[2,4,64,1024]{3,2,1,0:T(8,128)(2,1)} %fusion.53), channel_id=1, source_target_pairs={{0,8},{4,12},{1,9},{5,13},{2,10},{6,14},{3,11},{7,15},{8,0},{12,4}... | collective-permute-start | bytes 3145736 | tf_op jit(solution)/shard_map/ppermute | solution.py:75
  936.0 28.7 %collective-permute-start.82 = (bf16[2,2,4,32,1152]{4,3,2,1,0:T(8,128)(2,1)}, bf16[2,2,4,32,1152]{4,3,2,1,0:T(8,128)(2,1)}, u32[]{:S(2)}, u32[]{:S(2)}) collective-permute-start(bf16[2,2,4,32,1152]{4,3,2,1,0:T(8,128)(2,1)} %fusion.48), channel_id=1, source_target_pairs={{0,8},{4,12},{1,9},{5,13},{2,10},{6,14},{3,11},{7,15},{8,0},{12,4}... | collective-permute-start | bytes 3538952 | tf_op jit(solution)/shard_map/ppermute | solution.py:75
  942.0 26.5 %collective-permute-start.105 = (bf16[4,64,1024]{2,1,0:T(8,128)(2,1)}, bf16[4,64,1024]{2,1,0:T(8,128)(2,1)}, u32[]{:S(2)}, u32[]{:S(2)}) collective-permute-start(bf16[4,64,1024]{2,1,0:T(8,128)(2,1)} %fusion.64), channel_id=1, source_target_pairs={{0,16},{4,20},{1,17},{5,21},{2,18},{6,22},{3,19},{7,23},{8,24},{12... | collective-permute-start | bytes 1572872 | tf_op jit(solution)/shard_map/ppermute | solution.py:75
  956.3 28.2 %collective-permute-start.87 = (bf16[2,2,4,32,1024]{4,3,1,2,0:T(8,128)(2,1)S(1)}, bf16[2,2,4,32,1024]{4,3,1,2,0:T(8,128)(2,1)S(1)}, u32[]{:S(2)}, u32[]{:S(2)}) collective-permute-start(bf16[2,2,4,32,1024]{4,3,1,2,0:T(8,128)(2,1)S(1)} %fusion.50), channel_id=1, source_target_pairs={{0,16},{4,20},{1,17},{5,21},{2,18},{6,22},{3,19},{7,23},{8,24},{12... | collective-permute-start | bytes 3145736 | tf_op jit(solution)/shard_map/ppermute | solution.py:75
  967.0 29.0 %collective-permute-start.83 = (bf16[2,4,32,1152]{3,2,1,0:T(8,128)(2,1)S(1)}, bf16[2,4,32,1152]{3,2,1,0:T(8,128)(2,1)S(1)}, u32[]{:S(2)}, u32[]{:S(2)}) collective-permute-start(bf16[2,4,32,1152]{3,2,1,0:T(8,128)(2,1)S(1)} %fusion.60), channel_id=1, source_target_pairs={{0,16},{4,20},{1,17},{5,21},{2,18},{6,22},{3,19},{7,23},{8,24},{12... | collective-permute-start | bytes 1769480 | tf_op jit(solution)/shard_map/ppermute | solution.py:75
  969.8 54.8 %collective-permute-start.106 = (bf16[64,1024]{1,0:T(8,128)(2,1)S(1)}, bf16[64,1024]{1,0:T(8,128)(2,1)S(1)}, u32[]{:S(2)}, u32[]{:S(2)}) collective-permute-start(bf16[64,1024]{1,0:T(8,128)(2,1)S(1)} %get-tuple-element.246), channel_id=1, source_target_pairs={{0,1},{4,5},{1,2},{5,6},{2,3},{6,7},{3,0},{7,4},{8,9},{12,13},{9,1... | collective-permute-start | bytes 393224 | tf_op jit(solution)/shard_map/ppermute | solution.py:75
  970.1 54.5 %collective-permute-start.107 = (bf16[64,1024]{1,0:T(8,128)(2,1)S(1)}, bf16[64,1024]{1,0:T(8,128)(2,1)S(1)}, u32[]{:S(2)}, u32[]{:S(2)}) collective-permute-start(bf16[64,1024]{1,0:T(8,128)(2,1)S(1)} %get-tuple-element.248), channel_id=1, source_target_pairs={{0,2},{4,6},{1,3},{5,7},{2,0},{6,4},{3,1},{7,5},{8,10},{12,14},{9,... | collective-permute-start | bytes 393224 | tf_op jit(solution)/shard_map/ppermute | solution.py:75
  (304 other events, 3197.8 us)

commit v2 on v1

--- a/solution.py
+++ b/solution.py
@@ -22,6 +22,7 @@
 BF16 = jnp.bfloat16
 LANES = 128
 HALO = 8
+EXTRA = 16
 Q_SHARE = QH // CORES
 M_SHARE = SH // CORES
 VMEM = 56 * 2**20
@@ -54,6 +55,9 @@
         }
         self.chip = index // CORES
         self.chips = chips
+        self.scalars = jnp.stack(
+            [self.at["a"], self.at["b"], self.at["z"], self.at["c"], self.chip]
+        ).astype(jnp.int32)
         self.flat = index * groups + self.at["z"]
 
     def flat_of(self, a, b, z, c):
@@ -80,31 +84,136 @@
     def by_core(self, zero, one):
         return jnp.where(self.at["c"] == 0, zero, one)
 
-    def place(self, parts, dim, axis):
-        n, v = self.size[dim], self.at[dim]
-        if n == 2:
-            return jnp.stack(
-                [jnp.where(v == 0, parts[0], parts[1]), jnp.where(v == 0, parts[1], parts[0])],
-                axis,
-            )
-        shape = parts[0].shape
-        out = jnp.zeros(shape[:axis] + (n,) + shape[axis:], parts[0].dtype)
-        for k, part in enumerate(parts):
-            out = lax.dynamic_update_index_in_dim(out, part, (v - k) % n, axis)
-        return out
-
-    def gather(self, x, dim, axis):
-        n = self.size[dim]
-        return self.place([x] + [self.shift(x, dim, k) for k in range(1, n)], dim, axis)
-
-    def exchange(self, x, dim, axis):
-        n, v = self.size[dim], self.at[dim]
-        parts = [lax.dynamic_index_in_dim(x, v, axis, False)]
-        for k in range(1, n):
-            parts.append(
-                self.shift(lax.dynamic_index_in_dim(x, (v + k) % n, axis, False), dim, k)
-            )
-        return self.place(parts, dim, axis)
+    def chip_pairs(self, by):
+        groups = self.size["z"]
+        return [
+            ((chip * CORES + c) * groups + z, (((chip + by) % self.chips) * CORES + c) * groups + z)
+            for chip in range(self.chips)
+            for c in range(CORES)
+            for z in range(groups)
+        ]
+
+    def spread_z(self, x):
+        return [x] + [self.shift(x, "z", k) for k in range(1, self.size["z"])]
+
+    def spread_plane(self, x, b_first):
+        found = {(0, 0): x}
+        for dim in ("b", "a") if b_first else ("a", "b"):
+            for key, value in list(found.items()):
+                for k in range(1, self.size[dim]):
+                    to = (key[0], k) if dim == "b" else (k, key[1])
+                    found[to] = self.shift(value, dim, k)
+        return found
+
+    def place_z(self, parts, halves):
+        groups = self.size["z"]
+        rows = parts[0].shape[0]
+        outs = [
+            jax.ShapeDtypeStruct((groups * rows, sum(size for _, size, _ in half)), parts[0].dtype)
+            for half in halves
+        ]
+        plan = []
+        for index, half in enumerate(halves):
+            to = 0
+            for start, size, count in half:
+                block = rows // count
+                for r in range(groups):
+                    for m in range(count):
+
+                        def source(at, m=m, start=start, size=size, block=block):
+                            return pl.ds(m * block, block), pl.ds(start, size)
+
+                        def goal(at, m=m, r=r, to=to, size=size, block=block):
+                            z = lax.rem(at[2] + groups - r, groups)
+                            return pl.ds((m * groups + z) * block, block), pl.ds(to, size)
+
+                        plan.append((r, source, index, goal))
+                to += size
+        return moved(self, parts, outs, plan)
+
+    def gather_plane(self, halves, wanted):
+        rows = halves[0].shape[0]
+        near = [self.spread_plane(half, index % 2 == 0) for index, half in enumerate(halves)]
+        keys = sorted(near[0])
+        na, nb = self.size["a"], self.size["b"]
+        widths = {}
+        for _, _, size, array, column in wanted:
+            widths[array] = max(widths.get(array, 0), column + size)
+        outs = [
+            jax.ShapeDtypeStruct((self.chips * rows, widths[k]), halves[0].dtype)
+            for k in range(len(widths))
+        ]
+        plan = []
+        for half, start, size, array, column in wanted:
+            for index, (da, db) in enumerate(keys):
+
+                def source(at, start=start, size=size):
+                    return pl.ds(0, rows), pl.ds(start, size)
+
+                def goal(at, da=da, db=db, column=column, size=size):
+                    chip = lax.rem(at[0] + na - da, na) * nb + lax.rem(at[1] + nb - db, nb)
+                    return pl.ds(chip * rows, rows), pl.ds(column, size)
+
+                plan.append((half * len(keys) + index, source, array, goal))
+        return moved(self, [n[key] for n in near for key in keys], outs, plan)
+
+    def reduce_far(self, grads):
+        cores = [[chip * CORES + c for chip in range(self.chips)] for c in range(CORES)]
+        groups, chips = self.size["z"], self.chips
+        rows = grads[0][0].shape[0] // chips
+        widths = [grad.shape[1] for grad, _ in grads]
+        stacked = len(set(widths)) == 1
+        high = len(grads) * rows if stacked else rows
+        wide = widths[0] if stacked else sum(widths)
+        corner = [
+            (k * rows, 0) if stacked else (0, sum(widths[:k])) for k in range(len(grads))
+        ]
+        outs = [jax.ShapeDtypeStruct((chips * high, wide), BF16)]
+        plan = []
+        for k, (row, column) in enumerate(corner):
+            for chip in range(chips):
+
+                def source(at, chip=chip, size=widths[k]):
+                    return pl.ds(chip * rows, rows), pl.ds(0, size)
+
+                def goal(at, chip=chip, row=row, column=column, size=widths[k]):
+                    return pl.ds(chip * high + row, rows), pl.ds(column, size)
+
+                plan.append((k, source, 0, goal))
+        (flat,) = moved(self, [grad for grad, _ in grads], outs, plan)
+        flat = lax.psum_scatter(
+            flat, "ctx", scatter_dimension=0, tiled=True, axis_index_groups=cores
+        )
+        share, deep = rows // groups, high // groups
+
+        def finish(flat):
+            plan = []
+            for k, (row, column) in enumerate(corner):
+                count = grads[k][1]
+                block = share // count
+                for z in range(groups):
+                    for m in range(count):
+
+                        def source(at, z=z, m=m, row=row, column=column, size=widths[k], block=block):
+                            return (
+                                pl.ds(row + (m * groups + z) * block, block),
+                                pl.ds(column, size),
+                            )
+
+                        def goal(
+                            at, z=z, m=m, row=row, column=column, size=widths[k], block=block
+                        ):
+                            return (
+                                pl.ds(z * deep + row // groups + m * block, block),
+                                pl.ds(column, size),
+                            )
+
+                        plan.append((0, source, 0, goal))
+            outs = [jax.ShapeDtypeStruct((high, wide), BF16)]
+            (flat,) = moved(self, [flat], outs, plan)
+            return lax.psum_scatter(flat, "sp", scatter_dimension=0, tiled=True)
+
+        return flat, finish
 
     def reduce(self, x, dim, axis):
         n, v = self.size[dim], self.at[dim]
@@ -114,18 +223,75 @@
             total = total + self.shift(piece, dim, k).astype(F32)
         return total
 
-    def gather_chips(self, x, z_axis, b_first):
-        x = self.gather(x, "z", z_axis)
-        if b_first:
-            return self.gather(self.gather(x, "b", 0), "a", 0)
-        return self.gather(self.gather(x, "a", 0), "b", 1)
-
-    def reduce_chips(self, x, z_axis, b_first):
-        if b_first:
-            x = self.reduce(self.reduce(x, "a", 0), "b", 0)
-        else:
-            x = self.reduce(self.reduce(x, "b", 1), "a", 0)
-        return self.reduce(x, "z", z_axis)
+    def reduce_chips(self, grads, firsts):
+        left = []
+        for grad, b_first in zip(grads, firsts):
+            if b_first:
+                left.append(self.reduce(self.reduce(grad, "a", 0), "b", 0))
+            else:
+                left.append(self.reduce(self.reduce(grad, "b", 1), "a", 0))
+        n, v = self.size["z"], self.at["z"]
+
+        def cut(x, index):
+            piece = lax.dynamic_index_in_dim(x, index, 1, False)
+            return piece.reshape(-1, piece.shape[-1])
+
+        totals = [cut(x, v) for x in left]
+        for k in range(1, n):
+            sent = jnp.concatenate([cut(x, (v + k) % n).astype(BF16) for x in left], axis=-1)
+            got = self.shift(sent, "z", k).astype(F32)
+            start = 0
+            for index, total in enumerate(totals):
+                stop = start + total.shape[-1]
+                totals[index] = total + got[:, start:stop]
+                start = stop
+        return totals
+
+    def sum_all(self, x):
+        for dim in ("z", "b", "a"):
+            step = 1
+            while step < self.size[dim]:
+                found = []
+                for a in range(self.size["a"]):
+                    for b in range(self.size["b"]):
+                        for z in range(self.size["z"]):
+                            for c in range(CORES):
+                                spot = {"a": a, "b": b, "z": z, "c": c}
+                                goal = dict(spot)
+                                goal[dim] = spot[dim] ^ step
+                                found.append((self.flat_of(**spot), self.flat_of(**goal)))
+                x = x + lax.ppermute(x, AXES, found)
+                step *= 2
+        return x
+
+
+def moved_kernel(at_ref, *refs, plan, count):
+    sems = refs[-1]
+    copies = [
+        pltpu.make_async_copy(
+            refs[source].at[where(at_ref)], refs[count + goal].at[to(at_ref)], sems.at[index]
+        )
+        for index, (source, where, goal, to) in enumerate(plan)
+    ]
+    for copy in copies:
+        copy.start()
+    for copy in copies:
+        copy.wait()
+
+
+def moved(place, sources, outs, plan):
+    size = sum(math.prod(out.shape) * out.dtype.itemsize for out in outs)
+    return pl.pallas_call(
+        functools.partial(moved_kernel, plan=plan, count=len(sources)),
+        in_specs=[pl.BlockSpec(memory_space=pltpu.SMEM)]
+        + [pl.BlockSpec(memory_space=pl.ANY)] * len(sources),
+        out_specs=[pl.BlockSpec(memory_space=pltpu.VMEM)] * len(outs),
+        out_shape=outs,
+        scratch_shapes=[pltpu.SemaphoreType.DMA((len(plan),))],
+        compiler_params=pltpu.CompilerParams(vmem_limit_bytes=VMEM),
+        cost_estimate=pl.CostEstimate(flops=0, bytes_accessed=2 * size, transcendentals=0),
+        name="moved",
+    )(place.scalars, *sources)
 
 
 def rotary_tables(positions, width):
@@ -348,8 +514,9 @@
 
 def chunk_kernel(
     f_ref, b_ref, c_ref, raw_ref, raw_t_ref, bias_ref, bias_t_ref, rate_ref, rate_t_ref, skip_ref,
-    out_ref, state_ref, logs_ref,
+    at_ref, out_ref, logs_ref, *rest,
 ):
+    state_refs, held = rest[:-1], rest[-1]
     steps, steps_t, logs, logs_t = chunk_terms(
         raw_ref, raw_t_ref, bias_ref, bias_t_ref, rate_ref, rate_t_ref
     )
@@ -371,21 +538,33 @@
         weight = paired(
             tail[:, 2 * pair : 2 * pair + 1], tail[:, 2 * pair + 1 : 2 * pair + 2], wide.shape
         )
-        state_ref[0, lanes, :] = mm((wide * weight).astype(BF16), inject, TN).astype(BF16)
-
-
-def carry_kernel(out_ref, c_ref, state_ref, logs_ref, ssd_ref):
+        state = mm((wide * weight).astype(BF16), inject, TN).astype(BF16)
+        keep_heads(held, state, pair)
+    decay = jnp.exp(logs[rows - 1 :])
+    line = lax.broadcasted_iota(jnp.int32, (EXTRA, LANES), 0)
+    high = decay.astype(BF16).astype(F32)
+    extra = jnp.where(line == 0, high, jnp.where(line == 1, decay - high, 0.0)).astype(BF16)
+    for group in range(len(state_refs)):
+        held[group, held.shape[1] - EXTRA :, :] = extra
+    send_groups(held, state_refs, at_ref)
+
+
+def carry_kernel(out_ref, c_ref, logs_ref, *rest):
+    groups = len(rest) - 3
+    at_ref, ssd_ref, held = rest[groups], rest[groups + 1], rest[groups + 2]
+    take_groups(held, rest[:groups], at_ref)
     decay = jnp.exp(logs_ref[0])
     for pair in range(M_SHARE // 2):
         lanes = slice(pair * LANES, (pair + 1) * LANES)
-        read = mm(c_ref[0], state_ref[0, lanes, :], NT)
+        read = mm(c_ref[0], pair_rows(held, pair), NT)
         weight = paired(
             decay[:, 2 * pair : 2 * pair + 1], decay[:, 2 * pair + 1 : 2 * pair + 2], read.shape
         )
         ssd_ref[0, :, lanes] = (out_ref[0, :, lanes] + read * weight).astype(BF16)
 
 
-def direct_kernel(d_ref, c_ref, logs_ref, direct_ref):
+def direct_kernel(d_ref, c_ref, logs_ref, at_ref, *rest):
+    held = rest[-1]
     decay = jnp.exp(logs_ref[0])
     for pair in range(M_SHARE // 2):
         lanes = slice(pair * LANES, (pair + 1) * LANES)
@@ -393,14 +572,21 @@
         weight = paired(
             decay[:, 2 * pair : 2 * pair + 1], decay[:, 2 * pair + 1 : 2 * pair + 2], grad.shape
         )
-        direct_ref[0, lanes, :] = mm((grad * weight).astype(BF16), c_ref[0], TN).astype(BF16)
+        state = mm((grad * weight).astype(BF16), c_ref[0], TN).astype(BF16)
+        keep_heads(held, state, pair)
+    send_groups(held, rest[:-1], at_ref)
 
 
 def chunk_back_kernel(
     f_ref, b_ref, c_ref, raw_ref, raw_t_ref, bias_ref, bias_t_ref, rate_ref, rate_t_ref, skip_ref,
-    d_ref, state_ref, later_ref, agree_ref, df_ref, db_ref, dc_ref, draw_ref, sums_ref,
-    columns, row_sums,
+    d_ref, *rest,
 ):
+    groups = (len(rest) - 10) // 2
+    at_ref = rest[2 * groups]
+    df_ref, db_ref, dc_ref, draw_ref, sums_ref = rest[2 * groups + 1 : 2 * groups + 6]
+    columns, row_sums, states, laters = rest[2 * groups + 6 :]
+    take_groups(states, rest[:groups], at_ref)
+    take_groups(laters, rest[groups : 2 * groups], at_ref)
     steps, steps_t, logs, logs_t = chunk_terms(
         raw_ref, raw_t_ref, bias_ref, bias_t_ref, rate_ref, rate_t_ref
     )
@@ -419,13 +605,15 @@
     to_state = jnp.zeros((rows, LANES), F32)
     from_state = jnp.zeros((rows, LANES), F32)
     skips = jnp.zeros((1, LANES), F32)
+    agree = jnp.zeros((1, LANES), F32)
     head_lane = lax.broadcasted_iota(jnp.int32, (rows, LANES), 1)
     for pair in range(M_SHARE // 2):
         lanes = slice(pair * LANES, (pair + 1) * LANES)
         feats, grad = f_ref[0, :, lanes], d_ref[0, :, lanes]
         wide, wide_grad = feats.astype(F32), grad.astype(F32)
-        later = later_ref[0, lanes, :]
-        state = state_ref[0, lanes, :]
+        later = pair_rows(laters, pair)
+        state = pair_rows(states, pair)
+        agreed = later.astype(F32) * state.astype(F32)
         pushed = mm(inject, later, NT)
         read = mm(readout, state, NT)
         push_part = wide * pushed
@@ -454,6 +642,9 @@
             from_state = from_state + jnp.where(
                 here, jnp.sum(jnp.where(mine, read_part, 0.0), axis=1, keepdims=True), 0.0
             )
+            same = agreed[half * SHD : (half + 1) * SHD]
+            same = jnp.sum(jnp.sum(same, axis=0, keepdims=True), axis=1, keepdims=True)
+            agree = agree + jnp.where(here[:1], same, 0.0)
             skips = skips + jnp.where(
                 here[:1],
                 jnp.sum(
@@ -478,7 +669,7 @@
     direct = columns[...].T[:rows]
     push = end_decay * to_state
     dlogs = row_sums[...] - steps * direct + decay * from_state - steps * push
-    end = jnp.sum(steps * push, axis=0, keepdims=True) + decay[rows - 1 :] * agree_ref[0]
+    end = jnp.sum(steps * push, axis=0, keepdims=True) + decay[rows - 1 :] * agree
     last = lax.broadcasted_iota(jnp.int32, (rows, LANES), 0) == rows - 1
     dlogs = dlogs + jnp.where(last, end, 0.0)
     summed = mm(lower(rows, True).astype(F32), dlogs, NN, lax.Precision.HIGHEST)
@@ -493,7 +684,7 @@
     )
 
 
-def over_pieces(kernel, name, args, whole, outs, flops, scratch=()):
+def over_pieces(kernel, name, args, whole, outs, flops, at, scratch=()):
     pieces = args[0].shape[0]
 
     def spec(shape, split):
@@ -507,54 +698,165 @@
     return pl.pallas_call(
         kernel,
         grid=(pieces,),
-        in_specs=[spec(shape, split) for shape, split in shapes],
+        in_specs=[spec(shape, split) for shape, split in shapes]
+        + [pl.BlockSpec(memory_space=pltpu.SMEM)],
         out_specs=[spec(shape, True) for shape, _ in outs],
         out_shape=[jax.ShapeDtypeStruct(shape, dtype) for shape, dtype in outs],
         scratch_shapes=list(scratch),
         compiler_params=pltpu.CompilerParams(vmem_limit_bytes=VMEM),
         cost_estimate=pl.CostEstimate(flops=flops, bytes_accessed=nbytes, transcendentals=0),
         name=name,
-    )(*args)
-
-
-def carried(place, states, decays, reverse):
-    groups = place.size["z"]
-    z, chips = place.at["z"], place.chips
-    e, slots = states.shape[:2]
+    )(*args, at)
+
+
+def keep_heads(held, state, pair):
+    share = M_SHARE // held.shape[0]
+    for half in range(2):
+        group, spot = divmod(2 * pair + half, share)
+        held[group, spot * SHD : (spot + 1) * SHD, :] = state[half * SHD : (half + 1) * SHD]
+
+
+def pair_rows(held, pair):
+    share = M_SHARE // held.shape[0]
+    found = []
+    for half in range(2):
+        group, spot = divmod(2 * pair + half, share)
+        found.append(held[group, spot * SHD : (spot + 1) * SHD, :])
+    return jnp.concatenate(found, axis=0)
+
+
+def send_groups(held, refs, at_ref):
+    for r, ref in enumerate(refs):
+        ref[0] = held[lax.rem(at_ref[2] + r, len(refs))]
+
+
+def take_groups(held, refs, at_ref):
+    for r, ref in enumerate(refs):
+        held[lax.rem(at_ref[2] + len(refs) - r, len(refs))] = ref[0]
+
+
+def scan_kernel(at_ref, *refs, groups, chips, share, reverse, last):
+    rows = share * SHD
+    states, marks = refs[:groups], refs[groups : 2 * groups]
+    refs = refs[2 * groups :]
+    chip, z, core = at_ref[4], at_ref[2], at_ref[3]
+    lane = lax.broadcasted_iota(jnp.int32, (1, LANES), 1)
+
+    def pick(pair, offset):
+        both = pair[0:1].astype(F32) + pair[1:2].astype(F32)
+        return [
+            jnp.sum(jnp.where(lane == offset + i, both, 0.0), axis=1, keepdims=True)
+            for i in range(share)
+        ]
+
+    def step(run, factors, new):
+        return jnp.concatenate(
+            [
+                factors[i] * run[i * SHD : (i + 1) * SHD] + new[i * SHD : (i + 1) * SHD]
+                for i in range(share)
+            ],
+            axis=0,
+        )
+
+    if last:
+        totals, fades = refs[: chips - 1], refs[chips - 1 : 2 * chips - 2]
+        outs, held, decay, entered = (
+            refs[2 * chips - 2 : 2 * chips - 2 + groups],
+            refs[-3],
+            refs[-2],
+            refs[-1],
+        )
+    else:
+        total_ref, held, decay = refs
+    for r in range(groups):
+        to = lax.rem(z + groups - r, groups)
+        held[to] = states[r][:, 0, :rows]
+        decay[to] = marks[r][:, 0]
+    run = jnp.zeros((rows, NS), F32)
+    if last:
+        for k in range(chips - 1, 0, -1):
+            part = chips - k if reverse else k
+            reached = chip + k < chips if reverse else chip >= k
+            new = step(run, pick(fades[part - 1][0], 0), totals[part - 1][0, :rows].astype(F32))
+            run = jnp.where(reached, new, run)
+    fade = [jnp.ones((1, 1), F32)] * share
+    order = [(h, k) for h in range(CORES) for k in range(groups)]
+    for h, k in order[::-1] if reverse else order:
+        e = lax.rem(h + core, CORES)
+        if last:
+            entered[k, e] = run.astype(BF16)
+        factors = pick(decay[k, e], z * share)
+        run = step(run, factors, held[k, e].astype(F32))
+        fade = [one * two for one, two in zip(fade, factors)]
+    if last:
+        for r in range(groups):
+            outs[r][:, 0] = entered[lax.rem(z + r, groups)]
+        return
+    line = lax.broadcasted_iota(jnp.int32, (EXTRA, LANES), 0)
+    place = lax.broadcasted_iota(jnp.int32, (EXTRA, LANES), 1)
+    extra = jnp.zeros((EXTRA, LANES), F32)
+    for i in range(share):
+        high = fade[i].astype(BF16).astype(F32)
+        extra = extra + jnp.where((line == 0) & (place == i), high, 0.0)
+        extra = extra + jnp.where((line == 1) & (place == i), fade[i] - high, 0.0)
+    total_ref[0, :rows] = run.astype(BF16)
+    total_ref[0, rows:] = extra.astype(BF16)
+
+
+def carried(place, at, states, marks, fades, reverse):
+    groups, chips = place.size["z"], place.chips
     share = M_SHARE // groups
-    parts = states.reshape(e, slots, groups, share * SHD, NS)
-    parts = place.exchange(parts, "z", 2)
-    by_h = place.by_core(parts, parts[::-1]).astype(F32).reshape(e, slots, groups, share, SHD, NS)
-    mine = lax.dynamic_slice_in_dim(decays, z * share, share, 4)
-    here = lax.dynamic_index_in_dim(mine, place.chip, 0, False)
-    order = [(h, k) for h in range(CORES) for k in range(groups)]
-    if reverse:
-        order = order[::-1]
-    run = jnp.zeros((slots, share, SHD, NS), F32)
-    fade = jnp.ones((slots, share), F32)
-    entered, faded = {}, {}
-    for h, k in order:
-        entered[h, k], faded[h, k] = run, fade
-        factor = here[k, h]
-        run = factor[..., None, None] * run + by_h[h, :, k]
-        fade = factor * fade
-    totals = place.gather(place.gather(run.astype(BF16), "b", 0), "a", 0)
-    totals = totals.reshape(chips, slots, share, SHD, NS)
-    fades = jnp.prod(mine, axis=(1, 2))
-    carry = jnp.zeros_like(run)
-    for chip in range(chips)[::-1] if reverse else range(chips):
-        reached = chip > place.chip if reverse else chip < place.chip
-        new = fades[chip][..., None, None] * carry + totals[chip].astype(F32)
-        carry = jnp.where(reached, new, carry)
-    whole = [
-        jnp.stack(
-            [entered[h, k] + faded[h, k][..., None, None] * carry for k in range(groups)], 1
-        ).astype(BF16)
-        for h in range(CORES)
+    rows = share * SHD
+    slots = states[0].shape[1]
+    parts = [part if r == 0 else place.shift(part, "z", r) for r, part in enumerate(states)]
+    marks = parts if marks is None else marks
+    block = [pl.BlockSpec((CORES, 1, part.shape[2], NS), lambda s, *_: (0, s, 0, 0)) for part in parts]
+    mark = pl.BlockSpec((CORES, 1, EXTRA, NS), lambda s, *_: (0, s, rows // EXTRA, 0))
+    total = pl.BlockSpec((1, rows + EXTRA, NS), lambda s, *_: (s, 0, 0))
+    fade = pl.BlockSpec((1, EXTRA, NS), lambda s, *_: (s, rows // EXTRA, 0))
+    result = pl.BlockSpec((CORES, 1, rows, NS), lambda s, *_: (0, s, 0, 0))
+    scratch = [
+        pltpu.VMEM((groups, CORES, rows, NS), BF16),
+        pltpu.VMEM((groups, CORES, EXTRA, NS), BF16),
     ]
-    back = jnp.stack([place.by_core(whole[0], whole[1]), place.by_core(whole[1], whole[0])])
-    back = place.exchange(back.reshape(e, slots, groups, share * SHD, NS), "z", 2)
-    return back.reshape(e, slots, M_SHARE * SHD, NS)
+
+    def call(last, args, specs, outs, out_specs, more):
+        return pl.pallas_call(
+            functools.partial(
+                scan_kernel, groups=groups, chips=chips, share=share, reverse=reverse, last=last
+            ),
+            grid_spec=pltpu.PrefetchScalarGridSpec(
+                num_scalar_prefetch=1,
+                grid=(slots,),
+                in_specs=block + [mark] * groups + specs,
+                out_specs=out_specs,
+                scratch_shapes=scratch + more,
+            ),
+            out_shape=outs,
+            compiler_params=pltpu.CompilerParams(vmem_limit_bytes=VMEM),
+            cost_estimate=pl.CostEstimate(
+                flops=4 * slots * CORES * groups * rows * NS,
+                bytes_accessed=4 * slots * CORES * groups * rows * NS,
+                transcendentals=0,
+            ),
+            name="scan",
+        )(at, *parts, *marks, *args)
+
+    leaving = call(
+        False, [], [], jax.ShapeDtypeStruct((slots, rows + EXTRA, NS), BF16), total, []
+    )
+    totals = [lax.ppermute(leaving, AXES, place.chip_pairs(k)) for k in range(1, chips)]
+    fades = totals if fades is None else fades
+    entering = call(
+        True,
+        [*totals, *fades],
+        [total] * (chips - 1) + [fade] * (chips - 1),
+        [jax.ShapeDtypeStruct((CORES, slots, rows, NS), BF16)] * groups,
+        [result] * groups,
+        [pltpu.VMEM((groups, CORES, rows, NS), BF16)],
+    )
+    found = [part if r == 0 else place.shift(part, "z", r) for r, part in enumerate(entering)]
+    return [part.reshape(CORES * slots, rows, NS) for part in found], marks, fades
 
 
 def shards(
@@ -588,8 +890,10 @@
     rows_all = CORES * slots * piece
     rows_halo = CORES * slots * (piece + HALO)
     q_cols, m_cols = Q_SHARE * HD, M_SHARE * SHD
-    az_cols = q_cols + 2 * HD + m_cols
+    lin_cols = q_cols + 2 * HD
     c_cols = m_cols + NS
+    f_cols = m_cols // 2
+    at = place.scalars
     shard_rows = attn_in_weight.shape[0]
     out_rows, mix_rows, ff_rows = (
         attn_out_weight.shape[0],
@@ -614,55 +918,70 @@
     dy = jnp.stack([dy_low, place.swap(dy_low)]).reshape(rows_all, width)
 
     small = jnp.concatenate([input_gain, mixer_gain, post_gain, conv_bias, conv_weight.reshape(-1)])
+    vector_size = small.shape[0]
+    terms = jnp.stack([step_bias, decay_log, skip_scale])
+    term_size = terms.size
+    split_terms = []
+    for _ in range(3):
+        part = lax.reduce_precision(terms, 8, 7)
+        split_terms.append(part.reshape(-1).astype(BF16))
+        terms = terms - part
+    small = jnp.concatenate([small, *split_terms])
     small_cols = -(-small.shape[0] // shard_rows)
     small = jnp.pad(small, (0, small_cols * shard_rows - small.shape[0]))
     small = small.reshape(shard_rows, small_cols)
-    step_at = c_cols
-    small_at = step_at + M_SHARE
+    small_at = M_SHARE
     ms_cols = -(-(small_at + small_cols) // LANES) * LANES
+    a_cols, b_cols = lin_cols + f_cols, c_cols - f_cols + ms_cols
 
     def ff_columns(weight, half):
         return weight.reshape(shard_rows, chips, CORES, -1)[:, :, half].reshape(shard_rows, -1)
 
-    def half_columns(half):
+    def early_columns(half):
         return jnp.concatenate(
             [
                 attn_in_weight[:, half * q_cols : (half + 1) * q_cols],
                 attn_in_weight[:, QH * HD + half * HD : QH * HD + (half + 1) * HD],
                 attn_in_weight[:, (QH + KVH + half) * HD : (QH + KVH + half + 1) * HD],
-                zgate_weight[:, half * m_cols : (half + 1) * m_cols],
                 mixer_in_weight[:, half * m_cols : (half + 1) * m_cols],
                 mixer_in_weight[:, SH * SHD + half * NS : SH * SHD + (half + 1) * NS],
                 step_weight[:, half * M_SHARE : (half + 1) * M_SHARE],
                 small,
                 jnp.zeros((shard_rows, ms_cols - small_at - small_cols), BF16),
-                ff_columns(gate_weight, half),
-                ff_columns(up_weight, half),
             ],
             axis=1,
         )
 
-    halves = (half_columns(0), half_columns(1))
-    kept = place.by_core(*halves)
-    got = place.swap(place.by_core(halves[1], halves[0]))
-    both = jnp.stack([place.by_core(kept, got), place.by_core(got, kept)])
-    cut = (0, az_cols, az_cols + ms_cols, az_cols + ms_cols + ff_half, both.shape[2])
-    w_az, w_ms, w_gate, w_up = (
-        place.gather_chips(both[:, :, cut[i] : cut[i + 1]], 1, i % 2 == 0).reshape(width, -1)
-        for i in range(4)
-    )
-    w_out = place.gather_chips(
-        jnp.concatenate([attn_out_weight, mixer_out_weight], axis=0), 0, True
-    )
-    w_out = w_out.reshape(2, chips // 2, groups, out_rows + mix_rows, width)
-    kept = lax.dynamic_index_in_dim(w_out, core, 0, False)
-    got = place.swap(lax.dynamic_index_in_dim(w_out, 1 - core, 0, False))
-    w_out = jnp.stack([place.by_core(kept, got), place.by_core(got, kept)], 1)
-    w_attn_out = w_out[..., :out_rows, :].reshape(q_cols, width)
-    w_mixer_out = w_out[..., out_rows:, :].reshape(m_cols, width)
-    w_down = place.gather_chips(down_weight, 0, False).reshape(ff_half, width)
-
-    vectors = w_ms[:, small_at : small_at + small_cols].reshape(devices, -1).astype(F32)
+    def zgate_columns(half):
+        return zgate_weight[:, half * m_cols : (half + 1) * m_cols]
+
+    def late_columns(half):
+        return jnp.concatenate([ff_columns(gate_weight, half), ff_columns(up_weight, half)], axis=1)
+
+    def sorted_halves(columns):
+        halves = (columns(0), columns(1))
+        kept = place.by_core(*halves)
+        got = place.swap(place.by_core(halves[1], halves[0]))
+        return jnp.concatenate([place.by_core(kept, got), place.by_core(got, kept)], axis=0)
+
+    early = place.spread_z(sorted_halves(early_columns))
+    late_one = jnp.concatenate(
+        [
+            sorted_halves(zgate_columns),
+            jnp.concatenate([attn_out_weight, mixer_out_weight], axis=0),
+        ],
+        axis=1,
+    )
+    early, late_one = lax.optimization_barrier((early, late_one))
+    w_a, w_b = place.gather_plane(
+        place.place_z(early, [[(0, a_cols, 2)], [(a_cols, b_cols, 2)]]),
+        [(0, 0, a_cols, 0, 0), (1, 0, b_cols, 1, 0)],
+    )
+    late_one = place.spread_z(late_one)
+
+    tail_at = c_cols - f_cols
+    vectors = w_b[:, tail_at + small_at : tail_at + small_at + small_cols]
+    vectors = vectors.reshape(devices, -1).astype(F32)
     sizes = [input_gain.shape[0], mixer_gain.shape[0], post_gain.shape[0], conv_bias.shape[0]]
     ends = [sum(sizes[: k + 1]) for k in range(4)]
     gain_in = vectors[:, : ends[0]].reshape(-1)
@@ -670,7 +989,7 @@
     gain_mixer = place.by_core(gain_mixer[:m_cols], gain_mixer[m_cols:])
     gain_post = vectors[:, ends[1] : ends[2]].reshape(-1)
     shift_all = vectors[:, ends[2] : ends[3]].reshape(-1)
-    taps_all = vectors[:, ends[3] : ends[3] + KC * sizes[3]].reshape(devices, KC, sizes[3])
+    taps_all = vectors[:, ends[3] : vector_size].reshape(devices, KC, sizes[3])
     taps_all = jnp.transpose(taps_all, (1, 0, 2)).reshape(KC, -1)
 
     def conv_half(value):
@@ -683,9 +1002,12 @@
         return place.by_core(first, second)
 
     taps, shift = conv_half(taps_all), conv_half(shift_all)
-    head_terms = lax.all_gather(jnp.stack([step_bias, decay_log, skip_scale]), "sp", axis=1, tiled=True)
-    head_terms = lax.dynamic_slice_in_dim(head_terms, core * M_SHARE, M_SHARE, 1)
-    bias, log_rates, skip = head_terms[0], head_terms[1], head_terms[2]
+    terms = vectors[:groups, vector_size : vector_size + 3 * term_size]
+    terms = terms.reshape(groups, 3, 3, SH // groups)
+    terms = terms[:, 0] + terms[:, 1] + terms[:, 2]
+    terms = jnp.transpose(terms, (1, 0, 2)).reshape(3, SH)
+    terms = place.by_core(terms[:, :M_SHARE], terms[:, M_SHARE:])
+    bias, log_rates, skip = terms[0], terms[1], terms[2]
     rates = -jnp.exp(log_rates)
 
     scale_in = inverse_rms(tokens)
@@ -694,11 +1016,43 @@
     def body_rows(value):
         return value.reshape(CORES, slots, piece + HALO, -1)[:, :, HALO:]
 
-    linear = body_rows(mm(normed, w_az[:, : q_cols + 2 * HD]))
-    zgate = body_rows(mm(normed, w_az[:, q_cols + 2 * HD :]).astype(BF16))
-    mixed_step = mm(normed, w_ms).astype(BF16).reshape(CORES, slots, piece + HALO, ms_cols)
-    mixed = mixed_step[..., :c_cols]
-    step_raw = mixed_step[:, :, HALO:, step_at:small_at].astype(F32)
+    linear = body_rows(mm(normed, w_a[:, :lin_cols]))
+    mixed_step = mm(normed, w_b).astype(BF16)
+    mixed = jnp.concatenate(
+        [mm(normed, w_a[:, lin_cols:]).astype(BF16), mixed_step[:, :tail_at]], axis=-1
+    ).reshape(CORES, slots, piece + HALO, c_cols)
+    step_raw = body_rows(mixed_step[:, tail_at : tail_at + M_SHARE]).astype(F32)
+
+    late_one, mixed = lax.optimization_barrier((late_one, mixed))
+    w_z, w_out = place.gather_plane(
+        place.place_z(late_one, [[(0, m_cols, 2)], [(m_cols, width, 1)]]),
+        [(0, 0, m_cols, 0, 0), (1, 0, width, 1, 0)],
+    )
+    late_two = jnp.concatenate([sorted_halves(late_columns), down_weight], axis=1)
+    late_two, late_one = lax.optimization_barrier((late_two, late_one))
+    late_two = place.spread_z(late_two)
+    w_out = w_out.reshape(2, chips // 2, groups, out_rows + mix_rows, width)
+    kept = lax.dynamic_index_in_dim(w_out, core, 0, False)
+    got = place.swap(lax.dynamic_index_in_dim(w_out, 1 - core, 0, False))
+    w_out = jnp.stack([place.by_core(kept, got), place.by_core(got, kept)], 1)
+    w_attn_out = w_out[..., :out_rows, :].reshape(q_cols, width)
+    w_mixer_out = w_out[..., out_rows:, :].reshape(m_cols, width)
+    half = width // 2
+    w_gate, w_up, w_down = place.gather_plane(
+        place.place_z(
+            late_two,
+            [
+                [(0, ff_half, 2), (2 * ff_half, half, 1)],
+                [(ff_half, ff_half, 2), (2 * ff_half + half, half, 1)],
+            ],
+        ),
+        [
+            (0, 0, ff_half, 0, 0),
+            (1, 0, ff_half, 1, 0),
+            (0, ff_half, half, 2, 0),
+            (1, ff_half, half, 2, half),
+        ],
+    )
 
     cos_part, sin_part = rotary_tables(positions, HD)
     cos_part, sin_part = cos_part[:, None, :, None], sin_part[:, None, :, None]
@@ -709,13 +1063,24 @@
         linear[..., q_cols : q_cols + HD][..., None, :], cos_part, sin_part
     ).astype(BF16)[..., 0, :]
     kv_own = jnp.concatenate([keys, linear[..., q_cols + HD :].astype(BF16)], axis=-1)
-    kv_own = place.by_core(kv_own, kv_own[::-1])
-    kv = jnp.stack(
-        [
-            place.gather_chips(kv_own[:, s], 1, s % 2 == 0).reshape(-1, 2 * HD)
-            for s in range(slots)
-        ]
-    )
+    kv_parts = [part.reshape(-1, 2 * HD) for part in place.spread_z(kv_own)]
+    plan = []
+    for r in range(groups):
+        for e in range(CORES):
+            for s in range(slots):
+
+                def source(at, e=e, s=s):
+                    return pl.ds((e * slots + s) * piece, piece), pl.ds(0, 2 * HD)
+
+                def goal(at, r=r, e=e):
+                    z = lax.rem(at[2] + groups - r, groups)
+                    h = lax.rem(at[3] + e, CORES)
+                    return pl.ds((h * groups + z) * piece, piece), pl.ds(0, 2 * HD)
+
+                plan.append((r, source, s, goal))
+    kv_size = jax.ShapeDtypeStruct((CORES * groups * piece, 2 * HD), BF16)
+    kv = moved(place, kv_parts, [kv_size] * slots, plan)
+    kv = place.gather_plane(kv, [(s, 0, 2 * HD, s, 0) for s in range(slots)])
 
     def by_heads(value, before, after):
         value = jnp.transpose(value, (1, 0, 3, 2, 4)).reshape(slots, CORES, Q_SHARE * piece, HD)
@@ -727,8 +1092,13 @@
 
     scale = HD ** (-0.5)
     queries = by_heads(queries * jnp.asarray(scale, BF16), 0, HD)
-    heads_out, lse = attend(pieces_at, lengths, queries, kv, piece)
-    attended = from_heads(heads_out[..., HD:]).reshape(rows_all, q_cols)
+    heads_out, lse = zip(
+        *[
+            attend(pieces_at, lengths[s : s + 1], queries[s : s + 1], kv[s][None], piece)
+            for s in range(slots)
+        ]
+    )
+    attended = from_heads(jnp.concatenate(heads_out)[..., HD:]).reshape(rows_all, q_cols)
 
     pre = shift
     for tap in range(KC):
@@ -752,35 +1122,37 @@
     chunk_args = [
         features, inject, readout, raw, raw_t, bias_row, bias_col, rate_row, rate_col, skip_row,
     ]
-    within, local_state, logs = over_pieces(
+    share_rows = m_cols // groups
+    held = pltpu.VMEM((groups, share_rows, NS), BF16)
+    held_more = pltpu.VMEM((groups, share_rows + EXTRA, NS), BF16)
+    within, logs, *local = over_pieces(
         chunk_kernel,
         "chunk",
         chunk_args,
         range(5, 10),
         [
             ((pieces, piece, m_cols), F32),
-            ((pieces, m_cols, NS), BF16),
             ((pieces, piece, LANES), F32),
+            *[((pieces, share_rows + EXTRA, NS), BF16)] * groups,
         ],
         state_flops,
-    )
-    decays = jnp.exp(logs[:, piece - 1, :M_SHARE]).reshape(CORES, slots, M_SHARE)
-    decays_h = place.by_core(decays, decays[::-1])
-    all_decays = lax.all_gather(decays_h, AXES, axis=0, tiled=False)
-    all_decays = all_decays.reshape(chips, CORES, groups, CORES, slots, M_SHARE)
-    all_decays = lax.dynamic_index_in_dim(all_decays, core, 1, False)
-    state_in = carried(
-        place, local_state.reshape(CORES, slots, m_cols, NS), all_decays, False
-    ).reshape(pieces, m_cols, NS)
+        at,
+        [held_more],
+    )
+    local = [part.reshape(CORES, slots, share_rows + EXTRA, NS) for part in local]
+    state_in, marks, fades = carried(place, at, local, None, None, False)
     (ssd,) = over_pieces(
         carry_kernel,
         "carry",
-        [within, readout, state_in, logs],
+        [within, readout, logs, *state_in],
         (),
         [((pieces, piece, m_cols), BF16)],
         2 * pieces * piece * m_cols * NS,
+        at,
+        [held],
     )
     ssd = ssd.reshape(CORES, slots, piece, m_cols).astype(F32)
+    zgate = body_rows(mm(normed, w_z).astype(BF16))
     gate_value, gate_slope = silu_and_slope(zgate.astype(F32))
     gated_raw = ssd * gate_value
     squares = jnp.sum(gated_raw * gated_raw, axis=-1)
@@ -810,17 +1182,19 @@
     dgate = (dhidden * up_lin * gate_act_slope).astype(BF16)
     dup = (dhidden * gate_act).astype(BF16)
 
-    def scatter_parity(grad, rows, b_first):
-        return place.reduce_chips(grad.reshape(na, nb, groups, rows, width), 0, b_first)
-
-    def scatter_columns(grad, b_first):
-        return place.reduce_chips(
-            grad.reshape(na, nb, CORES, groups, shard_rows, -1), 1, b_first
-        )
-
-    grad_down = scatter_parity(mm(hidden, dy, TN), ff_rows, True)
-    grad_gate = scatter_columns(mm(post, dgate, TN), False)
-    grad_up = scatter_columns(mm(post, dup, TN), True)
+    def by_parity(grad):
+        return grad.reshape(na, nb, 1, groups, -1, grad.shape[-1])
+
+    def by_columns(grad):
+        return grad.reshape(na, nb, CORES, groups, shard_rows, grad.shape[-1])
+
+    ff_grads, ff_finish = place.reduce_far(
+        [
+            (mm(post, dgate, TN).astype(BF16), 2),
+            (mm(post, dup, TN).astype(BF16), 2),
+            (mm(hidden, dy, TN).astype(BF16), 1),
+        ]
+    )
     dpost = own_sum(mm(dgate, w_gate, NT) + mm(dup, w_up, NT))
     dresidual = dy_own.reshape(-1, width) + rms_back(residual, scale_post, gain_post, dpost)
     grad_post_gain = jnp.sum(dpost * residual * scale_post, axis=0)
@@ -835,11 +1209,10 @@
         ],
         axis=3,
     )
+    grad_outs = grad_outs.astype(BF16)
     kept = lax.dynamic_index_in_dim(grad_outs, core, 1, False)
-    got = place.swap(lax.dynamic_index_in_dim(grad_outs, 1 - core, 1, False).astype(BF16))
-    got = got.astype(F32)
+    got = place.swap(lax.dynamic_index_in_dim(grad_outs, 1 - core, 1, False))
     grad_outs = jnp.concatenate([place.by_core(kept, got), place.by_core(got, kept)], axis=0)
-    grad_outs = scatter_parity(grad_outs, out_rows + mix_rows, False)
     scaled = dgated * gain_mixer
     inner = jnp.sum(scaled * gated_raw, axis=-1)
     inner = (inner + place.swap(inner)[::-1])[..., None] / (SH * SHD)
@@ -848,41 +1221,63 @@
     dssd = (dgated_raw * gate_value).astype(BF16).reshape(pieces, piece, m_cols)
     dzgate = (dgated_raw * ssd * gate_slope).astype(BF16)
 
-    (direct,) = over_pieces(
+    def halo_rows(value):
+        value = value.reshape(CORES, slots, piece, -1)
+        return jnp.pad(value, ((0, 0), (0, 0), (HALO, 0), (0, 0)))
+
+    dzgate = halo_rows(dzgate).reshape(rows_halo, m_cols)
+    mid_grads, mid_finish = place.reduce_far(
+        [
+            (grad_outs.reshape(-1, width), 1),
+            (mm(normed, dzgate, TN).astype(BF16), 2),
+        ]
+    )
+    dnormed = mm(dzgate, w_z, NT)
+
+    direct = over_pieces(
         direct_kernel,
         "direct",
         [dssd, readout, logs],
         (),
-        [((pieces, m_cols, NS), BF16)],
+        [((pieces, share_rows, NS), BF16)] * groups,
         2 * pieces * piece * m_cols * NS,
-    )
-    later = carried(
-        place, direct.reshape(CORES, slots, m_cols, NS), all_decays, True
-    ).reshape(pieces, m_cols, NS)
+        at,
+        [held],
+    )
+    direct = [part.reshape(CORES, slots, share_rows, NS) for part in direct]
+    dattended, direct = lax.optimization_barrier((dattended, direct))
+    later, _, _ = carried(place, at, direct, marks, fades, True)
 
     dout = by_heads(
         dattended.reshape(CORES, slots, piece, Q_SHARE, HD), HD, 0
     )
-    dqueries, dkv = attend_back(pieces_at, lengths, queries, kv, heads_out, dout, lse, piece)
-    dkv_own = jnp.stack(
-        [
-            place.reduce_chips(
-                dkv[s].reshape(na, nb, CORES, groups, piece, 2 * HD), 1, s % 2 == 0
+    dqueries, dkv = zip(
+        *[
+            attend_back(
+                pieces_at,
+                lengths[s : s + 1],
+                queries[s : s + 1],
+                kv[s][None],
+                heads_out[s],
+                dout[s : s + 1],
+                lse[s],
+                piece,
             )
             for s in range(slots)
-        ],
-        axis=1,
-    )
+        ]
+    )
+    dqueries = jnp.concatenate(dqueries)
+    dkv_own = place.reduce_chips(
+        [dkv[s].reshape(na, nb, CORES, groups, piece, 2 * HD) for s in range(slots)],
+        [s % 2 == 0 for s in range(slots)],
+    )
+    dkv_own = jnp.stack([part.reshape(CORES, piece, 2 * HD) for part in dkv_own], axis=1)
     dkv_own = place.by_core(dkv_own, dkv_own[::-1])
 
-    agree = jnp.sum(
-        later.astype(F32) * state_in.astype(F32), axis=-1
-    ).reshape(pieces, M_SHARE, SHD)
-    agree = jnp.pad(jnp.sum(agree, axis=-1), ((0, 0), (0, LANES - M_SHARE)))[:, None]
     dfeatures, dinject, dreadout, draw, sums = over_pieces(
         chunk_back_kernel,
         "chunk_back",
-        chunk_args + [dssd, state_in, later, agree],
+        chunk_args + [dssd, *state_in, *later],
         range(5, 10),
         [
             ((pieces, piece, m_cols), F32),
@@ -892,16 +1287,11 @@
             ((pieces, 8, LANES), F32),
         ],
         4 * state_flops,
-        [pltpu.VMEM((LANES, 2 * LANES), F32), pltpu.VMEM((piece, LANES), F32)],
-    )
-    head_sums = jnp.sum(sums, axis=0)[:3, :M_SHARE]
-    nothing = jnp.zeros_like(head_sums)
-    head_sums = jnp.concatenate(
-        [place.by_core(head_sums, nothing), place.by_core(nothing, head_sums)], axis=1
-    )
-    head_sums = lax.psum(head_sums, AXES)
-    head_sums = lax.dynamic_slice_in_dim(head_sums, place.at["z"] * (SH // groups), SH // groups, 1)
-
+        at,
+        [pltpu.VMEM((LANES, 2 * LANES), F32), pltpu.VMEM((piece, LANES), F32), held, held],
+    )
+    ff_grads, mid_grads, dfeatures = lax.optimization_barrier((ff_grads, mid_grads, dfeatures))
+    ff_grads, mid_grads = ff_finish(ff_grads), mid_finish(mid_grads)
     dinject = dinject.reshape(CORES, slots, piece, NS)
     dreadout = dreadout.reshape(CORES, slots, piece, NS)
     dshared = place.by_core(dinject, dreadout) + place.swap(
@@ -921,25 +1311,22 @@
     grad_shift = jnp.sum(dpre, axis=(0, 1, 2))
     dmixed = dmixed.astype(BF16)
 
-    def halo_rows(value):
-        value = value.reshape(CORES, slots, piece, -1)
-        return jnp.pad(value, ((0, 0), (0, 0), (HALO, 0), (0, 0)))
-
     dstep = draw[..., :M_SHARE].astype(BF16)
-    dms = jnp.concatenate(
+    db_low = jnp.concatenate(
         [
-            dmixed,
+            dmixed[..., f_cols:],
             halo_rows(dstep),
             jnp.zeros((CORES, slots, piece + HALO, ms_cols - small_at), BF16),
         ],
         axis=-1,
-    ).reshape(rows_halo, ms_cols)
+    ).reshape(rows_halo, b_cols)
     dq_rows = from_heads(dqueries[..., :HD] * scale)
     dq_rows = rotate(dq_rows, cos_part, -sin_part).reshape(CORES, slots, piece, q_cols)
     dk_rows = rotate(dkv_own[..., None, :HD], cos_part, -sin_part)[..., 0, :]
     dlin = jnp.concatenate([dq_rows, dk_rows, dkv_own[..., HD:]], axis=-1).astype(BF16)
-    daz = halo_rows(jnp.concatenate([dlin, dzgate], axis=-1)).reshape(rows_halo, az_cols)
-    dnormed = mm(daz, w_az, NT) + mm(dms, w_ms, NT)
+    da_low = jnp.concatenate([halo_rows(dlin), dmixed[..., :f_cols]], axis=-1)
+    da_low = da_low.reshape(rows_halo, a_cols)
+    dnormed = dnormed + mm(da_low, w_a, NT) + mm(db_low, w_b, NT)
     dnormed = own_sum(dnormed).reshape(slots, piece + HALO, width)
     rim_back = lax.ppermute(
         dnormed[:, HALO - KC + 1 : HALO].astype(BF16),
@@ -977,40 +1364,58 @@
         ],
         axis=1,
     )
-    vector_size = vector_grads.shape[1]
     vector_grads = jnp.pad(
         vector_grads, ((0, 0), (0, small_cols * shard_rows - vector_size))
     ).reshape(width, small_cols)
-    grad_az = scatter_columns(mm(normed, daz, TN), False)
-    grad_ms = mm(normed, dms, TN)
-    grad_ms = lax.dynamic_update_slice(grad_ms, vector_grads, (0, small_at))
-    grad_ms = scatter_columns(grad_ms, True)
-
-    columns = jnp.concatenate([grad_az, grad_ms, grad_gate, grad_up], axis=-1)
-    kept = lax.dynamic_index_in_dim(columns, core, 0, False)
-    got = place.swap(lax.dynamic_index_in_dim(columns, 1 - core, 0, False))
-    first, second = place.by_core(kept, got), place.by_core(got, kept)
+    grad_b = mm(normed, db_low, TN)
+    grad_b = lax.dynamic_update_slice(grad_b, vector_grads, (0, tail_at + small_at))
+    grad_a = mm(normed, da_low, TN)
+    head_sums = jnp.sum(sums, axis=0)[:3, :M_SHARE]
+    head_sums, grad_a = lax.optimization_barrier((head_sums, grad_a))
+    head_sums = place.sum_all(head_sums)
+    other_sums = place.swap(head_sums)
+    head_sums = jnp.concatenate(
+        [place.by_core(head_sums, other_sums), place.by_core(other_sums, head_sums)], axis=1
+    )
+    head_sums = lax.dynamic_slice_in_dim(head_sums, place.at["z"] * (SH // groups), SH // groups, 1)
+
+    grad_a, grad_b = place.reduce_chips(
+        [by_columns(grad_a), by_columns(grad_b)], [True, False]
+    )
+
+    def between_cores(columns):
+        columns = columns.reshape(CORES, shard_rows, -1)
+        kept = lax.dynamic_index_in_dim(columns, core, 0, False)
+        got = place.swap(lax.dynamic_index_in_dim(columns, 1 - core, 0, False))
+        return place.by_core(kept, got), place.by_core(got, kept)
+
+    def ff_whole(pair):
+        parts = [half.reshape(shard_rows, chips, 1, -1) for half in pair]
+        return jnp.concatenate(parts, axis=2).reshape(shard_rows, -1)
+
+    ff_rows_each = ff_grads.shape[0] // 3
+    both = between_cores(
+        jnp.concatenate([ff_grads[:ff_rows_each], ff_grads[ff_rows_each : 2 * ff_rows_each]], axis=1)
+    )
+    grad_gate = ff_whole([half[:, :ff_half] for half in both]).astype(F32)
+    grad_up = ff_whole([half[:, ff_half:] for half in both]).astype(F32)
+    grad_down = ff_grads[2 * ff_rows_each :].astype(F32)
+    grad_outs = mid_grads[:, :width].astype(F32)
+    grad_zgate = jnp.concatenate(between_cores(mid_grads[:, width:]), axis=1).astype(F32)
+    first, second = between_cores(jnp.concatenate([grad_a, grad_b], axis=1))
 
     def both_halves(start, size):
         return jnp.concatenate([first[:, start : start + size], second[:, start : start + size]], 1)
 
-    def ff_whole(start):
-        parts = [
-            half[:, start : start + ff_half].reshape(shard_rows, chips, 1, -1)
-            for half in (first, second)
-        ]
-        return jnp.concatenate(parts, axis=2).reshape(shard_rows, -1)
-
     grad_attn_in = jnp.concatenate(
         [both_halves(0, q_cols), both_halves(q_cols, HD), both_halves(q_cols + HD, HD)], axis=1
     )
-    grad_zgate = both_halves(q_cols + 2 * HD, m_cols)
     grad_mixer_in = jnp.concatenate(
-        [both_halves(az_cols, m_cols), both_halves(az_cols + m_cols, NS)], axis=1
-    )
-    grad_step = both_halves(az_cols + step_at, M_SHARE)
-    small_sum = first + second
-    small_sum = small_sum[:, az_cols + small_at : az_cols + small_at + small_cols].reshape(-1)
+        [both_halves(lin_cols, m_cols), both_halves(lin_cols + m_cols, NS)], axis=1
+    )
+    grad_step = both_halves(lin_cols + c_cols, M_SHARE)
+    small_at = lin_cols + c_cols + small_at
+    small_sum = (first + second)[:, small_at : small_at + small_cols].reshape(-1)
 
     return (
         layer_out.reshape(slots, piece, width),
@@ -1029,8 +1434,8 @@
         small_sum[ends[0] : ends[1]],
         grad_outs[out_rows:],
         small_sum[ends[1] : ends[2]],
-        ff_whole(az_cols + ms_cols),
-        ff_whole(az_cols + ms_cols + ff_half),
+        grad_gate,
+        grad_up,
         grad_down,
     )
 

time: 1020 us -> 766 us (0.75); the launches traced: 1040 us -> 753 us
  blocking collectives: 119 us -> 0 us
  waiting for transfers between devices: 281 us -> 186 us
  local copies, waits for them, and re-layouts: 170 us -> 96.3 us
  Pallas kernels: 74.2 us -> 147 us
  other arithmetic: 128 us -> 76.6 us
  starting transfers between devices: 199 us -> 168 us
  between operations: 5.59 us -> 17.1 us
    ppermute x112 -> x83, waiting for transfers between devices: 281 us -> 156 us  [shift(): return lax.ppermute(x, AXES, self.pairs(dim, by))]
    all_gather x2 -> x0, blocking collectives: 78.3 us -> none  [the longest x1 66.4 us: shards(): all_decays = lax.all_gather(decays_h, AXES, axis=0, tiled=False)]
    ppermute x112 -> x83, starting transfers between devices: 195 us -> 132 us  [shift(): return lax.ppermute(x, AXES, self.pairs(dim, by))]
    pallas_call x0 -> x16, Pallas kernels: none -> 61 us  [the longest x12 49 us: moved(): pl.pallas_call(functools.partial(moved_kernel, plan=plan, count=len(sourc...]
    psum x1 -> x0, blocking collectives: 40.9 us -> none  [shards(): head_sums = lax.psum(head_sums, AXES)]
    another operation x54 -> x6, other arithmetic: 36.7 us -> 1.5 us  [the longest x39 31.2 us: place(): jnp.stack([jnp.where(v == 0, parts[0], parts[1]), jnp.where(v == 0, parts...]
    ppermute x0 -> x10, starting transfers between devices: none -> 29.2 us  [the longest x6 20.5 us: carried(): lax.ppermute(leaving, AXES, place.chip_pairs(k))]
    ppermute x0 -> x10, waiting for transfers between devices: none -> 28.7 us  [the longest x6 22.5 us: carried(): lax.ppermute(leaving, AXES, place.chip_pairs(k))]
  transfers between devices with their start and end apart: 114 -> 99, of which waited for: 50 -> 33; matrix products, arithmetic and copies ran while one was open for 29% -> 22% of each run, Pallas kernels for 7% -> 19%
where the time goes in v2:
time: 766 us; the launch traced here: 753 us
  waiting for transfers between devices  186 us (24%)
  starting transfers between devices  168 us (22%)
  Pallas kernels  147 us (19%)
  local copies, waits for them, and re-layouts  96.3 us (13%)
  other arithmetic  76.6 us (10%)
  matrix products  62.8 us (8%)
  between operations  17.1 us (2%)
    ppermute x83, waiting for transfers between devices, shift(): return lax.ppermute(x, AXES, self.pairs(dim, by))  156 us
    ppermute x83, starting transfers between devices, shift(): return lax.ppermute(x, AXES, self.pairs(dim, by))  132 us
    dot_general x25, matrix products, mm(): lax.dot_general(left, right, dims, precision=precision, preferred_element...  62.8 us
    pallas_call x12, Pallas kernels, moved(): pl.pallas_call(functools.partial(moved_kernel, plan=plan, count=len(sourc...  49 us
    pallas_call x4, Pallas kernels, over_pieces(): pl.pallas_call(kernel, grid=(pieces,), in_specs=[spec(shape, split) for s...  47.7 us
    ppermute x6, waiting for transfers between devices, carried(): lax.ppermute(leaving, AXES, place.chip_pairs(k))  22.5 us
    unnamed x278, local copies, waits for them, and re-layouts  22.2 us
    pallas_call x2, Pallas kernels, attend_back(): pl.pallas_call(functools.partial(attend_back_kernel, piece=piece), grid_s...  22.1 us
  transfers between devices with their start and end apart: 99, of which 33 were waited for; matrix products, arithmetic and copies ran while one was open for 22% of the time, Pallas kernels for 19%

profile of v2, /device:TPU:0, one launch (start us, length us, event | category | flops | bytes accessed | tf_op | source)
XLA Modules:
  0.0 753.4 jit_solution(529768088301003068)
XLA Ops:
  18.2 4.9 collective-permute-start
  39.2 6.8 collective-permute-done.4.refs_2_
  55.0 7.6 %collective-permute-done.11.refs_6_ = bf16[256,640]{1,0:T(8,128)(2,1)} collective-permute-done((bf16[256,640]{1,0:T(8,128)(2,1)}, bf16[256,640]{1,0:T(8,128)(2,1)}, u32[]{:S(2)}, u32[]{:S(2)}) %collective-permute-start.11) | collective-permute-done | bytes 327712 | tf_op jit(solution)/shard_map/ppermute | solution.py:79
  62.6 3.7 collective-permute-start.22
  78.1 4.1 moved.13
  96.7 3.8 collective-permute-start.13
  115.3 8.8 %chunk.1 = (f32[4,192,768]{2,1,0:T(8,128)}, f32[4,192,128]{2,1,0:T(8,128)}, bf16[4,208,128]{2,1,0:T(8,128)(2,1)}, bf16[4,208,128]{2,1,0:T(8,128)(2,1)}, bf16[4,2...) custom-call(bf16[4,192,768]{2,1,0:T(8,128)(2,1)} %bitcast.361, bf16[4,192,128]{2,1,0:T(8,128)(2,1)} %bitcast.428, ...), custom_call_target="tpu_custom_call" | custom-call | flops 528482304 | bytes 5623936 | tf_op jit(solution)/shard_map/chunk/pallas_call | solution.py:698
  137.4 39.4 %collective-permute-done.34.refs_2_.refs_6_ = bf16[2,2,208,128]{3,2,1,0:T(8,128)(2,1)S(1)} collective-permute-done((bf16[2,2,208,128]{3,2,1,0:T(8,128)(2,1)}, bf16[2,2,208,128]{3,2,1,0:T(8,128)(2,1)S(1)}, u32[]{:S(2)}, u32[]{:S(2)}) %collective-permute-start.34) | collective-permute-done | bytes 213024 | tf_op jit(solution)/shard_map/ppermute | solution.py:79
  203.7 4.9 collective-permute-start.39
  216.4 4.0 collective-permute-start.40
  220.4 3.7 collective-permute-start.41
  236.4 4.8 carry.1
  243.8 4.3 moved.15
  248.0 7.9 %attend.2 = (bf16[1,2,768,128]{3,2,1,0:T(8,128)(2,1)}, f32[1,2,1,768]{3,2,1,0:T(1,128)}) custom-call(s32[2]{0:T(128)} %copy-done.123, s32[1]{0:T(128)} %get-tuple-element.391.lengths, bf16[1,2,768,128]{3,2,1,0:T(8,128)(2,1)} %get-tuple-element.318.q_ref, bf16[1,6144,128]{2,1,0:T(8,128)(2,1)} %bitcast.474), custom_call_target="tpu_custom_call" | custom-call | flops 2415919104 | bytes 3145728 | tf_op jit(solution)/shard_map/attend/pallas_call | solution.py:378
  255.9 7.9 %attend.3 = (bf16[1,2,768,128]{3,2,1,0:T(8,128)(2,1)}, f32[1,2,1,768]{3,2,1,0:T(1,128)}) custom-call(s32[2]{0:T(128)} %copy-done.123, s32[1]{0:T(128)} %get-tuple-element.392.lengths, bf16[1,2,768,128]{3,2,1,0:T(8,128)(2,1)} %get-tuple-element.319.q_ref, bf16[1,6144,128]{2,1,0:T(8,128)(2,1)} %bitcast.472), custom_call_target="tpu_custom_call" | custom-call | flops 2415919104 | bytes 3145728 | tf_op jit(solution)/shard_map/attend/pallas_call | solution.py:378
  263.8 22.3 %collective-permute-start.53 = (bf16[256,1536]{1,0:T(8,128)(2,1)}, bf16[256,1536]{1,0:T(8,128)(2,1)}, u32[]{:S(2)}, u32[]{:S(2)}) collective-permute-start(bf16[256,1536]{1,0:T(8,128)(2,1)} %get-tuple-element.124.refs_4_), channel_id=1, source_target_pairs={{0,16},{4,20},{1,17},{5,21},{2,18},{6,22},{3,19},{7,23},{8,24},{12... | collective-permute-start | bytes 2359304 | tf_op jit(solution)/shard_map/ppermute | solution.py:79
  287.1 4.7 moved.17
  326.0 10.6 %collective-permute-done.50.refs_2_ = bf16[256,1536]{1,0:T(8,128)(2,1)S(1)} collective-permute-done((bf16[256,1536]{1,0:T(8,128)(2,1)}, bf16[256,1536]{1,0:T(8,128)(2,1)S(1)}, u32[]{:S(2)}, u32[]{:S(2)}) %collective-permute-start.50) | collective-permute-done | bytes 786464 | tf_op jit(solution)/shard_map/ppermute | solution.py:79
  336.7 15.8 %collective-permute-done.51.refs_3_ = bf16[256,1536]{1,0:T(8,128)(2,1)S(1)} collective-permute-done((bf16[256,1536]{1,0:T(8,128)(2,1)}, bf16[256,1536]{1,0:T(8,128)(2,1)S(1)}, u32[]{:S(2)}, u32[]{:S(2)}) %collective-permute-start.51) | collective-permute-done | bytes 786464 | tf_op jit(solution)/shard_map/ppermute | solution.py:79
  354.4 6.3 moved.19
  381.4 4.8 fusion.69
  408.0 4.7 moved.21
  412.8 5.2 convolution_convert_fusion.1.refs_1_
  424.4 6.4 moved.20
  439.5 5.4 direct.1
  453.6 11.0 %attend_back.2 = (f32[1,2,768,128]{3,2,1,0:T(8,128)}, bf16[1,6144,128]{2,1,0:T(8,128)(2,1)}) custom-call(s32[2]{0:T(128)} %copy-done.123, s32[1]{0:T(128)} %get-tuple-element.391.lengths, bf16[1,2,768,128]{3,2,1,0:T(8,128)(2,1)} %get-tuple-element.318.q_ref, bf16[1,6144,128]{2,1,0:T(8,128)(2,1)} %bitcast.475, ...), custom_call_target="tpu_custom_call" | custom-call | flops 6039797760 | bytes 4718592 | tf_op jit(solution)/shard_map/attend_back/pallas_call | solution.py:465
  464.6 11.1 %attend_back.3 = (f32[1,2,768,128]{3,2,1,0:T(8,128)}, bf16[1,6144,128]{2,1,0:T(8,128)(2,1)}) custom-call(s32[2]{0:T(128)} %copy-done.123, s32[1]{0:T(128)} %get-tuple-element.392.lengths, bf16[1,2,768,128]{3,2,1,0:T(8,128)(2,1)} %get-tuple-element.319.q_ref, bf16[1,6144,128]{2,1,0:T(8,128)(2,1)} %bitcast.473, ...), custom_call_target="tpu_custom_call" | custom-call | flops 6039797760 | bytes 4718592 | tf_op jit(solution)/shard_map/attend_back/pallas_call | solution.py:465
  482.2 12.1 %collective-permute-start.62 = (bf16[2,2,4,192,128]{4,3,2,1,0:T(8,128)(2,1)}, bf16[2,2,4,192,128]{4,3,2,1,0:T(8,128)(2,1)}, u32[]{:S(2)}, u32[]{:S(2)}) collective-permute-start(bf16[2,2,4,192,128]{4,3,2,1,0:T(8,128)(2,1)} %dynamic-slice_bitcast_fusion.1), channel_id=1, source_target_pairs={{0,8},{4,12},{1,9},{5,13},{2,10},{6,14},{3,11},{7,15},{8,0},{12,4}... | collective-permute-start | bytes 2359304 | tf_op jit(solution)/shard_map/ppermute | solution.py:79
  494.4 4.9 fusion.93
  502.3 15.9 %collective-permute-start.72 = (bf16[2,208,128]{2,1,0:T(8,128)(2,1)}, bf16[2,208,128]{2,1,0:T(8,128)(2,1)S(1)}, u32[]{:S(2)}, u32[]{:S(2)}) collective-permute-start(bf16[2,208,128]{2,1,0:T(8,128)(2,1)} %scan.6), channel_id=1, source_target_pairs={{0,16},{1,17},{2,18},{3,19},{4,20},{5,21},{6,22},{7,23},{8,24},{9,... | collective-permute-start | bytes 319496 | tf_op jit(solution)/shard_map/ppermute | solution.py:848
  520.7 16.1 %collective-permute-done.71.refs_8_ = bf16[2,208,128]{2,1,0:T(8,128)(2,1)S(1)} collective-permute-done((bf16[2,208,128]{2,1,0:T(8,128)(2,1)}, bf16[2,208,128]{2,1,0:T(8,128)(2,1)S(1)}, u32[]{:S(2)}, u32[]{:S(2)}) %collective-permute-start.71) | collective-permute-done | bytes 106528 | tf_op jit(solution)/shard_map/ppermute | solution.py:848
  541.3 3.7 collective-permute-start.76
  545.5 3.7 collective-permute-done.74
  549.2 5.1 collective-permute-done.75
  554.3 28.8 %chunk_back.1 = (f32[4,192,768]{2,1,0:T(8,128)}, f32[4,192,128]{2,1,0:T(8,128)}, f32[4,192,128]{2,1,0:T(8,128)}, f32[4,192,128]{2,1,0:T(8,128)}, f32[4,8,128]{2,1,0:T(8,128)}) custom-call(bf16[4,192,768]{2,1,0:T(8,128)(2,1)} %bitcast.362, bf16[4,192,128]{2,1,0:T(8,128)(2,1)} %bitcast.429, bf16[4,192,128]{2,1,0:T(8,128)(2,1)} %bitcast.378, ...), custom_call_target="tpu_custom_call" | custom-call | flops 2113929216 | bytes 8327296 | tf_op jit(solution)/shard_map/chunk_back/pallas_call | solution.py:698
  588.6 3.8 collective-permute-start.61
  594.9 7.0 collective-permute-done.61
  602.1 3.7 collective-permute-done.63
  606.0 3.8 collective-permute-start.64
  615.7 7.5 collective-permute-done.65
  625.7 4.9 fusion.6
  635.8 4.7 collective-permute-start.89
  649.7 4.5 add_add_fusion
  684.5 3.7 dynamic_update_slice.3
  695.8 12.7 %collective-permute-done.82 = bf16[2,2,4,32,640]{4,3,2,1,0:T(8,128)(2,1)S(1)} collective-permute-done((bf16[2,2,4,32,640]{4,3,2,1,0:T(8,128)(2,1)S(1)}, bf16[2,2,4,32,640]{4,3,2,1,0:T(8,128)(2,1)S(1)}, u32[]{:S(2)}, u32[]{:S(2)}) %collective-permute-start.82) | collective-permute-done | bytes 655392 | tf_op jit(solution)/shard_map/ppermute | solution.py:79
  710.9 6.0 collective-permute-done.81
  718.7 4.1 collective-permute-start.85
  728.1 6.1 collective-permute-done.85
  (783 shorter events, 348.8 us)
Async XLA Ops:
  7.2 618.5 %reduce-scatter.7.cloned.1.call-start = ((), (), s32[]{:S(2)}) async-start(), calls=%async_computation.5 | async-start | bytes 4587520 | tf_op jit(solution)/shard_map/reduce_scatter | solution.py:184
  25.6 27.6 %collective-permute-start.45 = (bf16[32,2048]{1,0:T(8,128)(2,1)S(1)}, bf16[32,2048]{1,0:T(8,128)(2,1)S(1)}, u32[]{:S(2)}, u32[]{:S(2)}) collective-permute-start(bf16[32,2048]{1,0:T(8,128)(2,1)S(1)} %broadcast_select_fusion.7), channel_id=1, source_target_pairs={{0,4},{4,0},{1,5},{5,1},{2,6},{6,2},{3,7},{7,3},{8,12},{12,8},{9,1... | collective-permute-start | bytes 393224 | tf_op jit(solution)/shard_map/ppermute | solution.py:79
  29.2 37.7 %collective-permute-start.1 = (bf16[2,200,1024]{2,1,0:T(8,128)(2,1)S(1)}, bf16[2,200,1024]{2,1,0:T(8,128)(2,1)S(1)}, u32[]{:S(2)}, u32[]{:S(2)}) collective-permute-start(bf16[2,200,1024]{2,1,0:T(8,128)(2,1)S(1)} %get-tuple-element.302), channel_id=1, source_target_pairs={{0,4},{4,0},{1,5},{5,1},{2,6},{6,2},{3,7},{7,3},{8,12},{12,8},{9,1... | collective-permute-start | bytes 2457608 | tf_op jit(solution)/shard_map/ppermute | solution.py:79
  54.0 19.0 %collective-permute-start.8 = (bf16[256,768]{1,0:T(8,128)(2,1)}, bf16[256,768]{1,0:T(8,128)(2,1)}, u32[]{:S(2)}, u32[]{:S(2)}) collective-permute-start(bf16[256,768]{1,0:T(8,128)(2,1)} %get-tuple-element.92.refs_0_), channel_id=1, source_target_pairs={{0,16},{4,20},{1,17},{5,21},{2,18},{6,22},{3,19},{7,23},{8,24},{12... | collective-permute-start | bytes 1179656 | tf_op jit(solution)/shard_map/ppermute | solution.py:79
  62.6 41.2 %collective-permute-start.22 = (bf16[64,1792]{1,0:T(8,128)(2,1)}, bf16[64,1792]{1,0:T(8,128)(2,1)}, u32[]{:S(2)}, u32[]{:S(2)}) collective-permute-start(bf16[64,1792]{1,0:T(8,128)(2,1)} %maximum_maximum_fusion.refs_0_), channel_id=1, source_target_pairs={{0,1},{4,5},{1,2},{5,6},{2,3},{6,7},{3,0},{7,4},{8,9},{12,13},{9,1... | collective-permute-start | bytes 688136 | tf_op jit(solution)/shard_map/ppermute | solution.py:79
  70.5 34.5 %collective-permute-start.23 = (bf16[64,1792]{1,0:T(8,128)(2,1)}, bf16[64,1792]{1,0:T(8,128)(2,1)}, u32[]{:S(2)}, u32[]{:S(2)}) collective-permute-start(bf16[64,1792]{1,0:T(8,128)(2,1)} %maximum_maximum_fusion.refs_0_), channel_id=1, source_target_pairs={{0,2},{4,6},{1,3},{5,7},{2,0},{6,4},{3,1},{7,5},{8,10},{12,14},{9,... | collective-permute-start | bytes 688136 | tf_op jit(solution)/shard_map/ppermute | solution.py:79
  72.9 32.1 %collective-permute-start.24 = (bf16[64,1792]{1,0:T(8,128)(2,1)}, bf16[64,1792]{1,0:T(8,128)(2,1)}, u32[]{:S(2)}, u32[]{:S(2)}) collective-permute-start(bf16[64,1792]{1,0:T(8,128)(2,1)} %maximum_maximum_fusion.refs_0_), channel_id=1, source_target_pairs={{0,3},{4,7},{1,0},{5,4},{2,1},{6,5},{3,2},{7,6},{8,11},{12,15},{9,... | collective-permute-start | bytes 688136 | tf_op jit(solution)/shard_map/ppermute | solution.py:79
  96.7 29.7 %collective-permute-start.13 = (bf16[2,2,192,128]{3,2,1,0:T(8,128)(2,1)}, bf16[2,2,192,128]{3,2,1,0:T(8,128)(2,1)}, u32[]{:S(2)}, u32[]{:S(2)}) collective-permute-start(bf16[2,2,192,128]{3,2,1,0:T(8,128)(2,1)} %pad_maximum_fusion.18), channel_id=1, source_target_pairs={{0,1},{4,5},{1,2},{5,6},{2,3},{6,7},{3,0},{7,4},{8,9},{12,13},{9,1... | collective-permute-start | bytes 589832 | tf_op jit(solution)/shard_map/ppermute | solution.py:79
  100.5 29.2 %collective-permute-start.14 = (bf16[2,2,192,128]{3,2,1,0:T(8,128)(2,1)}, bf16[2,2,192,128]{3,2,1,0:T(8,128)(2,1)}, u32[]{:S(2)}, u32[]{:S(2)}) collective-permute-start(bf16[2,2,192,128]{3,2,1,0:T(8,128)(2,1)} %pad_maximum_fusion.18), channel_id=1, source_target_pairs={{0,2},{4,6},{1,3},{5,7},{2,0},{6,4},{3,1},{7,5},{8,10},{12,14},{9,... | collective-permute-start | bytes 589832 | tf_op jit(solution)/shard_map/ppermute | solution.py:79
  103.8 26.9 %collective-permute-start.15 = (bf16[2,2,192,128]{3,2,1,0:T(8,128)(2,1)}, bf16[2,2,192,128]{3,2,1,0:T(8,128)(2,1)}, u32[]{:S(2)}, u32[]{:S(2)}) collective-permute-start(bf16[2,2,192,128]{3,2,1,0:T(8,128)(2,1)} %pad_maximum_fusion.18), channel_id=1, source_target_pairs={{0,3},{4,7},{1,0},{5,4},{2,1},{6,5},{3,2},{7,6},{8,11},{12,15},{9,... | collective-permute-start | bytes 589832 | tf_op jit(solution)/shard_map/ppermute | solution.py:79
  126.3 55.5 %collective-permute-start.46 = (bf16[64,3072]{1,0:T(8,128)(2,1)S(1)}, bf16[64,3072]{1,0:T(8,128)(2,1)S(1)}, u32[]{:S(2)}, u32[]{:S(2)}) collective-permute-start(bf16[64,3072]{1,0:T(8,128)(2,1)S(1)} %pad_maximum_fusion.12.refs_0_), channel_id=1, source_target_pairs={{0,1},{4,5},{1,2},{5,6},{2,3},{6,7},{3,0},{7,4},{8,9},{12,13},{9,1... | collective-permute-start | bytes 1179656 | tf_op jit(solution)/shard_map/ppermute | solution.py:79
  126.5 56.9 %collective-permute-start.47 = (bf16[64,3072]{1,0:T(8,128)(2,1)S(1)}, bf16[64,3072]{1,0:T(8,128)(2,1)S(1)}, u32[]{:S(2)}, u32[]{:S(2)}) collective-permute-start(bf16[64,3072]{1,0:T(8,128)(2,1)S(1)} %pad_maximum_fusion.12.refs_0_), channel_id=1, source_target_pairs={{0,2},{4,6},{1,3},{5,7},{2,0},{6,4},{3,1},{7,5},{8,10},{12,14},{9,... | collective-permute-start | bytes 1179656 | tf_op jit(solution)/shard_map/ppermute | solution.py:79
  129.7 54.4 %collective-permute-start.48 = (bf16[64,3072]{1,0:T(8,128)(2,1)S(1)}, bf16[64,3072]{1,0:T(8,128)(2,1)S(1)}, u32[]{:S(2)}, u32[]{:S(2)}) collective-permute-start(bf16[64,3072]{1,0:T(8,128)(2,1)S(1)} %pad_maximum_fusion.12.refs_0_), channel_id=1, source_target_pairs={{0,3},{4,7},{1,0},{5,4},{2,1},{6,5},{3,2},{7,6},{8,11},{12,15},{9,... | collective-permute-start | bytes 1179656 | tf_op jit(solution)/shard_map/ppermute | solution.py:79
  130.8 46.1 %collective-permute-start.34 = (bf16[2,2,208,128]{3,2,1,0:T(8,128)(2,1)}, bf16[2,2,208,128]{3,2,1,0:T(8,128)(2,1)S(1)}, u32[]{:S(2)}, u32[]{:S(2)}) collective-permute-start(bf16[2,2,208,128]{3,2,1,0:T(8,128)(2,1)} %bitcast.477), channel_id=1, source_target_pairs={{0,2},{4,6},{1,3},{5,7},{2,0},{6,4},{3,1},{7,5},{8,10},{12,14},{9,... | collective-permute-start | bytes 638984 | tf_op jit(solution)/shard_map/ppermute | solution.py:79
  134.4 42.9 %collective-permute-start.35 = (bf16[2,2,208,128]{3,2,1,0:T(8,128)(2,1)}, bf16[2,2,208,128]{3,2,1,0:T(8,128)(2,1)S(1)}, u32[]{:S(2)}, u32[]{:S(2)}) collective-permute-start(bf16[2,2,208,128]{3,2,1,0:T(8,128)(2,1)} %bitcast.476), channel_id=1, source_target_pairs={{0,3},{4,7},{1,0},{5,4},{2,1},{6,5},{3,2},{7,6},{8,11},{12,15},{9,... | collective-permute-start | bytes 638984 | tf_op jit(solution)/shard_map/ppermute | solution.py:79
  176.8 26.9 %collective-permute-start.25 = (bf16[256,768]{1,0:T(8,128)(2,1)}, bf16[256,768]{1,0:T(8,128)(2,1)}, u32[]{:S(2)}, u32[]{:S(2)}) collective-permute-start(bf16[256,768]{1,0:T(8,128)(2,1)} %get-tuple-element.107.refs_0_), channel_id=1, source_target_pairs={{0,8},{4,12},{1,9},{5,13},{2,10},{6,14},{3,11},{7,15},{8,0},{12,4}... | collective-permute-start | bytes 1179656 | tf_op jit(solution)/shard_map/ppermute | solution.py:79
  177.3 31.4 %collective-permute-start.29 = (bf16[256,1024]{1,0:T(8,128)(2,1)}, bf16[256,1024]{1,0:T(8,128)(2,1)}, u32[]{:S(2)}, u32[]{:S(2)}) collective-permute-start(bf16[256,1024]{1,0:T(8,128)(2,1)} %get-tuple-element.108.refs_4_), channel_id=1, source_target_pairs={{0,16},{4,20},{1,17},{5,21},{2,18},{6,22},{3,19},{7,23},{8,24},{12... | collective-permute-start | bytes 1572872 | tf_op jit(solution)/shard_map/ppermute | solution.py:79
  197.2 19.3 %collective-permute-start.17 = (bf16[1536,128]{1,0:T(8,128)(2,1)}, bf16[1536,128]{1,0:T(8,128)(2,1)}, u32[]{:S(2)}, u32[]{:S(2)}) collective-permute-start(bf16[1536,128]{1,0:T(8,128)(2,1)} %get-tuple-element.96.refs_0_), channel_id=1, source_target_pairs={{0,16},{4,20},{1,17},{5,21},{2,18},{6,22},{3,19},{7,23},{8,24},{12... | collective-permute-start | bytes 1179656 | tf_op jit(solution)/shard_map/ppermute | solution.py:79
  208.8 32.3 %collective-permute-start.19 = (bf16[1536,128]{1,0:T(8,128)(2,1)}, bf16[1536,128]{1,0:T(8,128)(2,1)}, u32[]{:S(2)}, u32[]{:S(2)}) collective-permute-start(bf16[1536,128]{1,0:T(8,128)(2,1)} %get-tuple-element.97.refs_4_), channel_id=1, source_target_pairs={{0,8},{4,12},{1,9},{5,13},{2,10},{6,14},{3,11},{7,15},{8,0},{12,4}... | collective-permute-start | bytes 1179656 | tf_op jit(solution)/shard_map/ppermute | solution.py:79
  209.4 33.4 %collective-permute-start.18 = (bf16[1536,128]{1,0:T(8,128)(2,1)}, bf16[1536,128]{1,0:T(8,128)(2,1)}, u32[]{:S(2)}, u32[]{:S(2)}) collective-permute-start(bf16[1536,128]{1,0:T(8,128)(2,1)} %collective-permute-done.16.refs_1_), channel_id=1, source_target_pairs={{0,16},{4,20},{1,17},{5,21},{2,18},{6,22},{3,19},{7,23},{8,24},{12... | collective-permute-start | bytes 1179656 | tf_op jit(solution)/shard_map/ppermute | solution.py:79
  210.9 32.4 %collective-permute-start.21 = (bf16[1536,128]{1,0:T(8,128)(2,1)}, bf16[1536,128]{1,0:T(8,128)(2,1)}, u32[]{:S(2)}, u32[]{:S(2)}) collective-permute-start(bf16[1536,128]{1,0:T(8,128)(2,1)} %collective-permute-done.20.refs_6_), channel_id=1, source_target_pairs={{0,8},{4,12},{1,9},{5,13},{2,10},{6,14},{3,11},{7,15},{8,0},{12,4}... | collective-permute-start | bytes 1179656 | tf_op jit(solution)/shard_map/ppermute | solution.py:79
  229.0 57.1 %collective-permute-start.28 = (bf16[256,1024]{1,0:T(8,128)(2,1)S(1)}, bf16[256,1024]{1,0:T(8,128)(2,1)S(1)}, u32[]{:S(2)}, u32[]{:S(2)}) collective-permute-start(bf16[256,1024]{1,0:T(8,128)(2,1)S(1)} %copy-done.79), channel_id=1, source_target_pairs={{0,8},{4,12},{1,9},{5,13},{2,10},{6,14},{3,11},{7,15},{8,0},{12,4}... | collective-permute-start | bytes 1572872 | tf_op jit(solution)/shard_map/ppermute | solution.py:79
  229.6 56.6 %collective-permute-start.30 = (bf16[256,1024]{1,0:T(8,128)(2,1)}, bf16[256,1024]{1,0:T(8,128)(2,1)}, u32[]{:S(2)}, u32[]{:S(2)}) collective-permute-start(bf16[256,1024]{1,0:T(8,128)(2,1)} %collective-permute-done.29.refs_6_), channel_id=1, source_target_pairs={{0,8},{4,12},{1,9},{5,13},{2,10},{6,14},{3,11},{7,15},{8,0},{12,4}... | collective-permute-start | bytes 1572872 | tf_op jit(solution)/shard_map/ppermute | solution.py:79
  241.2 22.7 %collective-permute-start.26 = (bf16[256,768]{1,0:T(8,128)(2,1)S(1)}, bf16[256,768]{1,0:T(8,128)(2,1)S(1)}, u32[]{:S(2)}, u32[]{:S(2)}) collective-permute-start(bf16[256,768]{1,0:T(8,128)(2,1)S(1)} %copy-done.90), channel_id=1, source_target_pairs={{0,16},{4,20},{1,17},{5,21},{2,18},{6,22},{3,19},{7,23},{8,24},{12... | collective-permute-start | bytes 1179656 | tf_op jit(solution)/shard_map/ppermute | solution.py:79
  242.8 73.3 %collective-permute-start.49 = (bf16[256,1536]{1,0:T(8,128)(2,1)}, bf16[256,1536]{1,0:T(8,128)(2,1)}, u32[]{:S(2)}, u32[]{:S(2)}) collective-permute-start(bf16[256,1536]{1,0:T(8,128)(2,1)} %get-tuple-element.123.refs_0_), channel_id=1, source_target_pairs={{0,8},{4,12},{1,9},{5,13},{2,10},{6,14},{3,11},{7,15},{8,0},{12,4}... | collective-permute-start | bytes 2359304 | tf_op jit(solution)/shard_map/ppermute | solution.py:79
  243.3 42.9 %collective-permute-start.27 = (bf16[256,768]{1,0:T(8,128)(2,1)}, bf16[256,768]{1,0:T(8,128)(2,1)S(1)}, u32[]{:S(2)}, u32[]{:S(2)}) collective-permute-start(bf16[256,768]{1,0:T(8,128)(2,1)} %collective-permute-done.25.refs_1_), channel_id=1, source_target_pairs={{0,16},{4,20},{1,17},{5,21},{2,18},{6,22},{3,19},{7,23},{8,24},{12... | collective-permute-start | bytes 1179656 | tf_op jit(solution)/shard_map/ppermute | solution.py:79
  263.8 52.3 %collective-permute-start.53 = (bf16[256,1536]{1,0:T(8,128)(2,1)}, bf16[256,1536]{1,0:T(8,128)(2,1)}, u32[]{:S(2)}, u32[]{:S(2)}) collective-permute-start(bf16[256,1536]{1,0:T(8,128)(2,1)} %get-tuple-element.124.refs_4_), channel_id=1, source_target_pairs={{0,16},{4,20},{1,17},{5,21},{2,18},{6,22},{3,19},{7,23},{8,24},{12... | collective-permute-start | bytes 2359304 | tf_op jit(solution)/shard_map/ppermute | solution.py:79
  316.0 20.6 %collective-permute-start.50 = (bf16[256,1536]{1,0:T(8,128)(2,1)}, bf16[256,1536]{1,0:T(8,128)(2,1)S(1)}, u32[]{:S(2)}, u32[]{:S(2)}) collective-permute-start(bf16[256,1536]{1,0:T(8,128)(2,1)} %get-tuple-element.123.refs_0_), channel_id=1, source_target_pairs={{0,16},{4,20},{1,17},{5,21},{2,18},{6,22},{3,19},{7,23},{8,24},{12... | collective-permute-start | bytes 2359304 | tf_op jit(solution)/shard_map/ppermute | solution.py:79
  316.1 20.6 %collective-permute-start.52 = (bf16[256,1536]{1,0:T(8,128)(2,1)}, bf16[256,1536]{1,0:T(8,128)(2,1)S(1)}, u32[]{:S(2)}, u32[]{:S(2)}) collective-permute-start(bf16[256,1536]{1,0:T(8,128)(2,1)} %get-tuple-element.124.refs_4_), channel_id=1, source_target_pairs={{0,8},{4,12},{1,9},{5,13},{2,10},{6,14},{3,11},{7,15},{8,0},{12,4}... | collective-permute-start | bytes 2359304 | tf_op jit(solution)/shard_map/ppermute | solution.py:79
  316.1 36.4 %collective-permute-start.51 = (bf16[256,1536]{1,0:T(8,128)(2,1)}, bf16[256,1536]{1,0:T(8,128)(2,1)S(1)}, u32[]{:S(2)}, u32[]{:S(2)}) collective-permute-start(bf16[256,1536]{1,0:T(8,128)(2,1)} %collective-permute-done.49.refs_1_), channel_id=1, source_target_pairs={{0,16},{4,20},{1,17},{5,21},{2,18},{6,22},{3,19},{7,23},{8,24},{12... | collective-permute-start | bytes 2359304 | tf_op jit(solution)/shard_map/ppermute | solution.py:79
  319.0 33.6 %collective-permute-start.54 = (bf16[256,1536]{1,0:T(8,128)(2,1)}, bf16[256,1536]{1,0:T(8,128)(2,1)S(1)}, u32[]{:S(2)}, u32[]{:S(2)}) collective-permute-start(bf16[256,1536]{1,0:T(8,128)(2,1)} %collective-permute-done.53.refs_6_), channel_id=1, source_target_pairs={{0,8},{4,12},{1,9},{5,13},{2,10},{6,14},{3,11},{7,15},{8,0},{12,4}... | collective-permute-start | bytes 2359304 | tf_op jit(solution)/shard_map/ppermute | solution.py:79
  324.5 36.4 %collective-permute-start.44 = (bf16[384,1024]{1,0:T(8,128)(2,1)}, bf16[384,1024]{1,0:T(8,128)(2,1)}, u32[]{:S(2)}, u32[]{:S(2)}) collective-permute-start(bf16[384,1024]{1,0:T(8,128)(2,1)} %multiply_convert_fusion.6), channel_id=1, source_target_pairs={{0,4},{4,0},{1,5},{5,1},{2,6},{6,2},{3,7},{7,3},{8,12},{12,8},{9,1... | collective-permute-start | bytes 2359304 | tf_op jit(solution)/shard_map/ppermute | solution.py:79
  412.7 213.0 %reduce-scatter.5.cloned.1.call-start = ((), (), s32[]{:S(2)}) async-start(), calls=%async_computation.4 | async-start | bytes 7864320 | tf_op jit(solution)/shard_map/reduce_scatter | solution.py:184
  430.8 292.1 %reduce-scatter.9.cloned.1.call-start = ((), (), s32[]{:S(2)}) async-start(), calls=%async_computation.6 | async-start | bytes 1146880 | tf_op jit(solution)/shard_map/reduce_scatter | solution.py:214
  444.8 54.4 %collective-permute-start.68 = (bf16[2,2,192,128]{3,2,1,0:T(8,128)(2,1)}, bf16[2,2,192,128]{3,2,1,0:T(8,128)(2,1)}, u32[]{:S(2)}, u32[]{:S(2)}) collective-permute-start(bf16[2,2,192,128]{3,2,1,0:T(8,128)(2,1)} %bitcast.482), channel_id=1, source_target_pairs={{0,1},{4,5},{1,2},{5,6},{2,3},{6,7},{3,0},{7,4},{8,9},{12,13},{9,1... | collective-permute-start | bytes 589832 | tf_op jit(solution)/shard_map/ppermute | solution.py:79
  447.0 52.3 %collective-permute-start.69 = (bf16[2,2,192,128]{3,2,1,0:T(8,128)(2,1)}, bf16[2,2,192,128]{3,2,1,0:T(8,128)(2,1)}, u32[]{:S(2)}, u32[]{:S(2)}) collective-permute-start(bf16[2,2,192,128]{3,2,1,0:T(8,128)(2,1)} %bitcast.481), channel_id=1, source_target_pairs={{0,2},{4,6},{1,3},{5,7},{2,0},{6,4},{3,1},{7,5},{8,10},{12,14},{9,... | collective-permute-start | bytes 589832 | tf_op jit(solution)/shard_map/ppermute | solution.py:79
  447.0 52.3 %collective-permute-start.70 = (bf16[2,2,192,128]{3,2,1,0:T(8,128)(2,1)}, bf16[2,2,192,128]{3,2,1,0:T(8,128)(2,1)}, u32[]{:S(2)}, u32[]{:S(2)}) collective-permute-start(bf16[2,2,192,128]{3,2,1,0:T(8,128)(2,1)} %bitcast.480), channel_id=1, source_target_pairs={{0,3},{4,7},{1,0},{5,4},{2,1},{6,5},{3,2},{7,6},{8,11},{12,15},{9,... | collective-permute-start | bytes 589832 | tf_op jit(solution)/shard_map/ppermute | solution.py:79
  482.2 110.2 %collective-permute-start.62 = (bf16[2,2,4,192,128]{4,3,2,1,0:T(8,128)(2,1)}, bf16[2,2,4,192,128]{4,3,2,1,0:T(8,128)(2,1)}, u32[]{:S(2)}, u32[]{:S(2)}) collective-permute-start(bf16[2,2,4,192,128]{4,3,2,1,0:T(8,128)(2,1)} %dynamic-slice_bitcast_fusion.1), channel_id=1, source_target_pairs={{0,8},{4,12},{1,9},{5,13},{2,10},{6,14},{3,11},{7,15},{8,0},{12,4}... | collective-permute-start | bytes 2359304 | tf_op jit(solution)/shard_map/ppermute | solution.py:79
  502.2 34.6 %collective-permute-start.71 = (bf16[2,208,128]{2,1,0:T(8,128)(2,1)}, bf16[2,208,128]{2,1,0:T(8,128)(2,1)S(1)}, u32[]{:S(2)}, u32[]{:S(2)}) collective-permute-start(bf16[2,208,128]{2,1,0:T(8,128)(2,1)} %scan.6), channel_id=1, source_target_pairs={{0,8},{1,9},{2,10},{3,11},{4,12},{5,13},{6,14},{7,15},{8,16},{9,17... | collective-permute-start | bytes 319496 | tf_op jit(solution)/shard_map/ppermute | solution.py:848
  502.3 34.5 %collective-permute-start.72 = (bf16[2,208,128]{2,1,0:T(8,128)(2,1)}, bf16[2,208,128]{2,1,0:T(8,128)(2,1)S(1)}, u32[]{:S(2)}, u32[]{:S(2)}) collective-permute-start(bf16[2,208,128]{2,1,0:T(8,128)(2,1)} %scan.6), channel_id=1, source_target_pairs={{0,16},{1,17},{2,18},{3,19},{4,20},{5,21},{6,22},{7,23},{8,24},{9,... | collective-permute-start | bytes 319496 | tf_op jit(solution)/shard_map/ppermute | solution.py:848
  518.2 18.6 %collective-permute-start.73 = (bf16[2,208,128]{2,1,0:T(8,128)(2,1)}, bf16[2,208,128]{2,1,0:T(8,128)(2,1)S(1)}, u32[]{:S(2)}, u32[]{:S(2)}) collective-permute-start(bf16[2,208,128]{2,1,0:T(8,128)(2,1)} %scan.6), channel_id=1, source_target_pairs={{0,24},{1,25},{2,26},{3,27},{4,28},{5,29},{6,30},{7,31},{8,0},{9,1... | collective-permute-start | bytes 319496 | tf_op jit(solution)/shard_map/ppermute | solution.py:848
  520.1 66.7 %collective-permute-start.60 = (bf16[2,2,4,192,128]{4,3,2,1,0:T(8,128)(2,1)}, bf16[2,2,4,192,128]{4,3,2,1,0:T(8,128)(2,1)}, u32[]{:S(2)}, u32[]{:S(2)}) collective-permute-start(bf16[2,2,4,192,128]{4,3,2,1,0:T(8,128)(2,1)} %dynamic-slice_bitcast_fusion.2), channel_id=1, source_target_pairs={{0,16},{4,20},{1,17},{5,21},{2,18},{6,22},{3,19},{7,23},{8,24},{12... | collective-permute-start | bytes 2359304 | tf_op jit(solution)/shard_map/ppermute | solution.py:79
  635.8 23.0 %collective-permute-start.89 = (f32[3,12]{1,0:T(4,128)S(1)}, f32[3,12]{1,0:T(4,128)S(1)}, u32[]{:S(2)}, u32[]{:S(2)}) collective-permute-start(f32[3,12]{1,0:T(4,128)S(1)} %slice.628), channel_id=1, source_target_pairs={{0,1},{4,5},{1,0},{5,4},{2,3},{6,7},{3,2},{7,6},{8,9},{12,13},{9,8... | collective-permute-start | bytes 440 | tf_op jit(solution)/shard_map/ppermute | solution.py:263
  641.4 36.6 %collective-permute-start.80 = (bf16[2,2,4,32,768]{4,3,2,1,0:T(8,128)(2,1)}, bf16[2,2,4,32,768]{4,3,2,1,0:T(8,128)(2,1)}, u32[]{:S(2)}, u32[]{:S(2)}) collective-permute-start(bf16[2,2,4,32,768]{4,3,2,1,0:T(8,128)(2,1)} %fusion.41), channel_id=1, source_target_pairs={{0,16},{4,20},{1,17},{5,21},{2,18},{6,22},{3,19},{7,23},{8,24},{12... | collective-permute-start | bytes 2359304 | tf_op jit(solution)/shard_map/ppermute | solution.py:79
  648.3 92.1 %reduce-scatter.11.cloned.1.call-start = ((), (), s32[]{:S(2)}) async-start(), calls=%async_computation.7 | async-start | bytes 1966080 | tf_op jit(solution)/shard_map/reduce_scatter | solution.py:214
  655.3 19.3 %collective-permute-start.78 = (bf16[400,1024]{1,0:T(8,128)(2,1)}, bf16[400,1024]{1,0:T(8,128)(2,1)}, u32[]{:S(2)}, u32[]{:S(2)}) collective-permute-start(bf16[400,1024]{1,0:T(8,128)(2,1)} %slice.959), channel_id=1, source_target_pairs={{0,4},{4,0},{1,5},{5,1},{2,6},{6,2},{3,7},{7,3},{8,12},{12,8},{9,1... | collective-permute-start | bytes 2457608 | tf_op jit(solution)/shard_map/ppermute | solution.py:79
  689.8 18.8 %collective-permute-start.82 = (bf16[2,2,4,32,640]{4,3,2,1,0:T(8,128)(2,1)S(1)}, bf16[2,2,4,32,640]{4,3,2,1,0:T(8,128)(2,1)S(1)}, u32[]{:S(2)}, u32[]{:S(2)}) collective-permute-start(bf16[2,2,4,32,640]{4,3,2,1,0:T(8,128)(2,1)S(1)} %fusion.46), channel_id=1, source_target_pairs={{0,8},{4,12},{1,9},{5,13},{2,10},{6,14},{3,11},{7,15},{8,0},{12,4}... | collective-permute-start | bytes 1966088 | tf_op jit(solution)/shard_map/ppermute | solution.py:79
  694.1 22.7 %collective-permute-start.81 = (bf16[2,4,32,768]{3,2,1,0:T(8,128)(2,1)S(1)}, bf16[2,4,32,768]{3,2,1,0:T(8,128)(2,1)S(1)}, u32[]{:S(2)}, u32[]{:S(2)}) collective-permute-start(bf16[2,4,32,768]{3,2,1,0:T(8,128)(2,1)S(1)} %fusion.52), channel_id=1, source_target_pairs={{0,8},{4,12},{1,9},{5,13},{2,10},{6,14},{3,11},{7,15},{8,0},{12,4}... | collective-permute-start | bytes 1179656 | tf_op jit(solution)/shard_map/ppermute | solution.py:79
  (186 other events, 1584.5 us)
Sparse Core Ops, SparseCore 0:
  412.9 46.6 reduce-scatter.6
  462.6 96.7 reduce-scatter.4
  648.5 24.6 reduce-scatter.8
  675.3 34.1 reduce-scatter.10

commit v3 on v2

--- a/solution.py
+++ b/solution.py
@@ -36,6 +36,14 @@
     return lax.dot_general(
         left, right, dims, precision=precision, preferred_element_type=F32
     )
+
+
+def tie(*values):
+    return lax.optimization_barrier(values)
+
+
+def cost(micros):
+    return pl.CostEstimate(flops=int(micros * 1.15e9), bytes_accessed=0, transcendentals=0)
 
 
 class Place:
@@ -96,13 +104,19 @@
     def spread_z(self, x):
         return [x] + [self.shift(x, "z", k) for k in range(1, self.size["z"])]
 
-    def spread_plane(self, x, b_first):
-        found = {(0, 0): x}
-        for dim in ("b", "a") if b_first else ("a", "b"):
-            for key, value in list(found.items()):
-                for k in range(1, self.size[dim]):
-                    to = (key[0], k) if dim == "b" else (k, key[1])
-                    found[to] = self.shift(value, dim, k)
+    def plane_first(self, halves):
+        found = []
+        for index, half in enumerate(halves):
+            dim = "ab"[index % 2 == 0]
+            found.append([half] + [self.shift(half, dim, k) for k in range(1, self.size[dim])])
+        return found
+
+    def plane_second(self, halves):
+        found = []
+        for index, parts in enumerate(halves):
+            dim = "ba"[index % 2 == 0]
+            moves = range(1, self.size[dim])
+            found.append([parts] + [[self.shift(part, dim, k) for part in parts] for k in moves])
         return found
 
     def place_z(self, parts, halves):
@@ -131,18 +145,19 @@
                 to += size
         return moved(self, parts, outs, plan)
 
-    def gather_plane(self, halves, wanted):
-        rows = halves[0].shape[0]
-        near = [self.spread_plane(half, index % 2 == 0) for index, half in enumerate(halves)]
-        keys = sorted(near[0])
+    def plane_third(self, halves, wanted):
+        rows, dtype = halves[0][0][0].shape[0], halves[0][0][0].dtype
         na, nb = self.size["a"], self.size["b"]
+        keys = [(da, db) for da in range(na) for db in range(nb)]
         widths = {}
         for _, _, size, array, column in wanted:
             widths[array] = max(widths.get(array, 0), column + size)
         outs = [
-            jax.ShapeDtypeStruct((self.chips * rows, widths[k]), halves[0].dtype)
-            for k in range(len(widths))
+            jax.ShapeDtypeStruct((self.chips * rows, widths[k]), dtype) for k in range(len(widths))
         ]
+        sources = []
+        for index, half in enumerate(halves):
+            sources += [half[da][db] if index % 2 == 0 else half[db][da] for da, db in keys]
         plan = []
         for half, start, size, array, column in wanted:
             for index, (da, db) in enumerate(keys):
@@ -155,7 +170,7 @@
                     return pl.ds(chip * rows, rows), pl.ds(column, size)
 
                 plan.append((half * len(keys) + index, source, array, goal))
-        return moved(self, [n[key] for n in near for key in keys], outs, plan)
+        return moved(self, sources, outs, plan)
 
     def reduce_far(self, grads):
         cores = [[chip * CORES + c for chip in range(self.chips)] for c in range(CORES)]
@@ -181,9 +196,12 @@
 
                 plan.append((k, source, 0, goal))
         (flat,) = moved(self, [grad for grad, _ in grads], outs, plan)
-        flat = lax.psum_scatter(
-            flat, "ctx", scatter_dimension=0, tiled=True, axis_index_groups=cores
-        )
+
+        def start(flat):
+            return lax.psum_scatter(
+                flat, "ctx", scatter_dimension=0, tiled=True, axis_index_groups=cores
+            )
+
         share, deep = rows // groups, high // groups
 
         def finish(flat):
@@ -213,7 +231,7 @@
             (flat,) = moved(self, [flat], outs, plan)
             return lax.psum_scatter(flat, "sp", scatter_dimension=0, tiled=True)
 
-        return flat, finish
+        return flat, start, finish
 
     def reduce(self, x, dim, axis):
         n, v = self.size[dim], self.at[dim]
@@ -223,13 +241,13 @@
             total = total + self.shift(piece, dim, k).astype(F32)
         return total
 
-    def reduce_chips(self, grads, firsts):
-        left = []
-        for grad, b_first in zip(grads, firsts):
-            if b_first:
-                left.append(self.reduce(self.reduce(grad, "a", 0), "b", 0))
-            else:
-                left.append(self.reduce(self.reduce(grad, "b", 1), "a", 0))
+    def reduce_first(self, grad, b_first):
+        return self.reduce(grad, "a", 0) if b_first else self.reduce(grad, "b", 1)
+
+    def reduce_second(self, grad, b_first):
+        return self.reduce(grad, "b" if b_first else "a", 0)
+
+    def reduce_z(self, left):
         n, v = self.size["z"], self.at["z"]
 
         def cut(x, index):
@@ -247,20 +265,23 @@
                 start = stop
         return totals
 
-    def sum_all(self, x):
-        for dim in ("z", "b", "a"):
+    def sum_step(self, x, dim, step):
+        found = []
+        for a in range(self.size["a"]):
+            for b in range(self.size["b"]):
+                for z in range(self.size["z"]):
+                    for c in range(CORES):
+                        spot = {"a": a, "b": b, "z": z, "c": c}
+                        goal = dict(spot)
+                        goal[dim] = spot[dim] ^ step
+                        found.append((self.flat_of(**spot), self.flat_of(**goal)))
+        return x + lax.ppermute(x, AXES, found)
+
+    def sum_along(self, x, dims):
+        for dim in dims:
             step = 1
             while step < self.size[dim]:
-                found = []
-                for a in range(self.size["a"]):
-                    for b in range(self.size["b"]):
-                        for z in range(self.size["z"]):
-                            for c in range(CORES):
-                                spot = {"a": a, "b": b, "z": z, "c": c}
-                                goal = dict(spot)
-                                goal[dim] = spot[dim] ^ step
-                                found.append((self.flat_of(**spot), self.flat_of(**goal)))
-                x = x + lax.ppermute(x, AXES, found)
+                x = self.sum_step(x, dim, step)
                 step *= 2
         return x
 
@@ -399,11 +420,7 @@
             jax.ShapeDtypeStruct((slots, CORES, 1, columns), F32),
         ],
         compiler_params=pltpu.CompilerParams(vmem_limit_bytes=VMEM),
-        cost_estimate=pl.CostEstimate(
-            flops=2 * 2 * slots * CORES * columns * length * width // 2,
-            bytes_accessed=slots * length * width * 4,
-            transcendentals=slots * CORES * columns * length // 2,
-        ),
+        cost_estimate=cost(20),
         name="attend",
     )(places, lengths, queries, kv)
 
@@ -482,11 +499,7 @@
             jax.ShapeDtypeStruct(kv.shape, BF16),
         ],
         compiler_params=pltpu.CompilerParams(vmem_limit_bytes=VMEM),
-        cost_estimate=pl.CostEstimate(
-            flops=5 * 2 * slots * CORES * columns * length * width // 2,
-            bytes_accessed=slots * length * width * 6,
-            transcendentals=slots * CORES * columns * length // 2,
-        ),
+        cost_estimate=cost(25),
         name="attend_back",
     )(places, lengths, queries, kv, out, dout, lse)
 
@@ -684,7 +697,7 @@
     )
 
 
-def over_pieces(kernel, name, args, whole, outs, flops, at, scratch=()):
+def over_pieces(kernel, name, args, whole, outs, micros, at, scratch=()):
     pieces = args[0].shape[0]
 
     def spec(shape, split):
@@ -693,8 +706,6 @@
         return pl.BlockSpec(shape, lambda i: (0,) * len(shape))
 
     shapes = [(arg.shape, index not in whole) for index, arg in enumerate(args)]
-    nbytes = sum(arg.size * arg.dtype.itemsize for arg in args)
-    nbytes += sum(math.prod(shape) * dtype.dtype.itemsize for shape, dtype in outs)
     return pl.pallas_call(
         kernel,
         grid=(pieces,),
@@ -704,7 +715,7 @@
         out_shape=[jax.ShapeDtypeStruct(shape, dtype) for shape, dtype in outs],
         scratch_shapes=list(scratch),
         compiler_params=pltpu.CompilerParams(vmem_limit_bytes=VMEM),
-        cost_estimate=pl.CostEstimate(flops=flops, bytes_accessed=nbytes, transcendentals=0),
+        cost_estimate=cost(micros),
         name=name,
     )(*args, at)
 
@@ -803,12 +814,24 @@
     total_ref[0, rows:] = extra.astype(BF16)
 
 
-def carried(place, at, states, marks, fades, reverse):
+def carried(
+    place,
+    at,
+    states,
+    marks,
+    fades,
+    reverse,
+    before=lambda x: x,
+    between=lambda x: x,
+    after=lambda x: x,
+):
     groups, chips = place.size["z"], place.chips
     share = M_SHARE // groups
     rows = share * SHD
     slots = states[0].shape[1]
-    parts = [part if r == 0 else place.shift(part, "z", r) for r, part in enumerate(states)]
+    parts = before(
+        [part if r == 0 else place.shift(part, "z", r) for r, part in enumerate(states)]
+    )
     marks = parts if marks is None else marks
     block = [pl.BlockSpec((CORES, 1, part.shape[2], NS), lambda s, *_: (0, s, 0, 0)) for part in parts]
     mark = pl.BlockSpec((CORES, 1, EXTRA, NS), lambda s, *_: (0, s, rows // EXTRA, 0))
@@ -834,11 +857,7 @@
             ),
             out_shape=outs,
             compiler_params=pltpu.CompilerParams(vmem_limit_bytes=VMEM),
-            cost_estimate=pl.CostEstimate(
-                flops=4 * slots * CORES * groups * rows * NS,
-                bytes_accessed=4 * slots * CORES * groups * rows * NS,
-                transcendentals=0,
-            ),
+            cost_estimate=cost(3),
             name="scan",
         )(at, *parts, *marks, *args)
 
@@ -846,6 +865,7 @@
         False, [], [], jax.ShapeDtypeStruct((slots, rows + EXTRA, NS), BF16), total, []
     )
     totals = [lax.ppermute(leaving, AXES, place.chip_pairs(k)) for k in range(1, chips)]
+    totals = between(totals)
     fades = totals if fades is None else fades
     entering = call(
         True,
@@ -855,6 +875,7 @@
         [result] * groups,
         [pltpu.VMEM((groups, CORES, rows, NS), BF16)],
     )
+    entering = after(entering)
     found = [part if r == 0 else place.shift(part, "z", r) for r, part in enumerate(entering)]
     return [part.reshape(CORES * slots, rows, NS) for part in found], marks, fades
 
@@ -892,7 +913,6 @@
     q_cols, m_cols = Q_SHARE * HD, M_SHARE * SHD
     lin_cols = q_cols + 2 * HD
     c_cols = m_cols + NS
-    f_cols = m_cols // 2
     at = place.scalars
     shard_rows = attn_in_weight.shape[0]
     out_rows, mix_rows, ff_rows = (
@@ -932,10 +952,7 @@
     small = small.reshape(shard_rows, small_cols)
     small_at = M_SHARE
     ms_cols = -(-(small_at + small_cols) // LANES) * LANES
-    a_cols, b_cols = lin_cols + f_cols, c_cols - f_cols + ms_cols
-
-    def ff_columns(weight, half):
-        return weight.reshape(shard_rows, chips, CORES, -1)[:, :, half].reshape(shard_rows, -1)
+    a_cols, b_cols = lin_cols + ms_cols, c_cols
 
     def early_columns(half):
         return jnp.concatenate(
@@ -943,20 +960,14 @@
                 attn_in_weight[:, half * q_cols : (half + 1) * q_cols],
                 attn_in_weight[:, QH * HD + half * HD : QH * HD + (half + 1) * HD],
                 attn_in_weight[:, (QH + KVH + half) * HD : (QH + KVH + half + 1) * HD],
-                mixer_in_weight[:, half * m_cols : (half + 1) * m_cols],
-                mixer_in_weight[:, SH * SHD + half * NS : SH * SHD + (half + 1) * NS],
                 step_weight[:, half * M_SHARE : (half + 1) * M_SHARE],
                 small,
                 jnp.zeros((shard_rows, ms_cols - small_at - small_cols), BF16),
+                mixer_in_weight[:, half * m_cols : (half + 1) * m_cols],
+                mixer_in_weight[:, SH * SHD + half * NS : SH * SHD + (half + 1) * NS],
             ],
             axis=1,
         )
-
-    def zgate_columns(half):
-        return zgate_weight[:, half * m_cols : (half + 1) * m_cols]
-
-    def late_columns(half):
-        return jnp.concatenate([ff_columns(gate_weight, half), ff_columns(up_weight, half)], axis=1)
 
     def sorted_halves(columns):
         halves = (columns(0), columns(1))
@@ -965,22 +976,19 @@
         return jnp.concatenate([place.by_core(kept, got), place.by_core(got, kept)], axis=0)
 
     early = place.spread_z(sorted_halves(early_columns))
-    late_one = jnp.concatenate(
-        [
-            sorted_halves(zgate_columns),
-            jnp.concatenate([attn_out_weight, mixer_out_weight], axis=0),
-        ],
-        axis=1,
-    )
-    early, late_one = lax.optimization_barrier((early, late_one))
-    w_a, w_b = place.gather_plane(
-        place.place_z(early, [[(0, a_cols, 2)], [(a_cols, b_cols, 2)]]),
-        [(0, 0, a_cols, 0, 0), (1, 0, b_cols, 1, 0)],
-    )
-    late_one = place.spread_z(late_one)
-
-    tail_at = c_cols - f_cols
-    vectors = w_b[:, tail_at + small_at : tail_at + small_at + small_cols]
+
+    def side_by_side(weight):
+        return weight.reshape(2, shard_rows, width).transpose(1, 0, 2).reshape(shard_rows, 2 * width)
+
+    out_weights = jnp.concatenate([attn_out_weight, mixer_out_weight], axis=0)
+    middle = jnp.concatenate([zgate_weight, side_by_side(out_weights)], axis=1)
+    middle = lax.all_gather(middle, AXES, axis=0, tiled=True)
+    ff_all = jnp.concatenate([gate_weight, up_weight, side_by_side(down_weight)], axis=1)
+    early = place.place_z(early, [[(0, a_cols, 2)], [(a_cols, b_cols, 2)]])
+    early = place.plane_second(place.plane_first(early))
+    w_a, w_b = place.plane_third(early, [(0, 0, a_cols, 0, 0), (1, 0, b_cols, 1, 0)])
+    tail_at = lin_cols
+    vectors = w_a[:, tail_at + small_at : tail_at + small_at + small_cols]
     vectors = vectors.reshape(devices, -1).astype(F32)
     sizes = [input_gain.shape[0], mixer_gain.shape[0], post_gain.shape[0], conv_bias.shape[0]]
     ends = [sum(sizes[: k + 1]) for k in range(4)]
@@ -1017,43 +1025,48 @@
         return value.reshape(CORES, slots, piece + HALO, -1)[:, :, HALO:]
 
     linear = body_rows(mm(normed, w_a[:, :lin_cols]))
-    mixed_step = mm(normed, w_b).astype(BF16)
-    mixed = jnp.concatenate(
-        [mm(normed, w_a[:, lin_cols:]).astype(BF16), mixed_step[:, :tail_at]], axis=-1
-    ).reshape(CORES, slots, piece + HALO, c_cols)
-    step_raw = body_rows(mixed_step[:, tail_at : tail_at + M_SHARE]).astype(F32)
-
-    late_one, mixed = lax.optimization_barrier((late_one, mixed))
-    w_z, w_out = place.gather_plane(
-        place.place_z(late_one, [[(0, m_cols, 2)], [(m_cols, width, 1)]]),
-        [(0, 0, m_cols, 0, 0), (1, 0, width, 1, 0)],
-    )
-    late_two = jnp.concatenate([sorted_halves(late_columns), down_weight], axis=1)
-    late_two, late_one = lax.optimization_barrier((late_two, late_one))
-    late_two = place.spread_z(late_two)
-    w_out = w_out.reshape(2, chips // 2, groups, out_rows + mix_rows, width)
-    kept = lax.dynamic_index_in_dim(w_out, core, 0, False)
-    got = place.swap(lax.dynamic_index_in_dim(w_out, 1 - core, 0, False))
-    w_out = jnp.stack([place.by_core(kept, got), place.by_core(got, kept)], 1)
-    w_attn_out = w_out[..., :out_rows, :].reshape(q_cols, width)
-    w_mixer_out = w_out[..., out_rows:, :].reshape(m_cols, width)
-    half = width // 2
-    w_gate, w_up, w_down = place.gather_plane(
-        place.place_z(
-            late_two,
+    mixed = mm(normed, w_b).astype(BF16).reshape(CORES, slots, piece + HALO, c_cols)
+    step_raw = mm(normed, w_a[:, tail_at:]).astype(BF16)
+    step_raw = body_rows(step_raw[:, :M_SHARE]).astype(F32)
+
+    def rows_plan(source, start, pieces_of):
+        found = []
+        for device in range(devices // 2):
+            for first, count, output, to, pitch in pieces_of:
+                side, row = divmod(first, shard_rows)
+
+                def where(at, device=device, side=side, row=row, count=count):
+                    first = (at[3] * (devices // 2) + device) * shard_rows + row
+                    return pl.ds(first, count), pl.ds(start + side * width, width)
+
+                def goal(at, device=device, to=to, pitch=pitch, count=count):
+                    return pl.ds(device * pitch + to, count), pl.ds(0, width)
+
+                found.append((source, where, output, goal))
+        return found
+
+    def columns_plan(source, start, size, output):
+        def where(at):
+            return pl.ds(0, width), pl.ds(pl.multiple_of(start + at[3] * size, LANES), size)
+
+        return [(source, where, output, lambda at: (pl.ds(0, width), pl.ds(0, size)))]
+
+    low = jax.ShapeDtypeStruct
+    w_z, w_attn_out, w_mixer_out = moved(
+        place,
+        [middle],
+        [low((width, m_cols), BF16), low((q_cols, width), BF16), low((m_cols, width), BF16)],
+        columns_plan(0, 0, m_cols, 0)
+        + rows_plan(
+            0,
+            2 * m_cols,
             [
-                [(0, ff_half, 2), (2 * ff_half, half, 1)],
-                [(ff_half, ff_half, 2), (2 * ff_half + half, half, 1)],
+                (0, out_rows, 1, 0, out_rows),
+                (out_rows, shard_rows - out_rows, 2, 0, mix_rows),
+                (shard_rows, shard_rows, 2, shard_rows - out_rows, mix_rows),
             ],
         ),
-        [
-            (0, 0, ff_half, 0, 0),
-            (1, 0, ff_half, 1, 0),
-            (0, ff_half, half, 2, 0),
-            (1, ff_half, half, 2, half),
-        ],
-    )
-
+    )
     cos_part, sin_part = rotary_tables(positions, HD)
     cos_part, sin_part = cos_part[:, None, :, None], sin_part[:, None, :, None]
     queries = rotate(
@@ -1080,8 +1093,7 @@
                 plan.append((r, source, s, goal))
     kv_size = jax.ShapeDtypeStruct((CORES * groups * piece, 2 * HD), BF16)
     kv = moved(place, kv_parts, [kv_size] * slots, plan)
-    kv = place.gather_plane(kv, [(s, 0, 2 * HD, s, 0) for s in range(slots)])
-
+    kv = place.plane_first(kv)
     def by_heads(value, before, after):
         value = jnp.transpose(value, (1, 0, 3, 2, 4)).reshape(slots, CORES, Q_SHARE * piece, HD)
         return jnp.pad(value, ((0, 0), (0, 0), (0, 0), (before, after)))
@@ -1092,14 +1104,6 @@
 
     scale = HD ** (-0.5)
     queries = by_heads(queries * jnp.asarray(scale, BF16), 0, HD)
-    heads_out, lse = zip(
-        *[
-            attend(pieces_at, lengths[s : s + 1], queries[s : s + 1], kv[s][None], piece)
-            for s in range(slots)
-        ]
-    )
-    attended = from_heads(jnp.concatenate(heads_out)[..., HD:]).reshape(rows_all, q_cols)
-
     pre = shift
     for tap in range(KC):
         first = HALO - KC + 1 + tap
@@ -1118,7 +1122,6 @@
     bias_col, rate_col = bias_row[0, :16, None], rate_row[0, :16, None]
     skip_row = jnp.repeat(skip, SHD)[None]
     pieces = CORES * slots
-    state_flops = 2 * pieces * piece * m_cols * (piece + 2 * NS)
     chunk_args = [
         features, inject, readout, raw, raw_t, bias_row, bias_col, rate_row, rate_col, skip_row,
     ]
@@ -1135,19 +1138,65 @@
             ((pieces, piece, LANES), F32),
             *[((pieces, share_rows + EXTRA, NS), BF16)] * groups,
         ],
-        state_flops,
+        9,
         at,
         [held_more],
     )
     local = [part.reshape(CORES, slots, share_rows + EXTRA, NS) for part in local]
-    state_in, marks, fades = carried(place, at, local, None, None, False)
+    held_back = {"kv": kv}
+
+    def before_states(parts):
+        parts, held_back["kv"], columns = tie(parts, held_back["kv"], ff_all)
+        held_back["ff"] = lax.all_gather(columns, AXES, axis=0, tiled=True)
+        held_back["kv"] = place.plane_second(held_back["kv"])
+        return parts
+
+    def between_states(totals):
+        totals, held_back["kv"] = tie(totals, held_back["kv"])
+        return totals
+
+    def after_states(entering):
+        entering, held_back["queries"] = tie(entering, queries)
+        return entering
+
+    state_in, marks, fades = carried(
+        place, at, local, None, None, False, before_states, between_states, after_states
+    )
+    queries = held_back["queries"]
+    kv = place.plane_third(held_back["kv"], [(s, 0, 2 * HD, s, 0) for s in range(slots)])
+    ff_whole = held_back["ff"]
+    w_gate, w_up, w_down = moved(
+        place,
+        [ff_whole],
+        [low((width, ff_half), BF16), low((width, ff_half), BF16), low((ff_half, width), BF16)],
+        columns_plan(0, 0, ff_half, 0)
+        + columns_plan(0, 2 * ff_half, ff_half, 1)
+        + rows_plan(
+            0,
+            4 * ff_half,
+            [
+                (0, shard_rows, 2, 0, ff_rows),
+                (shard_rows, shard_rows, 2, shard_rows, ff_rows),
+            ],
+        ),
+    )
+
+    heads_out, lse = zip(
+        *[
+            attend(pieces_at, lengths[s : s + 1], queries[s : s + 1], kv[s][None], piece)
+            for s in range(slots)
+        ]
+    )
+    attended = from_heads(jnp.concatenate(heads_out)[..., HD:]).reshape(rows_all, q_cols)
+
+    attended, state_in = tie(attended, state_in)
     (ssd,) = over_pieces(
         carry_kernel,
         "carry",
         [within, readout, logs, *state_in],
         (),
         [((pieces, piece, m_cols), BF16)],
-        2 * pieces * piece * m_cols * NS,
+        5,
         at,
         [held],
     )
@@ -1182,19 +1231,13 @@
     dgate = (dhidden * up_lin * gate_act_slope).astype(BF16)
     dup = (dhidden * gate_act).astype(BF16)
 
-    def by_parity(grad):
-        return grad.reshape(na, nb, 1, groups, -1, grad.shape[-1])
-
-    def by_columns(grad):
-        return grad.reshape(na, nb, CORES, groups, shard_rows, grad.shape[-1])
-
-    ff_grads, ff_finish = place.reduce_far(
-        [
-            (mm(post, dgate, TN).astype(BF16), 2),
-            (mm(post, dup, TN).astype(BF16), 2),
-            (mm(hidden, dy, TN).astype(BF16), 1),
-        ]
-    )
+    def own_parity(grad):
+        grad = grad.astype(BF16).reshape(chips // 2, CORES, -1, width)
+        kept = lax.dynamic_index_in_dim(grad, core, 1, False)
+        got = place.swap(lax.dynamic_index_in_dim(grad, 1 - core, 1, False))
+        grad = jnp.concatenate([place.by_core(kept, got), place.by_core(got, kept)], axis=0)
+        return grad.reshape(-1, width)
+
     dpost = own_sum(mm(dgate, w_gate, NT) + mm(dup, w_up, NT))
     dresidual = dy_own.reshape(-1, width) + rms_back(residual, scale_post, gain_post, dpost)
     grad_post_gain = jnp.sum(dpost * residual * scale_post, axis=0)
@@ -1202,17 +1245,6 @@
 
     dattended = mm(dmix, w_attn_out, NT).astype(BF16)
     dgated = mm(dmix, w_mixer_out, NT).reshape(CORES, slots, piece, m_cols)
-    grad_outs = jnp.concatenate(
-        [
-            mm(attended, dmix, TN).reshape(chips // 2, CORES, groups, out_rows, width),
-            mm(gated, dmix, TN).reshape(chips // 2, CORES, groups, mix_rows, width),
-        ],
-        axis=3,
-    )
-    grad_outs = grad_outs.astype(BF16)
-    kept = lax.dynamic_index_in_dim(grad_outs, core, 1, False)
-    got = place.swap(lax.dynamic_index_in_dim(grad_outs, 1 - core, 1, False))
-    grad_outs = jnp.concatenate([place.by_core(kept, got), place.by_core(got, kept)], axis=0)
     scaled = dgated * gain_mixer
     inner = jnp.sum(scaled * gated_raw, axis=-1)
     inner = (inner + place.swap(inner)[::-1])[..., None] / (SH * SHD)
@@ -1226,13 +1258,6 @@
         return jnp.pad(value, ((0, 0), (0, 0), (HALO, 0), (0, 0)))
 
     dzgate = halo_rows(dzgate).reshape(rows_halo, m_cols)
-    mid_grads, mid_finish = place.reduce_far(
-        [
-            (grad_outs.reshape(-1, width), 1),
-            (mm(normed, dzgate, TN).astype(BF16), 2),
-        ]
-    )
-    dnormed = mm(dzgate, w_z, NT)
 
     direct = over_pieces(
         direct_kernel,
@@ -1240,13 +1265,55 @@
         [dssd, readout, logs],
         (),
         [((pieces, share_rows, NS), BF16)] * groups,
-        2 * pieces * piece * m_cols * NS,
+        5,
         at,
         [held],
     )
     direct = [part.reshape(CORES, slots, share_rows, NS) for part in direct]
-    dattended, direct = lax.optimization_barrier((dattended, direct))
-    later, _, _ = carried(place, at, direct, marks, fades, True)
+    dgate, dup, hidden, direct = tie(dgate, dup, hidden, direct)
+    ff_grads, ff_start, ff_finish = place.reduce_far(
+        [
+            (mm(post, dgate, TN).astype(BF16), 2),
+            (mm(post, dup, TN).astype(BF16), 2),
+            (own_parity(mm(hidden, dy, TN)), 1),
+        ]
+    )
+    out_side = {}
+
+    def before_scan(parts):
+        parts, flat = tie(parts, ff_grads)
+        out_side["ff"] = ff_start(flat)
+        return parts
+
+    def between_scans(totals):
+        totals, out_side["dz"], dmix_late = tie(totals, dzgate, dmix)
+        grad_outs = jnp.concatenate(
+            [
+                mm(attended, dmix_late, TN).astype(BF16).reshape(devices // 2, out_rows, width),
+                mm(gated, dmix_late, TN).astype(BF16).reshape(devices // 2, mix_rows, width),
+            ],
+            axis=1,
+        )
+        mid_grads, mid_start, out_side["finish"] = place.reduce_far(
+            [
+                (own_parity(grad_outs), 1),
+                (mm(normed, out_side["dz"], TN).astype(BF16), 2),
+            ]
+        )
+        totals, mid_grads = tie(totals, mid_grads)
+        out_side["mid"] = mid_start(mid_grads)
+        return totals
+
+    def after_scans(entering):
+        entering, out_side["dattended"] = tie(entering, dattended)
+        return entering
+
+    later, _, _ = carried(
+        place, at, direct, marks, fades, True, before_scan, between_scans, after_scans
+    )
+    ff_grads, mid_grads, mid_finish = out_side["ff"], out_side["mid"], out_side["finish"]
+    dattended = out_side["dattended"]
+    dnormed = mm(out_side["dz"], w_z, NT)
 
     dout = by_heads(
         dattended.reshape(CORES, slots, piece, Q_SHARE, HD), HD, 0
@@ -1267,12 +1334,11 @@
         ]
     )
     dqueries = jnp.concatenate(dqueries)
-    dkv_own = place.reduce_chips(
-        [dkv[s].reshape(na, nb, CORES, groups, piece, 2 * HD) for s in range(slots)],
-        [s % 2 == 0 for s in range(slots)],
-    )
-    dkv_own = jnp.stack([part.reshape(CORES, piece, 2 * HD) for part in dkv_own], axis=1)
-    dkv_own = place.by_core(dkv_own, dkv_own[::-1])
+    dkv, later = tie(dkv, later)
+    dkv = [
+        place.reduce_first(dkv[s].reshape(na, nb, CORES, groups, piece, 2 * HD), s % 2 == 0)
+        for s in range(slots)
+    ]
 
     dfeatures, dinject, dreadout, draw, sums = over_pieces(
         chunk_back_kernel,
@@ -1286,12 +1352,12 @@
             ((pieces, piece, LANES), F32),
             ((pieces, 8, LANES), F32),
         ],
-        4 * state_flops,
+        28,
         at,
         [pltpu.VMEM((LANES, 2 * LANES), F32), pltpu.VMEM((piece, LANES), F32), held, held],
     )
-    ff_grads, mid_grads, dfeatures = lax.optimization_barrier((ff_grads, mid_grads, dfeatures))
-    ff_grads, mid_grads = ff_finish(ff_grads), mid_finish(mid_grads)
+    ff_grads, dkv, dfeatures = tie(ff_grads, dkv, dfeatures)
+    dkv = [place.reduce_second(dkv[s], s % 2 == 0) for s in range(slots)]
     dinject = dinject.reshape(CORES, slots, piece, NS)
     dreadout = dreadout.reshape(CORES, slots, piece, NS)
     dshared = place.by_core(dinject, dreadout) + place.swap(
@@ -1311,22 +1377,37 @@
     grad_shift = jnp.sum(dpre, axis=(0, 1, 2))
     dmixed = dmixed.astype(BF16)
 
+    def by_columns(grad):
+        return grad.reshape(na, nb, CORES, groups, shard_rows, grad.shape[-1])
+
+
     dstep = draw[..., :M_SHARE].astype(BF16)
-    db_low = jnp.concatenate(
-        [
-            dmixed[..., f_cols:],
-            halo_rows(dstep),
-            jnp.zeros((CORES, slots, piece + HALO, ms_cols - small_at), BF16),
-        ],
-        axis=-1,
-    ).reshape(rows_halo, b_cols)
+    db_low = dmixed.reshape(rows_halo, b_cols)
+    dkv, db_low = tie(dkv, db_low)
+    grad_b = place.reduce_first(by_columns(mm(normed, db_low, TN)), False)
+    dkv_own = place.reduce_z(dkv)
+    ff_grads, db_late = tie(ff_grads, db_low)
+    ff_grads = ff_finish(ff_grads)
+    dnormed = dnormed + mm(db_late, w_b, NT)
+    head_sums = place.sum_along(jnp.sum(sums, axis=0)[:3, :M_SHARE], "z")
+    dkv_own, grad_b, dnormed, head_sums = tie(dkv_own, grad_b, dnormed, head_sums)
+    dkv_own = jnp.stack([part.reshape(CORES, piece, 2 * HD) for part in dkv_own], axis=1)
+    dkv_own = place.by_core(dkv_own, dkv_own[::-1])
+    grad_b = place.reduce_second(grad_b, False)
     dq_rows = from_heads(dqueries[..., :HD] * scale)
     dq_rows = rotate(dq_rows, cos_part, -sin_part).reshape(CORES, slots, piece, q_cols)
     dk_rows = rotate(dkv_own[..., None, :HD], cos_part, -sin_part)[..., 0, :]
+    tail_zeros = jnp.zeros((CORES, slots, piece, ms_cols - M_SHARE), BF16)
     dlin = jnp.concatenate([dq_rows, dk_rows, dkv_own[..., HD:]], axis=-1).astype(BF16)
-    da_low = jnp.concatenate([halo_rows(dlin), dmixed[..., :f_cols]], axis=-1)
-    da_low = da_low.reshape(rows_halo, a_cols)
-    dnormed = dnormed + mm(da_low, w_a, NT) + mm(db_low, w_b, NT)
+    da_low = halo_rows(
+        jnp.concatenate(
+            [dlin, dstep.reshape(CORES, slots, piece, -1), tail_zeros], axis=-1
+        )
+    ).reshape(rows_halo, a_cols)
+    dnormed = dnormed + mm(da_low, w_a, NT)
+    grad_input_gain = jnp.sum(
+        dnormed.reshape(CORES, slots, piece + HALO, width) * (tokens * scale_in), axis=(0, 1, 2)
+    )
     dnormed = own_sum(dnormed).reshape(slots, piece + HALO, width)
     rim_back = lax.ppermute(
         dnormed[:, HALO - KC + 1 : HALO].astype(BF16),
@@ -1338,7 +1419,6 @@
     input_grad = dresidual.reshape(slots, piece, width) + rms_back(
         own, own_scale, gain_in, dnormed
     )
-    grad_input_gain = jnp.sum(dnormed * own * own_scale, axis=(0, 1))
 
     zero_half = jnp.zeros((m_cols,), F32)
 
@@ -1367,21 +1447,26 @@
     vector_grads = jnp.pad(
         vector_grads, ((0, 0), (0, small_cols * shard_rows - vector_size))
     ).reshape(width, small_cols)
-    grad_b = mm(normed, db_low, TN)
-    grad_b = lax.dynamic_update_slice(grad_b, vector_grads, (0, tail_at + small_at))
     grad_a = mm(normed, da_low, TN)
-    head_sums = jnp.sum(sums, axis=0)[:3, :M_SHARE]
-    head_sums, grad_a = lax.optimization_barrier((head_sums, grad_a))
-    head_sums = place.sum_all(head_sums)
+    grad_a = grad_a + jnp.pad(
+        vector_grads,
+        ((0, 0), (tail_at + small_at, a_cols - tail_at - small_at - small_cols)),
+    )
+    mid_grads, grad_a, grad_b = tie(mid_grads, grad_a, grad_b)
+    mid_grads = mid_finish(mid_grads)
+    grad_b = place.reduce_z([grad_b])[0]
+    grad_a = place.reduce_first(by_columns(grad_a), True)
+    head_sums = place.sum_along(head_sums, "b")
+    grad_a, grad_b, head_sums = tie(grad_a, grad_b, head_sums)
+    grad_a = place.reduce_second(grad_a, True)
+    head_sums = place.sum_along(head_sums, "a")
+    grad_a, head_sums = tie(grad_a, head_sums)
+    (grad_a,) = place.reduce_z([grad_a])
     other_sums = place.swap(head_sums)
     head_sums = jnp.concatenate(
         [place.by_core(head_sums, other_sums), place.by_core(other_sums, head_sums)], axis=1
     )
     head_sums = lax.dynamic_slice_in_dim(head_sums, place.at["z"] * (SH // groups), SH // groups, 1)
-
-    grad_a, grad_b = place.reduce_chips(
-        [by_columns(grad_a), by_columns(grad_b)], [True, False]
-    )
 
     def between_cores(columns):
         columns = columns.reshape(CORES, shard_rows, -1)
@@ -1389,20 +1474,17 @@
         got = place.swap(lax.dynamic_index_in_dim(columns, 1 - core, 0, False))
         return place.by_core(kept, got), place.by_core(got, kept)
 
-    def ff_whole(pair):
-        parts = [half.reshape(shard_rows, chips, 1, -1) for half in pair]
-        return jnp.concatenate(parts, axis=2).reshape(shard_rows, -1)
-
     ff_rows_each = ff_grads.shape[0] // 3
     both = between_cores(
         jnp.concatenate([ff_grads[:ff_rows_each], ff_grads[ff_rows_each : 2 * ff_rows_each]], axis=1)
     )
-    grad_gate = ff_whole([half[:, :ff_half] for half in both]).astype(F32)
-    grad_up = ff_whole([half[:, ff_half:] for half in both]).astype(F32)
+    grad_gate = jnp.concatenate([half[:, :ff_half] for half in both], axis=1).astype(F32)
+    grad_up = jnp.concatenate([half[:, ff_half:] for half in both], axis=1).astype(F32)
     grad_down = ff_grads[2 * ff_rows_each :].astype(F32)
     grad_outs = mid_grads[:, :width].astype(F32)
     grad_zgate = jnp.concatenate(between_cores(mid_grads[:, width:]), axis=1).astype(F32)
-    first, second = between_cores(jnp.concatenate([grad_a, grad_b], axis=1))
+    conv_first, conv_second = between_cores(grad_b)
+    first, second = between_cores(grad_a)
 
     def both_halves(start, size):
         return jnp.concatenate([first[:, start : start + size], second[:, start : start + size]], 1)
@@ -1411,10 +1493,11 @@
         [both_halves(0, q_cols), both_halves(q_cols, HD), both_halves(q_cols + HD, HD)], axis=1
     )
     grad_mixer_in = jnp.concatenate(
-        [both_halves(lin_cols, m_cols), both_halves(lin_cols + m_cols, NS)], axis=1
-    )
-    grad_step = both_halves(lin_cols + c_cols, M_SHARE)
-    small_at = lin_cols + c_cols + small_at
+        [conv_first[:, :m_cols], conv_second[:, :m_cols], conv_first[:, m_cols:], conv_second[:, m_cols:]],
+        axis=1,
+    )
+    grad_step = both_halves(lin_cols, M_SHARE)
+    small_at = lin_cols + small_at
     small_sum = (first + second)[:, small_at : small_at + small_cols].reshape(-1)
 
     return (

time: 766 us -> 695 us (0.907); the launches traced: 753 us -> 699 us
  waiting for transfers between devices: 186 us -> 112 us
  other arithmetic: 76.6 us -> 97.2 us
    ppermute x83 -> x67, waiting for transfers between devices: 156 us -> 76.8 us  [shift(): return lax.ppermute(x, AXES, self.pairs(dim, by))]
    ppermute x6, starting transfers between devices: 20.5 us -> 36.9 us  [carried(): lax.ppermute(leaving, AXES, place.chip_pairs(k))]
    ppermute x83 -> x67, starting transfers between devices: 132 us -> 122 us  [shift(): return lax.ppermute(x, AXES, self.pairs(dim, by))]
    pallas_call x12 -> x10, Pallas kernels: 49 us -> 42.7 us  [moved(): pl.pallas_call(functools.partial(moved_kernel, plan=plan, count=len(sourc...]
    unnamed x278 -> x248, local copies, waits for them, and re-layouts: 22.2 us -> 17.1 us
  transfers between devices with their start and end apart: 99 -> 85, of which waited for: 33 -> 27; matrix products, arithmetic and copies ran while one was open for 22% -> 31% of each run, Pallas kernels for 19% -> 18%
where the time goes in v3:
time: 695 us; the launch traced here: 699 us
  starting transfers between devices  170 us (24%)
  Pallas kernels  140 us (20%)
  waiting for transfers between devices  112 us (16%)
  local copies, waits for them, and re-layouts  97.8 us (14%)
  other arithmetic  97.2 us (14%)
  matrix products  65.3 us (9%)
  between operations  16.8 us (2%)
    ppermute x67, starting transfers between devices, shift(): return lax.ppermute(x, AXES, self.pairs(dim, by))  122 us
    ppermute x67, waiting for transfers between devices, shift(): return lax.ppermute(x, AXES, self.pairs(dim, by))  76.8 us
    dot_general x25, matrix products, mm(): lax.dot_general(left, right, dims, precision=precision, preferred_element...  65.3 us
    pallas_call x4, Pallas kernels, over_pieces(): pl.pallas_call(kernel, grid=(pieces,), in_specs=[spec(shape, split) for s...  47.9 us
    pallas_call x10, Pallas kernels, moved(): pl.pallas_call(functools.partial(moved_kernel, plan=plan, count=len(sourc...  42.7 us
    ppermute x6, starting transfers between devices, carried(): lax.ppermute(leaving, AXES, place.chip_pairs(k))  36.9 us
    ppermute x6, waiting for transfers between devices, carried(): lax.ppermute(leaving, AXES, place.chip_pairs(k))  23.7 us
    pallas_call x2, Pallas kernels, attend_back(): pl.pallas_call(functools.partial(attend_back_kernel, piece=piece), grid_s...  22 us
  transfers between devices with their start and end apart: 85, of which 27 were waited for; matrix products, arithmetic and copies ran while one was open for 31% of the time, Pallas kernels for 18%

profile of v3, /device:TPU:0, one launch (start us, length us, event | category | flops | bytes accessed | tf_op | source)
XLA Modules:
  0.0 698.9 jit_solution(7980119430454215101)
XLA Ops:
  19.4 4.5 collective-permute-start
  30.6 6.0 collective-permute-done.3.refs_1_
  36.6 7.6 %collective-permute-done.4.refs_2_ = bf16[64,1408]{1,0:T(8,128)(2,1)} collective-permute-done((bf16[64,1408]{1,0:T(8,128)(2,1)S(1)}, bf16[64,1408]{1,0:T(8,128)(2,1)}, u32[]{:S(2)}, u32[]{:S(2)}) %collective-permute-start.4) | collective-permute-done | bytes 180256 | tf_op jit(solution)/shard_map/ppermute | solution.py:87
  50.8 12.0 %collective-permute-done.10.refs_6_ = bf16[256,896]{1,0:T(8,128)(2,1)S(1)} collective-permute-done((bf16[256,896]{1,0:T(8,128)(2,1)}, bf16[256,896]{1,0:T(8,128)(2,1)S(1)}, u32[]{:S(2)}, u32[]{:S(2)}) %collective-permute-start.10) | collective-permute-done | bytes 458784 | tf_op jit(solution)/shard_map/ppermute | solution.py:87
  70.5 8.5 %collective-permute-done.7.refs_2_ = bf16[256,512]{1,0:T(8,128)(2,1)} collective-permute-done((bf16[256,512]{1,0:T(8,128)(2,1)}, bf16[256,512]{1,0:T(8,128)(2,1)}, u32[]{:S(2)}, u32[]{:S(2)}) %collective-permute-start.7) | collective-permute-done | bytes 262176 | tf_op jit(solution)/shard_map/ppermute | solution.py:87
  78.9 9.4 %collective-permute-done.8.refs_3_ = bf16[256,512]{1,0:T(8,128)(2,1)} collective-permute-done((bf16[256,512]{1,0:T(8,128)(2,1)}, bf16[256,512]{1,0:T(8,128)(2,1)}, u32[]{:S(2)}, u32[]{:S(2)}) %collective-permute-start.8) | collective-permute-done | bytes 262176 | tf_op jit(solution)/shard_map/ppermute | solution.py:87
  89.8 4.1 moved.11
  136.6 8.8 %chunk.1 = (f32[4,192,768]{2,1,0:T(8,128)}, f32[4,192,128]{2,1,0:T(8,128)}, bf16[4,208,128]{2,1,0:T(8,128)(2,1)}, bf16[4,208,128]{2,1,0:T(8,128)(2,1)}, bf16[4,2...) custom-call(bf16[4,192,768]{2,1,0:T(8,128)(2,1)} %bitcast.406, bf16[4,192,128]{2,1,0:T(8,128)(2,1)} %bitcast.447, ...), custom_call_target="tpu_custom_call" | custom-call | flops 10350000128 | tf_op jit(solution)/shard_map/chunk/pallas_call | solution.py:709
  150.1 5.7 collective-permute-done.13.refs_1_.refs_5_
  155.8 8.2 %collective-permute-done.14.refs_2_.refs_6_ = bf16[2,2,208,128]{3,2,1,0:T(8,128)(2,1)} collective-permute-done((bf16[2,2,208,128]{3,2,1,0:T(8,128)(2,1)}, bf16[2,2,208,128]{3,2,1,0:T(8,128)(2,1)}, u32[]{:S(2)}, u32[]{:S(2)}) %collective-permute-start.14) | collective-permute-done | bytes 213024 | tf_op jit(solution)/shard_map/ppermute | solution.py:87
  176.3 13.3 %collective-permute-done.21.refs_8_.refs_11_ = bf16[2,208,128]{2,1,0:T(8,128)(2,1)S(1)} collective-permute-done((bf16[2,208,128]{2,1,0:T(8,128)(2,1)}, bf16[2,208,128]{2,1,0:T(8,128)(2,1)S(1)}, u32[]{:S(2)}, u32[]{:S(2)}) %collective-permute-start.21) | collective-permute-done | bytes 106528 | tf_op jit(solution)/shard_map/ppermute | solution.py:867
  204.9 6.1 collective-permute-start.28
  213.6 4.3 moved.13
  218.8 7.9 %attend.2 = (bf16[1,2,768,128]{3,2,1,0:T(8,128)(2,1)}, f32[1,2,1,768]{3,2,1,0:T(1,128)}) custom-call(s32[2]{0:T(128)} %copy-done.99, s32[1]{0:T(128)} %get-tuple-element.486.lengths, bf16[1,2,768,128]{3,2,1,0:T(8,128)(2,1)} %get-tuple-element.413.q_ref, bf16[1,6144,128]{2,1,0:T(8,128)(2,1)} %bitcast.462), custom_call_target="tpu_custom_call" | custom-call | flops 23000000512 | tf_op jit(solution)/shard_map/attend/pallas_call | solution.py:399
  226.7 8.0 %attend.3 = (bf16[1,2,768,128]{3,2,1,0:T(8,128)(2,1)}, f32[1,2,1,768]{3,2,1,0:T(1,128)}) custom-call(s32[2]{0:T(128)} %copy-done.99, s32[1]{0:T(128)} %get-tuple-element.487.lengths, bf16[1,2,768,128]{3,2,1,0:T(8,128)(2,1)} %get-tuple-element.414.q_ref, bf16[1,6144,128]{2,1,0:T(8,128)(2,1)} %bitcast.464), custom_call_target="tpu_custom_call" | custom-call | flops 23000000512 | tf_op jit(solution)/shard_map/attend/pallas_call | solution.py:399
  241.9 5.1 carry.1
  247.1 4.9 moved.14
  276.9 6.5 moved.15
  283.4 3.5 fusion.82
  289.0 3.3 multiply_convert_fusion.2
  305.2 4.5 fusion.60
  312.0 3.5 multiply_reduce_fusion.2
  316.7 4.1 fusion.12
  320.8 5.5 direct.1
  335.6 4.6 convolution_convert_fusion.1.refs_1_
  346.3 6.2 moved.16
  361.2 11.1 %collective-permute-start.43 = (bf16[2,208,128]{2,1,0:T(8,128)(2,1)}, bf16[2,208,128]{2,1,0:T(8,128)(2,1)S(1)}, u32[]{:S(2)}, u32[]{:S(2)}) collective-permute-start(bf16[2,208,128]{2,1,0:T(8,128)(2,1)} %scan.6), channel_id=1, source_target_pairs={{0,8},{1,9},{2,10},{3,11},{4,12},{5,13},{6,14},{7,15},{8,16},{9,17... | collective-permute-start | bytes 319496 | tf_op jit(solution)/shard_map/ppermute | solution.py:867
  372.3 21.6 %collective-permute-start.44 = (bf16[2,208,128]{2,1,0:T(8,128)(2,1)}, bf16[2,208,128]{2,1,0:T(8,128)(2,1)S(1)}, u32[]{:S(2)}, u32[]{:S(2)}) collective-permute-start(bf16[2,208,128]{2,1,0:T(8,128)(2,1)} %scan.6), channel_id=1, source_target_pairs={{0,16},{1,17},{2,18},{3,19},{4,20},{5,21},{6,22},{7,23},{8,24},{9,... | collective-permute-start | bytes 319496 | tf_op jit(solution)/shard_map/ppermute | solution.py:867
  394.5 5.0 collective-permute-done.43.refs_8_
  413.5 4.6 moved.17
  428.9 11.0 %attend_back.3 = (f32[1,2,768,128]{3,2,1,0:T(8,128)}, bf16[1,6144,128]{2,1,0:T(8,128)(2,1)}) custom-call(s32[2]{0:T(128)} %copy-done.99, s32[1]{0:T(128)} %get-tuple-element.487.lengths, bf16[1,2,768,128]{3,2,1,0:T(8,128)(2,1)} %get-tuple-element.414.q_ref, bf16[1,6144,128]{2,1,0:T(8,128)(2,1)} %bitcast.465, ...), custom_call_target="tpu_custom_call" | custom-call | flops 28750000128 | tf_op jit(solution)/shard_map/attend_back/pallas_call | solution.py:482
  439.9 11.0 %attend_back.2 = (f32[1,2,768,128]{3,2,1,0:T(8,128)}, bf16[1,6144,128]{2,1,0:T(8,128)(2,1)}) custom-call(s32[2]{0:T(128)} %copy-done.99, s32[1]{0:T(128)} %get-tuple-element.486.lengths, bf16[1,2,768,128]{3,2,1,0:T(8,128)(2,1)} %get-tuple-element.413.q_ref, bf16[1,6144,128]{2,1,0:T(8,128)(2,1)} %bitcast.463, ...), custom_call_target="tpu_custom_call" | custom-call | flops 28750000128 | tf_op jit(solution)/shard_map/attend_back/pallas_call | solution.py:482
  456.7 16.8 %collective-permute-start.51 = (bf16[2,2,4,192,128]{4,3,2,1,0:T(8,128)(2,1)}, bf16[2,2,4,192,128]{4,3,2,1,0:T(8,128)(2,1)S(1)}, u32[]{:S(2)}, u32[]{:S(2)}) collective-permute-start(bf16[2,2,4,192,128]{4,3,2,1,0:T(8,128)(2,1)} %dynamic-slice_bitcast_fusion.2), channel_id=1, source_target_pairs={{0,8},{4,12},{1,9},{5,13},{2,10},{6,14},{3,11},{7,15},{8,0},{12,4}... | collective-permute-start | bytes 2359304 | tf_op jit(solution)/shard_map/ppermute | solution.py:87
  474.5 23.3 %collective-permute-start.50 = (bf16[2,2,4,192,128]{4,3,2,1,0:T(8,128)(2,1)}, bf16[2,2,4,192,128]{4,3,2,1,0:T(8,128)(2,1)}, u32[]{:S(2)}, u32[]{:S(2)}) collective-permute-start(bf16[2,2,4,192,128]{4,3,2,1,0:T(8,128)(2,1)} %dynamic-slice_bitcast_fusion.3), channel_id=1, source_target_pairs={{0,16},{4,20},{1,17},{5,21},{2,18},{6,22},{3,19},{7,23},{8,24},{12... | collective-permute-start | bytes 2359304 | tf_op jit(solution)/shard_map/ppermute | solution.py:87
  497.8 28.5 %chunk_back.1 = (f32[4,192,768]{2,1,0:T(8,128)}, f32[4,192,128]{2,1,0:T(8,128)}, f32[4,192,128]{2,1,0:T(8,128)}, f32[4,192,128]{2,1,0:T(8,128)}, f32[4,8,128]{2,1,0:T(8,128)}) custom-call(bf16[4,192,768]{2,1,0:T(8,128)(2,1)} %bitcast.407, bf16[4,192,128]{2,1,0:T(8,128)(2,1)} %bitcast.448, bf16[4,192,128]{2,1,0:T(8,128)(2,1)} %bitcast.446, ...), custom_call_target="tpu_custom_call" | custom-call | flops 32199999488 | tf_op jit(solution)/shard_map/chunk_back/pallas_call | solution.py:709
  528.7 3.4 collective-permute-done.59
  532.9 3.8 collective-permute-done.60
  542.6 6.6 fusion.4
  552.9 5.3 broadcast_multiply_fusion.3
  559.0 5.5 add_convert_fusion
  566.0 3.6 moved.19
  569.7 3.6 fusion.27
  577.5 3.8 collective-permute-start.57
  581.4 6.0 convolution_add_fusion.2
  605.7 4.8 multiply_reduce_fusion
  616.8 4.0 bitcast_add_fusion
  623.5 13.5 %collective-permute-start.65 = (bf16[64,896]{1,0:T(8,128)(2,1)}, bf16[64,896]{1,0:T(8,128)(2,1)S(1)}, u32[]{:S(2)}, u32[]{:S(2)}) collective-permute-start(bf16[64,896]{1,0:T(8,128)(2,1)} %bitcast.156), channel_id=1, source_target_pairs={{0,1},{4,5},{1,2},{5,6},{2,3},{6,7},{3,0},{7,4},{8,9},{12,13},{9,1... | collective-permute-start | bytes 344072 | tf_op jit(solution)/shard_map/ppermute | solution.py:87
  662.6 6.1 collective-permute-done.69
  (696 shorter events, 313.0 us)
Async XLA Ops:
  7.2 239.8 %all-gather.3.cloned.1.call-start = ((), (), s32[]{:S(2)}) async-start(), calls=%async_computation.4 | async-start | bytes 7569408 | tf_op jit(solution)/shard_map/all_gather | solution.py:985
  10.0 266.9 %all-gather.5.cloned.1.call-start = ((), (), s32[]{:S(2)}) async-start(), calls=%async_computation.5 | async-start | bytes 12976128 | tf_op jit(solution)/shard_map/all_gather | solution.py:1150
  25.7 18.5 %collective-permute-start.4 = (bf16[64,1408]{1,0:T(8,128)(2,1)S(1)}, bf16[64,1408]{1,0:T(8,128)(2,1)}, u32[]{:S(2)}, u32[]{:S(2)}) collective-permute-start(bf16[64,1408]{1,0:T(8,128)(2,1)S(1)} %pad_maximum_fusion.21.refs_0_), channel_id=1, source_target_pairs={{0,2},{4,6},{1,3},{5,7},{2,0},{6,4},{3,1},{7,5},{8,10},{12,14},{9,... | collective-permute-start | bytes 540680 | tf_op jit(solution)/shard_map/ppermute | solution.py:87
  26.8 17.4 %collective-permute-start.5 = (bf16[64,1408]{1,0:T(8,128)(2,1)S(1)}, bf16[64,1408]{1,0:T(8,128)(2,1)}, u32[]{:S(2)}, u32[]{:S(2)}) collective-permute-start(bf16[64,1408]{1,0:T(8,128)(2,1)S(1)} %pad_maximum_fusion.21.refs_0_), channel_id=1, source_target_pairs={{0,3},{4,7},{1,0},{5,4},{2,1},{6,5},{3,2},{7,6},{8,11},{12,15},{9,... | collective-permute-start | bytes 540680 | tf_op jit(solution)/shard_map/ppermute | solution.py:87
  29.8 40.2 %collective-permute-start.1 = (bf16[2,200,1024]{2,1,0:T(8,128)(2,1)S(1)}, bf16[2,200,1024]{2,1,0:T(8,128)(2,1)S(1)}, u32[]{:S(2)}, u32[]{:S(2)}) collective-permute-start(bf16[2,200,1024]{2,1,0:T(8,128)(2,1)S(1)} %get-tuple-element.400), channel_id=1, source_target_pairs={{0,4},{4,0},{1,5},{5,1},{2,6},{6,2},{3,7},{7,3},{8,12},{12,8},{9,1... | collective-permute-start | bytes 2457608 | tf_op jit(solution)/shard_map/ppermute | solution.py:87
  47.0 15.8 %collective-permute-start.10 = (bf16[256,896]{1,0:T(8,128)(2,1)}, bf16[256,896]{1,0:T(8,128)(2,1)S(1)}, u32[]{:S(2)}, u32[]{:S(2)}) collective-permute-start(bf16[256,896]{1,0:T(8,128)(2,1)} %get-tuple-element.149.refs_4_), channel_id=1, source_target_pairs={{0,16},{4,20},{1,17},{5,21},{2,18},{6,22},{3,19},{7,23},{8,24},{12... | collective-permute-start | bytes 1376264 | tf_op jit(solution)/shard_map/ppermute | solution.py:87
  48.7 20.5 %collective-permute-start.6 = (bf16[256,512]{1,0:T(8,128)(2,1)}, bf16[256,512]{1,0:T(8,128)(2,1)}, u32[]{:S(2)}, u32[]{:S(2)}) collective-permute-start(bf16[256,512]{1,0:T(8,128)(2,1)} %get-tuple-element.148.refs_0_), channel_id=1, source_target_pairs={{0,8},{4,12},{1,9},{5,13},{2,10},{6,14},{3,11},{7,15},{8,0},{12,4}... | collective-permute-start | bytes 786440 | tf_op jit(solution)/shard_map/ppermute | solution.py:87
  50.2 28.8 %collective-permute-start.9 = (bf16[256,896]{1,0:T(8,128)(2,1)}, bf16[256,896]{1,0:T(8,128)(2,1)}, u32[]{:S(2)}, u32[]{:S(2)}) collective-permute-start(bf16[256,896]{1,0:T(8,128)(2,1)} %get-tuple-element.149.refs_4_), channel_id=1, source_target_pairs={{0,8},{4,12},{1,9},{5,13},{2,10},{6,14},{3,11},{7,15},{8,0},{12,4}... | collective-permute-start | bytes 1376264 | tf_op jit(solution)/shard_map/ppermute | solution.py:87
  62.8 27.1 %collective-permute-start.11 = (bf16[256,896]{1,0:T(8,128)(2,1)S(1)}, bf16[256,896]{1,0:T(8,128)(2,1)}, u32[]{:S(2)}, u32[]{:S(2)}) collective-permute-start(bf16[256,896]{1,0:T(8,128)(2,1)S(1)} %collective-permute-done.10.refs_6_), channel_id=1, source_target_pairs={{0,8},{4,12},{1,9},{5,13},{2,10},{6,14},{3,11},{7,15},{8,0},{12,4}... | collective-permute-start | bytes 1376264 | tf_op jit(solution)/shard_map/ppermute | solution.py:87
  69.2 19.1 %collective-permute-start.8 = (bf16[256,512]{1,0:T(8,128)(2,1)}, bf16[256,512]{1,0:T(8,128)(2,1)}, u32[]{:S(2)}, u32[]{:S(2)}) collective-permute-start(bf16[256,512]{1,0:T(8,128)(2,1)} %collective-permute-done.6.refs_1_), channel_id=1, source_target_pairs={{0,16},{4,20},{1,17},{5,21},{2,18},{6,22},{3,19},{7,23},{8,24},{12... | collective-permute-start | bytes 786440 | tf_op jit(solution)/shard_map/ppermute | solution.py:87
  100.4 29.9 %collective-permute-start.16 = (bf16[2,2,192,128]{3,2,1,0:T(8,128)(2,1)}, bf16[2,2,192,128]{3,2,1,0:T(8,128)(2,1)}, u32[]{:S(2)}, u32[]{:S(2)}) collective-permute-start(bf16[2,2,192,128]{3,2,1,0:T(8,128)(2,1)} %pad_maximum_fusion.17), channel_id=1, source_target_pairs={{0,1},{4,5},{1,2},{5,6},{2,3},{6,7},{3,0},{7,4},{8,9},{12,13},{9,1... | collective-permute-start | bytes 589832 | tf_op jit(solution)/shard_map/ppermute | solution.py:87
  102.9 27.5 %collective-permute-start.17 = (bf16[2,2,192,128]{3,2,1,0:T(8,128)(2,1)}, bf16[2,2,192,128]{3,2,1,0:T(8,128)(2,1)}, u32[]{:S(2)}, u32[]{:S(2)}) collective-permute-start(bf16[2,2,192,128]{3,2,1,0:T(8,128)(2,1)} %pad_maximum_fusion.17), channel_id=1, source_target_pairs={{0,2},{4,6},{1,3},{5,7},{2,0},{6,4},{3,1},{7,5},{8,10},{12,14},{9,... | collective-permute-start | bytes 589832 | tf_op jit(solution)/shard_map/ppermute | solution.py:87
  105.2 25.2 %collective-permute-start.18 = (bf16[2,2,192,128]{3,2,1,0:T(8,128)(2,1)}, bf16[2,2,192,128]{3,2,1,0:T(8,128)(2,1)}, u32[]{:S(2)}, u32[]{:S(2)}) collective-permute-start(bf16[2,2,192,128]{3,2,1,0:T(8,128)(2,1)} %pad_maximum_fusion.17), channel_id=1, source_target_pairs={{0,3},{4,7},{1,0},{5,4},{2,1},{6,5},{3,2},{7,6},{8,11},{12,15},{9,... | collective-permute-start | bytes 589832 | tf_op jit(solution)/shard_map/ppermute | solution.py:87
  120.7 14.0 %collective-permute-start.12 = (bf16[2,2,192,128]{3,2,1,0:T(8,128)(2,1)}, bf16[2,2,192,128]{3,2,1,0:T(8,128)(2,1)}, u32[]{:S(2)}, u32[]{:S(2)}) collective-permute-start(bf16[2,2,192,128]{3,2,1,0:T(8,128)(2,1)} %slice.631), channel_id=1, source_target_pairs={{0,4},{4,0},{1,5},{5,1},{2,6},{6,2},{3,7},{7,3},{8,12},{12,8},{9,1... | collective-permute-start | bytes 589832 | tf_op jit(solution)/shard_map/ppermute | solution.py:87
  133.2 30.8 %collective-permute-start.19 = (bf16[1536,128]{1,0:T(8,128)(2,1)}, bf16[1536,128]{1,0:T(8,128)(2,1)}, u32[]{:S(2)}, u32[]{:S(2)}) collective-permute-start(bf16[1536,128]{1,0:T(8,128)(2,1)} %get-tuple-element.174.refs_0_), channel_id=1, source_target_pairs={{0,8},{4,12},{1,9},{5,13},{2,10},{6,14},{3,11},{7,15},{8,0},{12,4}... | collective-permute-start | bytes 1179656 | tf_op jit(solution)/shard_map/ppermute | solution.py:87
  133.3 30.7 %collective-permute-start.20 = (bf16[1536,128]{1,0:T(8,128)(2,1)}, bf16[1536,128]{1,0:T(8,128)(2,1)}, u32[]{:S(2)}, u32[]{:S(2)}) collective-permute-start(bf16[1536,128]{1,0:T(8,128)(2,1)} %get-tuple-element.178.refs_4_), channel_id=1, source_target_pairs={{0,16},{4,20},{1,17},{5,21},{2,18},{6,22},{3,19},{7,23},{8,24},{12... | collective-permute-start | bytes 1179656 | tf_op jit(solution)/shard_map/ppermute | solution.py:87
  146.2 17.8 %collective-permute-start.14 = (bf16[2,2,208,128]{3,2,1,0:T(8,128)(2,1)}, bf16[2,2,208,128]{3,2,1,0:T(8,128)(2,1)}, u32[]{:S(2)}, u32[]{:S(2)}) collective-permute-start(bf16[2,2,208,128]{3,2,1,0:T(8,128)(2,1)} %bitcast.467), channel_id=1, source_target_pairs={{0,2},{4,6},{1,3},{5,7},{2,0},{6,4},{3,1},{7,5},{8,10},{12,14},{9,... | collective-permute-start | bytes 638984 | tf_op jit(solution)/shard_map/ppermute | solution.py:87
  146.5 17.5 %collective-permute-start.15 = (bf16[2,2,208,128]{3,2,1,0:T(8,128)(2,1)}, bf16[2,2,208,128]{3,2,1,0:T(8,128)(2,1)}, u32[]{:S(2)}, u32[]{:S(2)}) collective-permute-start(bf16[2,2,208,128]{3,2,1,0:T(8,128)(2,1)} %bitcast.466), channel_id=1, source_target_pairs={{0,3},{4,7},{1,0},{5,4},{2,1},{6,5},{3,2},{7,6},{8,11},{12,15},{9,... | collective-permute-start | bytes 638984 | tf_op jit(solution)/shard_map/ppermute | solution.py:87
  164.0 378.5 %reduce-scatter.5.cloned.1.call-start = ((), (), s32[]{:S(2)}) async-start(), calls=%async_computation.6 | async-start | bytes 7864320 | tf_op jit(solution)/shard_map/reduce_scatter | solution.py:201
  164.2 37.6 %collective-permute-start.24 = (bf16[1536,128]{1,0:T(8,128)(2,1)}, bf16[1536,128]{1,0:T(8,128)(2,1)}, u32[]{:S(2)}, u32[]{:S(2)}) collective-permute-start(bf16[1536,128]{1,0:T(8,128)(2,1)} %get-tuple-element.174.refs_0_), channel_id=1, source_target_pairs={{0,16},{4,20},{1,17},{5,21},{2,18},{6,22},{3,19},{7,23},{8,24},{12... | collective-permute-start | bytes 1179656 | tf_op jit(solution)/shard_map/ppermute | solution.py:87
  165.1 36.7 %collective-permute-start.25 = (bf16[1536,128]{1,0:T(8,128)(2,1)}, bf16[1536,128]{1,0:T(8,128)(2,1)}, u32[]{:S(2)}, u32[]{:S(2)}) collective-permute-start(bf16[1536,128]{1,0:T(8,128)(2,1)} %collective-permute-done.19.refs_1_), channel_id=1, source_target_pairs={{0,16},{4,20},{1,17},{5,21},{2,18},{6,22},{3,19},{7,23},{8,24},{12... | collective-permute-start | bytes 1179656 | tf_op jit(solution)/shard_map/ppermute | solution.py:87
  166.2 35.6 %collective-permute-start.26 = (bf16[1536,128]{1,0:T(8,128)(2,1)}, bf16[1536,128]{1,0:T(8,128)(2,1)}, u32[]{:S(2)}, u32[]{:S(2)}) collective-permute-start(bf16[1536,128]{1,0:T(8,128)(2,1)} %get-tuple-element.178.refs_4_), channel_id=1, source_target_pairs={{0,8},{4,12},{1,9},{5,13},{2,10},{6,14},{3,11},{7,15},{8,0},{12,4}... | collective-permute-start | bytes 1179656 | tf_op jit(solution)/shard_map/ppermute | solution.py:87
  167.4 34.4 %collective-permute-start.27 = (bf16[1536,128]{1,0:T(8,128)(2,1)}, bf16[1536,128]{1,0:T(8,128)(2,1)}, u32[]{:S(2)}, u32[]{:S(2)}) collective-permute-start(bf16[1536,128]{1,0:T(8,128)(2,1)} %collective-permute-done.20.refs_6_), channel_id=1, source_target_pairs={{0,8},{4,12},{1,9},{5,13},{2,10},{6,14},{3,11},{7,15},{8,0},{12,4}... | collective-permute-start | bytes 1179656 | tf_op jit(solution)/shard_map/ppermute | solution.py:87
  171.0 18.6 %collective-permute-start.21 = (bf16[2,208,128]{2,1,0:T(8,128)(2,1)}, bf16[2,208,128]{2,1,0:T(8,128)(2,1)S(1)}, u32[]{:S(2)}, u32[]{:S(2)}) collective-permute-start(bf16[2,208,128]{2,1,0:T(8,128)(2,1)} %scan.4), channel_id=1, source_target_pairs={{0,8},{1,9},{2,10},{3,11},{4,12},{5,13},{6,14},{7,15},{8,16},{9,17... | collective-permute-start | bytes 319496 | tf_op jit(solution)/shard_map/ppermute | solution.py:867
  204.9 36.4 %collective-permute-start.28 = (bf16[2,2,192,128]{3,2,1,0:T(8,128)(2,1)}, bf16[2,2,192,128]{3,2,1,0:T(8,128)(2,1)S(1)}, u32[]{:S(2)}, u32[]{:S(2)}) collective-permute-start(bf16[2,2,192,128]{3,2,1,0:T(8,128)(2,1)} %get-tuple-element.187), channel_id=1, source_target_pairs={{0,1},{4,5},{1,2},{5,6},{2,3},{6,7},{3,0},{7,4},{8,9},{12,13},{9,1... | collective-permute-start | bytes 589832 | tf_op jit(solution)/shard_map/ppermute | solution.py:87
  210.9 30.3 %collective-permute-start.29 = (bf16[2,2,192,128]{3,2,1,0:T(8,128)(2,1)}, bf16[2,2,192,128]{3,2,1,0:T(8,128)(2,1)}, u32[]{:S(2)}, u32[]{:S(2)}) collective-permute-start(bf16[2,2,192,128]{3,2,1,0:T(8,128)(2,1)} %get-tuple-element.188), channel_id=1, source_target_pairs={{0,2},{4,6},{1,3},{5,7},{2,0},{6,4},{3,1},{7,5},{8,10},{12,14},{9,... | collective-permute-start | bytes 589832 | tf_op jit(solution)/shard_map/ppermute | solution.py:87
  211.0 30.3 %collective-permute-start.30 = (bf16[2,2,192,128]{3,2,1,0:T(8,128)(2,1)}, bf16[2,2,192,128]{3,2,1,0:T(8,128)(2,1)}, u32[]{:S(2)}, u32[]{:S(2)}) collective-permute-start(bf16[2,2,192,128]{3,2,1,0:T(8,128)(2,1)} %get-tuple-element.189), channel_id=1, source_target_pairs={{0,3},{4,7},{1,0},{5,4},{2,1},{6,5},{3,2},{7,6},{8,11},{12,15},{9,... | collective-permute-start | bytes 589832 | tf_op jit(solution)/shard_map/ppermute | solution.py:87
  330.9 21.7 %collective-permute-start.39 = (bf16[2,2,192,128]{3,2,1,0:T(8,128)(2,1)}, bf16[2,2,192,128]{3,2,1,0:T(8,128)(2,1)S(1)}, u32[]{:S(2)}, u32[]{:S(2)}) collective-permute-start(bf16[2,2,192,128]{3,2,1,0:T(8,128)(2,1)} %bitcast.474), channel_id=1, source_target_pairs={{0,1},{4,5},{1,2},{5,6},{2,3},{6,7},{3,0},{7,4},{8,9},{12,13},{9,1... | collective-permute-start | bytes 589832 | tf_op jit(solution)/shard_map/ppermute | solution.py:87
  331.8 20.8 %collective-permute-start.40 = (bf16[2,2,192,128]{3,2,1,0:T(8,128)(2,1)}, bf16[2,2,192,128]{3,2,1,0:T(8,128)(2,1)}, u32[]{:S(2)}, u32[]{:S(2)}) collective-permute-start(bf16[2,2,192,128]{3,2,1,0:T(8,128)(2,1)} %bitcast.473), channel_id=1, source_target_pairs={{0,2},{4,6},{1,3},{5,7},{2,0},{6,4},{3,1},{7,5},{8,10},{12,14},{9,... | collective-permute-start | bytes 589832 | tf_op jit(solution)/shard_map/ppermute | solution.py:87
  333.0 19.6 %collective-permute-start.41 = (bf16[2,2,192,128]{3,2,1,0:T(8,128)(2,1)}, bf16[2,2,192,128]{3,2,1,0:T(8,128)(2,1)}, u32[]{:S(2)}, u32[]{:S(2)}) collective-permute-start(bf16[2,2,192,128]{3,2,1,0:T(8,128)(2,1)} %bitcast.472), channel_id=1, source_target_pairs={{0,3},{4,7},{1,0},{5,4},{2,1},{6,5},{3,2},{7,6},{8,11},{12,15},{9,... | collective-permute-start | bytes 589832 | tf_op jit(solution)/shard_map/ppermute | solution.py:87
  353.3 269.4 %reduce-scatter.7.cloned.1.call-start = ((), (), s32[]{:S(2)}) async-start(), calls=%async_computation.7 | async-start | bytes 4587520 | tf_op jit(solution)/shard_map/reduce_scatter | solution.py:201
  361.2 38.4 %collective-permute-start.43 = (bf16[2,208,128]{2,1,0:T(8,128)(2,1)}, bf16[2,208,128]{2,1,0:T(8,128)(2,1)S(1)}, u32[]{:S(2)}, u32[]{:S(2)}) collective-permute-start(bf16[2,208,128]{2,1,0:T(8,128)(2,1)} %scan.6), channel_id=1, source_target_pairs={{0,8},{1,9},{2,10},{3,11},{4,12},{5,13},{6,14},{7,15},{8,16},{9,17... | collective-permute-start | bytes 319496 | tf_op jit(solution)/shard_map/ppermute | solution.py:867
  372.3 29.3 %collective-permute-start.44 = (bf16[2,208,128]{2,1,0:T(8,128)(2,1)}, bf16[2,208,128]{2,1,0:T(8,128)(2,1)S(1)}, u32[]{:S(2)}, u32[]{:S(2)}) collective-permute-start(bf16[2,208,128]{2,1,0:T(8,128)(2,1)} %scan.6), channel_id=1, source_target_pairs={{0,16},{1,17},{2,18},{3,19},{4,20},{5,21},{6,22},{7,23},{8,24},{9,... | collective-permute-start | bytes 319496 | tf_op jit(solution)/shard_map/ppermute | solution.py:867
  422.5 32.0 %collective-permute-start.47 = (bf16[2,2,192,128]{3,2,1,0:T(8,128)(2,1)}, bf16[2,2,192,128]{3,2,1,0:T(8,128)(2,1)S(1)}, u32[]{:S(2)}, u32[]{:S(2)}) collective-permute-start(bf16[2,2,192,128]{3,2,1,0:T(8,128)(2,1)} %get-tuple-element.238), channel_id=1, source_target_pairs={{0,1},{4,5},{1,2},{5,6},{2,3},{6,7},{3,0},{7,4},{8,9},{12,13},{9,1... | collective-permute-start | bytes 589832 | tf_op jit(solution)/shard_map/ppermute | solution.py:87
  423.1 31.4 %collective-permute-start.48 = (bf16[2,2,192,128]{3,2,1,0:T(8,128)(2,1)}, bf16[2,2,192,128]{3,2,1,0:T(8,128)(2,1)}, u32[]{:S(2)}, u32[]{:S(2)}) collective-permute-start(bf16[2,2,192,128]{3,2,1,0:T(8,128)(2,1)} %get-tuple-element.239), channel_id=1, source_target_pairs={{0,2},{4,6},{1,3},{5,7},{2,0},{6,4},{3,1},{7,5},{8,10},{12,14},{9,... | collective-permute-start | bytes 589832 | tf_op jit(solution)/shard_map/ppermute | solution.py:87
  424.4 30.1 %collective-permute-start.49 = (bf16[2,2,192,128]{3,2,1,0:T(8,128)(2,1)}, bf16[2,2,192,128]{3,2,1,0:T(8,128)(2,1)}, u32[]{:S(2)}, u32[]{:S(2)}) collective-permute-start(bf16[2,2,192,128]{3,2,1,0:T(8,128)(2,1)} %get-tuple-element.240), channel_id=1, source_target_pairs={{0,3},{4,7},{1,0},{5,4},{2,1},{6,5},{3,2},{7,6},{8,11},{12,15},{9,... | collective-permute-start | bytes 589832 | tf_op jit(solution)/shard_map/ppermute | solution.py:87
  454.3 229.7 %reduce-scatter.11.cloned.1.call-start = ((), (), s32[]{:S(2)}) async-start(), calls=%async_computation.9 | async-start | bytes 1966080 | tf_op jit(solution)/shard_map/reduce_scatter | solution.py:232
  456.7 80.6 %collective-permute-start.51 = (bf16[2,2,4,192,128]{4,3,2,1,0:T(8,128)(2,1)}, bf16[2,2,4,192,128]{4,3,2,1,0:T(8,128)(2,1)S(1)}, u32[]{:S(2)}, u32[]{:S(2)}) collective-permute-start(bf16[2,2,4,192,128]{4,3,2,1,0:T(8,128)(2,1)} %dynamic-slice_bitcast_fusion.2), channel_id=1, source_target_pairs={{0,8},{4,12},{1,9},{5,13},{2,10},{6,14},{3,11},{7,15},{8,0},{12,4}... | collective-permute-start | bytes 2359304 | tf_op jit(solution)/shard_map/ppermute | solution.py:87
  474.5 64.6 %collective-permute-start.50 = (bf16[2,2,4,192,128]{4,3,2,1,0:T(8,128)(2,1)}, bf16[2,2,4,192,128]{4,3,2,1,0:T(8,128)(2,1)}, u32[]{:S(2)}, u32[]{:S(2)}) collective-permute-start(bf16[2,2,4,192,128]{4,3,2,1,0:T(8,128)(2,1)} %dynamic-slice_bitcast_fusion.3), channel_id=1, source_target_pairs={{0,16},{4,20},{1,17},{5,21},{2,18},{6,22},{3,19},{7,23},{8,24},{12... | collective-permute-start | bytes 2359304 | tf_op jit(solution)/shard_map/ppermute | solution.py:87
  550.1 14.4 %collective-permute-start.53 = (bf16[2,4,192,128]{3,2,1,0:T(8,128)(2,1)}, bf16[2,4,192,128]{3,2,1,0:T(8,128)(2,1)S(1)}, u32[]{:S(2)}, u32[]{:S(2)}) collective-permute-start(bf16[2,4,192,128]{3,2,1,0:T(8,128)(2,1)} %fusion.37), channel_id=1, source_target_pairs={{0,16},{4,20},{1,17},{5,21},{2,18},{6,22},{3,19},{7,23},{8,24},{12... | collective-permute-start | bytes 1179656 | tf_op jit(solution)/shard_map/ppermute | solution.py:87
  574.4 18.9 %collective-permute-start.58 = (bf16[2,2,4,32,896]{4,3,2,1,0:T(8,128)(2,1)}, bf16[2,2,4,32,896]{4,3,2,1,0:T(8,128)(2,1)}, u32[]{:S(2)}, u32[]{:S(2)}) collective-permute-start(bf16[2,2,4,32,896]{4,3,2,1,0:T(8,128)(2,1)} %fusion.30), channel_id=1, source_target_pairs={{0,8},{4,12},{1,9},{5,13},{2,10},{6,14},{3,11},{7,15},{8,0},{12,4}... | collective-permute-start | bytes 2752520 | tf_op jit(solution)/shard_map/ppermute | solution.py:87
  577.5 13.3 %collective-permute-start.57 = (bf16[384,256]{1,0:T(8,128)(2,1)}, bf16[384,256]{1,0:T(8,128)(2,1)}, u32[]{:S(2)}, u32[]{:S(2)}) collective-permute-start(bf16[384,256]{1,0:T(8,128)(2,1)} %pad_maximum_fusion.20), channel_id=1, source_target_pairs={{0,3},{4,7},{1,0},{5,4},{2,1},{6,5},{3,2},{7,6},{8,11},{12,15},{9,... | collective-permute-start | bytes 589832 | tf_op jit(solution)/shard_map/ppermute | solution.py:87
  581.3 104.7 %reduce-scatter.9.cloned.1.call-start = ((), (), s32[]{:S(2)}) async-start(), calls=%async_computation.8 | async-start | bytes 1146880 | tf_op jit(solution)/shard_map/reduce_scatter | solution.py:232
  594.8 26.0 %collective-permute-start.68 = (f32[3,12]{1,0:T(4,128)S(1)}, f32[3,12]{1,0:T(4,128)}, u32[]{:S(2)}, u32[]{:S(2)}) collective-permute-start(f32[3,12]{1,0:T(4,128)S(1)} %copy-done.96), channel_id=1, source_target_pairs={{0,8},{4,12},{1,9},{5,13},{2,10},{6,14},{3,11},{7,15},{8,0},{12,4}... | collective-permute-start | bytes 440 | tf_op jit(solution)/shard_map/ppermute | solution.py:278
  597.4 24.1 %collective-permute-start.63 = (bf16[2,4,32,896]{3,2,1,0:T(8,128)(2,1)}, bf16[2,4,32,896]{3,2,1,0:T(8,128)(2,1)}, u32[]{:S(2)}, u32[]{:S(2)}) collective-permute-start(bf16[2,4,32,896]{3,2,1,0:T(8,128)(2,1)} %fusion.35), channel_id=1, source_target_pairs={{0,16},{4,20},{1,17},{5,21},{2,18},{6,22},{3,19},{7,23},{8,24},{12... | collective-permute-start | bytes 1376264 | tf_op jit(solution)/shard_map/ppermute | solution.py:87
  616.8 29.5 %collective-permute-start.61 = (bf16[400,1024]{1,0:T(8,128)(2,1)}, bf16[400,1024]{1,0:T(8,128)(2,1)}, u32[]{:S(2)}, u32[]{:S(2)}) collective-permute-start(bf16[400,1024]{1,0:T(8,128)(2,1)} %slice.853), channel_id=1, source_target_pairs={{0,4},{4,0},{1,5},{5,1},{2,6},{6,2},{3,7},{7,3},{8,12},{12,8},{9,1... | collective-permute-start | bytes 2457608 | tf_op jit(solution)/shard_map/ppermute | solution.py:87
  623.5 26.0 %collective-permute-start.65 = (bf16[64,896]{1,0:T(8,128)(2,1)}, bf16[64,896]{1,0:T(8,128)(2,1)S(1)}, u32[]{:S(2)}, u32[]{:S(2)}) collective-permute-start(bf16[64,896]{1,0:T(8,128)(2,1)} %bitcast.156), channel_id=1, source_target_pairs={{0,1},{4,5},{1,2},{5,6},{2,3},{6,7},{3,0},{7,4},{8,9},{12,13},{9,1... | collective-permute-start | bytes 344072 | tf_op jit(solution)/shard_map/ppermute | solution.py:87
  642.4 14.1 %collective-permute-start.64 = (bf16[2,2,4,32,512]{4,3,2,1,0:T(8,128)(2,1)}, bf16[2,2,4,32,512]{4,3,2,1,0:T(8,128)(2,1)}, u32[]{:S(2)}, u32[]{:S(2)}) collective-permute-start(bf16[2,2,4,32,512]{4,3,2,1,0:T(8,128)(2,1)} %fusion.33), channel_id=1, source_target_pairs={{0,16},{4,20},{1,17},{5,21},{2,18},{6,22},{3,19},{7,23},{8,24},{12... | collective-permute-start | bytes 1572872 | tf_op jit(solution)/shard_map/ppermute | solution.py:87
  (158 other events, 1683.5 us)
Sparse Core Ops, SparseCore 0:
  11.4 100.5 all-gather.2
  164.1 112.7 all-gather.4
  352.8 103.6 reduce-scatter.4
  459.3 92.0 reduce-scatter.6
  581.4 36.1 reduce-scatter.10
  645.4 25.7 reduce-scatter.8

commit v4 on v3

--- a/solution.py
+++ b/solution.py
@@ -150,88 +150,75 @@
         na, nb = self.size["a"], self.size["b"]
         keys = [(da, db) for da in range(na) for db in range(nb)]
         widths = {}
-        for _, _, size, array, column in wanted:
+        heights = {}
+        for _, _, size, array, column, *base in wanted:
             widths[array] = max(widths.get(array, 0), column + size)
-        outs = [
-            jax.ShapeDtypeStruct((self.chips * rows, widths[k]), dtype) for k in range(len(widths))
-        ]
+            heights[array] = max(heights.get(array, 0), sum(base) + self.chips * rows)
+        outs = [jax.ShapeDtypeStruct((heights[k], widths[k]), dtype) for k in range(len(widths))]
         sources = []
         for index, half in enumerate(halves):
             sources += [half[da][db] if index % 2 == 0 else half[db][da] for da, db in keys]
         plan = []
-        for half, start, size, array, column in wanted:
+        for half, start, size, array, column, *base in wanted:
             for index, (da, db) in enumerate(keys):
 
                 def source(at, start=start, size=size):
                     return pl.ds(0, rows), pl.ds(start, size)
 
-                def goal(at, da=da, db=db, column=column, size=size):
+                def goal(at, da=da, db=db, column=column, size=size, base=sum(base)):
                     chip = lax.rem(at[0] + na - da, na) * nb + lax.rem(at[1] + nb - db, nb)
-                    return pl.ds(chip * rows, rows), pl.ds(column, size)
+                    return pl.ds(base + chip * rows, rows), pl.ds(column, size)
 
                 plan.append((half * len(keys) + index, source, array, goal))
         return moved(self, sources, outs, plan)
 
-    def reduce_far(self, grads):
+    def stack_far(self, grads):
         cores = [[chip * CORES + c for chip in range(self.chips)] for c in range(CORES)]
-        groups, chips = self.size["z"], self.chips
-        rows = grads[0][0].shape[0] // chips
-        widths = [grad.shape[1] for grad, _ in grads]
-        stacked = len(set(widths)) == 1
-        high = len(grads) * rows if stacked else rows
-        wide = widths[0] if stacked else sum(widths)
-        corner = [
-            (k * rows, 0) if stacked else (0, sum(widths[:k])) for k in range(len(grads))
-        ]
-        outs = [jax.ShapeDtypeStruct((chips * high, wide), BF16)]
+        chips = self.chips
+        rows, wide = grads[0].shape[0] // chips, grads[0].shape[1]
+        high = len(grads) * rows
         plan = []
-        for k, (row, column) in enumerate(corner):
+        for k in range(len(grads)):
             for chip in range(chips):
 
-                def source(at, chip=chip, size=widths[k]):
-                    return pl.ds(chip * rows, rows), pl.ds(0, size)
-
-                def goal(at, chip=chip, row=row, column=column, size=widths[k]):
-                    return pl.ds(chip * high + row, rows), pl.ds(column, size)
+                def source(at, chip=chip):
+                    return pl.ds(chip * rows, rows), pl.ds(0, wide)
+
+                def goal(at, chip=chip, row=k * rows):
+                    return pl.ds(chip * high + row, rows), pl.ds(0, wide)
 
                 plan.append((k, source, 0, goal))
-        (flat,) = moved(self, [grad for grad, _ in grads], outs, plan)
+        (flat,) = moved(self, grads, [jax.ShapeDtypeStruct((chips * high, wide), BF16)], plan)
 
         def start(flat):
             return lax.psum_scatter(
                 flat, "ctx", scatter_dimension=0, tiled=True, axis_index_groups=cores
             )
 
-        share, deep = rows // groups, high // groups
-
-        def finish(flat):
-            plan = []
-            for k, (row, column) in enumerate(corner):
-                count = grads[k][1]
-                block = share // count
+        return flat, start
+
+    def finish_far(self, flats, counts):
+        groups, wide = self.size["z"], flats[0].shape[1]
+        height = sum(flat.shape[0] for flat in flats)
+        deep = height // groups
+        plan, to = [], 0
+        for index, (flat, ms) in enumerate(zip(flats, counts)):
+            share = flat.shape[0] // len(ms)
+            for k, count in enumerate(ms):
+                block = share // groups // count
                 for z in range(groups):
                     for m in range(count):
 
-                        def source(at, z=z, m=m, row=row, column=column, size=widths[k], block=block):
-                            return (
-                                pl.ds(row + (m * groups + z) * block, block),
-                                pl.ds(column, size),
-                            )
-
-                        def goal(
-                            at, z=z, m=m, row=row, column=column, size=widths[k], block=block
-                        ):
-                            return (
-                                pl.ds(z * deep + row // groups + m * block, block),
-                                pl.ds(column, size),
-                            )
-
-                        plan.append((0, source, 0, goal))
-            outs = [jax.ShapeDtypeStruct((high, wide), BF16)]
-            (flat,) = moved(self, [flat], outs, plan)
-            return lax.psum_scatter(flat, "sp", scatter_dimension=0, tiled=True)
-
-        return flat, start, finish
+                        def source(at, row=k * share + (m * groups + z) * block, block=block):
+                            return pl.ds(row, block), pl.ds(0, wide)
+
+                        def goal(at, row=z * deep + to + m * block, block=block):
+                            return pl.ds(row, block), pl.ds(0, wide)
+
+                        plan.append((index, source, 0, goal))
+                to += share // groups
+        (flat,) = moved(self, flats, [jax.ShapeDtypeStruct((height, wide), BF16)], plan)
+        return lax.psum_scatter(flat, "sp", scatter_dimension=0, tiled=True)
 
     def reduce(self, x, dim, axis):
         n, v = self.size[dim], self.at[dim]
@@ -354,16 +341,42 @@
     return key <= first_query + column - head * piece
 
 
-def attend_kernel(places, lengths, q_ref, kv_ref, out_ref, lse_ref, acc, top, total, *, piece):
+def stack_heads(block, high):
+    found = []
+    for head in range(Q_SHARE):
+        pair = block[:, head // 2 * LANES : (head // 2 + 1) * LANES].astype(F32)
+        if (head % 2 == 1) != high:
+            pair = pltpu.roll(pair, HD, 1)
+        lane = lax.broadcasted_iota(jnp.int32, pair.shape, 1)
+        found.append(jnp.where((lane >= HD) if high else (lane < HD), pair, 0.0))
+    return jnp.concatenate(found, axis=0).astype(BF16)
+
+
+def unstack_heads(stacked, piece, high):
+    found = []
+    for pair in range(Q_SHARE // 2):
+        first = stacked[2 * pair * piece : (2 * pair + 1) * piece]
+        second = stacked[(2 * pair + 1) * piece : (2 * pair + 2) * piece]
+        if high:
+            first = pltpu.roll(first, HD, 1)
+        else:
+            second = pltpu.roll(second, HD, 1)
+        lane = lax.broadcasted_iota(jnp.int32, first.shape, 1)
+        found.append(jnp.where(lane < HD, first, second))
+    return jnp.concatenate(found, axis=1)
+
+
+def attend_kernel(places, lengths, q_ref, kv_ref, out_ref, lse_ref, acc, top, total, held, *, piece):
     slot, which = pl.program_id(0), pl.program_id(1)
     first_query = places[which]
-    columns = q_ref.shape[2]
+    columns = held.shape[0]
     block = columns
     out_ref[...] = jnp.zeros_like(out_ref)
     lse_ref[...] = jnp.zeros_like(lse_ref)
 
     @pl.when(first_query < lengths[slot])
     def _():
+        held[...] = stack_heads(q_ref[0, 0], False)
         acc[...] = jnp.zeros_like(acc)
         top[...] = jnp.full_like(top, MASKED)
         total[...] = jnp.zeros_like(total)
@@ -372,7 +385,7 @@
         def visit(index, masked):
             start = pl.multiple_of(index * block, block)
             kv = kv_ref[0, pl.ds(start, block), :]
-            scores = mm(kv, q_ref[0, 0], NT)
+            scores = mm(kv, held[...], NT)
             if masked:
                 keep = causal_keep(start, first_query, block, piece, columns)
                 scores = jnp.where(keep, scores, MASKED)
@@ -389,30 +402,33 @@
             visit(index, False)
 
         visit(whole, True)
-        out_ref[0, 0] = (acc[...] / total[...]).T.astype(BF16)
+        out_ref[0, 0] = unstack_heads((acc[...] / total[...]).T, piece, True).astype(BF16)
         lse_ref[0, 0] = top[...] + jnp.log(total[...])
 
 
 def attend(places, lengths, queries, kv, piece):
-    slots, _, columns, width = queries.shape
-    length = kv.shape[1]
+    _, slots, _, wide = queries.shape
+    length, width = kv.shape[1:]
+    columns = Q_SHARE * piece
+    rows = pl.BlockSpec((1, 1, piece, wide), lambda s, e, *_: (e, s, 0, 0))
     return pl.pallas_call(
         functools.partial(attend_kernel, piece=piece),
         grid_spec=pltpu.PrefetchScalarGridSpec(
             num_scalar_prefetch=2,
             grid=(slots, CORES),
             in_specs=[
-                pl.BlockSpec((1, 1, columns, width), lambda s, e, *_: (s, e, 0, 0)),
+                rows,
                 pl.BlockSpec((1, length, width), lambda s, e, *_: (s, 0, 0)),
             ],
             out_specs=[
-                pl.BlockSpec((1, 1, columns, width), lambda s, e, *_: (s, e, 0, 0)),
+                rows,
                 pl.BlockSpec((1, 1, 1, columns), lambda s, e, *_: (s, e, 0, 0)),
             ],
             scratch_shapes=[
                 pltpu.VMEM((width, columns), F32),
                 pltpu.VMEM((1, columns), F32),
                 pltpu.VMEM((1, columns), F32),
+                pltpu.VMEM((columns, width), BF16),
             ],
         ),
         out_shape=[
@@ -430,7 +446,7 @@
 ):
     slot, which = pl.program_id(0), pl.program_id(1)
     first_query = places[which]
-    columns = q_ref.shape[2]
+    columns = dq.shape[1]
     block = columns
     dq_ref[...] = jnp.zeros_like(dq_ref)
 
@@ -441,9 +457,9 @@
     @pl.when(first_query < lengths[slot])
     def _():
         dq[...] = jnp.zeros_like(dq)
-        queries = q_ref[0, 0]
-        dout = dout_ref[0, 0]
-        both = dout.astype(F32) * out_ref[0, 0].astype(F32)
+        queries = stack_heads(q_ref[0, 0], False)
+        dout = stack_heads(dout_ref[0, 0], True)
+        both = dout.astype(F32) * stack_heads(out_ref[0, 0], True).astype(F32)
         delta = mm(jnp.ones((8, both.shape[1]), F32), both, NT, lax.Precision.HIGHEST)[:1]
         lse = lse_ref[0, 0]
         whole = first_query // block
@@ -467,7 +483,7 @@
             visit(index, False)
 
         visit(whole, True)
-        dq_ref[0, 0] = dq[...].T.astype(dq_ref.dtype)
+        dq_ref[0, 0] = unstack_heads(dq[...].T, piece, False)
 
     @pl.when(which == CORES - 1)
     def _():
@@ -475,9 +491,10 @@
 
 
 def attend_back(places, lengths, queries, kv, out, dout, lse, piece):
-    slots, _, columns, width = queries.shape
-    length = kv.shape[1]
-    rows = pl.BlockSpec((1, 1, columns, width), lambda s, e, *_: (s, e, 0, 0))
+    _, slots, _, wide = queries.shape
+    length, width = kv.shape[1:]
+    columns = Q_SHARE * piece
+    rows = pl.BlockSpec((1, 1, piece, wide), lambda s, e, *_: (e, s, 0, 0))
     keys = pl.BlockSpec((1, length, width), lambda s, e, *_: (s, 0, 0))
     return pl.pallas_call(
         functools.partial(attend_back_kernel, piece=piece),
@@ -515,24 +532,25 @@
     return jnp.where(lane < SHD, first, second)
 
 
-def chunk_terms(raw_ref, raw_t_ref, bias_ref, bias_t_ref, rate_ref, rate_t_ref):
-    rows = raw_ref.shape[1]
-    steps = jax.nn.softplus(raw_ref[0] + bias_ref[...])
-    steps_t = jax.nn.softplus(raw_t_ref[0] + bias_t_ref[...])
-    high = lax.Precision.HIGHEST
-    logs = mm(lower(rows).astype(F32), steps * rate_ref[...], NN, high)
-    logs_t = mm(steps_t * rate_t_ref[...], lower(rows, True).astype(F32), NN, high)
-    return steps, steps_t, logs, logs_t
+def chunk_terms(raw_ref, bias_ref, rate_ref):
+    raw = raw_ref[0].astype(F32)[HALO:] + bias_ref[...]
+    rows = raw.shape[0]
+    steps = jax.nn.softplus(raw)
+    logs = mm(lower(rows).astype(F32), steps * rate_ref[...], NN, lax.Precision.HIGHEST)
+
+    def turned(value):
+        more = jnp.zeros((2 * LANES - rows, LANES), F32)
+        return jnp.concatenate([value, more], axis=0).T[:, :rows]
+
+    return raw, steps, turned(steps), logs, turned(logs)
 
 
 def chunk_kernel(
-    f_ref, b_ref, c_ref, raw_ref, raw_t_ref, bias_ref, bias_t_ref, rate_ref, rate_t_ref, skip_ref,
+    f_ref, b_ref, c_ref, raw_ref, bias_ref, rate_ref, skip_ref,
     at_ref, out_ref, logs_ref, *rest,
 ):
     state_refs, held = rest[:-1], rest[-1]
-    steps, steps_t, logs, logs_t = chunk_terms(
-        raw_ref, raw_t_ref, bias_ref, bias_t_ref, rate_ref, rate_t_ref
-    )
+    raw, steps, steps_t, logs, logs_t = chunk_terms(raw_ref, bias_ref, rate_ref)
     logs_ref[0] = logs
     rows = logs.shape[0]
     inject = b_ref[0]
@@ -591,7 +609,7 @@
 
 
 def chunk_back_kernel(
-    f_ref, b_ref, c_ref, raw_ref, raw_t_ref, bias_ref, bias_t_ref, rate_ref, rate_t_ref, skip_ref,
+    f_ref, b_ref, c_ref, raw_ref, bias_ref, rate_ref, skip_ref,
     d_ref, *rest,
 ):
     groups = (len(rest) - 10) // 2
@@ -600,9 +618,7 @@
     columns, row_sums, states, laters = rest[2 * groups + 6 :]
     take_groups(states, rest[:groups], at_ref)
     take_groups(laters, rest[groups : 2 * groups], at_ref)
-    steps, steps_t, logs, logs_t = chunk_terms(
-        raw_ref, raw_t_ref, bias_ref, bias_t_ref, rate_ref, rate_t_ref
-    )
+    raw, steps, steps_t, logs, logs_t = chunk_terms(raw_ref, bias_ref, rate_ref)
     rows = logs.shape[0]
     inject, readout = b_ref[0], c_ref[0]
     keep = lower(rows)
@@ -687,7 +703,7 @@
     dlogs = dlogs + jnp.where(last, end, 0.0)
     summed = mm(lower(rows, True).astype(F32), dlogs, NN, lax.Precision.HIGHEST)
     dsteps = direct + push + summed * rate_ref[...]
-    draw = dsteps * jax.nn.sigmoid(raw_ref[0] + bias_ref[...])
+    draw = dsteps * jax.nn.sigmoid(raw)
     draw_ref[0] = draw
     line = lax.broadcasted_iota(jnp.int32, (8, LANES), 0)
     dbias = jnp.sum(draw, axis=0, keepdims=True)
@@ -695,6 +711,30 @@
     sums_ref[0] = jnp.where(
         line == 0, dbias, jnp.where(line == 1, dlog, jnp.where(line == 2, skips, 0.0))
     )
+
+
+def conv_back_kernel(mixed_ref, df_ref, dshared_ref, taps_ref, shift_ref, _, dmixed_ref, sums_ref):
+    mixed = mixed_ref[0].astype(F32)
+    rows = df_ref.shape[1]
+    first = HALO - KC + 1
+    pre = shift_ref[...]
+    for tap in range(KC):
+        pre = pre + taps_ref[tap : tap + 1, :] * mixed[first + tap : first + tap + rows]
+    gate = jax.nn.sigmoid(pre)
+    slope = gate + pre * gate * (1.0 - gate)
+    dpre = jnp.concatenate([df_ref[0], dshared_ref[0]], axis=1) * slope
+    line = lax.broadcasted_iota(jnp.int32, (8, dpre.shape[1]), 0)
+    sums = jnp.where(line == KC, jnp.sum(dpre, axis=0, keepdims=True), 0.0)
+    none = jnp.zeros((HALO, dpre.shape[1]), F32)
+    padded = jnp.concatenate([none, dpre, none], axis=0)
+    total = jnp.zeros(mixed.shape, F32)
+    for tap in range(KC):
+        seen = mixed[first + tap : first + tap + rows]
+        sums = sums + jnp.where(line == tap, jnp.sum(dpre * seen, axis=0, keepdims=True), 0.0)
+        start = HALO - first - tap
+        total = total + taps_ref[tap : tap + 1, :] * padded[start : start + rows + HALO]
+    dmixed_ref[0] = total.astype(BF16)
+    sums_ref[0] = sums
 
 
 def over_pieces(kernel, name, args, whole, outs, micros, at, scratch=()):
@@ -1027,7 +1067,6 @@
     linear = body_rows(mm(normed, w_a[:, :lin_cols]))
     mixed = mm(normed, w_b).astype(BF16).reshape(CORES, slots, piece + HALO, c_cols)
     step_raw = mm(normed, w_a[:, tail_at:]).astype(BF16)
-    step_raw = body_rows(step_raw[:, :M_SHARE]).astype(F32)
 
     def rows_plan(source, start, pieces_of):
         found = []
@@ -1094,36 +1133,25 @@
     kv_size = jax.ShapeDtypeStruct((CORES * groups * piece, 2 * HD), BF16)
     kv = moved(place, kv_parts, [kv_size] * slots, plan)
     kv = place.plane_first(kv)
-    def by_heads(value, before, after):
-        value = jnp.transpose(value, (1, 0, 3, 2, 4)).reshape(slots, CORES, Q_SHARE * piece, HD)
-        return jnp.pad(value, ((0, 0), (0, 0), (0, 0), (before, after)))
-
-    def from_heads(value):
-        value = value.reshape(slots, CORES, Q_SHARE, piece, HD)
-        return jnp.transpose(value, (1, 0, 3, 2, 4))
-
     scale = HD ** (-0.5)
-    queries = by_heads(queries * jnp.asarray(scale, BF16), 0, HD)
+    queries = (queries * jnp.asarray(scale, BF16)).reshape(CORES, slots, piece, q_cols)
     pre = shift
     for tap in range(KC):
         first = HALO - KC + 1 + tap
         pre = pre + taps[tap] * mixed[:, :, first : first + piece].astype(F32)
-    conv_out, conv_slope = silu_and_slope(pre)
-    conv_out = conv_out.astype(BF16)
+    conv_out = jax.nn.silu(pre).astype(BF16)
     features = conv_out[..., :m_cols].reshape(CORES * slots, piece, m_cols)
     shared = conv_out[..., m_cols:]
     shared_other = place.swap(shared)[::-1]
     inject = place.by_core(shared, shared_other).reshape(CORES * slots, piece, NS)
     readout = place.by_core(shared_other, shared).reshape(CORES * slots, piece, NS)
-    raw = jnp.pad(step_raw.reshape(CORES * slots, piece, M_SHARE), ((0, 0), (0, 0), (0, LANES - M_SHARE)))
-    raw_t = jnp.transpose(raw[..., :16], (0, 2, 1))
+    raw = step_raw.reshape(CORES * slots, piece + HALO, ms_cols)
     bias_row = jnp.pad(bias, (0, LANES - M_SHARE))[None]
     rate_row = jnp.pad(rates, (0, LANES - M_SHARE))[None]
-    bias_col, rate_col = bias_row[0, :16, None], rate_row[0, :16, None]
     skip_row = jnp.repeat(skip, SHD)[None]
     pieces = CORES * slots
     chunk_args = [
-        features, inject, readout, raw, raw_t, bias_row, bias_col, rate_row, rate_col, skip_row,
+        features, inject, readout, raw, bias_row, rate_row, skip_row,
     ]
     share_rows = m_cols // groups
     held = pltpu.VMEM((groups, share_rows, NS), BF16)
@@ -1132,7 +1160,7 @@
         chunk_kernel,
         "chunk",
         chunk_args,
-        range(5, 10),
+        range(4, 7),
         [
             ((pieces, piece, m_cols), F32),
             ((pieces, piece, LANES), F32),
@@ -1163,7 +1191,11 @@
         place, at, local, None, None, False, before_states, between_states, after_states
     )
     queries = held_back["queries"]
-    kv = place.plane_third(held_back["kv"], [(s, 0, 2 * HD, s, 0) for s in range(slots)])
+    rows = chips * CORES * groups * piece
+    (kv,) = place.plane_third(
+        held_back["kv"], [(s, 0, 2 * HD, 0, 0, s * rows) for s in range(slots)]
+    )
+    kv = kv.reshape(slots, rows, 2 * HD)
     ff_whole = held_back["ff"]
     w_gate, w_up, w_down = moved(
         place,
@@ -1181,14 +1213,8 @@
         ),
     )
 
-    heads_out, lse = zip(
-        *[
-            attend(pieces_at, lengths[s : s + 1], queries[s : s + 1], kv[s][None], piece)
-            for s in range(slots)
-        ]
-    )
-    attended = from_heads(jnp.concatenate(heads_out)[..., HD:]).reshape(rows_all, q_cols)
-
+    heads_out, lse = attend(pieces_at, lengths, queries, kv, piece)
+    attended = heads_out.reshape(rows_all, q_cols)
     attended, state_in = tie(attended, state_in)
     (ssd,) = over_pieces(
         carry_kernel,
@@ -1271,11 +1297,11 @@
     )
     direct = [part.reshape(CORES, slots, share_rows, NS) for part in direct]
     dgate, dup, hidden, direct = tie(dgate, dup, hidden, direct)
-    ff_grads, ff_start, ff_finish = place.reduce_far(
+    ff_grads, ff_start = place.stack_far(
         [
-            (mm(post, dgate, TN).astype(BF16), 2),
-            (mm(post, dup, TN).astype(BF16), 2),
-            (own_parity(mm(hidden, dy, TN)), 1),
+            mm(post, dgate, TN).astype(BF16),
+            mm(post, dup, TN).astype(BF16),
+            own_parity(mm(hidden, dy, TN)),
         ]
     )
     out_side = {}
@@ -1294,11 +1320,9 @@
             ],
             axis=1,
         )
-        mid_grads, mid_start, out_side["finish"] = place.reduce_far(
-            [
-                (own_parity(grad_outs), 1),
-                (mm(normed, out_side["dz"], TN).astype(BF16), 2),
-            ]
+        wide_dz = jnp.pad(out_side["dz"], ((0, 0), (0, width - m_cols)))
+        mid_grads, mid_start = place.stack_far(
+            [own_parity(grad_outs), mm(normed, wide_dz, TN).astype(BF16)]
         )
         totals, mid_grads = tie(totals, mid_grads)
         out_side["mid"] = mid_start(mid_grads)
@@ -1311,29 +1335,20 @@
     later, _, _ = carried(
         place, at, direct, marks, fades, True, before_scan, between_scans, after_scans
     )
-    ff_grads, mid_grads, mid_finish = out_side["ff"], out_side["mid"], out_side["finish"]
+    ff_grads, mid_grads = out_side["ff"], out_side["mid"]
     dattended = out_side["dattended"]
     dnormed = mm(out_side["dz"], w_z, NT)
 
-    dout = by_heads(
-        dattended.reshape(CORES, slots, piece, Q_SHARE, HD), HD, 0
-    )
-    dqueries, dkv = zip(
-        *[
-            attend_back(
-                pieces_at,
-                lengths[s : s + 1],
-                queries[s : s + 1],
-                kv[s][None],
-                heads_out[s],
-                dout[s : s + 1],
-                lse[s],
-                piece,
-            )
-            for s in range(slots)
-        ]
-    )
-    dqueries = jnp.concatenate(dqueries)
+    dqueries, dkv = attend_back(
+        pieces_at,
+        lengths,
+        queries,
+        kv,
+        heads_out,
+        dattended.reshape(heads_out.shape),
+        lse,
+        piece,
+    )
     dkv, later = tie(dkv, later)
     dkv = [
         place.reduce_first(dkv[s].reshape(na, nb, CORES, groups, piece, 2 * HD), s % 2 == 0)
@@ -1344,7 +1359,7 @@
         chunk_back_kernel,
         "chunk_back",
         chunk_args + [dssd, *state_in, *later],
-        range(5, 10),
+        range(4, 7),
         [
             ((pieces, piece, m_cols), F32),
             ((pieces, piece, NS), F32),
@@ -1363,19 +1378,23 @@
     dshared = place.by_core(dinject, dreadout) + place.swap(
         place.by_core(dreadout, dinject).astype(BF16)
     )[::-1].astype(F32)
-    dconv = jnp.concatenate([dfeatures.reshape(CORES, slots, piece, m_cols), dshared], axis=-1)
-    dpre = dconv * conv_slope
-    grad_taps = []
-    dmixed = jnp.zeros((CORES, slots, piece + HALO, c_cols), F32)
-    for tap in range(KC):
-        first = HALO - KC + 1 + tap
-        seen = mixed[:, :, first : first + piece].astype(F32)
-        grad_taps.append(jnp.sum(dpre * seen, axis=(0, 1, 2)))
-        dmixed = dmixed + jnp.pad(
-            dpre * taps[tap], ((0, 0), (0, 0), (first, KC - 1 - tap), (0, 0))
-        )
-    grad_shift = jnp.sum(dpre, axis=(0, 1, 2))
-    dmixed = dmixed.astype(BF16)
+    dmixed, conv_sums = over_pieces(
+        conv_back_kernel,
+        "conv_back",
+        [
+            mixed.reshape(pieces, piece + HALO, c_cols),
+            dfeatures,
+            dshared.reshape(pieces, piece, NS),
+            taps,
+            shift[None],
+        ],
+        range(3, 5),
+        [((pieces, piece + HALO, c_cols), BF16), ((pieces, 8, c_cols), F32)],
+        6,
+        at,
+    )
+    conv_sums = jnp.sum(conv_sums, axis=0)
+    grad_taps, grad_shift = conv_sums[:KC], conv_sums[KC]
 
     def by_columns(grad):
         return grad.reshape(na, nb, CORES, groups, shard_rows, grad.shape[-1])
@@ -1386,15 +1405,16 @@
     dkv, db_low = tie(dkv, db_low)
     grad_b = place.reduce_first(by_columns(mm(normed, db_low, TN)), False)
     dkv_own = place.reduce_z(dkv)
-    ff_grads, db_late = tie(ff_grads, db_low)
-    ff_grads = ff_finish(ff_grads)
-    dnormed = dnormed + mm(db_late, w_b, NT)
+    dnormed = dnormed + mm(db_low, w_b, NT)
     head_sums = place.sum_along(jnp.sum(sums, axis=0)[:3, :M_SHARE], "z")
-    dkv_own, grad_b, dnormed, head_sums = tie(dkv_own, grad_b, dnormed, head_sums)
+    dkv_own, grad_b, dnormed, head_sums, ff_grads, mid_grads = tie(
+        dkv_own, grad_b, dnormed, head_sums, ff_grads, mid_grads
+    )
+    far_grads = place.finish_far([ff_grads, mid_grads], [[2, 2, 1], [1, 2]])
     dkv_own = jnp.stack([part.reshape(CORES, piece, 2 * HD) for part in dkv_own], axis=1)
     dkv_own = place.by_core(dkv_own, dkv_own[::-1])
     grad_b = place.reduce_second(grad_b, False)
-    dq_rows = from_heads(dqueries[..., :HD] * scale)
+    dq_rows = (dqueries * scale).reshape(CORES, slots, piece, Q_SHARE, HD)
     dq_rows = rotate(dq_rows, cos_part, -sin_part).reshape(CORES, slots, piece, q_cols)
     dk_rows = rotate(dkv_own[..., None, :HD], cos_part, -sin_part)[..., 0, :]
     tail_zeros = jnp.zeros((CORES, slots, piece, ms_cols - M_SHARE), BF16)
@@ -1433,7 +1453,7 @@
     grad_mixer_gain = jnp.concatenate(
         [place.by_core(grad_mixer_gain, zero_half), place.by_core(zero_half, grad_mixer_gain)]
     )
-    grad_taps = conv_whole(jnp.stack(grad_taps)).reshape(KC, devices, -1)
+    grad_taps = conv_whole(grad_taps).reshape(KC, devices, -1)
     vector_grads = jnp.concatenate(
         [
             grad_input_gain.reshape(devices, -1),
@@ -1452,8 +1472,7 @@
         vector_grads,
         ((0, 0), (tail_at + small_at, a_cols - tail_at - small_at - small_cols)),
     )
-    mid_grads, grad_a, grad_b = tie(mid_grads, grad_a, grad_b)
-    mid_grads = mid_finish(mid_grads)
+    grad_a, grad_b = tie(grad_a, grad_b)
     grad_b = place.reduce_z([grad_b])[0]
     grad_a = place.reduce_first(by_columns(grad_a), True)
     head_sums = place.sum_along(head_sums, "b")
@@ -1474,15 +1493,17 @@
         got = place.swap(lax.dynamic_index_in_dim(columns, 1 - core, 0, False))
         return place.by_core(kept, got), place.by_core(got, kept)
 
-    ff_rows_each = ff_grads.shape[0] // 3
-    both = between_cores(
-        jnp.concatenate([ff_grads[:ff_rows_each], ff_grads[ff_rows_each : 2 * ff_rows_each]], axis=1)
-    )
+    part = far_grads.shape[0] // 5
+    far_grads = [far_grads[k * part : (k + 1) * part] for k in range(5)]
+    both = between_cores(jnp.concatenate([far_grads[0], far_grads[1], far_grads[4]], axis=1))
     grad_gate = jnp.concatenate([half[:, :ff_half] for half in both], axis=1).astype(F32)
-    grad_up = jnp.concatenate([half[:, ff_half:] for half in both], axis=1).astype(F32)
-    grad_down = ff_grads[2 * ff_rows_each :].astype(F32)
-    grad_outs = mid_grads[:, :width].astype(F32)
-    grad_zgate = jnp.concatenate(between_cores(mid_grads[:, width:]), axis=1).astype(F32)
+    grad_up = jnp.concatenate([half[:, ff_half : 2 * ff_half] for half in both], axis=1)
+    grad_up = grad_up.astype(F32)
+    grad_down = far_grads[2].astype(F32)
+    grad_outs = far_grads[3].astype(F32)
+    grad_zgate = jnp.concatenate(
+        [half[:, 2 * ff_half : 2 * ff_half + m_cols] for half in both], axis=1
+    ).astype(F32)
     conv_first, conv_second = between_cores(grad_b)
     first, second = between_cores(grad_a)
 

time: 695 us -> 637 us (0.917); the launches traced: 699 us -> 624 us
  starting transfers between devices: 170 us -> 117 us
  waiting for transfers between devices: 112 us -> 143 us
  other arithmetic: 97.2 us -> 70.8 us
  local copies, waits for them, and re-layouts: 97.8 us -> 78.3 us
    ppermute x6, starting transfers between devices: 36.9 us -> 10.4 us  [carried(): lax.ppermute(leaving, AXES, place.chip_pairs(k))]
    ppermute x67 -> x66, starting transfers between devices: 122 us -> 97 us  [shift(): return lax.ppermute(x, AXES, self.pairs(dim, by))]
    ppermute x67 -> x66, waiting for transfers between devices: 76.8 us -> 93.5 us  [shift(): return lax.ppermute(x, AXES, self.pairs(dim, by))]
    ppermute x6, waiting for transfers between devices: 23.7 us -> 32.5 us  [carried(): lax.ppermute(leaving, AXES, place.chip_pairs(k))]
    all_gather x1, waiting for transfers between devices: 0.91 us -> 9.09 us  [before_states(): held_back['ff'] = lax.all_gather(columns, AXES, axis=0, tiled=True)]
    pallas_call x4 -> x5, Pallas kernels: 47.9 us -> 54.6 us  [over_pieces(): pl.pallas_call(kernel, grid=(pieces,), in_specs=[spec(shape, split) for s...]
    pallas_call x2 -> x1, Pallas kernels: 22 us -> 17.1 us  [attend_back(): pl.pallas_call(functools.partial(attend_back_kernel, piece=piece), grid_s...]
    pallas_call x2 -> x1, Pallas kernels: 15.9 us -> 12.3 us  [attend(): pl.pallas_call(functools.partial(attend_kernel, piece=piece), grid_spec=p...]
  transfers between devices with their start and end apart: 85 -> 83, of which waited for: 27 -> 31; matrix products, arithmetic and copies ran while one was open for 31% -> 26% of each run, Pallas kernels for 18% -> 19%
where the time goes in v4:
time: 637 us; the launch traced here: 624 us
  waiting for transfers between devices  143 us (22%)
  Pallas kernels  137 us (22%)
  starting transfers between devices  117 us (18%)
  local copies, waits for them, and re-layouts  78.3 us (12%)
  other arithmetic  70.8 us (11%)
  matrix products  61.6 us (10%)
  between operations  16.5 us (3%)
    ppermute x66, starting transfers between devices, shift(): return lax.ppermute(x, AXES, self.pairs(dim, by))  97 us
    ppermute x66, waiting for transfers between devices, shift(): return lax.ppermute(x, AXES, self.pairs(dim, by))  93.5 us
    dot_general x25, matrix products, mm(): lax.dot_general(left, right, dims, precision=precision, preferred_element...  61.6 us
    pallas_call x5, Pallas kernels, over_pieces(): pl.pallas_call(kernel, grid=(pieces,), in_specs=[spec(shape, split) for s...  54.6 us
    pallas_call x9, Pallas kernels, moved(): pl.pallas_call(functools.partial(moved_kernel, plan=plan, count=len(sourc...  41.1 us
    ppermute x6, waiting for transfers between devices, carried(): lax.ppermute(leaving, AXES, place.chip_pairs(k))  32.5 us
    pallas_call x1, Pallas kernels, attend_back(): pl.pallas_call(functools.partial(attend_back_kernel, piece=piece), grid_s...  17.1 us
    unnamed x247, local copies, waits for them, and re-layouts  16.2 us
  transfers between devices with their start and end apart: 83, of which 31 were waited for; matrix products, arithmetic and copies ran while one was open for 26% of the time, Pallas kernels for 19%

profile of v4, /device:TPU:0, one launch (start us, length us, event | category | flops | bytes accessed | tf_op | source)
XLA Modules:
  0.0 624.4 jit_solution(10778217175133340169)
XLA Ops:
  17.1 4.5 collective-permute-start
  28.3 6.0 collective-permute-done.3.refs_1_
  34.3 8.5 %collective-permute-done.4.refs_2_ = bf16[64,1408]{1,0:T(8,128)(2,1)S(1)} collective-permute-done((bf16[64,1408]{1,0:T(8,128)(2,1)S(1)}, bf16[64,1408]{1,0:T(8,128)(2,1)S(1)}, u32[]{:S(2)}, u32[]{:S(2)}) %collective-permute-start.4) | collective-permute-done | bytes 180256 | tf_op jit(solution)/shard_map/ppermute | solution.py:87
  51.4 11.7 %collective-permute-done.10.refs_6_ = bf16[256,896]{1,0:T(8,128)(2,1)S(1)} collective-permute-done((bf16[256,896]{1,0:T(8,128)(2,1)}, bf16[256,896]{1,0:T(8,128)(2,1)S(1)}, u32[]{:S(2)}, u32[]{:S(2)}) %collective-permute-start.10) | collective-permute-done | bytes 458784 | tf_op jit(solution)/shard_map/ppermute | solution.py:87
  70.8 8.2 %collective-permute-done.7.refs_2_ = bf16[256,512]{1,0:T(8,128)(2,1)} collective-permute-done((bf16[256,512]{1,0:T(8,128)(2,1)}, bf16[256,512]{1,0:T(8,128)(2,1)}, u32[]{:S(2)}, u32[]{:S(2)}) %collective-permute-start.7) | collective-permute-done | bytes 262176 | tf_op jit(solution)/shard_map/ppermute | solution.py:87
  79.0 9.7 %collective-permute-done.8.refs_3_ = bf16[256,512]{1,0:T(8,128)(2,1)} collective-permute-done((bf16[256,512]{1,0:T(8,128)(2,1)}, bf16[256,512]{1,0:T(8,128)(2,1)}, u32[]{:S(2)}, u32[]{:S(2)}) %collective-permute-start.8) | collective-permute-done | bytes 262176 | tf_op jit(solution)/shard_map/ppermute | solution.py:87
  90.5 4.1 moved.10
  131.0 9.3 %chunk.1 = (f32[4,192,768]{2,1,0:T(8,128)}, f32[4,192,128]{2,1,0:T(8,128)}, bf16[4,208,128]{2,1,0:T(8,128)(2,1)}, bf16[4,208,128]{2,1,0:T(8,128)(2,1)}, bf16[4,2...) custom-call(bf16[4,192,768]{2,1,0:T(8,128)(2,1)} %bitcast.383, bf16[4,192,128]{2,1,0:T(8,128)(2,1)} %bitcast.422, ...), custom_call_target="tpu_custom_call" | custom-call | flops 10350000128 | tf_op jit(solution)/shard_map/chunk/pallas_call | solution.py:749
  145.3 5.3 collective-permute-done.13.refs_1_.refs_5_
  150.6 8.1 %collective-permute-done.14.refs_2_.refs_6_ = bf16[2,2,208,128]{3,2,1,0:T(8,128)(2,1)S(1)} collective-permute-done((bf16[2,2,208,128]{3,2,1,0:T(8,128)(2,1)}, bf16[2,2,208,128]{3,2,1,0:T(8,128)(2,1)S(1)}, u32[]{:S(2)}, u32[]{:S(2)}) %collective-permute-start.14) | collective-permute-done | bytes 213024 | tf_op jit(solution)/shard_map/ppermute | solution.py:87
  167.5 17.6 %collective-permute-done.21.refs_8_.refs_11_ = bf16[2,208,128]{2,1,0:T(8,128)(2,1)} collective-permute-done((bf16[2,208,128]{2,1,0:T(8,128)(2,1)}, bf16[2,208,128]{2,1,0:T(8,128)(2,1)}, u32[]{:S(2)}, u32[]{:S(2)}) %collective-permute-start.21) | collective-permute-done | bytes 106528 | tf_op jit(solution)/shard_map/ppermute | solution.py:907
  191.9 4.8 collective-permute-done.23.refs_10_.refs_13_
  201.4 7.1 %collective-permute-start.28 = (bf16[2,2,192,128]{3,2,1,0:T(8,128)(2,1)}, bf16[2,2,192,128]{3,2,1,0:T(8,128)(2,1)S(1)}, u32[]{:S(2)}, u32[]{:S(2)}) collective-permute-start(bf16[2,2,192,128]{3,2,1,0:T(8,128)(2,1)} %get-tuple-element.178), channel_id=1, source_target_pairs={{0,1},{4,5},{1,2},{5,6},{2,3},{6,7},{3,0},{7,4},{8,9},{12,13},{9,1... | collective-permute-start | bytes 589832 | tf_op jit(solution)/shard_map/ppermute | solution.py:87
  210.9 4.3 moved.12
  215.1 12.3 %attend.1 = (bf16[2,2,192,256]{3,2,1,0:T(8,128)(2,1)}, f32[2,2,1,768]{3,2,1,0:T(1,128)}) custom-call(s32[2]{0:T(128)} %copy-done.88, s32[2]{0:T(128)} %lengths.3, bf16[2,2,192,256]{3,2,1,0:T(8,128)(2,1)} %copy.98.q_ref, bf16[2,6144,128]{2,1,0:T(8,128)(2,1)} %bitcast.352), custom_call_target="tpu_custom_call" | custom-call | flops 23000000512 | tf_op jit(solution)/shard_map/attend/pallas_call | solution.py:414
  228.3 5.0 carry.1
  233.3 5.0 moved.13
  262.8 9.1 %all-gather.5.cloned.1.call-done.refs_0_ = bf16[1024,6144]{1,0:T(8,128)(2,1)} async-done(((bf16[32,6144]{1,0:T(8,128)(2,1)}), bf16[1024,6144]{1,0:T(8,128)(2,1)}) %all-gather.5.cloned.1.call-update) | async-done | bytes 12582928 | tf_op jit(solution)/shard_map/all_gather | solution.py:1178
  271.9 6.5 %moved.14 = (bf16[1024,1024]{1,0:T(8,128)(2,1)}, bf16[1024,1024]{1,0:T(8,128)(2,1)}, bf16[1024,1024]{1,0:T(8,128)(2,1)}) custom-call(s32[5]{0:T(128)} %stack.97.at_ref.rest_4_.rest_8_._, bf16[1024,6144]{1,0:T(8,128)(2,1)} %all-gather.5.cloned.1.call-done.refs_0_), custom_call_target="tpu_custom_call" | custom-call | bytes 12582912 | tf_op jit(solution)/shard_map/moved/pallas_call | solution.py:292
  278.4 3.5 fusion.69
  284.1 3.3 multiply_convert_fusion.2
  300.2 4.5 fusion.49
  307.1 3.5 multiply_reduce_fusion.2
  311.8 3.9 fusion.4
  315.7 5.5 direct.1
  329.2 5.0 convolution_convert_fusion.2.refs_1_
  334.3 3.3 convolution_convert_fusion.3.refs_0_
  339.2 6.2 moved.15
  356.2 5.0 collective-permute-start.44
  361.9 5.0 collective-permute-done.43.refs_8_
  374.5 3.1 fusion.72
  377.6 3.7 convolution_convert_fusion.refs_1_
  383.0 5.1 moved.16
  388.1 3.1 scan.7
  396.4 17.1 %attend_back.1 = (f32[2,2,192,256]{3,2,1,0:T(8,128)}, bf16[2,6144,128]{2,1,0:T(8,128)(2,1)}) custom-call(s32[2]{0:T(128)} %copy-done.88, s32[2]{0:T(128)} %lengths.3, bf16[2,2,192,256]{3,2,1,0:T(8,128)(2,1)} %copy.98.q_ref, bf16[2,6144,128]{2,1,0:T(8,128)(2,1)} %bitcast.353, bf16[2,2,192,256]{3,2,1,0:T(8,128)(2,1)} %get-tuple-element.176.out_ref, ...), custom_call_target="tpu_custom_call" | custom-call | flops 28750000128 | tf_op jit(solution)/shard_map/attend_back/pallas_call | solution.py:499
  420.3 11.2 %collective-permute-start.51 = (bf16[2,2,4,192,128]{4,3,2,1,0:T(8,128)(2,1)}, bf16[2,2,4,192,128]{4,3,2,1,0:T(8,128)(2,1)}, u32[]{:S(2)}, u32[]{:S(2)}) collective-permute-start(bf16[2,2,4,192,128]{4,3,2,1,0:T(8,128)(2,1)} %dynamic-slice_bitcast_fusion.2), channel_id=1, source_target_pairs={{0,8},{4,12},{1,9},{5,13},{2,10},{6,14},{3,11},{7,15},{8,0},{12,4}... | collective-permute-start | bytes 2359304 | tf_op jit(solution)/shard_map/ppermute | solution.py:87
  432.4 5.5 collective-permute-start.50
  438.0 26.5 %chunk_back.1 = (f32[4,192,768]{2,1,0:T(8,128)}, f32[4,192,128]{2,1,0:T(8,128)}, f32[4,192,128]{2,1,0:T(8,128)}, f32[4,192,128]{2,1,0:T(8,128)}, f32[4,8,128]{2,1,0:T(8,128)}) custom-call(bf16[4,192,768]{2,1,0:T(8,128)(2,1)} %bitcast.384, bf16[4,192,128]{2,1,0:T(8,128)(2,1)} %bitcast.423, bf16[4,192,128]{2,1,0:T(8,128)(2,1)} %bitcast.421, ...), custom_call_target="tpu_custom_call" | custom-call | flops 32199999488 | tf_op jit(solution)/shard_map/chunk_back/pallas_call | solution.py:749
  468.6 3.6 collective-permute-done.59
  482.7 8.3 %conv_back.1 = (bf16[4,200,896]{2,1,0:T(8,128)(2,1)}, f32[4,8,896]{2,1,0:T(8,128)}) custom-call(bf16[4,200,896]{2,1,0:T(8,128)(2,1)} %bitcast.323, f32[4,192,768]{2,1,0:T(8,128)} %get-tuple-element.238.df_ref, f32[4,192,128]{2,1,0:T(8,128)} %bitcast.408, f32[4,896]{1,0:T(4,128)} %copy-done.74, f32[1,896]{1,0:T(1,128)} %broadcast_select_fusion.9.shift_ref, ...), custom_call_target="tpu_custom_call" | custom-call | flops 6899999744 | tf_op jit(solution)/shard_map/conv_back/pallas_call | solution.py:749
  514.3 3.7 convolution_add_fusion.2
  518.8 5.5 collective-permute-done.56
  528.7 4.2 moved.17
  542.6 4.8 multiply_reduce_fusion
  566.7 8.4 %collective-permute-done.66 = bf16[64,896]{1,0:T(8,128)(2,1)S(1)} collective-permute-done((bf16[64,896]{1,0:T(8,128)(2,1)S(1)}, bf16[64,896]{1,0:T(8,128)(2,1)S(1)}, u32[]{:S(2)}, u32[]{:S(2)}) %collective-permute-start.66) | collective-permute-done | bytes 114720 | tf_op jit(solution)/shard_map/ppermute | solution.py:87
  582.8 5.9 collective-permute-done.69
  588.9 10.6 %collective-permute-start.71 = (bf16[64,512]{1,0:T(8,128)(2,1)S(1)}, bf16[64,512]{1,0:T(8,128)(2,1)S(1)}, u32[]{:S(2)}, u32[]{:S(2)}) collective-permute-start(bf16[64,512]{1,0:T(8,128)(2,1)S(1)} %bitcast.430), channel_id=1, source_target_pairs={{0,1},{4,5},{1,2},{5,6},{2,3},{6,7},{3,0},{7,4},{8,9},{12,13},{9,1... | collective-permute-start | bytes 196616 | tf_op jit(solution)/shard_map/ppermute | solution.py:87
  602.2 3.7 collective-permute-done.72
  (668 shorter events, 277.9 us)
Async XLA Ops:
  7.2 226.0 %all-gather.3.cloned.1.call-start = ((), (), s32[]{:S(2)}) async-start(), calls=%async_computation.3 | async-start | bytes 7569408 | tf_op jit(solution)/shard_map/all_gather | solution.py:1025
  10.1 261.9 %all-gather.5.cloned.1.call-start = ((), (), s32[]{:S(2)}) async-start(), calls=%async_computation.4 | async-start | bytes 12976128 | tf_op jit(solution)/shard_map/all_gather | solution.py:1178
  23.4 19.4 %collective-permute-start.4 = (bf16[64,1408]{1,0:T(8,128)(2,1)S(1)}, bf16[64,1408]{1,0:T(8,128)(2,1)S(1)}, u32[]{:S(2)}, u32[]{:S(2)}) collective-permute-start(bf16[64,1408]{1,0:T(8,128)(2,1)S(1)} %pad_maximum_fusion.19.refs_0_), channel_id=1, source_target_pairs={{0,2},{4,6},{1,3},{5,7},{2,0},{6,4},{3,1},{7,5},{8,10},{12,14},{9,... | collective-permute-start | bytes 540680 | tf_op jit(solution)/shard_map/ppermute | solution.py:87
  24.5 18.3 %collective-permute-start.5 = (bf16[64,1408]{1,0:T(8,128)(2,1)S(1)}, bf16[64,1408]{1,0:T(8,128)(2,1)S(1)}, u32[]{:S(2)}, u32[]{:S(2)}) collective-permute-start(bf16[64,1408]{1,0:T(8,128)(2,1)S(1)} %pad_maximum_fusion.19.refs_0_), channel_id=1, source_target_pairs={{0,3},{4,7},{1,0},{5,4},{2,1},{6,5},{3,2},{7,6},{8,11},{12,15},{9,... | collective-permute-start | bytes 540680 | tf_op jit(solution)/shard_map/ppermute | solution.py:87
  27.5 42.7 %collective-permute-start.1 = (bf16[2,200,1024]{2,1,0:T(8,128)(2,1)S(1)}, bf16[2,200,1024]{2,1,0:T(8,128)(2,1)S(1)}, u32[]{:S(2)}, u32[]{:S(2)}) collective-permute-start(bf16[2,200,1024]{2,1,0:T(8,128)(2,1)S(1)} %get-tuple-element.380), channel_id=1, source_target_pairs={{0,4},{4,0},{1,5},{5,1},{2,6},{6,2},{3,7},{7,3},{8,12},{12,8},{9,1... | collective-permute-start | bytes 2457608 | tf_op jit(solution)/shard_map/ppermute | solution.py:87
  47.0 16.1 %collective-permute-start.10 = (bf16[256,896]{1,0:T(8,128)(2,1)}, bf16[256,896]{1,0:T(8,128)(2,1)S(1)}, u32[]{:S(2)}, u32[]{:S(2)}) collective-permute-start(bf16[256,896]{1,0:T(8,128)(2,1)} %get-tuple-element.143.refs_4_), channel_id=1, source_target_pairs={{0,16},{4,20},{1,17},{5,21},{2,18},{6,22},{3,19},{7,23},{8,24},{12... | collective-permute-start | bytes 1376264 | tf_op jit(solution)/shard_map/ppermute | solution.py:87
  49.4 20.4 %collective-permute-start.6 = (bf16[256,512]{1,0:T(8,128)(2,1)}, bf16[256,512]{1,0:T(8,128)(2,1)}, u32[]{:S(2)}, u32[]{:S(2)}) collective-permute-start(bf16[256,512]{1,0:T(8,128)(2,1)} %get-tuple-element.142.refs_0_), channel_id=1, source_target_pairs={{0,8},{4,12},{1,9},{5,13},{2,10},{6,14},{3,11},{7,15},{8,0},{12,4}... | collective-permute-start | bytes 786440 | tf_op jit(solution)/shard_map/ppermute | solution.py:87
  50.8 28.2 %collective-permute-start.9 = (bf16[256,896]{1,0:T(8,128)(2,1)}, bf16[256,896]{1,0:T(8,128)(2,1)}, u32[]{:S(2)}, u32[]{:S(2)}) collective-permute-start(bf16[256,896]{1,0:T(8,128)(2,1)} %get-tuple-element.143.refs_4_), channel_id=1, source_target_pairs={{0,8},{4,12},{1,9},{5,13},{2,10},{6,14},{3,11},{7,15},{8,0},{12,4}... | collective-permute-start | bytes 1376264 | tf_op jit(solution)/shard_map/ppermute | solution.py:87
  63.1 27.4 %collective-permute-start.11 = (bf16[256,896]{1,0:T(8,128)(2,1)S(1)}, bf16[256,896]{1,0:T(8,128)(2,1)}, u32[]{:S(2)}, u32[]{:S(2)}) collective-permute-start(bf16[256,896]{1,0:T(8,128)(2,1)S(1)} %collective-permute-done.10.refs_6_), channel_id=1, source_target_pairs={{0,8},{4,12},{1,9},{5,13},{2,10},{6,14},{3,11},{7,15},{8,0},{12,4}... | collective-permute-start | bytes 1376264 | tf_op jit(solution)/shard_map/ppermute | solution.py:87
  69.7 19.0 %collective-permute-start.8 = (bf16[256,512]{1,0:T(8,128)(2,1)}, bf16[256,512]{1,0:T(8,128)(2,1)}, u32[]{:S(2)}, u32[]{:S(2)}) collective-permute-start(bf16[256,512]{1,0:T(8,128)(2,1)} %collective-permute-done.6.refs_1_), channel_id=1, source_target_pairs={{0,16},{4,20},{1,17},{5,21},{2,18},{6,22},{3,19},{7,23},{8,24},{12... | collective-permute-start | bytes 786440 | tf_op jit(solution)/shard_map/ppermute | solution.py:87
  100.5 23.9 %collective-permute-start.16 = (bf16[2,2,192,128]{3,2,1,0:T(8,128)(2,1)}, bf16[2,2,192,128]{3,2,1,0:T(8,128)(2,1)}, u32[]{:S(2)}, u32[]{:S(2)}) collective-permute-start(bf16[2,2,192,128]{3,2,1,0:T(8,128)(2,1)} %pad_maximum_fusion.15), channel_id=1, source_target_pairs={{0,1},{4,5},{1,2},{5,6},{2,3},{6,7},{3,0},{7,4},{8,9},{12,13},{9,1... | collective-permute-start | bytes 589832 | tf_op jit(solution)/shard_map/ppermute | solution.py:87
  103.0 21.4 %collective-permute-start.17 = (bf16[2,2,192,128]{3,2,1,0:T(8,128)(2,1)}, bf16[2,2,192,128]{3,2,1,0:T(8,128)(2,1)}, u32[]{:S(2)}, u32[]{:S(2)}) collective-permute-start(bf16[2,2,192,128]{3,2,1,0:T(8,128)(2,1)} %pad_maximum_fusion.15), channel_id=1, source_target_pairs={{0,2},{4,6},{1,3},{5,7},{2,0},{6,4},{3,1},{7,5},{8,10},{12,14},{9,... | collective-permute-start | bytes 589832 | tf_op jit(solution)/shard_map/ppermute | solution.py:87
  105.5 18.9 %collective-permute-start.18 = (bf16[2,2,192,128]{3,2,1,0:T(8,128)(2,1)}, bf16[2,2,192,128]{3,2,1,0:T(8,128)(2,1)}, u32[]{:S(2)}, u32[]{:S(2)}) collective-permute-start(bf16[2,2,192,128]{3,2,1,0:T(8,128)(2,1)} %pad_maximum_fusion.15), channel_id=1, source_target_pairs={{0,3},{4,7},{1,0},{5,4},{2,1},{6,5},{3,2},{7,6},{8,11},{12,15},{9,... | collective-permute-start | bytes 589832 | tf_op jit(solution)/shard_map/ppermute | solution.py:87
  127.2 31.5 %collective-permute-start.19 = (bf16[1536,128]{1,0:T(8,128)(2,1)}, bf16[1536,128]{1,0:T(8,128)(2,1)}, u32[]{:S(2)}, u32[]{:S(2)}) collective-permute-start(bf16[1536,128]{1,0:T(8,128)(2,1)} %get-tuple-element.168.refs_0_), channel_id=1, source_target_pairs={{0,8},{4,12},{1,9},{5,13},{2,10},{6,14},{3,11},{7,15},{8,0},{12,4}... | collective-permute-start | bytes 1179656 | tf_op jit(solution)/shard_map/ppermute | solution.py:87
  127.6 31.1 %collective-permute-start.20 = (bf16[1536,128]{1,0:T(8,128)(2,1)}, bf16[1536,128]{1,0:T(8,128)(2,1)}, u32[]{:S(2)}, u32[]{:S(2)}) collective-permute-start(bf16[1536,128]{1,0:T(8,128)(2,1)} %get-tuple-element.172.refs_4_), channel_id=1, source_target_pairs={{0,16},{4,20},{1,17},{5,21},{2,18},{6,22},{3,19},{7,23},{8,24},{12... | collective-permute-start | bytes 1179656 | tf_op jit(solution)/shard_map/ppermute | solution.py:87
  140.8 17.9 %collective-permute-start.14 = (bf16[2,2,208,128]{3,2,1,0:T(8,128)(2,1)}, bf16[2,2,208,128]{3,2,1,0:T(8,128)(2,1)S(1)}, u32[]{:S(2)}, u32[]{:S(2)}) collective-permute-start(bf16[2,2,208,128]{3,2,1,0:T(8,128)(2,1)} %bitcast.436), channel_id=1, source_target_pairs={{0,2},{4,6},{1,3},{5,7},{2,0},{6,4},{3,1},{7,5},{8,10},{12,14},{9,... | collective-permute-start | bytes 638984 | tf_op jit(solution)/shard_map/ppermute | solution.py:87
  142.1 16.7 %collective-permute-start.15 = (bf16[2,2,208,128]{3,2,1,0:T(8,128)(2,1)}, bf16[2,2,208,128]{3,2,1,0:T(8,128)(2,1)S(1)}, u32[]{:S(2)}, u32[]{:S(2)}) collective-permute-start(bf16[2,2,208,128]{3,2,1,0:T(8,128)(2,1)} %bitcast.435), channel_id=1, source_target_pairs={{0,3},{4,7},{1,0},{5,4},{2,1},{6,5},{3,2},{7,6},{8,11},{12,15},{9,... | collective-permute-start | bytes 638984 | tf_op jit(solution)/shard_map/ppermute | solution.py:87
  158.8 323.9 %reduce-scatter.4.cloned.1.call-start = ((), (), s32[]{:S(2)}) async-start(), calls=%async_computation.5 | async-start | bytes 7864320 | tf_op jit(solution)/shard_map/reduce_scatter | solution.py:194
  158.9 37.8 %collective-permute-start.24 = (bf16[1536,128]{1,0:T(8,128)(2,1)}, bf16[1536,128]{1,0:T(8,128)(2,1)}, u32[]{:S(2)}, u32[]{:S(2)}) collective-permute-start(bf16[1536,128]{1,0:T(8,128)(2,1)} %get-tuple-element.168.refs_0_), channel_id=1, source_target_pairs={{0,16},{4,20},{1,17},{5,21},{2,18},{6,22},{3,19},{7,23},{8,24},{12... | collective-permute-start | bytes 1179656 | tf_op jit(solution)/shard_map/ppermute | solution.py:87
  159.5 37.2 %collective-permute-start.25 = (bf16[1536,128]{1,0:T(8,128)(2,1)}, bf16[1536,128]{1,0:T(8,128)(2,1)}, u32[]{:S(2)}, u32[]{:S(2)}) collective-permute-start(bf16[1536,128]{1,0:T(8,128)(2,1)} %collective-permute-done.19.refs_1_), channel_id=1, source_target_pairs={{0,16},{4,20},{1,17},{5,21},{2,18},{6,22},{3,19},{7,23},{8,24},{12... | collective-permute-start | bytes 1179656 | tf_op jit(solution)/shard_map/ppermute | solution.py:87
  161.0 35.7 %collective-permute-start.26 = (bf16[1536,128]{1,0:T(8,128)(2,1)}, bf16[1536,128]{1,0:T(8,128)(2,1)}, u32[]{:S(2)}, u32[]{:S(2)}) collective-permute-start(bf16[1536,128]{1,0:T(8,128)(2,1)} %get-tuple-element.172.refs_4_), channel_id=1, source_target_pairs={{0,8},{4,12},{1,9},{5,13},{2,10},{6,14},{3,11},{7,15},{8,0},{12,4}... | collective-permute-start | bytes 1179656 | tf_op jit(solution)/shard_map/ppermute | solution.py:87
  162.2 34.5 %collective-permute-start.27 = (bf16[1536,128]{1,0:T(8,128)(2,1)}, bf16[1536,128]{1,0:T(8,128)(2,1)}, u32[]{:S(2)}, u32[]{:S(2)}) collective-permute-start(bf16[1536,128]{1,0:T(8,128)(2,1)} %collective-permute-done.20.refs_6_), channel_id=1, source_target_pairs={{0,8},{4,12},{1,9},{5,13},{2,10},{6,14},{3,11},{7,15},{8,0},{12,4}... | collective-permute-start | bytes 1179656 | tf_op jit(solution)/shard_map/ppermute | solution.py:87
  165.8 19.4 %collective-permute-start.21 = (bf16[2,208,128]{2,1,0:T(8,128)(2,1)}, bf16[2,208,128]{2,1,0:T(8,128)(2,1)}, u32[]{:S(2)}, u32[]{:S(2)}) collective-permute-start(bf16[2,208,128]{2,1,0:T(8,128)(2,1)} %scan.4), channel_id=1, source_target_pairs={{0,8},{1,9},{2,10},{3,11},{4,12},{5,13},{6,14},{7,15},{8,16},{9,17... | collective-permute-start | bytes 319496 | tf_op jit(solution)/shard_map/ppermute | solution.py:907
  201.4 26.1 %collective-permute-start.28 = (bf16[2,2,192,128]{3,2,1,0:T(8,128)(2,1)}, bf16[2,2,192,128]{3,2,1,0:T(8,128)(2,1)S(1)}, u32[]{:S(2)}, u32[]{:S(2)}) collective-permute-start(bf16[2,2,192,128]{3,2,1,0:T(8,128)(2,1)} %get-tuple-element.178), channel_id=1, source_target_pairs={{0,1},{4,5},{1,2},{5,6},{2,3},{6,7},{3,0},{7,4},{8,9},{12,13},{9,1... | collective-permute-start | bytes 589832 | tf_op jit(solution)/shard_map/ppermute | solution.py:87
  208.5 18.9 %collective-permute-start.29 = (bf16[2,2,192,128]{3,2,1,0:T(8,128)(2,1)}, bf16[2,2,192,128]{3,2,1,0:T(8,128)(2,1)S(1)}, u32[]{:S(2)}, u32[]{:S(2)}) collective-permute-start(bf16[2,2,192,128]{3,2,1,0:T(8,128)(2,1)} %get-tuple-element.179), channel_id=1, source_target_pairs={{0,2},{4,6},{1,3},{5,7},{2,0},{6,4},{3,1},{7,5},{8,10},{12,14},{9,... | collective-permute-start | bytes 589832 | tf_op jit(solution)/shard_map/ppermute | solution.py:87
  208.5 19.0 %collective-permute-start.30 = (bf16[2,2,192,128]{3,2,1,0:T(8,128)(2,1)}, bf16[2,2,192,128]{3,2,1,0:T(8,128)(2,1)S(1)}, u32[]{:S(2)}, u32[]{:S(2)}) collective-permute-start(bf16[2,2,192,128]{3,2,1,0:T(8,128)(2,1)} %get-tuple-element.180), channel_id=1, source_target_pairs={{0,3},{4,7},{1,0},{5,4},{2,1},{6,5},{3,2},{7,6},{8,11},{12,15},{9,... | collective-permute-start | bytes 589832 | tf_op jit(solution)/shard_map/ppermute | solution.py:87
  324.1 13.5 %collective-permute-start.42 = (bf16[2,256,1024]{2,1,0:T(8,128)(2,1)}, bf16[2,256,1024]{2,1,0:T(8,128)(2,1)S(1)}, u32[]{:S(2)}, u32[]{:S(2)}) collective-permute-start(bf16[2,256,1024]{2,1,0:T(8,128)(2,1)} %dynamic-slice_bitcast_fusion.1), channel_id=1, source_target_pairs={{0,4},{4,0},{1,5},{5,1},{2,6},{6,2},{3,7},{7,3},{8,12},{12,8},{9,1... | collective-permute-start | bytes 3145736 | tf_op jit(solution)/shard_map/ppermute | solution.py:87
  324.4 21.1 %collective-permute-start.39 = (bf16[2,2,192,128]{3,2,1,0:T(8,128)(2,1)}, bf16[2,2,192,128]{3,2,1,0:T(8,128)(2,1)S(1)}, u32[]{:S(2)}, u32[]{:S(2)}) collective-permute-start(bf16[2,2,192,128]{3,2,1,0:T(8,128)(2,1)} %bitcast.449), channel_id=1, source_target_pairs={{0,1},{4,5},{1,2},{5,6},{2,3},{6,7},{3,0},{7,4},{8,9},{12,13},{9,1... | collective-permute-start | bytes 589832 | tf_op jit(solution)/shard_map/ppermute | solution.py:87
  325.2 20.3 %collective-permute-start.40 = (bf16[2,2,192,128]{3,2,1,0:T(8,128)(2,1)}, bf16[2,2,192,128]{3,2,1,0:T(8,128)(2,1)}, u32[]{:S(2)}, u32[]{:S(2)}) collective-permute-start(bf16[2,2,192,128]{3,2,1,0:T(8,128)(2,1)} %bitcast.448), channel_id=1, source_target_pairs={{0,2},{4,6},{1,3},{5,7},{2,0},{6,4},{3,1},{7,5},{8,10},{12,14},{9,... | collective-permute-start | bytes 589832 | tf_op jit(solution)/shard_map/ppermute | solution.py:87
  326.5 19.0 %collective-permute-start.41 = (bf16[2,2,192,128]{3,2,1,0:T(8,128)(2,1)}, bf16[2,2,192,128]{3,2,1,0:T(8,128)(2,1)}, u32[]{:S(2)}, u32[]{:S(2)}) collective-permute-start(bf16[2,2,192,128]{3,2,1,0:T(8,128)(2,1)} %bitcast.447), channel_id=1, source_target_pairs={{0,3},{4,7},{1,0},{5,4},{2,1},{6,5},{3,2},{7,6},{8,11},{12,15},{9,... | collective-permute-start | bytes 589832 | tf_op jit(solution)/shard_map/ppermute | solution.py:87
  346.2 181.6 %reduce-scatter.6.cloned.1.call-start = ((), (), s32[]{:S(2)}) async-start(), calls=%async_computation.6 | async-start | bytes 5242880 | tf_op jit(solution)/shard_map/reduce_scatter | solution.py:194
  356.2 12.8 %collective-permute-start.44 = (bf16[2,208,128]{2,1,0:T(8,128)(2,1)}, bf16[2,208,128]{2,1,0:T(8,128)(2,1)S(1)}, u32[]{:S(2)}, u32[]{:S(2)}) collective-permute-start(bf16[2,208,128]{2,1,0:T(8,128)(2,1)} %scan.6), channel_id=1, source_target_pairs={{0,16},{1,17},{2,18},{3,19},{4,20},{5,21},{6,22},{7,23},{8,24},{9,... | collective-permute-start | bytes 319496 | tf_op jit(solution)/shard_map/ppermute | solution.py:907
  391.2 25.2 %collective-permute-start.47 = (bf16[2,2,192,128]{3,2,1,0:T(8,128)(2,1)}, bf16[2,2,192,128]{3,2,1,0:T(8,128)(2,1)S(1)}, u32[]{:S(2)}, u32[]{:S(2)}) collective-permute-start(bf16[2,2,192,128]{3,2,1,0:T(8,128)(2,1)} %get-tuple-element.227), channel_id=1, source_target_pairs={{0,1},{4,5},{1,2},{5,6},{2,3},{6,7},{3,0},{7,4},{8,9},{12,13},{9,1... | collective-permute-start | bytes 589832 | tf_op jit(solution)/shard_map/ppermute | solution.py:87
  392.2 24.3 %collective-permute-start.48 = (bf16[2,2,192,128]{3,2,1,0:T(8,128)(2,1)}, bf16[2,2,192,128]{3,2,1,0:T(8,128)(2,1)S(1)}, u32[]{:S(2)}, u32[]{:S(2)}) collective-permute-start(bf16[2,2,192,128]{3,2,1,0:T(8,128)(2,1)} %get-tuple-element.228), channel_id=1, source_target_pairs={{0,2},{4,6},{1,3},{5,7},{2,0},{6,4},{3,1},{7,5},{8,10},{12,14},{9,... | collective-permute-start | bytes 589832 | tf_op jit(solution)/shard_map/ppermute | solution.py:87
  393.6 22.9 %collective-permute-start.49 = (bf16[2,2,192,128]{3,2,1,0:T(8,128)(2,1)}, bf16[2,2,192,128]{3,2,1,0:T(8,128)(2,1)S(1)}, u32[]{:S(2)}, u32[]{:S(2)}) collective-permute-start(bf16[2,2,192,128]{3,2,1,0:T(8,128)(2,1)} %get-tuple-element.229), channel_id=1, source_target_pairs={{0,3},{4,7},{1,0},{5,4},{2,1},{6,5},{3,2},{7,6},{8,11},{12,15},{9,... | collective-permute-start | bytes 589832 | tf_op jit(solution)/shard_map/ppermute | solution.py:87
  416.4 194.7 %reduce-scatter.8.cloned.1.call-start = ((), (), s32[]{:S(2)}) async-start(), calls=%async_computation.7 | async-start | bytes 3276800 | tf_op jit(solution)/shard_map/reduce_scatter | solution.py:221
  420.3 58.5 %collective-permute-start.51 = (bf16[2,2,4,192,128]{4,3,2,1,0:T(8,128)(2,1)}, bf16[2,2,4,192,128]{4,3,2,1,0:T(8,128)(2,1)}, u32[]{:S(2)}, u32[]{:S(2)}) collective-permute-start(bf16[2,2,4,192,128]{4,3,2,1,0:T(8,128)(2,1)} %dynamic-slice_bitcast_fusion.2), channel_id=1, source_target_pairs={{0,8},{4,12},{1,9},{5,13},{2,10},{6,14},{3,11},{7,15},{8,0},{12,4}... | collective-permute-start | bytes 2359304 | tf_op jit(solution)/shard_map/ppermute | solution.py:87
  432.4 48.8 %collective-permute-start.50 = (bf16[2,2,4,192,128]{4,3,2,1,0:T(8,128)(2,1)}, bf16[2,2,4,192,128]{4,3,2,1,0:T(8,128)(2,1)}, u32[]{:S(2)}, u32[]{:S(2)}) collective-permute-start(bf16[2,2,4,192,128]{4,3,2,1,0:T(8,128)(2,1)} %dynamic-slice_bitcast_fusion.3), channel_id=1, source_target_pairs={{0,16},{4,20},{1,17},{5,21},{2,18},{6,22},{3,19},{7,23},{8,24},{12... | collective-permute-start | bytes 2359304 | tf_op jit(solution)/shard_map/ppermute | solution.py:87
  506.9 20.6 %collective-permute-start.58 = (bf16[2,2,4,32,896]{4,3,2,1,0:T(8,128)(2,1)S(1)}, bf16[2,2,4,32,896]{4,3,2,1,0:T(8,128)(2,1)S(1)}, u32[]{:S(2)}, u32[]{:S(2)}) collective-permute-start(bf16[2,2,4,32,896]{4,3,2,1,0:T(8,128)(2,1)S(1)} %fusion.20), channel_id=1, source_target_pairs={{0,8},{4,12},{1,9},{5,13},{2,10},{6,14},{3,11},{7,15},{8,0},{12,4}... | collective-permute-start | bytes 2752520 | tf_op jit(solution)/shard_map/ppermute | solution.py:87
  510.1 14.2 %collective-permute-start.56 = (bf16[384,256]{1,0:T(8,128)(2,1)S(1)}, bf16[384,256]{1,0:T(8,128)(2,1)S(1)}, u32[]{:S(2)}, u32[]{:S(2)}) collective-permute-start(bf16[384,256]{1,0:T(8,128)(2,1)S(1)} %pad_maximum_fusion.17), channel_id=1, source_target_pairs={{0,2},{4,6},{1,3},{5,7},{2,0},{6,4},{3,1},{7,5},{8,10},{12,14},{9,... | collective-permute-start | bytes 589832 | tf_op jit(solution)/shard_map/ppermute | solution.py:87
  533.6 20.8 %collective-permute-start.68 = (f32[3,12]{1,0:T(4,128)S(1)}, f32[3,12]{1,0:T(4,128)}, u32[]{:S(2)}, u32[]{:S(2)}) collective-permute-start(f32[3,12]{1,0:T(4,128)S(1)} %copy-done.81), channel_id=1, source_target_pairs={{0,8},{4,12},{1,9},{5,13},{2,10},{6,14},{3,11},{7,15},{8,0},{12,4}... | collective-permute-start | bytes 440 | tf_op jit(solution)/shard_map/ppermute | solution.py:265
  536.2 18.9 %collective-permute-start.63 = (bf16[2,4,32,896]{3,2,1,0:T(8,128)(2,1)}, bf16[2,4,32,896]{3,2,1,0:T(8,128)(2,1)}, u32[]{:S(2)}, u32[]{:S(2)}) collective-permute-start(bf16[2,4,32,896]{3,2,1,0:T(8,128)(2,1)} %fusion.24), channel_id=1, source_target_pairs={{0,16},{4,20},{1,17},{5,21},{2,18},{6,22},{3,19},{7,23},{8,24},{12... | collective-permute-start | bytes 1376264 | tf_op jit(solution)/shard_map/ppermute | solution.py:87
  558.2 17.0 %collective-permute-start.66 = (bf16[64,896]{1,0:T(8,128)(2,1)S(1)}, bf16[64,896]{1,0:T(8,128)(2,1)S(1)}, u32[]{:S(2)}, u32[]{:S(2)}) collective-permute-start(bf16[64,896]{1,0:T(8,128)(2,1)S(1)} %bitcast.426), channel_id=1, source_target_pairs={{0,2},{4,6},{1,3},{5,7},{2,0},{6,4},{3,1},{7,5},{8,10},{12,14},{9,... | collective-permute-start | bytes 344072 | tf_op jit(solution)/shard_map/ppermute | solution.py:87
  560.8 14.4 %collective-permute-start.67 = (bf16[64,896]{1,0:T(8,128)(2,1)S(1)}, bf16[64,896]{1,0:T(8,128)(2,1)S(1)}, u32[]{:S(2)}, u32[]{:S(2)}) collective-permute-start(bf16[64,896]{1,0:T(8,128)(2,1)S(1)} %bitcast.425), channel_id=1, source_target_pairs={{0,3},{4,7},{1,0},{5,4},{2,1},{6,5},{3,2},{7,6},{8,11},{12,15},{9,... | collective-permute-start | bytes 344072 | tf_op jit(solution)/shard_map/ppermute | solution.py:87
  561.7 16.5 %collective-permute-start.64 = (bf16[2,2,4,32,512]{4,3,2,1,0:T(8,128)(2,1)S(1)}, bf16[2,2,4,32,512]{4,3,2,1,0:T(8,128)(2,1)S(1)}, u32[]{:S(2)}, u32[]{:S(2)}) collective-permute-start(bf16[2,2,4,32,512]{4,3,2,1,0:T(8,128)(2,1)S(1)} %fusion.23), channel_id=1, source_target_pairs={{0,16},{4,20},{1,17},{5,21},{2,18},{6,22},{3,19},{7,23},{8,24},{12... | collective-permute-start | bytes 1572872 | tf_op jit(solution)/shard_map/ppermute | solution.py:87
  563.5 12.9 %collective-permute-start.62 = (bf16[2,3,1024]{2,1,0:T(4,128)(2,1)S(1)}, bf16[2,3,1024]{2,1,0:T(4,128)(2,1)S(1)}, u32[]{:S(2)}, u32[]{:S(2)}) collective-permute-start(bf16[2,3,1024]{2,1,0:T(4,128)(2,1)S(1)} %slice.826), channel_id=1, source_target_pairs={{1,0},{2,1},{3,2},{4,3},{5,4},{6,5},{7,6},{8,7},{9,8},{10,9},{11,1... | collective-permute-start | bytes 36872 | tf_op jit(solution)/shard_map/ppermute | solution.py:1432
  588.8 13.2 %collective-permute-start.77 = (f32[3,12]{1,0:T(4,128)S(1)}, f32[3,12]{1,0:T(4,128)S(1)}, u32[]{:S(2)}, u32[]{:S(2)}) collective-permute-start(f32[3,12]{1,0:T(4,128)S(1)} %add.506), channel_id=1, source_target_pairs={{0,4},{4,0},{1,5},{5,1},{2,6},{6,2},{3,7},{7,3},{8,12},{12,8},{9,1... | collective-permute-start | bytes 440 | tf_op jit(solution)/shard_map/ppermute | solution.py:87
  588.9 13.3 %collective-permute-start.71 = (bf16[64,512]{1,0:T(8,128)(2,1)S(1)}, bf16[64,512]{1,0:T(8,128)(2,1)S(1)}, u32[]{:S(2)}, u32[]{:S(2)}) collective-permute-start(bf16[64,512]{1,0:T(8,128)(2,1)S(1)} %bitcast.430), channel_id=1, source_target_pairs={{0,1},{4,5},{1,2},{5,6},{2,3},{6,7},{3,0},{7,4},{8,9},{12,13},{9,1... | collective-permute-start | bytes 196616 | tf_op jit(solution)/shard_map/ppermute | solution.py:87
  (156 other events, 1493.6 us)
Sparse Core Ops, SparseCore 0:
  11.5 106.6 all-gather.2
  158.9 112.9 all-gather.4
  345.7 77.7 reduce-scatter.3
  426.3 71.3 reduce-scatter.5
  533.1 60.5 reduce-scatter.7

commit v5 on v4

--- a/solution.py
+++ b/solution.py
@@ -1180,7 +1180,10 @@
         return parts
 
     def between_states(totals):
-        totals, held_back["kv"] = tie(totals, held_back["kv"])
+        gates = mm(normed, w_z).astype(BF16)
+        totals, held_back["kv"], held_back["gates"], held_back["weights"] = tie(
+            totals, held_back["kv"], gates, (w_z, w_attn_out, w_mixer_out)
+        )
         return totals
 
     def after_states(entering):
@@ -1191,6 +1194,7 @@
         place, at, local, None, None, False, before_states, between_states, after_states
     )
     queries = held_back["queries"]
+    w_z_late, w_attn_out_late, w_mixer_out_late = held_back["weights"]
     rows = chips * CORES * groups * piece
     (kv,) = place.plane_third(
         held_back["kv"], [(s, 0, 2 * HD, 0, 0, s * rows) for s in range(slots)]
@@ -1227,7 +1231,7 @@
         [held],
     )
     ssd = ssd.reshape(CORES, slots, piece, m_cols).astype(F32)
-    zgate = body_rows(mm(normed, w_z).astype(BF16))
+    zgate = body_rows(held_back["gates"])
     gate_value, gate_slope = silu_and_slope(zgate.astype(F32))
     gated_raw = ssd * gate_value
     squares = jnp.sum(gated_raw * gated_raw, axis=-1)
@@ -1242,7 +1246,7 @@
     def with_other(value):
         return jnp.stack([value, place.swap(value)]).reshape(-1, value.shape[-1])
 
-    mixers = own_sum(mm(attended, w_attn_out) + mm(gated, w_mixer_out))
+    mixers = own_sum(mm(attended, w_attn_out_late) + mm(gated, w_mixer_out_late))
     residual = tokens[0][:, HALO:].reshape(-1, width) + mixers
     scale_post = inverse_rms(residual)
     post = with_other((residual * scale_post * gain_post).astype(BF16))
@@ -1269,8 +1273,8 @@
     grad_post_gain = jnp.sum(dpost * residual * scale_post, axis=0)
     dmix = with_other(dresidual.astype(BF16))
 
-    dattended = mm(dmix, w_attn_out, NT).astype(BF16)
-    dgated = mm(dmix, w_mixer_out, NT).reshape(CORES, slots, piece, m_cols)
+    dattended = mm(dmix, w_attn_out_late, NT).astype(BF16)
+    dgated = mm(dmix, w_mixer_out_late, NT).reshape(CORES, slots, piece, m_cols)
     scaled = dgated * gain_mixer
     inner = jnp.sum(scaled * gated_raw, axis=-1)
     inner = (inner + place.swap(inner)[::-1])[..., None] / (SH * SHD)
@@ -1337,7 +1341,7 @@
     )
     ff_grads, mid_grads = out_side["ff"], out_side["mid"]
     dattended = out_side["dattended"]
-    dnormed = mm(out_side["dz"], w_z, NT)
+    dnormed = mm(out_side["dz"], w_z_late, NT)
 
     dqueries, dkv = attend_back(
         pieces_at,

time: 637 us -> 646 us (1.014); the launches traced: 624 us -> 641 us
  starting transfers between devices: 117 us -> 131 us
    ppermute x6, waiting for transfers between devices: 32.5 us -> 7.87 us  [carried(): lax.ppermute(leaving, AXES, place.chip_pairs(k))]
    ppermute x66, waiting for transfers between devices: 93.5 us -> 111 us  [shift(): return lax.ppermute(x, AXES, self.pairs(dim, by))]
    ppermute x66, starting transfers between devices: 97 us -> 108 us  [shift(): return lax.ppermute(x, AXES, self.pairs(dim, by))]
    unnamed x247 -> x245, local copies, waits for them, and re-layouts: 16.2 us -> 14.3 us
  transfers between devices with their start and end apart: 83 -> 83, of which waited for: 31 -> 32; matrix products, arithmetic and copies ran while one was open for 26% -> 26% of each run, Pallas kernels for 19% -> 19%
where the time goes in v5:
time: 646 us; the launch traced here: 641 us
  waiting for transfers between devices  141 us (22%)
  Pallas kernels  137 us (21%)
  starting transfers between devices  131 us (20%)
  local copies, waits for them, and re-layouts  80.7 us (12%)
  other arithmetic  73.2 us (11%)
  matrix products  62.4 us (10%)
  between operations  16.3 us (3%)
    ppermute x66, waiting for transfers between devices, shift(): return lax.ppermute(x, AXES, self.pairs(dim, by))  111 us
    ppermute x66, starting transfers between devices, shift(): return lax.ppermute(x, AXES, self.pairs(dim, by))  108 us
    dot_general x25, matrix products, mm(): lax.dot_general(left, right, dims, precision=precision, preferred_element...  62.4 us
    pallas_call x5, Pallas kernels, over_pieces(): pl.pallas_call(kernel, grid=(pieces,), in_specs=[spec(shape, split) for s...  54.9 us
    pallas_call x9, Pallas kernels, moved(): pl.pallas_call(functools.partial(moved_kernel, plan=plan, count=len(sourc...  40.8 us
    pallas_call x1, Pallas kernels, attend_back(): pl.pallas_call(functools.partial(attend_back_kernel, piece=piece), grid_s...  17.2 us
    all_gather x1, waiting for transfers between devices, before_states(): held_back['ff'] = lax.all_gather(columns, AXES, axis=0, tiled=True)  14.7 us
    unnamed x245, local copies, waits for them, and re-layouts  14.3 us
  transfers between devices with their start and end apart: 83, of which 32 were waited for; matrix products, arithmetic and copies ran while one was open for 26% of the time, Pallas kernels for 19%

profile of v5, /device:TPU:0, one launch (start us, length us, event | category | flops | bytes accessed | tf_op | source)
XLA Modules:
  0.0 641.3 jit_solution(8267600414503064876)
XLA Ops:
  17.1 4.5 collective-permute-start
  28.3 6.0 collective-permute-done.3.refs_1_
  34.3 8.5 %collective-permute-done.4.refs_2_ = bf16[64,1408]{1,0:T(8,128)(2,1)S(1)} collective-permute-done((bf16[64,1408]{1,0:T(8,128)(2,1)S(1)}, bf16[64,1408]{1,0:T(8,128)(2,1)S(1)}, u32[]{:S(2)}, u32[]{:S(2)}) %collective-permute-start.4) | collective-permute-done | bytes 180256 | tf_op jit(solution)/shard_map/ppermute | solution.py:87
  51.4 11.7 %collective-permute-done.10.refs_6_ = bf16[256,896]{1,0:T(8,128)(2,1)S(1)} collective-permute-done((bf16[256,896]{1,0:T(8,128)(2,1)}, bf16[256,896]{1,0:T(8,128)(2,1)S(1)}, u32[]{:S(2)}, u32[]{:S(2)}) %collective-permute-start.10) | collective-permute-done | bytes 458784 | tf_op jit(solution)/shard_map/ppermute | solution.py:87
  70.8 8.2 %collective-permute-done.7.refs_2_ = bf16[256,512]{1,0:T(8,128)(2,1)} collective-permute-done((bf16[256,512]{1,0:T(8,128)(2,1)}, bf16[256,512]{1,0:T(8,128)(2,1)}, u32[]{:S(2)}, u32[]{:S(2)}) %collective-permute-start.7) | collective-permute-done | bytes 262176 | tf_op jit(solution)/shard_map/ppermute | solution.py:87
  79.0 9.7 %collective-permute-done.8.refs_3_ = bf16[256,512]{1,0:T(8,128)(2,1)} collective-permute-done((bf16[256,512]{1,0:T(8,128)(2,1)}, bf16[256,512]{1,0:T(8,128)(2,1)}, u32[]{:S(2)}, u32[]{:S(2)}) %collective-permute-start.8) | collective-permute-done | bytes 262176 | tf_op jit(solution)/shard_map/ppermute | solution.py:87
  90.5 4.0 moved.10
  130.9 9.3 %chunk.1 = (f32[4,192,768]{2,1,0:T(8,128)}, f32[4,192,128]{2,1,0:T(8,128)}, bf16[4,208,128]{2,1,0:T(8,128)(2,1)}, bf16[4,208,128]{2,1,0:T(8,128)(2,1)}, bf16[4,2...) custom-call(bf16[4,192,768]{2,1,0:T(8,128)(2,1)} %bitcast.383, bf16[4,192,128]{2,1,0:T(8,128)(2,1)} %bitcast.422, ...), custom_call_target="tpu_custom_call" | custom-call | flops 10350000128 | tf_op jit(solution)/shard_map/chunk/pallas_call | solution.py:749
  145.2 5.4 collective-permute-done.13.refs_1_.refs_5_
  150.6 8.2 %collective-permute-done.14.refs_2_.refs_6_ = bf16[2,2,208,128]{3,2,1,0:T(8,128)(2,1)} collective-permute-done((bf16[2,2,208,128]{3,2,1,0:T(8,128)(2,1)}, bf16[2,2,208,128]{3,2,1,0:T(8,128)(2,1)}, u32[]{:S(2)}, u32[]{:S(2)}) %collective-permute-start.14) | collective-permute-done | bytes 213024 | tf_op jit(solution)/shard_map/ppermute | solution.py:87
  174.0 5.0 moved.12
  181.2 3.9 convolution_convert_fusion.6
  186.8 8.2 %collective-permute-done.25.refs_3_ = bf16[1536,128]{1,0:T(8,128)(2,1)} collective-permute-done((bf16[1536,128]{1,0:T(8,128)(2,1)}, bf16[1536,128]{1,0:T(8,128)(2,1)}, u32[]{:S(2)}, u32[]{:S(2)}) %collective-permute-start.25) | collective-permute-done | bytes 393248 | tf_op jit(solution)/shard_map/ppermute | solution.py:87
  195.1 6.8 %collective-permute-done.27.refs_7_ = bf16[1536,128]{1,0:T(8,128)(2,1)S(1)} collective-permute-done((bf16[1536,128]{1,0:T(8,128)(2,1)}, bf16[1536,128]{1,0:T(8,128)(2,1)S(1)}, u32[]{:S(2)}, u32[]{:S(2)}) %collective-permute-start.27) | collective-permute-done | bytes 393248 | tf_op jit(solution)/shard_map/ppermute | solution.py:87
  206.1 8.9 %collective-permute-start.28 = (bf16[2,2,192,128]{3,2,1,0:T(8,128)(2,1)}, bf16[2,2,192,128]{3,2,1,0:T(8,128)(2,1)S(1)}, u32[]{:S(2)}, u32[]{:S(2)}) collective-permute-start(bf16[2,2,192,128]{3,2,1,0:T(8,128)(2,1)} %get-tuple-element.185), channel_id=1, source_target_pairs={{0,1},{4,5},{1,2},{5,6},{2,3},{6,7},{3,0},{7,4},{8,9},{12,13},{9,1... | collective-permute-start | bytes 589832 | tf_op jit(solution)/shard_map/ppermute | solution.py:87
  217.3 4.2 moved.13
  221.6 12.3 %attend.1 = (bf16[2,2,192,256]{3,2,1,0:T(8,128)(2,1)}, f32[2,2,1,768]{3,2,1,0:T(1,128)}) custom-call(s32[2]{0:T(128)} %copy-done.91, s32[2]{0:T(128)} %lengths.3, bf16[2,2,192,256]{3,2,1,0:T(8,128)(2,1)} %copy.99.q_ref, bf16[2,6144,128]{2,1,0:T(8,128)(2,1)} %bitcast.352), custom_call_target="tpu_custom_call" | custom-call | flops 23000000512 | tf_op jit(solution)/shard_map/attend/pallas_call | solution.py:414
  234.7 5.0 carry.1
  261.6 14.7 %all-gather.5.cloned.1.call-done.refs_0_ = bf16[1024,6144]{1,0:T(8,128)(2,1)} async-done(((bf16[32,6144]{1,0:T(8,128)(2,1)}), bf16[1024,6144]{1,0:T(8,128)(2,1)}) %all-gather.5.cloned.1.call-update) | async-done | bytes 12582928 | tf_op jit(solution)/shard_map/all_gather | solution.py:1178
  276.3 6.5 %moved.14 = (bf16[1024,1024]{1,0:T(8,128)(2,1)}, bf16[1024,1024]{1,0:T(8,128)(2,1)}, bf16[1024,1024]{1,0:T(8,128)(2,1)}) custom-call(s32[5]{0:T(128)} %stack.97.at_ref.rest_4_.rest_8_._, bf16[1024,6144]{1,0:T(8,128)(2,1)} %all-gather.5.cloned.1.call-done.refs_0_), custom_call_target="tpu_custom_call" | custom-call | bytes 12582912 | tf_op jit(solution)/shard_map/moved/pallas_call | solution.py:292
  282.8 3.5 fusion.69
  288.4 3.3 multiply_convert_fusion.2
  304.6 4.5 fusion.49
  311.5 3.5 multiply_reduce_fusion.2
  316.2 3.9 fusion.4
  320.1 5.7 direct.1
  333.5 5.0 convolution_convert_fusion.2.refs_1_
  338.6 3.3 convolution_convert_fusion.3.refs_0_
  343.5 6.2 moved.15
  360.4 5.6 collective-permute-start.44
  373.8 3.3 collective-permute-done.45.refs_10_
  385.6 3.6 convolution_convert_fusion.refs_1_
  390.9 5.0 moved.16
  404.0 17.2 %attend_back.1 = (f32[2,2,192,256]{3,2,1,0:T(8,128)}, bf16[2,6144,128]{2,1,0:T(8,128)(2,1)}) custom-call(s32[2]{0:T(128)} %copy-done.91, s32[2]{0:T(128)} %lengths.3, bf16[2,2,192,256]{3,2,1,0:T(8,128)(2,1)} %copy.99.q_ref, bf16[2,6144,128]{2,1,0:T(8,128)(2,1)} %bitcast.353, bf16[2,2,192,256]{3,2,1,0:T(8,128)(2,1)} %get-tuple-element.183.out_ref, ...), custom_call_target="tpu_custom_call" | custom-call | flops 28750000128 | tf_op jit(solution)/shard_map/attend_back/pallas_call | solution.py:499
  428.1 13.5 %collective-permute-start.51 = (bf16[2,2,4,192,128]{4,3,2,1,0:T(8,128)(2,1)}, bf16[2,2,4,192,128]{4,3,2,1,0:T(8,128)(2,1)}, u32[]{:S(2)}, u32[]{:S(2)}) collective-permute-start(bf16[2,2,4,192,128]{4,3,2,1,0:T(8,128)(2,1)} %dynamic-slice_bitcast_fusion.2), channel_id=1, source_target_pairs={{0,8},{4,12},{1,9},{5,13},{2,10},{6,14},{3,11},{7,15},{8,0},{12,4}... | collective-permute-start | bytes 2359304 | tf_op jit(solution)/shard_map/ppermute | solution.py:87
  442.5 11.5 %collective-permute-start.50 = (bf16[2,2,4,192,128]{4,3,2,1,0:T(8,128)(2,1)}, bf16[2,2,4,192,128]{4,3,2,1,0:T(8,128)(2,1)}, u32[]{:S(2)}, u32[]{:S(2)}) collective-permute-start(bf16[2,2,4,192,128]{4,3,2,1,0:T(8,128)(2,1)} %dynamic-slice_bitcast_fusion.3), channel_id=1, source_target_pairs={{0,16},{4,20},{1,17},{5,21},{2,18},{6,22},{3,19},{7,23},{8,24},{12... | collective-permute-start | bytes 2359304 | tf_op jit(solution)/shard_map/ppermute | solution.py:87
  454.0 26.5 %chunk_back.1 = (f32[4,192,768]{2,1,0:T(8,128)}, f32[4,192,128]{2,1,0:T(8,128)}, f32[4,192,128]{2,1,0:T(8,128)}, f32[4,192,128]{2,1,0:T(8,128)}, f32[4,8,128]{2,1,0:T(8,128)}) custom-call(bf16[4,192,768]{2,1,0:T(8,128)(2,1)} %bitcast.384, bf16[4,192,128]{2,1,0:T(8,128)(2,1)} %bitcast.423, bf16[4,192,128]{2,1,0:T(8,128)(2,1)} %bitcast.421, ...), custom_call_target="tpu_custom_call" | custom-call | flops 32199999488 | tf_op jit(solution)/shard_map/chunk_back/pallas_call | solution.py:749
  484.6 3.6 collective-permute-done.59
  498.6 8.3 %conv_back.1 = (bf16[4,200,896]{2,1,0:T(8,128)(2,1)}, f32[4,8,896]{2,1,0:T(8,128)}) custom-call(bf16[4,200,896]{2,1,0:T(8,128)(2,1)} %bitcast.323, f32[4,192,768]{2,1,0:T(8,128)} %get-tuple-element.245.df_ref, f32[4,192,128]{2,1,0:T(8,128)} %bitcast.408, f32[4,896]{1,0:T(4,128)} %copy-done.77, f32[1,896]{1,0:T(1,128)} %broadcast_select_fusion.9.shift_ref, ...), custom_call_target="tpu_custom_call" | custom-call | flops 6899999744 | tf_op jit(solution)/shard_map/conv_back/pallas_call | solution.py:749
  531.4 3.7 convolution_add_fusion.2
  535.4 5.9 collective-permute-done.56
  541.5 3.7 collective-permute-done.58
  546.4 4.2 moved.17
  559.8 4.8 multiply_reduce_fusion
  583.9 8.3 %collective-permute-done.66 = bf16[64,896]{1,0:T(8,128)(2,1)S(1)} collective-permute-done((bf16[64,896]{1,0:T(8,128)(2,1)S(1)}, bf16[64,896]{1,0:T(8,128)(2,1)S(1)}, u32[]{:S(2)}, u32[]{:S(2)}) %collective-permute-start.66) | collective-permute-done | bytes 114720 | tf_op jit(solution)/shard_map/ppermute | solution.py:87
  599.9 5.8 collective-permute-done.69
  605.9 10.6 %collective-permute-start.71 = (bf16[64,512]{1,0:T(8,128)(2,1)S(1)}, bf16[64,512]{1,0:T(8,128)(2,1)S(1)}, u32[]{:S(2)}, u32[]{:S(2)}) collective-permute-start(bf16[64,512]{1,0:T(8,128)(2,1)S(1)} %bitcast.430), channel_id=1, source_target_pairs={{0,1},{4,5},{1,2},{5,6},{2,3},{6,7},{3,0},{7,4},{8,9},{12,13},{9,1... | collective-permute-start | bytes 196616 | tf_op jit(solution)/shard_map/ppermute | solution.py:87
  619.2 3.7 collective-permute-done.72
  (666 shorter events, 286.3 us)
Async XLA Ops:
  7.2 166.8 %all-gather.3.cloned.1.call-start = ((), (), s32[]{:S(2)}) async-start(), calls=%async_computation.3 | async-start | bytes 7569408 | tf_op jit(solution)/shard_map/all_gather | solution.py:1025
  10.1 266.2 %all-gather.5.cloned.1.call-start = ((), (), s32[]{:S(2)}) async-start(), calls=%async_computation.4 | async-start | bytes 12976128 | tf_op jit(solution)/shard_map/all_gather | solution.py:1178
  23.4 19.4 %collective-permute-start.4 = (bf16[64,1408]{1,0:T(8,128)(2,1)S(1)}, bf16[64,1408]{1,0:T(8,128)(2,1)S(1)}, u32[]{:S(2)}, u32[]{:S(2)}) collective-permute-start(bf16[64,1408]{1,0:T(8,128)(2,1)S(1)} %pad_maximum_fusion.19.refs_0_), channel_id=1, source_target_pairs={{0,2},{4,6},{1,3},{5,7},{2,0},{6,4},{3,1},{7,5},{8,10},{12,14},{9,... | collective-permute-start | bytes 540680 | tf_op jit(solution)/shard_map/ppermute | solution.py:87
  24.5 18.3 %collective-permute-start.5 = (bf16[64,1408]{1,0:T(8,128)(2,1)S(1)}, bf16[64,1408]{1,0:T(8,128)(2,1)S(1)}, u32[]{:S(2)}, u32[]{:S(2)}) collective-permute-start(bf16[64,1408]{1,0:T(8,128)(2,1)S(1)} %pad_maximum_fusion.19.refs_0_), channel_id=1, source_target_pairs={{0,3},{4,7},{1,0},{5,4},{2,1},{6,5},{3,2},{7,6},{8,11},{12,15},{9,... | collective-permute-start | bytes 540680 | tf_op jit(solution)/shard_map/ppermute | solution.py:87
  27.5 42.7 %collective-permute-start.1 = (bf16[2,200,1024]{2,1,0:T(8,128)(2,1)S(1)}, bf16[2,200,1024]{2,1,0:T(8,128)(2,1)S(1)}, u32[]{:S(2)}, u32[]{:S(2)}) collective-permute-start(bf16[2,200,1024]{2,1,0:T(8,128)(2,1)S(1)} %get-tuple-element.388), channel_id=1, source_target_pairs={{0,4},{4,0},{1,5},{5,1},{2,6},{6,2},{3,7},{7,3},{8,12},{12,8},{9,1... | collective-permute-start | bytes 2457608 | tf_op jit(solution)/shard_map/ppermute | solution.py:87
  47.0 16.1 %collective-permute-start.10 = (bf16[256,896]{1,0:T(8,128)(2,1)}, bf16[256,896]{1,0:T(8,128)(2,1)S(1)}, u32[]{:S(2)}, u32[]{:S(2)}) collective-permute-start(bf16[256,896]{1,0:T(8,128)(2,1)} %get-tuple-element.147.refs_4_), channel_id=1, source_target_pairs={{0,16},{4,20},{1,17},{5,21},{2,18},{6,22},{3,19},{7,23},{8,24},{12... | collective-permute-start | bytes 1376264 | tf_op jit(solution)/shard_map/ppermute | solution.py:87
  49.4 20.4 %collective-permute-start.6 = (bf16[256,512]{1,0:T(8,128)(2,1)}, bf16[256,512]{1,0:T(8,128)(2,1)}, u32[]{:S(2)}, u32[]{:S(2)}) collective-permute-start(bf16[256,512]{1,0:T(8,128)(2,1)} %get-tuple-element.146.refs_0_), channel_id=1, source_target_pairs={{0,8},{4,12},{1,9},{5,13},{2,10},{6,14},{3,11},{7,15},{8,0},{12,4}... | collective-permute-start | bytes 786440 | tf_op jit(solution)/shard_map/ppermute | solution.py:87
  50.8 28.2 %collective-permute-start.9 = (bf16[256,896]{1,0:T(8,128)(2,1)}, bf16[256,896]{1,0:T(8,128)(2,1)}, u32[]{:S(2)}, u32[]{:S(2)}) collective-permute-start(bf16[256,896]{1,0:T(8,128)(2,1)} %get-tuple-element.147.refs_4_), channel_id=1, source_target_pairs={{0,8},{4,12},{1,9},{5,13},{2,10},{6,14},{3,11},{7,15},{8,0},{12,4}... | collective-permute-start | bytes 1376264 | tf_op jit(solution)/shard_map/ppermute | solution.py:87
  63.1 27.4 %collective-permute-start.11 = (bf16[256,896]{1,0:T(8,128)(2,1)S(1)}, bf16[256,896]{1,0:T(8,128)(2,1)}, u32[]{:S(2)}, u32[]{:S(2)}) collective-permute-start(bf16[256,896]{1,0:T(8,128)(2,1)S(1)} %collective-permute-done.10.refs_6_), channel_id=1, source_target_pairs={{0,8},{4,12},{1,9},{5,13},{2,10},{6,14},{3,11},{7,15},{8,0},{12,4}... | collective-permute-start | bytes 1376264 | tf_op jit(solution)/shard_map/ppermute | solution.py:87
  69.7 19.0 %collective-permute-start.8 = (bf16[256,512]{1,0:T(8,128)(2,1)}, bf16[256,512]{1,0:T(8,128)(2,1)}, u32[]{:S(2)}, u32[]{:S(2)}) collective-permute-start(bf16[256,512]{1,0:T(8,128)(2,1)} %collective-permute-done.6.refs_1_), channel_id=1, source_target_pairs={{0,16},{4,20},{1,17},{5,21},{2,18},{6,22},{3,19},{7,23},{8,24},{12... | collective-permute-start | bytes 786440 | tf_op jit(solution)/shard_map/ppermute | solution.py:87
  100.4 23.7 %collective-permute-start.16 = (bf16[2,2,192,128]{3,2,1,0:T(8,128)(2,1)}, bf16[2,2,192,128]{3,2,1,0:T(8,128)(2,1)}, u32[]{:S(2)}, u32[]{:S(2)}) collective-permute-start(bf16[2,2,192,128]{3,2,1,0:T(8,128)(2,1)} %pad_maximum_fusion.15), channel_id=1, source_target_pairs={{0,1},{4,5},{1,2},{5,6},{2,3},{6,7},{3,0},{7,4},{8,9},{12,13},{9,1... | collective-permute-start | bytes 589832 | tf_op jit(solution)/shard_map/ppermute | solution.py:87
  102.9 21.1 %collective-permute-start.17 = (bf16[2,2,192,128]{3,2,1,0:T(8,128)(2,1)}, bf16[2,2,192,128]{3,2,1,0:T(8,128)(2,1)}, u32[]{:S(2)}, u32[]{:S(2)}) collective-permute-start(bf16[2,2,192,128]{3,2,1,0:T(8,128)(2,1)} %pad_maximum_fusion.15), channel_id=1, source_target_pairs={{0,2},{4,6},{1,3},{5,7},{2,0},{6,4},{3,1},{7,5},{8,10},{12,14},{9,... | collective-permute-start | bytes 589832 | tf_op jit(solution)/shard_map/ppermute | solution.py:87
  105.4 18.7 %collective-permute-start.18 = (bf16[2,2,192,128]{3,2,1,0:T(8,128)(2,1)}, bf16[2,2,192,128]{3,2,1,0:T(8,128)(2,1)}, u32[]{:S(2)}, u32[]{:S(2)}) collective-permute-start(bf16[2,2,192,128]{3,2,1,0:T(8,128)(2,1)} %pad_maximum_fusion.15), channel_id=1, source_target_pairs={{0,3},{4,7},{1,0},{5,4},{2,1},{6,5},{3,2},{7,6},{8,11},{12,15},{9,... | collective-permute-start | bytes 589832 | tf_op jit(solution)/shard_map/ppermute | solution.py:87
  126.9 31.9 %collective-permute-start.19 = (bf16[1536,128]{1,0:T(8,128)(2,1)}, bf16[1536,128]{1,0:T(8,128)(2,1)}, u32[]{:S(2)}, u32[]{:S(2)}) collective-permute-start(bf16[1536,128]{1,0:T(8,128)(2,1)} %get-tuple-element.175.refs_0_), channel_id=1, source_target_pairs={{0,8},{4,12},{1,9},{5,13},{2,10},{6,14},{3,11},{7,15},{8,0},{12,4}... | collective-permute-start | bytes 1179656 | tf_op jit(solution)/shard_map/ppermute | solution.py:87
  127.5 31.3 %collective-permute-start.20 = (bf16[1536,128]{1,0:T(8,128)(2,1)}, bf16[1536,128]{1,0:T(8,128)(2,1)}, u32[]{:S(2)}, u32[]{:S(2)}) collective-permute-start(bf16[1536,128]{1,0:T(8,128)(2,1)} %get-tuple-element.179.refs_4_), channel_id=1, source_target_pairs={{0,16},{4,20},{1,17},{5,21},{2,18},{6,22},{3,19},{7,23},{8,24},{12... | collective-permute-start | bytes 1179656 | tf_op jit(solution)/shard_map/ppermute | solution.py:87
  141.1 17.7 %collective-permute-start.14 = (bf16[2,2,208,128]{3,2,1,0:T(8,128)(2,1)}, bf16[2,2,208,128]{3,2,1,0:T(8,128)(2,1)}, u32[]{:S(2)}, u32[]{:S(2)}) collective-permute-start(bf16[2,2,208,128]{3,2,1,0:T(8,128)(2,1)} %bitcast.436), channel_id=1, source_target_pairs={{0,2},{4,6},{1,3},{5,7},{2,0},{6,4},{3,1},{7,5},{8,10},{12,14},{9,... | collective-permute-start | bytes 638984 | tf_op jit(solution)/shard_map/ppermute | solution.py:87
  142.1 16.7 %collective-permute-start.15 = (bf16[2,2,208,128]{3,2,1,0:T(8,128)(2,1)}, bf16[2,2,208,128]{3,2,1,0:T(8,128)(2,1)}, u32[]{:S(2)}, u32[]{:S(2)}) collective-permute-start(bf16[2,2,208,128]{3,2,1,0:T(8,128)(2,1)} %bitcast.435), channel_id=1, source_target_pairs={{0,3},{4,7},{1,0},{5,4},{2,1},{6,5},{3,2},{7,6},{8,11},{12,15},{9,... | collective-permute-start | bytes 638984 | tf_op jit(solution)/shard_map/ppermute | solution.py:87
  158.9 339.7 %reduce-scatter.4.cloned.1.call-start = ((), (), s32[]{:S(2)}) async-start(), calls=%async_computation.5 | async-start | bytes 7864320 | tf_op jit(solution)/shard_map/reduce_scatter | solution.py:194
  170.6 14.5 %collective-permute-start.23 = (bf16[2,208,128]{2,1,0:T(8,128)(2,1)}, bf16[2,208,128]{2,1,0:T(8,128)(2,1)}, u32[]{:S(2)}, u32[]{:S(2)}) collective-permute-start(bf16[2,208,128]{2,1,0:T(8,128)(2,1)} %scan.4), channel_id=1, source_target_pairs={{0,24},{1,25},{2,26},{3,27},{4,28},{5,29},{6,30},{7,31},{8,0},{9,1... | collective-permute-start | bytes 319496 | tf_op jit(solution)/shard_map/ppermute | solution.py:907
  172.0 14.8 %collective-permute-start.24 = (bf16[1536,128]{1,0:T(8,128)(2,1)}, bf16[1536,128]{1,0:T(8,128)(2,1)}, u32[]{:S(2)}, u32[]{:S(2)}) collective-permute-start(bf16[1536,128]{1,0:T(8,128)(2,1)} %get-tuple-element.175.refs_0_), channel_id=1, source_target_pairs={{0,16},{4,20},{1,17},{5,21},{2,18},{6,22},{3,19},{7,23},{8,24},{12... | collective-permute-start | bytes 1179656 | tf_op jit(solution)/shard_map/ppermute | solution.py:87
  173.6 21.5 %collective-permute-start.25 = (bf16[1536,128]{1,0:T(8,128)(2,1)}, bf16[1536,128]{1,0:T(8,128)(2,1)}, u32[]{:S(2)}, u32[]{:S(2)}) collective-permute-start(bf16[1536,128]{1,0:T(8,128)(2,1)} %collective-permute-done.19.refs_1_), channel_id=1, source_target_pairs={{0,16},{4,20},{1,17},{5,21},{2,18},{6,22},{3,19},{7,23},{8,24},{12... | collective-permute-start | bytes 1179656 | tf_op jit(solution)/shard_map/ppermute | solution.py:87
  179.1 16.0 %collective-permute-start.26 = (bf16[1536,128]{1,0:T(8,128)(2,1)S(1)}, bf16[1536,128]{1,0:T(8,128)(2,1)S(1)}, u32[]{:S(2)}, u32[]{:S(2)}) collective-permute-start(bf16[1536,128]{1,0:T(8,128)(2,1)S(1)} %copy-done.61), channel_id=1, source_target_pairs={{0,8},{4,12},{1,9},{5,13},{2,10},{6,14},{3,11},{7,15},{8,0},{12,4}... | collective-permute-start | bytes 1179656 | tf_op jit(solution)/shard_map/ppermute | solution.py:87
  179.8 22.0 %collective-permute-start.27 = (bf16[1536,128]{1,0:T(8,128)(2,1)}, bf16[1536,128]{1,0:T(8,128)(2,1)S(1)}, u32[]{:S(2)}, u32[]{:S(2)}) collective-permute-start(bf16[1536,128]{1,0:T(8,128)(2,1)} %collective-permute-done.20.refs_6_), channel_id=1, source_target_pairs={{0,8},{4,12},{1,9},{5,13},{2,10},{6,14},{3,11},{7,15},{8,0},{12,4}... | collective-permute-start | bytes 1179656 | tf_op jit(solution)/shard_map/ppermute | solution.py:87
  206.1 27.8 %collective-permute-start.28 = (bf16[2,2,192,128]{3,2,1,0:T(8,128)(2,1)}, bf16[2,2,192,128]{3,2,1,0:T(8,128)(2,1)S(1)}, u32[]{:S(2)}, u32[]{:S(2)}) collective-permute-start(bf16[2,2,192,128]{3,2,1,0:T(8,128)(2,1)} %get-tuple-element.185), channel_id=1, source_target_pairs={{0,1},{4,5},{1,2},{5,6},{2,3},{6,7},{3,0},{7,4},{8,9},{12,13},{9,1... | collective-permute-start | bytes 589832 | tf_op jit(solution)/shard_map/ppermute | solution.py:87
  215.0 18.9 %collective-permute-start.29 = (bf16[2,2,192,128]{3,2,1,0:T(8,128)(2,1)}, bf16[2,2,192,128]{3,2,1,0:T(8,128)(2,1)S(1)}, u32[]{:S(2)}, u32[]{:S(2)}) collective-permute-start(bf16[2,2,192,128]{3,2,1,0:T(8,128)(2,1)} %get-tuple-element.186), channel_id=1, source_target_pairs={{0,2},{4,6},{1,3},{5,7},{2,0},{6,4},{3,1},{7,5},{8,10},{12,14},{9,... | collective-permute-start | bytes 589832 | tf_op jit(solution)/shard_map/ppermute | solution.py:87
  215.0 18.9 %collective-permute-start.30 = (bf16[2,2,192,128]{3,2,1,0:T(8,128)(2,1)}, bf16[2,2,192,128]{3,2,1,0:T(8,128)(2,1)S(1)}, u32[]{:S(2)}, u32[]{:S(2)}) collective-permute-start(bf16[2,2,192,128]{3,2,1,0:T(8,128)(2,1)} %get-tuple-element.187), channel_id=1, source_target_pairs={{0,3},{4,7},{1,0},{5,4},{2,1},{6,5},{3,2},{7,6},{8,11},{12,15},{9,... | collective-permute-start | bytes 589832 | tf_op jit(solution)/shard_map/ppermute | solution.py:87
  328.7 13.1 %collective-permute-start.42 = (bf16[2,256,1024]{2,1,0:T(8,128)(2,1)}, bf16[2,256,1024]{2,1,0:T(8,128)(2,1)S(1)}, u32[]{:S(2)}, u32[]{:S(2)}) collective-permute-start(bf16[2,256,1024]{2,1,0:T(8,128)(2,1)} %dynamic-slice_bitcast_fusion.1), channel_id=1, source_target_pairs={{0,4},{4,0},{1,5},{5,1},{2,6},{6,2},{3,7},{7,3},{8,12},{12,8},{9,1... | collective-permute-start | bytes 3145736 | tf_op jit(solution)/shard_map/ppermute | solution.py:87
  329.0 20.8 %collective-permute-start.39 = (bf16[2,2,192,128]{3,2,1,0:T(8,128)(2,1)}, bf16[2,2,192,128]{3,2,1,0:T(8,128)(2,1)S(1)}, u32[]{:S(2)}, u32[]{:S(2)}) collective-permute-start(bf16[2,2,192,128]{3,2,1,0:T(8,128)(2,1)} %bitcast.449), channel_id=1, source_target_pairs={{0,1},{4,5},{1,2},{5,6},{2,3},{6,7},{3,0},{7,4},{8,9},{12,13},{9,1... | collective-permute-start | bytes 589832 | tf_op jit(solution)/shard_map/ppermute | solution.py:87
  329.9 19.9 %collective-permute-start.40 = (bf16[2,2,192,128]{3,2,1,0:T(8,128)(2,1)}, bf16[2,2,192,128]{3,2,1,0:T(8,128)(2,1)}, u32[]{:S(2)}, u32[]{:S(2)}) collective-permute-start(bf16[2,2,192,128]{3,2,1,0:T(8,128)(2,1)} %bitcast.448), channel_id=1, source_target_pairs={{0,2},{4,6},{1,3},{5,7},{2,0},{6,4},{3,1},{7,5},{8,10},{12,14},{9,... | collective-permute-start | bytes 589832 | tf_op jit(solution)/shard_map/ppermute | solution.py:87
  331.1 18.7 %collective-permute-start.41 = (bf16[2,2,192,128]{3,2,1,0:T(8,128)(2,1)}, bf16[2,2,192,128]{3,2,1,0:T(8,128)(2,1)}, u32[]{:S(2)}, u32[]{:S(2)}) collective-permute-start(bf16[2,2,192,128]{3,2,1,0:T(8,128)(2,1)} %bitcast.447), channel_id=1, source_target_pairs={{0,3},{4,7},{1,0},{5,4},{2,1},{6,5},{3,2},{7,6},{8,11},{12,15},{9,... | collective-permute-start | bytes 589832 | tf_op jit(solution)/shard_map/ppermute | solution.py:87
  350.4 195.0 %reduce-scatter.6.cloned.1.call-start = ((), (), s32[]{:S(2)}) async-start(), calls=%async_computation.6 | async-start | bytes 5242880 | tf_op jit(solution)/shard_map/reduce_scatter | solution.py:194
  360.4 13.4 %collective-permute-start.44 = (bf16[2,208,128]{2,1,0:T(8,128)(2,1)}, bf16[2,208,128]{2,1,0:T(8,128)(2,1)S(1)}, u32[]{:S(2)}, u32[]{:S(2)}) collective-permute-start(bf16[2,208,128]{2,1,0:T(8,128)(2,1)} %scan.6), channel_id=1, source_target_pairs={{0,16},{1,17},{2,18},{3,19},{4,20},{5,21},{6,22},{7,23},{8,24},{9,... | collective-permute-start | bytes 319496 | tf_op jit(solution)/shard_map/ppermute | solution.py:907
  398.9 25.3 %collective-permute-start.47 = (bf16[2,2,192,128]{3,2,1,0:T(8,128)(2,1)}, bf16[2,2,192,128]{3,2,1,0:T(8,128)(2,1)S(1)}, u32[]{:S(2)}, u32[]{:S(2)}) collective-permute-start(bf16[2,2,192,128]{3,2,1,0:T(8,128)(2,1)} %get-tuple-element.234), channel_id=1, source_target_pairs={{0,1},{4,5},{1,2},{5,6},{2,3},{6,7},{3,0},{7,4},{8,9},{12,13},{9,1... | collective-permute-start | bytes 589832 | tf_op jit(solution)/shard_map/ppermute | solution.py:87
  399.9 24.4 %collective-permute-start.48 = (bf16[2,2,192,128]{3,2,1,0:T(8,128)(2,1)}, bf16[2,2,192,128]{3,2,1,0:T(8,128)(2,1)S(1)}, u32[]{:S(2)}, u32[]{:S(2)}) collective-permute-start(bf16[2,2,192,128]{3,2,1,0:T(8,128)(2,1)} %get-tuple-element.235), channel_id=1, source_target_pairs={{0,2},{4,6},{1,3},{5,7},{2,0},{6,4},{3,1},{7,5},{8,10},{12,14},{9,... | collective-permute-start | bytes 589832 | tf_op jit(solution)/shard_map/ppermute | solution.py:87
  401.1 23.1 %collective-permute-start.49 = (bf16[2,2,192,128]{3,2,1,0:T(8,128)(2,1)}, bf16[2,2,192,128]{3,2,1,0:T(8,128)(2,1)S(1)}, u32[]{:S(2)}, u32[]{:S(2)}) collective-permute-start(bf16[2,2,192,128]{3,2,1,0:T(8,128)(2,1)} %get-tuple-element.236), channel_id=1, source_target_pairs={{0,3},{4,7},{1,0},{5,4},{2,1},{6,5},{3,2},{7,6},{8,11},{12,15},{9,... | collective-permute-start | bytes 589832 | tf_op jit(solution)/shard_map/ppermute | solution.py:87
  424.0 204.1 %reduce-scatter.8.cloned.1.call-start = ((), (), s32[]{:S(2)}) async-start(), calls=%async_computation.7 | async-start | bytes 3276800 | tf_op jit(solution)/shard_map/reduce_scatter | solution.py:221
  428.1 66.7 %collective-permute-start.51 = (bf16[2,2,4,192,128]{4,3,2,1,0:T(8,128)(2,1)}, bf16[2,2,4,192,128]{4,3,2,1,0:T(8,128)(2,1)}, u32[]{:S(2)}, u32[]{:S(2)}) collective-permute-start(bf16[2,2,4,192,128]{4,3,2,1,0:T(8,128)(2,1)} %dynamic-slice_bitcast_fusion.2), channel_id=1, source_target_pairs={{0,8},{4,12},{1,9},{5,13},{2,10},{6,14},{3,11},{7,15},{8,0},{12,4}... | collective-permute-start | bytes 2359304 | tf_op jit(solution)/shard_map/ppermute | solution.py:87
  442.5 54.7 %collective-permute-start.50 = (bf16[2,2,4,192,128]{4,3,2,1,0:T(8,128)(2,1)}, bf16[2,2,4,192,128]{4,3,2,1,0:T(8,128)(2,1)}, u32[]{:S(2)}, u32[]{:S(2)}) collective-permute-start(bf16[2,2,4,192,128]{4,3,2,1,0:T(8,128)(2,1)} %dynamic-slice_bitcast_fusion.3), channel_id=1, source_target_pairs={{0,16},{4,20},{1,17},{5,21},{2,18},{6,22},{3,19},{7,23},{8,24},{12... | collective-permute-start | bytes 2359304 | tf_op jit(solution)/shard_map/ppermute | solution.py:87
  524.3 20.9 %collective-permute-start.58 = (bf16[2,2,4,32,896]{4,3,2,1,0:T(8,128)(2,1)S(1)}, bf16[2,2,4,32,896]{4,3,2,1,0:T(8,128)(2,1)S(1)}, u32[]{:S(2)}, u32[]{:S(2)}) collective-permute-start(bf16[2,2,4,32,896]{4,3,2,1,0:T(8,128)(2,1)S(1)} %fusion.20), channel_id=1, source_target_pairs={{0,8},{4,12},{1,9},{5,13},{2,10},{6,14},{3,11},{7,15},{8,0},{12,4}... | collective-permute-start | bytes 2752520 | tf_op jit(solution)/shard_map/ppermute | solution.py:87
  527.2 14.1 %collective-permute-start.56 = (bf16[384,256]{1,0:T(8,128)(2,1)S(1)}, bf16[384,256]{1,0:T(8,128)(2,1)S(1)}, u32[]{:S(2)}, u32[]{:S(2)}) collective-permute-start(bf16[384,256]{1,0:T(8,128)(2,1)S(1)} %pad_maximum_fusion.17), channel_id=1, source_target_pairs={{0,2},{4,6},{1,3},{5,7},{2,0},{6,4},{3,1},{7,5},{8,10},{12,14},{9,... | collective-permute-start | bytes 589832 | tf_op jit(solution)/shard_map/ppermute | solution.py:87
  551.2 20.3 %collective-permute-start.68 = (f32[3,12]{1,0:T(4,128)S(1)}, f32[3,12]{1,0:T(4,128)}, u32[]{:S(2)}, u32[]{:S(2)}) collective-permute-start(f32[3,12]{1,0:T(4,128)S(1)} %copy-done.84), channel_id=1, source_target_pairs={{0,8},{4,12},{1,9},{5,13},{2,10},{6,14},{3,11},{7,15},{8,0},{12,4}... | collective-permute-start | bytes 440 | tf_op jit(solution)/shard_map/ppermute | solution.py:265
  553.2 19.0 %collective-permute-start.63 = (bf16[2,4,32,896]{3,2,1,0:T(8,128)(2,1)}, bf16[2,4,32,896]{3,2,1,0:T(8,128)(2,1)}, u32[]{:S(2)}, u32[]{:S(2)}) collective-permute-start(bf16[2,4,32,896]{3,2,1,0:T(8,128)(2,1)} %fusion.24), channel_id=1, source_target_pairs={{0,16},{4,20},{1,17},{5,21},{2,18},{6,22},{3,19},{7,23},{8,24},{12... | collective-permute-start | bytes 1376264 | tf_op jit(solution)/shard_map/ppermute | solution.py:87
  575.5 16.7 %collective-permute-start.66 = (bf16[64,896]{1,0:T(8,128)(2,1)S(1)}, bf16[64,896]{1,0:T(8,128)(2,1)S(1)}, u32[]{:S(2)}, u32[]{:S(2)}) collective-permute-start(bf16[64,896]{1,0:T(8,128)(2,1)S(1)} %bitcast.426), channel_id=1, source_target_pairs={{0,2},{4,6},{1,3},{5,7},{2,0},{6,4},{3,1},{7,5},{8,10},{12,14},{9,... | collective-permute-start | bytes 344072 | tf_op jit(solution)/shard_map/ppermute | solution.py:87
  577.8 14.5 %collective-permute-start.67 = (bf16[64,896]{1,0:T(8,128)(2,1)S(1)}, bf16[64,896]{1,0:T(8,128)(2,1)S(1)}, u32[]{:S(2)}, u32[]{:S(2)}) collective-permute-start(bf16[64,896]{1,0:T(8,128)(2,1)S(1)} %bitcast.425), channel_id=1, source_target_pairs={{0,3},{4,7},{1,0},{5,4},{2,1},{6,5},{3,2},{7,6},{8,11},{12,15},{9,... | collective-permute-start | bytes 344072 | tf_op jit(solution)/shard_map/ppermute | solution.py:87
  578.7 16.5 %collective-permute-start.64 = (bf16[2,2,4,32,512]{4,3,2,1,0:T(8,128)(2,1)S(1)}, bf16[2,2,4,32,512]{4,3,2,1,0:T(8,128)(2,1)S(1)}, u32[]{:S(2)}, u32[]{:S(2)}) collective-permute-start(bf16[2,2,4,32,512]{4,3,2,1,0:T(8,128)(2,1)S(1)} %fusion.23), channel_id=1, source_target_pairs={{0,16},{4,20},{1,17},{5,21},{2,18},{6,22},{3,19},{7,23},{8,24},{12... | collective-permute-start | bytes 1572872 | tf_op jit(solution)/shard_map/ppermute | solution.py:87
  580.5 12.9 %collective-permute-start.62 = (bf16[2,3,1024]{2,1,0:T(4,128)(2,1)S(1)}, bf16[2,3,1024]{2,1,0:T(4,128)(2,1)S(1)}, u32[]{:S(2)}, u32[]{:S(2)}) collective-permute-start(bf16[2,3,1024]{2,1,0:T(4,128)(2,1)S(1)} %slice.826), channel_id=1, source_target_pairs={{1,0},{2,1},{3,2},{4,3},{5,4},{6,5},{7,6},{8,7},{9,8},{10,9},{11,1... | collective-permute-start | bytes 36872 | tf_op jit(solution)/shard_map/ppermute | solution.py:1436
  605.8 13.3 %collective-permute-start.77 = (f32[3,12]{1,0:T(4,128)S(1)}, f32[3,12]{1,0:T(4,128)S(1)}, u32[]{:S(2)}, u32[]{:S(2)}) collective-permute-start(f32[3,12]{1,0:T(4,128)S(1)} %add.506), channel_id=1, source_target_pairs={{0,4},{4,0},{1,5},{5,1},{2,6},{6,2},{3,7},{7,3},{8,12},{12,8},{9,1... | collective-permute-start | bytes 440 | tf_op jit(solution)/shard_map/ppermute | solution.py:87
  605.9 13.3 %collective-permute-start.71 = (bf16[64,512]{1,0:T(8,128)(2,1)S(1)}, bf16[64,512]{1,0:T(8,128)(2,1)S(1)}, u32[]{:S(2)}, u32[]{:S(2)}) collective-permute-start(bf16[64,512]{1,0:T(8,128)(2,1)S(1)} %bitcast.430), channel_id=1, source_target_pairs={{0,1},{4,5},{1,2},{5,6},{2,3},{6,7},{3,0},{7,4},{8,9},{12,13},{9,1... | collective-permute-start | bytes 196616 | tf_op jit(solution)/shard_map/ppermute | solution.py:87
  (155 other events, 1555.6 us)
Sparse Core Ops, SparseCore 0:
  11.5 106.5 all-gather.2
  159.0 117.2 all-gather.4
  349.9 78.2 reduce-scatter.3
  431.1 84.2 reduce-scatter.5
  550.7 59.9 reduce-scatter.7
